TPU v7x, 32 devices: a whole 2x2x4 slice. The times are simulated.
32 devices in a mesh: dp: 8 (over y, x, core), expert: 4 (over z).
Axes of the slice: x: 2, y: 2, z: 4, core: 2. Of those that a mesh axis runs over, the one named last changes fastest.
Arguments:
- tokens: bfloat16 [8192, 1536], P(('dp', 'expert')), may hold values from -6 to 6
- segment_ids: int32 [32, 256], P(('dp', 'expert')), may hold values from 0 to 3, never falling along the last dimension, each value on 1 to 192 neighbouring positions
- expert_choices: int32 [8192, 8], P(('dp', 'expert')), may hold values from 0 to 19, all different within a row; in each aligned block of 256 rows (0 to 255, 256 to 511, ...) at most 116 rows name the same one
- attn_gain: bfloat16 [1536], P('dp'), may hold values from 0.099609375 to 1.8984375
- query_weight: bfloat16 [1536, 1536], P('dp'), may hold values from -0.15625 to 0.15625
- key_weight: bfloat16 [1536, 512], P('dp'), may hold values from -0.15625 to 0.15625
- value_weight: bfloat16 [1536, 512], P('dp'), may hold values from -0.15625 to 0.15625
- output_weight: bfloat16 [1536, 1536], P('dp'), may hold values from -0.625 to 0.625
- ffn_gain: bfloat16 [1536], P('dp'), may hold values from 0.099609375 to 1.8984375
- router_weight: bfloat16 [1536, 20], P('dp'), may hold values from -0.078125 to 0.078125
- expert_gate: bfloat16 [20, 1536, 512], P('expert', 'dp'), may hold values from -0.15625 to 0.15625
- expert_up: bfloat16 [20, 1536, 512], P('expert', 'dp'), may hold values from -0.15625 to 0.15625
- expert_down: bfloat16 [20, 512, 1536], P('expert', None, 'dp'), may hold values from -1.5 to 1.5
- cotangent: bfloat16 [8192, 1536], P(('dp', 'expert')), may hold values from -6 to 6
Outputs:
- mixed: bfloat16 [8192, 1536], P(('dp', 'expert'))
- grad_tokens: float32 [8192, 1536], P(('dp', 'expert'))
- grad_attn_gain: float32 [1536], P('dp')
- grad_query: float32 [1536, 1536], P('dp')
- grad_key: float32 [1536, 512], P('dp')
- grad_value: float32 [1536, 512], P('dp')
- grad_output: float32 [1536, 1536], P('dp')
- grad_ffn_gain: float32 [1536], P('dp')
- grad_router: float32 [1536, 20], P('dp')
- grad_expert_gate: float32 [20, 1536, 512], P('expert', 'dp')
- grad_expert_up: float32 [20, 1536, 512], P('expert', 'dp')
- grad_expert_down: float32 [20, 512, 1536], P('expert', None, 'dp')
Inputs may be any that keep to these rules, and one draw needn't show every extreme that they name: `expert_choices`: each row names 8 different experts. Within the 256 tokens of one sequence no expert is named more than 116 times, a bound that some block reaches. `segment_ids`: within a sequence the numbers never fall; a document is a run of equal numbers of at most 192 tokens, one of them exactly 192.
All inputs are finite; a program needn't handle non-finite values.
Results may differ from a plain program's by a relative error of at most 0.02.
Values may be sent and summed in bfloat16 or wider, within the bound.
No kernel may reach another device: no remote copies, remote signals or barrier semaphores. Data moves between devices by JAX's collectives and lax.ppermute only.
A program may use at most 192 MiB of HBM per device.

v0:
```python
import jax
import jax.numpy as jnp
from jax import lax
from jax.sharding import PartitionSpec as P

HEADS = 24
KV_HEADS = 8
HEAD_DIM = 64
TOP = 8


norm_eps = 1e-06
masked_score = -1e30


def normalize_rows(values, gain):
    factor = lax.rsqrt(jnp.mean(values * values, axis=-1, keepdims=True) + norm_eps)
    normed = values * factor
    return (normed, factor, normed * gain)


def norm_backward(upstream, normed, factor, gain):
    scaled = upstream * gain
    inward = factor * (scaled - normed * jnp.mean(scaled * normed, axis=-1, keepdims=True))
    return (inward, jnp.sum(upstream * normed, axis=0))


def block_scores(queries, key_rows, doc_ids, row_start):
    block_len = queries.shape[0]
    scores = jnp.einsum(
        "qkgd,tkd->kgqt", queries, key_rows, preferred_element_type=jnp.float32
    ) * HEAD_DIM ** (-0.5)
    query_pos = row_start + jnp.arange(block_len, dtype=jnp.int32)
    key_pos = jnp.arange(key_rows.shape[0], dtype=jnp.int32)
    allowed = (doc_ids[:, None] == doc_ids[None, :]) & (query_pos[:, None] >= key_pos[None, :])
    return jnp.where(allowed, scores, masked_score)


def expert_hidden(row_block, gate_w, up_w):
    gate_pre = jnp.einsum("lscd,ldf->lscf", row_block, gate_w, preferred_element_type=jnp.float32)
    up_pre = jnp.einsum("lscd,ldf->lscf", row_block, up_w, preferred_element_type=jnp.float32)
    hidden = (gate_pre * jax.nn.sigmoid(gate_pre) * up_pre).astype(jnp.bfloat16)
    return (gate_pre, up_pre, hidden)


def body(
    tokens,
    segment_ids,
    expert_choices,
    attn_gain,
    query_weight,
    key_weight,
    value_weight,
    output_weight,
    ffn_gain,
    router_weight,
    expert_gate,
    expert_up,
    expert_down,
    cotangent,
):
    weights_one = (
        lax.all_gather(attn_gain, "dp", axis=0, tiled=True),
        lax.all_gather(query_weight, "dp", axis=0, tiled=True),
        lax.all_gather(key_weight, "dp", axis=0, tiled=True),
        lax.all_gather(value_weight, "dp", axis=0, tiled=True),
        lax.all_gather(output_weight, "dp", axis=0, tiled=True),
        lax.all_gather(ffn_gain, "dp", axis=0, tiled=True),
        lax.all_gather(router_weight, "dp", axis=0, tiled=True),
    )
    experts_one = (
        lax.all_gather(expert_gate, "dp", axis=1, tiled=True),
        lax.all_gather(expert_up, "dp", axis=1, tiled=True),
        lax.all_gather(expert_down, "dp", axis=2, tiled=True),
    )
    gain_one, w_query, w_key, w_value, w_output, gain_two, w_router = weights_one
    gate_w, up_w, down_w = experts_one
    seq_len = tokens.shape[0]
    width = tokens.shape[1]
    groups = HEADS // KV_HEADS
    per_owner = expert_gate.shape[0]
    owners = lax.axis_size("expert")
    expert_count = per_owner * owners
    capacity = (seq_len * TOP * 9 + 8 * expert_count - 1) // (8 * expert_count)
    block_len = min(512, seq_len)
    score_scale = HEAD_DIM ** (-0.5)
    doc_ids = segment_ids[0]
    inputs = tokens.astype(jnp.float32)
    normed_one, factor_one, scaled_one = normalize_rows(inputs, gain_one.astype(jnp.float32))
    low_one = scaled_one.astype(jnp.bfloat16)
    queries = (
        jnp.dot(low_one, w_query, preferred_element_type=jnp.float32)
        .astype(jnp.bfloat16)
        .reshape(seq_len, KV_HEADS, groups, HEAD_DIM)
    )
    key_rows = (
        jnp.dot(low_one, w_key, preferred_element_type=jnp.float32)
        .astype(jnp.bfloat16)
        .reshape(seq_len, KV_HEADS, HEAD_DIM)
    )
    value_rows = (
        jnp.dot(low_one, w_value, preferred_element_type=jnp.float32)
        .astype(jnp.bfloat16)
        .reshape(seq_len, KV_HEADS, HEAD_DIM)
    )
    row_start = 0
    scores = block_scores(queries, key_rows, doc_ids, row_start)
    top_score = jnp.max(scores, axis=-1, keepdims=True)
    shifted = jnp.exp(scores - top_score)
    summed = jnp.sum(shifted, axis=-1, keepdims=True)
    totals = [top_score + jnp.log(summed)]
    low_weights = (shifted / summed).astype(jnp.bfloat16)
    contexts = jnp.einsum(
        "kgqt,tkd->qkgd", low_weights, value_rows, preferred_element_type=jnp.float32
    ).astype(jnp.bfloat16)
    context = contexts.reshape(seq_len, HEADS * HEAD_DIM)
    mixed_one = inputs + jnp.dot(context, w_output, preferred_element_type=jnp.float32)
    normed_two, factor_two, scaled_two = normalize_rows(mixed_one, gain_two.astype(jnp.float32))
    low_two = scaled_two.astype(jnp.bfloat16)
    logits = jnp.dot(low_two, w_router, preferred_element_type=jnp.float32)
    choice_hot = (
        expert_choices[:, :, None] == jnp.arange(expert_count, dtype=jnp.int32)[None, None, :]
    )
    chosen = jnp.sum(jnp.where(choice_hot, logits[:, None, :], 0.0), axis=2)
    chosen_top = jnp.max(chosen, axis=-1, keepdims=True)
    chosen_exp = jnp.exp(chosen - chosen_top)
    gate_probs = chosen_exp / jnp.sum(chosen_exp, axis=-1, keepdims=True)
    flat_experts = expert_choices.reshape(-1)
    pair_hot = choice_hot.reshape(seq_len * TOP, expert_count).astype(jnp.int32)
    earlier = jnp.cumsum(pair_hot, axis=0) - pair_hot
    slot_idx = jnp.sum(earlier * pair_hot, axis=1)
    local_idx = flat_experts % per_owner
    owner_idx = flat_experts // per_owner
    send_rows = (
        jnp.zeros((per_owner, owners, capacity, width), jnp.bfloat16)
        .at[local_idx, owner_idx, slot_idx]
        .set(jnp.repeat(low_two, TOP, axis=0))
    )
    row_block = lax.all_to_all(send_rows, "expert", split_axis=1, concat_axis=1, tiled=True)
    gate_pre, up_pre, hidden = expert_hidden(row_block, gate_w, up_w)
    produced = jnp.einsum(
        "lscf,lfd->lscd", hidden, down_w, preferred_element_type=jnp.float32
    ).astype(jnp.bfloat16)
    returned = lax.all_to_all(produced, "expert", split_axis=1, concat_axis=1, tiled=True)
    returned_rows = returned[local_idx, owner_idx, slot_idx].reshape(seq_len, TOP, width)
    combined = jnp.einsum(
        "st,std->sd", gate_probs, returned_rows, preferred_element_type=jnp.float32
    )
    mixed = (mixed_one + combined).astype(jnp.bfloat16)
    weights_two = (
        lax.all_gather(attn_gain, "dp", axis=0, tiled=True),
        lax.all_gather(query_weight, "dp", axis=0, tiled=True),
        lax.all_gather(key_weight, "dp", axis=0, tiled=True),
        lax.all_gather(value_weight, "dp", axis=0, tiled=True),
        lax.all_gather(output_weight, "dp", axis=0, tiled=True),
        lax.all_gather(ffn_gain, "dp", axis=0, tiled=True),
        lax.all_gather(router_weight, "dp", axis=0, tiled=True),
    )
    experts_two = (
        lax.all_gather(expert_gate, "dp", axis=1, tiled=True),
        lax.all_gather(expert_up, "dp", axis=1, tiled=True),
        lax.all_gather(expert_down, "dp", axis=2, tiled=True),
    )
    gain_one_b, query_back, key_back, value_back, output_back, gain_two_b, router_back = weights_two
    gate_back, up_back, down_back = experts_two
    grad_out = cotangent.astype(jnp.float32)
    gate_grad = jnp.einsum(
        "sd,std->st", grad_out, returned_rows, preferred_element_type=jnp.float32
    )
    pair_grad = (
        (gate_probs[:, :, None] * grad_out[:, None, :])
        .astype(jnp.bfloat16)
        .reshape(seq_len * TOP, width)
    )
    grad_send = jnp.zeros_like(send_rows).at[local_idx, owner_idx, slot_idx].set(pair_grad)
    grad_arrived = lax.all_to_all(grad_send, "expert", split_axis=1, concat_axis=1, tiled=True)
    gate_pre, up_pre, hidden = expert_hidden(row_block, gate_back, up_back)
    grad_hidden = jnp.einsum(
        "lscd,lfd->lscf", grad_arrived, down_back, preferred_element_type=jnp.float32
    )
    sigmoid_gate = jax.nn.sigmoid(gate_pre)
    grad_gate_pre = (
        grad_hidden * up_pre * sigmoid_gate * (1.0 + gate_pre * (1.0 - sigmoid_gate))
    ).astype(jnp.bfloat16)
    grad_up_pre = (grad_hidden * gate_pre * sigmoid_gate).astype(jnp.bfloat16)
    grad_rows = jnp.einsum(
        "lscf,ldf->lscd", grad_gate_pre, gate_back, preferred_element_type=jnp.float32
    )
    grad_rows = (
        grad_rows
        + jnp.einsum("lscf,ldf->lscd", grad_up_pre, up_back, preferred_element_type=jnp.float32)
    ).astype(jnp.bfloat16)
    grad_returned = lax.all_to_all(grad_rows, "expert", split_axis=1, concat_axis=1, tiled=True)
    grad_two = jnp.sum(
        grad_returned[local_idx, owner_idx, slot_idx]
        .reshape(seq_len, TOP, width)
        .astype(jnp.float32),
        axis=1,
    )
    weighted = jnp.sum(gate_grad * gate_probs, axis=1, keepdims=True)
    chosen_grad = gate_probs * (gate_grad - weighted)
    logit_grad = jnp.sum(jnp.where(choice_hot, chosen_grad[:, :, None], 0.0), axis=1).astype(
        jnp.bfloat16
    )
    grad_router = jnp.einsum("sd,se->de", low_two, logit_grad, preferred_element_type=jnp.float32)
    grad_two = grad_two + jnp.einsum(
        "se,de->sd", logit_grad, router_back, preferred_element_type=jnp.float32
    )
    inward_two, grad_gain_two = norm_backward(
        grad_two, normed_two, factor_two, gain_two_b.astype(jnp.float32)
    )
    grad_mixed = grad_out + inward_two
    grad_attn = grad_mixed.astype(jnp.bfloat16)
    grad_output = jnp.einsum("sh,sd->hd", context, grad_attn, preferred_element_type=jnp.float32)
    grad_context = (
        jnp.einsum("sd,hd->sh", grad_attn, output_back, preferred_element_type=jnp.float32)
        .astype(jnp.bfloat16)
        .reshape(seq_len, KV_HEADS, groups, HEAD_DIM)
    )
    key_grad = jnp.zeros((seq_len, KV_HEADS, HEAD_DIM), jnp.float32)
    value_grad = jnp.zeros((seq_len, KV_HEADS, HEAD_DIM), jnp.float32)
    query_grads = []
    for block_number, row_start in enumerate(range(0, seq_len, block_len)):
        scores = block_scores(queries, key_rows, doc_ids, row_start)
        weights = jnp.exp(scores - totals[block_number])
        low_weights = weights.astype(jnp.bfloat16)
        value_grad = jnp.einsum(
            "kgqt,qkgd->tkd", low_weights, grad_context, preferred_element_type=jnp.float32
        )
        weight_grad = jnp.einsum(
            "qkgd,tkd->kgqt", grad_context, value_rows, preferred_element_type=jnp.float32
        )
        score_grad = (
            weights * (weight_grad - jnp.sum(weight_grad * weights, axis=-1, keepdims=True))
        ).astype(jnp.bfloat16)
        query_grads.append(
            (
                jnp.einsum(
                    "kgqt,tkd->qkgd", score_grad, key_rows, preferred_element_type=jnp.float32
                )
                * score_scale
            ).astype(jnp.bfloat16)
        )
        key_grad = (
            jnp.einsum("kgqt,qkgd->tkd", score_grad, queries, preferred_element_type=jnp.float32)
            * score_scale
        )
    query_low = query_grads[0].reshape(seq_len, HEADS * HEAD_DIM)
    key_low = key_grad.astype(jnp.bfloat16).reshape(seq_len, KV_HEADS * HEAD_DIM)
    value_low = value_grad.astype(jnp.bfloat16).reshape(seq_len, KV_HEADS * HEAD_DIM)
    grad_query = jnp.einsum("sd,sh->dh", low_one, query_low, preferred_element_type=jnp.float32)
    grad_key = jnp.einsum("sd,sh->dh", low_one, key_low, preferred_element_type=jnp.float32)
    grad_value = jnp.einsum("sd,sh->dh", low_one, value_low, preferred_element_type=jnp.float32)
    grad_one = jnp.einsum("sh,dh->sd", query_low, query_back, preferred_element_type=jnp.float32)
    grad_one = grad_one + jnp.einsum(
        "sh,dh->sd", key_low, key_back, preferred_element_type=jnp.float32
    )
    grad_one = grad_one + jnp.einsum(
        "sh,dh->sd", value_low, value_back, preferred_element_type=jnp.float32
    )
    inward_one, grad_gain_one = norm_backward(
        grad_one, normed_one, factor_one, gain_one_b.astype(jnp.float32)
    )
    grad_tokens = grad_mixed + inward_one
    mixer_shares = (
        lax.psum_scatter(
            grad_gain_one.astype(jnp.bfloat16), "dp", scatter_dimension=0, tiled=True
        ).astype(jnp.float32),
        lax.psum_scatter(
            grad_query.astype(jnp.bfloat16), "dp", scatter_dimension=0, tiled=True
        ).astype(jnp.float32),
        lax.psum_scatter(
            grad_key.astype(jnp.bfloat16), "dp", scatter_dimension=0, tiled=True
        ).astype(jnp.float32),
        lax.psum_scatter(
            grad_value.astype(jnp.bfloat16), "dp", scatter_dimension=0, tiled=True
        ).astype(jnp.float32),
        lax.psum_scatter(
            grad_output.astype(jnp.bfloat16), "dp", scatter_dimension=0, tiled=True
        ).astype(jnp.float32),
        lax.psum_scatter(
            grad_gain_two.astype(jnp.bfloat16), "dp", scatter_dimension=0, tiled=True
        ).astype(jnp.float32),
        lax.psum_scatter(
            grad_router.astype(jnp.bfloat16), "dp", scatter_dimension=0, tiled=True
        ).astype(jnp.float32),
    )
    mixer_totals = (
        lax.psum(mixer_shares[0].astype(jnp.bfloat16), "expert").astype(jnp.float32),
        lax.psum(mixer_shares[1].astype(jnp.bfloat16), "expert").astype(jnp.float32),
        lax.psum(mixer_shares[2].astype(jnp.bfloat16), "expert").astype(jnp.float32),
        lax.psum(mixer_shares[3].astype(jnp.bfloat16), "expert").astype(jnp.float32),
        lax.psum(mixer_shares[4].astype(jnp.bfloat16), "expert").astype(jnp.float32),
        lax.psum(mixer_shares[5].astype(jnp.bfloat16), "expert").astype(jnp.float32),
        lax.psum(mixer_shares[6].astype(jnp.bfloat16), "expert").astype(jnp.float32),
    )
    grad_down = jnp.einsum(
        "lscf,lscd->lfd", hidden, grad_arrived, preferred_element_type=jnp.float32
    )
    grad_gate = jnp.einsum(
        "lscd,lscf->ldf", row_block, grad_gate_pre, preferred_element_type=jnp.float32
    )
    grad_up = jnp.einsum(
        "lscd,lscf->ldf", row_block, grad_up_pre, preferred_element_type=jnp.float32
    )
    total_gate, total_up, total_down = (
        lax.psum_scatter(
            grad_gate.astype(jnp.bfloat16), "dp", scatter_dimension=1, tiled=True
        ).astype(jnp.float32),
        lax.psum_scatter(
            grad_up.astype(jnp.bfloat16), "dp", scatter_dimension=1, tiled=True
        ).astype(jnp.float32),
        lax.psum_scatter(
            grad_down.astype(jnp.bfloat16), "dp", scatter_dimension=2, tiled=True
        ).astype(jnp.float32),
    )
    (
        total_gain_one,
        total_query,
        total_key,
        total_value,
        total_output,
        total_gain_two,
        total_router,
    ) = mixer_totals
    return (
        mixed,
        grad_tokens,
        total_gain_one,
        total_query,
        total_key,
        total_value,
        total_output,
        total_gain_two,
        total_router,
        total_gate,
        total_up,
        total_down,
    )


def solution(mesh):
    return jax.shard_map(
        body,
        mesh=mesh,
        in_specs=(
            P(("dp", "expert"), None),
            P(("dp", "expert"), None),
            P(("dp", "expert"), None),
            P("dp"),
            P("dp", None),
            P("dp", None),
            P("dp", None),
            P("dp", None),
            P("dp"),
            P("dp", None),
            P("expert", "dp", None),
            P("expert", "dp", None),
            P("expert", None, "dp"),
            P(("dp", "expert"), None),
        ),
        out_specs=(
            P(("dp", "expert"), None),
            P(("dp", "expert"), None),
            P("dp"),
            P("dp", None),
            P("dp", None),
            P("dp", None),
            P("dp", None),
            P("dp"),
            P("dp", None),
            P("expert", "dp", None),
            P("expert", "dp", None),
            P("expert", None, "dp"),
        ),
        check_vma=False,
    )
```

profile of v0, /device:TPU:0, one launch (start us, length us, event | category | flops | bytes accessed | tf_op | source)
XLA Modules:
  0.0 1611.2 jit_solution(7887153683440506345)
XLA Ops:
  16.0 15.5 all-reduce.5
  43.2 23.0 %all-gather.9.cloned.1.call-done = bf16[1536,512]{1,0:T(8,128)(2,1)} async-done(((bf16[192,512]{1,0:T(8,128)(2,1)}), bf16[1536,512]{1,0:T(8,128)(2,1)}) %all-gather.9.cloned.1.call-update) | async-done | bytes 1572880 | tf_op jit(solution)/shard_map/all_gather | solution.py:66
  68.4 38.7 %all-gather.13.cloned.1.call-done = bf16[1536,1536]{1,0:T(8,128)(2,1)} async-done(((bf16[192,1536]{1,0:T(8,128)(2,1)}), bf16[1536,1536]{1,0:T(8,128)(2,1)}) %all-gather.13.cloned.1.call-update) | async-done | bytes 4718608 | tf_op jit(solution)/shard_map/all_gather | solution.py:64
  116.1 31.7 %all-gather.15.cloned.1.call-done = bf16[1536,1536]{1,0:T(8,128)(2,1)} async-done(((bf16[192,1536]{1,0:T(8,128)(2,1)}), bf16[1536,1536]{1,0:T(8,128)(2,1)}) %all-gather.15.cloned.1.call-update) | async-done | bytes 4718608 | tf_op jit(solution)/shard_map/all_gather | solution.py:67
  152.9 14.5 scatter_custom_fusion
  167.4 12.6 reshape.262
  201.7 153.2 %all-to-all-done = bf16[5,4,116,1536]{3,2,0,1:T(8,128)(2,1)} async-done(((bf16[5,4,116,1536]{3,2,0,1:T(8,128)(2,1)}), bf16[5,4,116,1536]{3,2,0,1:T(8,128)(2,1)}, u32[]{:S(2)}, u32[]{:S(2)}) %all-to-all-start) | async-done | bytes 7127072 | tf_op jit(solution)/shard_map/all_to_all | solution.py:139
  354.9 11.6 fusion.7
  366.5 13.1 multiply_convert_fusion.2
  402.2 21.0 %all-gather = bf16[8,192,20]{1,2,0:T(8,128)(2,1)S(1)} all-gather(bf16[1,192,20]{1,2,0:T(8,128)(2,1)S(1)} %bitcast.205), channel_id=1, replica_groups=mesh['dp'=8,'expert'=4] {'dp'}, dimensions={0}, use_global_device_ids=true | all-gather | bytes 69120 | tf_op jit(solution)/shard_map/all_gather | solution.py:69
  424.0 139.4 %all-to-all-done.1 = bf16[5,4,116,1536]{3,2,0,1:T(8,128)(2,1)} async-done(((bf16[5,4,116,1536]{3,2,0,1:T(8,128)(2,1)}), bf16[5,4,116,1536]{3,2,0,1:T(8,128)(2,1)}, u32[]{:S(2)}, u32[]{:S(2)}) %all-to-all-start.1) | async-done | bytes 7127072 | tf_op jit(solution)/shard_map/all_to_all | solution.py:144
  573.0 48.3 %gather_fusion = bf16[2048,1536]{1,0:T(8,128)(2,1)} fusion(bf16[5,4,116,1536]{3,1,2,0:T(4,128)(2,1)} %copy.110, s32[2048]{0:T(1024)S(1)} %bitcast.176), kind=kCustom, calls=%fused_computation | custom fusion | bytes 12607488 | tf_op jit(solution)/shard_map/gather | solution.py:145
  627.8 15.0 scatter_custom_fusion.1
  642.8 12.5 reshape.266
  659.7 165.0 %all_to_all.20 = bf16[5,4,116,1536]{3,2,0,1:T(8,128)(2,1)} all-to-all(bf16[5,4,116,1536]{3,2,0,1:T(8,128)(2,1)S(1)} %copy.112), channel_id=1, replica_groups=mesh['dp'=8,'expert'=4] {'expert'}, dimensions={1} | all-to-all | bytes 14254080 | tf_op jit(solution)/shard_map/all_to_all | solution.py:176
  824.8 12.1 multiply_convert_fusion.1
  836.9 11.6 fusion.1
  848.4 12.4 add_convert_fusion
  880.2 153.0 %all-to-all-done.3 = bf16[5,4,116,1536]{3,2,0,1:T(8,128)(2,1)} async-done(((bf16[5,4,116,1536]{3,2,0,1:T(8,128)(2,1)}), bf16[5,4,116,1536]{3,2,0,1:T(8,128)(2,1)}, u32[]{:S(2)}, u32[]{:S(2)}) %all-to-all-start.3) | async-done | bytes 7127072 | tf_op jit(solution)/shard_map/all_to_all | solution.py:193
  1042.9 48.5 %gather_fusion.1 = bf16[2048,1536]{1,0:T(8,128)(2,1)} fusion(bf16[5,4,116,1536]{3,1,2,0:T(4,128)(2,1)} %copy.115, s32[2048]{0:T(1024)S(1)} %bitcast.177), kind=kCustom, calls=%fused_computation.1 | custom fusion | bytes 12607488 | tf_op jit(solution)/shard_map/gather | solution.py:195
  1135.8 11.3 bitcast_convert_fusion
  1147.4 11.4 bitcast_convert_fusion.2
  1158.9 11.7 bitcast_convert_fusion.1
  1177.2 12.6 reduce-scatter.13.cloned.1.call-done
  1189.8 57.4 %reduce-scatter.17.cloned.1.call-done = bf16[192,1536]{1,0:T(8,128)(2,1)} async-done(((bf16[1536,1536]{1,0:T(8,128)(2,1)}), bf16[192,1536]{1,0:T(8,128)(2,1)}) %reduce-scatter.17.cloned.1.call-update) | async-done | bytes 589840 | tf_op jit(solution)/shard_map/reduce_scatter | solution.py:278
  1247.2 57.6 %reduce-scatter.11.cloned.1.call-done = bf16[192,1536]{1,0:T(8,128)(2,1)} async-done(((bf16[1536,1536]{1,0:T(8,128)(2,1)}), bf16[192,1536]{1,0:T(8,128)(2,1)}) %reduce-scatter.11.cloned.1.call-update) | async-done | bytes 589840 | tf_op jit(solution)/shard_map/reduce_scatter | solution.py:269
  1309.6 13.0 all-reduce.4
  1322.7 18.8 %all-reduce.6 = (bf16[192]{0:T(256)(128)(2,1)S(1)}, bf16[192]{0:T(256)(128)(2,1)S(1)}, bf16[192,20]{0,1:T(8,128)(2,1)S(1)}) all-reduce(bf16[192]{0:T(256)(128)(2,1)S(1)} %dynamic-slice.3, bf16[192]{0:T(256)(128)(2,1)S(1)} %dynamic-slice.5, bf16[192,20]{0,1:T(8,128)(2,1)S(1)} %copy.141), channel_id=1, replica_groups=mesh['dp'=8,'expert'=4] {'expert'}, use_global_device_ids=true, to_apply=%region_20.21 | all-reduce | flops 4224 | bytes 16896 | tf_op jit(solution)/shard_map/psum | solution.py:289
  1346.2 31.5 %reduce-scatter.23.cloned.1.call-done = bf16[5,512,192]{1,2,0:T(8,128)(2,1)} async-done(((bf16[5,512,1536]{1,2,0:T(8,128)(2,1)}), bf16[5,512,192]{1,2,0:T(8,128)(2,1)}) %reduce-scatter.23.cloned.1.call-update) | async-done | bytes 983056 | tf_op jit(solution)/shard_map/reduce_scatter | solution.py:313
  1380.4 70.3 %reduce-scatter.19.cloned.1.call-done = bf16[5,192,512]{2,1,0:T(8,128)(2,1)} async-done(((bf16[5,1536,512]{2,1,0:T(8,128)(2,1)}), bf16[5,192,512]{2,1,0:T(8,128)(2,1)}) %reduce-scatter.19.cloned.1.call-update) | async-done | bytes 983056 | tf_op jit(solution)/shard_map/reduce_scatter | solution.py:307
  1453.5 70.0 %reduce-scatter.21.cloned.1.call-done = bf16[5,192,512]{2,1,0:T(8,128)(2,1)} async-done(((bf16[5,1536,512]{2,1,0:T(8,128)(2,1)}), bf16[5,192,512]{2,1,0:T(8,128)(2,1)}) %reduce-scatter.21.cloned.1.call-update) | async-done | bytes 983056 | tf_op jit(solution)/shard_map/reduce_scatter | solution.py:310
  1526.2 70.2 %all-reduce.10.cloned.1.call-done = (bf16[192,1536]{1,0:T(8,128)(2,1)}, bf16[192,512]{1,0:T(8,128)(2,1)}, bf16[192,512]{1,0:T(8,128)(2,1)}, bf16[192,1536]{1,0:T(8,128)(2,1)}) async-done(((bf16[192,1536]{1,0:T(8,128)(2,1)}, bf16[192,512]{1,0:T(8,128)(2,1)}, bf16[192,512]{1,0:T(8,128)(2,1)}, bf16[192,1536]{1,0:T(8,128)(2,1)}), (bf16[192,1536]{1,0:T(8,128)(2,1)}, bf16[192,512]{1,0:T(8,128)(2,1)}, ...) | async-done | bytes 1572880 | tf_op jit(solution)/shard_map/psum | solution.py:290
  (213 shorter events, 206.3 us)
Async XLA Ops:
  7.2 33.2 %copy-start.28 = (s32[3]{0:T(128)S(1)}, s32[3]{0:T(128)}, u32[]{:S(2)}) copy-start(s32[3]{0:T(128)} %constant.57) | copy-start | bytes 40
  7.2 33.3 %copy-start.29 = (s32[3]{0:T(128)S(1)}, s32[3]{0:T(128)}, u32[]{:S(2)}) copy-start(s32[3]{0:T(128)} %constant.60) | copy-start | bytes 40
  7.2 33.4 %copy-start.1 = (bf16[256,1536]{1,0:T(8,128)(2,1)S(1)}, bf16[256,1536]{1,0:T(8,128)(2,1)}, u32[]{:S(2)}) copy-start(bf16[256,1536]{1,0:T(8,128)(2,1)} %param.14) | copy-start | bytes 2359300
  7.2 33.7 %copy-start.27 = (s32[1,256]{1,0:T(1,128)S(1)}, s32[1,256]{1,0:T(1,128)}, u32[]{:S(2)}) copy-start(s32[1,256]{1,0:T(1,128)} %param.15) | copy-start | bytes 3076
  7.2 33.8 %all-gather.11.cloned.1.call-start = ((), (), s32[]{:S(2)}) async-start(), calls=%async_computation.13 | async-start | bytes 1769472 | tf_op jit(solution)/shard_map/all_gather | solution.py:65
  8.0 58.2 %all-gather.9.cloned.1.call-start = ((), (), s32[]{:S(2)}) async-start(), calls=%async_computation.12 | async-start | bytes 1769472 | tf_op jit(solution)/shard_map/all_gather | solution.py:66
  8.7 98.3 %all-gather.13.cloned.1.call-start = ((), (), s32[]{:S(2)}) async-start(), calls=%async_computation.14 | async-start | bytes 5308416 | tf_op jit(solution)/shard_map/all_gather | solution.py:64
  9.4 138.3 %all-gather.15.cloned.1.call-start = ((), (), s32[]{:S(2)}) async-start(), calls=%async_computation.15 | async-start | bytes 5308416 | tf_op jit(solution)/shard_map/all_gather | solution.py:67
  10.0 191.7 %all-gather.17.cloned.1.call-start = ((), (), s32[]{:S(2)}) async-start(), calls=%async_computation.16 | async-start | bytes 8847360 | tf_op jit(solution)/shard_map/all_gather | solution.py:72
  10.6 355.9 %all-gather.19.cloned.1.call-start = ((), (), s32[]{:S(2)}) async-start(), calls=%async_computation.17 | async-start | bytes 8847360 | tf_op jit(solution)/shard_map/all_gather | solution.py:73
  31.6 75.4 %copy-start.17 = (f32[1536]{0:T(1024)}, f32[1536]{0:T(1024)S(1)}, u32[]{:S(2)}) copy-start(f32[1536]{0:T(1024)S(1)} %convert_element_type.182) | copy-start | bytes 18436
  31.6 120.0 %copy-start.20 = (f32[1536]{0:T(1024)}, f32[1536]{0:T(1024)S(1)}, u32[]{:S(2)}) copy-start(f32[1536]{0:T(1024)S(1)} %convert_element_type.190) | copy-start | bytes 18436
  40.9 66.1 %copy-start.22 = (f32[256]{0:T(256)}, f32[256]{0:T(256)S(1)}, u32[]{:S(2)}) copy-start(f32[256]{0:T(256)S(1)} %add_rsqrt_fusion.1) | copy-start | bytes 3076
  43.2 67.9 %copy-start.14 = (bf16[256,512]{0,1:T(8,128)(2,1)}, bf16[256,512]{0,1:T(8,128)(2,1)S(1)}, u32[]{:S(2)}) copy-start(bf16[256,512]{0,1:T(8,128)(2,1)S(1)} %copy.95) | copy-start | bytes 786436
  68.3 45.0 %copy-start.16 = (bf16[256,512]{0,1:T(8,128)(2,1)}, bf16[256,512]{0,1:T(8,128)(2,1)S(1)}, u32[]{:S(2)}) copy-start(bf16[256,512]{0,1:T(8,128)(2,1)S(1)} %copy.94) | copy-start | bytes 786436
  116.0 35.5 %copy-start.6 = (bf16[8,64,3,256]{3,1,2,0:T(8,128)(2,1)}, bf16[8,64,3,256]{3,1,2,0:T(8,128)(2,1)S(1)}, u32[]{:S(2)}) copy-start(bf16[8,64,3,256]{3,1,2,0:T(8,128)(2,1)S(1)} %fusion.59) | copy-start | bytes 2359300
  151.6 15.9 copy-start.24
  187.4 167.4 %all-to-all-start = ((bf16[5,4,116,1536]{3,2,0,1:T(8,128)(2,1)}), bf16[5,4,116,1536]{3,2,0,1:T(8,128)(2,1)}, u32[]{:S(2)}, u32[]{:S(2)}) async-start(bf16[5,4,116,1536]{3,2,0,1:T(8,128)(2,1)} %copy.106), calls=%async_computation | async-start | bytes 14745600 | tf_op jit(solution)/shard_map/all_to_all | solution.py:139
  193.0 186.6 %all-gather.21.cloned.1.call-start = ((), (), s32[]{:S(2)}) async-start(), calls=%async_computation.18 | async-start | bytes 8847360 | tf_op jit(solution)/shard_map/all_gather | solution.py:74
  396.7 26.7 %copy-start.11 = (bf16[256,1536]{1,0:T(8,128)(2,1)S(1)}, bf16[256,1536]{1,0:T(8,128)(2,1)}, u32[]{:S(2)}) copy-start(bf16[256,1536]{1,0:T(8,128)(2,1)} %param.27) | copy-start | bytes 2359300
  396.7 27.2 %copy-start.19 = (s32[256,8]{0,1:T(8,128)S(1)}, s32[256,8]{0,1:T(8,128)}, u32[]{:S(2)}) copy-start(s32[256,8]{0,1:T(8,128)} %param.16) | copy-start | bytes 24580
  396.7 166.7 %all-to-all-start.1 = ((bf16[5,4,116,1536]{3,2,0,1:T(8,128)(2,1)}), bf16[5,4,116,1536]{3,2,0,1:T(8,128)(2,1)}, u32[]{:S(2)}, u32[]{:S(2)}) async-start(bf16[5,4,116,1536]{3,2,0,1:T(8,128)(2,1)} %copy.109), calls=%async_computation.1 | async-start | bytes 14745600 | tf_op jit(solution)/shard_map/all_to_all | solution.py:144
  867.5 165.7 %all-to-all-start.3 = ((bf16[5,4,116,1536]{3,2,0,1:T(8,128)(2,1)}), bf16[5,4,116,1536]{3,2,0,1:T(8,128)(2,1)}, u32[]{:S(2)}, u32[]{:S(2)}) async-start(bf16[5,4,116,1536]{3,2,0,1:T(8,128)(2,1)} %copy.114), calls=%async_computation.3 | async-start | bytes 14745600 | tf_op jit(solution)/shard_map/all_to_all | solution.py:193
  873.0 298.4 %reduce-scatter.25.cloned.1.call-start = ((), (), s32[]{:S(2)}) async-start(), calls=%async_computation.26 | async-start | bytes 442368
  874.5 302.7 %reduce-scatter.15.cloned.1.call-start = ((), (), s32[]{:S(2)}) async-start(), calls=%async_computation.21 | async-start | bytes 1769472 | tf_op jit(solution)/shard_map/reduce_scatter | solution.py:275
  1110.9 78.9 %reduce-scatter.13.cloned.1.call-start = ((), (), s32[]{:S(2)}) async-start(), calls=%async_computation.20 | async-start | bytes 1769472 | tf_op jit(solution)/shard_map/reduce_scatter | solution.py:272
  1125.6 121.6 %reduce-scatter.17.cloned.1.call-start = ((), (), s32[]{:S(2)}) async-start(), calls=%async_computation.22 | async-start | bytes 5308416 | tf_op jit(solution)/shard_map/reduce_scatter | solution.py:278
  1129.3 175.5 %reduce-scatter.11.cloned.1.call-start = ((), (), s32[]{:S(2)}) async-start(), calls=%async_computation.19 | async-start | bytes 5308416 | tf_op jit(solution)/shard_map/reduce_scatter | solution.py:269
  1135.8 241.9 %reduce-scatter.23.cloned.1.call-start = ((), (), s32[]{:S(2)}) async-start(), calls=%async_computation.25 | async-start | bytes 8847360 | tf_op jit(solution)/shard_map/reduce_scatter | solution.py:313
  1147.1 303.7 %reduce-scatter.19.cloned.1.call-start = ((), (), s32[]{:S(2)}) async-start(), calls=%async_computation.23 | async-start | bytes 8847360 | tf_op jit(solution)/shard_map/reduce_scatter | solution.py:307
  1158.9 364.6 %reduce-scatter.21.cloned.1.call-start = ((), (), s32[]{:S(2)}) async-start(), calls=%async_computation.24 | async-start | bytes 8847360 | tf_op jit(solution)/shard_map/reduce_scatter | solution.py:310
  1170.7 425.7 %all-reduce.10.cloned.1.call-start = ((), (), s32[]{:S(2)}) async-start(), calls=%async_computation.27 | async-start | bytes 3145728 | tf_op jit(solution)/shard_map/psum | solution.py:290
  (20 other events, 98.7 us)
Sparse Core Ops, SparseCore 0:
  9.9 28.6 all-gather.10
  40.5 25.6 all-gather.8
  68.1 38.9 all-gather.12
  108.8 38.9 all-gather.14
  149.5 52.1 all-gather.16
  203.4 52.1 all-gather.18
  257.5 52.1 all-gather.20
  877.4 34.2 reduce-scatter.24
  1111.0 36.5 reduce-scatter.14
  1151.4 38.4 reduce-scatter.12
  1193.3 53.8 reduce-scatter.16
  1250.9 53.8 reduce-scatter.10
  1308.2 69.4 reduce-scatter.22
  1381.4 69.3 reduce-scatter.18
  1454.1 69.3 reduce-scatter.20
  1526.1 70.2 all-reduce.9
where the time goes:
time: 1630 us; the launch traced here: 1610 us
  waiting for transfers between devices  921 us (57%)
  blocking collectives  233 us (14%)
  local copies, waits for them, and re-layouts  196 us (12%)
  matrix products  168 us (10%)
  other arithmetic  59.1 us (4%)
  starting transfers between devices  17.6 us (1%)
  between operations  16.5 us (1%)
    all_to_all x1, blocking collectives, body(): lax.all_to_all(grad_send, 'expert', split_axis=1, concat_axis=1, tiled=True)  165 us
    all_to_all x1, waiting for transfers between devices, body(): lax.all_to_all(send_rows, 'expert', split_axis=1, concat_axis=1, tiled=True)  153 us
    all_to_all x1, waiting for transfers between devices, body(): lax.all_to_all(grad_rows, 'expert', split_axis=1, concat_axis=1, tiled=True)  153 us
    all_to_all x1, waiting for transfers between devices, body(): lax.all_to_all(produced, 'expert', split_axis=1, concat_axis=1, tiled=True)  139 us
    reduce_scatter x1, waiting for transfers between devices, body(): lax.psum_scatter(grad_gate.astype(jnp.bfloat16), 'dp', scatter_dimension=...  70.3 us
    psum x1, waiting for transfers between devices, body(): lax.psum(mixer_shares[1].astype(jnp.bfloat16), 'expert').astype(jnp.float32)  70.2 us
    reduce_scatter x1, waiting for transfers between devices, body(): lax.psum_scatter(grad_up.astype(jnp.bfloat16), 'dp', scatter_dimension=1,...  70 us
    reduce_scatter x1, waiting for transfers between devices, body(): lax.psum_scatter(grad_query.astype(jnp.bfloat16), 'dp', scatter_dimension...  57.6 us
  transfers between devices with their start and end apart: 19, of which 14 were waited for; matrix products, arithmetic and copies ran while one was open for 16% of the time, Pallas kernels for 0%

commit v1 on v0

v1 whole, which is shorter than its diff:
```python
import functools

import jax
import jax.numpy as jnp
from jax import lax
from jax.experimental import pallas as pl
from jax.experimental.pallas import tpu as pltpu
from jax.sharding import PartitionSpec as P

HEADS = 24
KV_HEADS = 8
HEAD_DIM = 64
TOP = 8
GROUPS = HEADS // KV_HEADS
QW = HEADS * HEAD_DIM
KW = KV_HEADS * HEAD_DIM
QKV = QW + 2 * KW
EXT = 128
HALVES = 2

norm_eps = 1e-06
masked_score = -1e30
BF = jnp.bfloat16
F32 = jnp.float32
ANY = pl.BlockSpec(memory_space=pl.ANY)
VMEM = pl.BlockSpec(memory_space=pltpu.VMEM)
SMEM = pl.BlockSpec(memory_space=pltpu.SMEM)
VMEM_LIMIT = 56 * 1024 * 1024


def dot(a, b, ca=1, cb=0):
    return lax.dot_general(a, b, (((ca,), (cb,)), ((), ())), preferred_element_type=F32)


def params():
    return pltpu.CompilerParams(vmem_limit_bytes=VMEM_LIMIT)


def cost(flops, nbytes, trans=0):
    return pl.CostEstimate(flops=int(flops), bytes_accessed=int(nbytes), transcendentals=int(trans))


def sds(shape, dtype):
    return jax.ShapeDtypeStruct(shape, dtype)


def swap(value, bit, size):
    return lax.ppermute(value, "dp", [(i, i ^ bit) for i in range(size)])


def gather_shards(shard, route, size):
    if size != 8:
        return [lax.all_gather(shard, "dp", axis=0, tiled=False)]
    across = swap(shard, 2, size)
    along = swap(shard, 4, size)
    corner = swap(across, 4, size) if route == 0 else swap(along, 2, size)
    found = {0: shard, 2: across, 4: along, 6: corner}
    for near in (0, 2, 4, 6):
        found[near + 1] = swap(found[near], 1, size)
    return [found[m] for m in range(8)]


def reduce_shards(parts, route, size):
    if size != 8:
        total = lax.psum_scatter(parts[0], "dp", scatter_dimension=0, tiled=True)
        return total[0].astype(F32)

    def add(a, b):
        return (a.astype(F32) + b.astype(F32)).astype(BF)

    own, other = parts
    other = swap(other, 1, size)
    if route == 0:
        sent = swap(add(own[1::2], other[1::2]), 2, size)
        kept = add(own[0::2], other[0::2])
        last = swap(add(kept[1], sent[1]), 4, size)
    else:
        sent = swap(add(own[2:], other[2:]), 4, size)
        kept = add(own[:2], other[:2])
        last = swap(add(kept[1], sent[1]), 2, size)
    return kept[0].astype(F32) + sent[0].astype(F32) + last.astype(F32)


def part_shapes(size, shape):
    if size != 8:
        return [sds((size,) + shape, BF)]
    return [sds((4,) + shape, BF), sds((4,) + shape, BF)]


def send_along(value, step):
    count = lax.axis_size("expert")
    return lax.ppermute(value, "expert", [(i, (i + step) % count) for i in range(count)])


def fetch(me, refs, target, sems, rows, size):
    copies = []
    for i in range(size):
        if len(refs) == 1:
            source, at = refs[0].at[i], i * rows
        else:
            source, at = refs[i], pl.multiple_of(jnp.bitwise_xor(me, i) * rows, rows)
        copies.append(pltpu.make_async_copy(source, target(pl.ds(at, rows)), sems.at[i]))
    for c in copies:
        c.start()
    return copies


def store_parts(me, source, outs, sems, rows, size):
    copies = []
    for i in range(size):
        if len(outs) == 1:
            target, at = outs[0].at[i], i * rows
        else:
            target = outs[i % 2].at[i // 2]
            at = pl.multiple_of(jnp.bitwise_xor(me, i) * rows, rows)
        copies.append(pltpu.make_async_copy(source(pl.ds(at, rows)), target, sems.at[i]))
    for c in copies:
        c.start()
    return copies


def attention_kernel(size, rows, me, tok, seg_row, seg_col, *rest):
    count = 1 if size != 8 else size
    refs, rest = rest[:count], rest[count:]
    low_out, qkv_out, ctx_out, prob_out, ext_out, w, sems = rest
    copies = fetch(me[0], refs, lambda s: w.at[s], sems, rows, size)
    seq = tok.shape[0]
    x = tok[...].astype(F32)
    factor = lax.rsqrt(jnp.mean(x * x, axis=-1, keepdims=True) + norm_eps)
    normed = x * factor
    same = seg_col[...] == seg_row[...]
    key_at = lax.broadcasted_iota(jnp.int32, (seq, seq), 0)
    query_at = lax.broadcasted_iota(jnp.int32, (seq, seq), 1)
    allowed = jnp.where(same & (key_at <= query_at), 0.0, masked_score)
    allowed = jnp.concatenate([allowed] * GROUPS, axis=1)
    for c in copies:
        c.wait()
    ext = w[:, QKV:].astype(F32).T[: ext_out.shape[0], :]
    ext_out[...] = ext
    experts_pad = ext_out.shape[0] - 16
    gain = ext[experts_pad : experts_pad + 1, :]
    low = (normed * gain).astype(BF)
    low_out[...] = low
    step = 512
    for j in range(QKV // step):
        part = dot(low, w[:, j * step : (j + 1) * step])
        qkv_out[j * step : (j + 1) * step, :] = part.T.astype(BF)
    for h in range(KV_HEADS):
        q = jnp.concatenate(
            [
                qkv_out[(GROUPS * h + g) * HEAD_DIM : (GROUPS * h + g + 1) * HEAD_DIM, :]
                for g in range(GROUPS)
            ],
            axis=1,
        )
        k = qkv_out[QW + h * HEAD_DIM : QW + (h + 1) * HEAD_DIM, :]
        v = qkv_out[QW + KW + h * HEAD_DIM : QW + KW + (h + 1) * HEAD_DIM, :]
        scores = dot(k, q, 0, 0) * HEAD_DIM ** (-0.5)
        scores = jnp.where(allowed < 0.0, masked_score, scores)
        top = jnp.max(scores, axis=0, keepdims=True)
        shifted = jnp.exp(scores - top)
        probs = (shifted * (1.0 / jnp.sum(shifted, axis=0, keepdims=True))).astype(BF)
        prob_out[h] = probs
        ctx = dot(v, probs).astype(BF)
        for g in range(GROUPS):
            at = (GROUPS * h + g) * HEAD_DIM
            ctx_out[at : at + HEAD_DIM, :] = ctx[:, g * seq : (g + 1) * seq]


def run_attention(me, tokens, seg_row, seg_col, pieces, size, ext_rows):
    seq, width = tokens.shape
    rows = width // size
    cols = QKV + EXT
    return pl.pallas_call(
        functools.partial(attention_kernel, size, rows),
        name="attention",
        out_shape=[
            sds((seq, width), BF),
            sds((QKV, seq), BF),
            sds((QW, seq), BF),
            sds((KV_HEADS, seq, GROUPS * seq), BF),
            sds((ext_rows, width), F32),
        ],
        in_specs=[SMEM, VMEM, VMEM, VMEM] + [ANY] * len(pieces),
        out_specs=[VMEM] * 5,
        scratch_shapes=[pltpu.VMEM((width, cols), BF), pltpu.SemaphoreType.DMA((size,))],
        compiler_params=params(),
        cost_estimate=cost(4e9, 16e6, 2e6),
    )(me, tokens, seg_row, seg_col, *pieces)


def residual_kernel(size, rows, me, tok, ctx, ext, *rest):
    count = 1 if size != 8 else size
    refs, rest = rest[:count], rest[count:]
    res_out, low_out, w, sems = rest
    copies = fetch(me[0], refs, lambda s: w.at[s], sems, rows, size)
    experts_pad = ext.shape[0] - 16
    for c in copies:
        c.wait()
    res = tok[...].astype(F32) + dot(ctx[...], w[...], 0, 0)
    res_out[...] = res
    factor = lax.rsqrt(jnp.mean(res * res, axis=-1, keepdims=True) + norm_eps)
    low_out[...] = (res * factor * ext[experts_pad + 8 : experts_pad + 9, :]).astype(BF)


def run_residual(me, tokens, ctx, ext, pieces, size):
    seq, width = tokens.shape
    rows = QW // size
    return pl.pallas_call(
        functools.partial(residual_kernel, size, rows),
        name="residual",
        out_shape=[sds((seq, width), F32), sds((seq, width), BF)],
        in_specs=[SMEM, VMEM, VMEM, VMEM] + [ANY] * len(pieces),
        out_specs=[VMEM] * 2,
        scratch_shapes=[pltpu.VMEM((QW, width), BF), pltpu.SemaphoreType.DMA((size,))],
        compiler_params=params(),
        cost_estimate=cost(1.2e9, 8e6),
    )(me, tokens, ctx, ext, *pieces)


def router_kernel(owners, per, z, ext, *rest):
    rows, rest = rest[:owners], rest[owners:]
    pos, rest = rest[:owners], rest[owners:]
    pos_out, p_out, own_out, gather_p, gather_pos = rest
    experts_pad = ext.shape[0] - 16
    router = ext[:experts_pad, :].astype(BF)
    at = z[0] * per
    for r in range(owners):
        logits = dot(router, rows[r][...], 1, 1)
        place = pos[r][...]
        named = place >= 0.0
        logits = jnp.where(named, logits, masked_score)
        top = jnp.max(logits, axis=0, keepdims=True)
        shifted = jnp.where(named, jnp.exp(logits - top), 0.0)
        probs = shifted / jnp.sum(shifted, axis=0, keepdims=True)
        if r == 0:
            own_out[...] = probs
        gather_p[...] = probs
        gather_pos[...] = place
        for l in range(per):
            p_out[l, r : r + 1, :] = gather_p[pl.ds(at + l, 1), :]
            pos_out[l, r : r + 1, :] = gather_pos[pl.ds(at + l, 1), :].astype(jnp.int32)


def run_router(z, ext, rows, pos, per):
    owners = len(rows)
    seq = rows[0].shape[0]
    experts_pad = ext.shape[0] - 16
    return pl.pallas_call(
        functools.partial(router_kernel, owners, per),
        name="router",
        out_shape=[
            sds((per, owners, seq), jnp.int32),
            sds((per, owners, seq), F32),
            sds((experts_pad, seq), F32),
        ],
        in_specs=[SMEM, VMEM] + [VMEM] * (2 * owners),
        out_specs=[VMEM] * 3,
        scratch_shapes=[pltpu.VMEM((experts_pad, seq), F32)] * 2,
        compiler_params=params(),
        cost_estimate=cost(1e8, 4e6),
    )(z, ext, *rows, *pos)


def expert_kernel(size, rows, owners, cap, number, me, pos, p, *rest):
    count = 1 if size != 8 else size
    outs_count = 1 if size != 8 else 2
    xs, rest = rest[:owners], rest[owners:]
    cs, rest = rest[:owners], rest[owners:]
    refs, rest = rest[:count], rest[count:]
    out_rows, back_rows, gate_out = rest[:3]
    rest = rest[3:]
    grads, rest = rest[:outs_count], rest[outs_count:]
    xv, cv, w, xr, cr, prow, hp, gg, ug, gate, ov, bv, g, sem_x, sem_c, sem_w, sem_o = rest
    ff = w.shape[2]
    copies_x = [pltpu.make_async_copy(xs[r], xv.at[r], sem_x.at[r]) for r in range(owners)]
    copies_c = [pltpu.make_async_copy(cs[r], cv.at[r], sem_c.at[r]) for r in range(owners)]
    for a, b in zip(copies_x, copies_c):
        a.start()
        b.start()
    copies_w = fetch(me[0], refs, lambda s: w.at[:, s, :], sem_w, rows, size)
    seq = xv.shape[1]
    slot = lax.broadcasted_iota(jnp.int32, (cap, seq), 0)
    for r in range(owners):
        copies_x[r].wait()
        copies_c[r].wait()
        hot = pos[number, r : r + 1, :] == slot
        low_hot = jnp.where(hot, 1.0, 0.0).astype(BF)
        at = pl.ds(r * cap, cap)
        xr[at, :] = dot(low_hot, xv[r]).astype(BF)
        cr[at, :] = dot(low_hot, cv[r]).astype(BF)
        prow[at, :] = jnp.sum(jnp.where(hot, p[number, r : r + 1, :], 0.0), axis=1, keepdims=True)
    for c in copies_w:
        c.wait()
    step = ff // HALVES
    gate[...] = jnp.zeros_like(gate)
    for j in range(HALVES):
        cols = slice(j * step, (j + 1) * step)
        gate_pre = dot(xr[...], w[0, :, cols])
        up_pre = dot(xr[...], w[1, :, cols])
        back = dot(cr[...], w[2, :, cols])
        probs = prow[...]
        s = jax.nn.sigmoid(gate_pre)
        silu = gate_pre * s
        hidden = silu * up_pre
        gate[...] += jnp.sum(hidden * back, axis=1, keepdims=True)
        hp[:, cols] = (hidden * probs).astype(BF)
        back = back * probs
        gg[:, cols] = (back * up_pre * (s + silu * (1.0 - s))).astype(BF)
        ug[:, cols] = (back * silu).astype(BF)
    for r in range(owners):
        hot = pos[number, r : r + 1, :] == slot
        at = pl.ds(r * cap, cap)
        gate_out[r : r + 1, :] = jnp.sum(jnp.where(hot, gate[at, :], 0.0), axis=0, keepdims=True)
    width = w.shape[1]
    tile = width // HALVES
    for j in range(HALVES):
        cols = slice(j * tile, (j + 1) * tile)
        g[0, cols, :] = dot(xr[:, cols], gg[...], 0, 0).astype(BF)
        g[1, cols, :] = dot(xr[:, cols], ug[...], 0, 0).astype(BF)
        g[2, cols, :] = dot(cr[:, cols], hp[...], 0, 0).astype(BF)
    copies_g = store_parts(me[0], lambda s: g.at[:, s, :], grads, sem_w, rows, size)
    for j in range(HALVES):
        cols = slice(j * tile, (j + 1) * tile)
        bv[:, cols] = (dot(gg[...], w[0, cols, :], 1, 1) + dot(ug[...], w[1, cols, :], 1, 1)).astype(BF)
    copy_b = pltpu.make_async_copy(bv, back_rows, sem_o.at[0])
    copy_b.start()
    for j in range(HALVES):
        cols = slice(j * tile, (j + 1) * tile)
        ov[:, cols] = dot(hp[...], w[2, cols, :], 1, 1).astype(BF)
    copy_o = pltpu.make_async_copy(ov, out_rows, sem_o.at[1])
    copy_o.start()
    for c in copies_g + [copy_b, copy_o]:
        c.wait()


def run_expert(me, pos, p, xs, cs, pieces, size, number, cap):
    owners = len(xs)
    seq, width = xs[0].shape
    ff = pieces[0].shape[-1]
    rows = width // size
    total = owners * cap
    grads = part_shapes(size, (3, rows, ff))
    return pl.pallas_call(
        functools.partial(expert_kernel, size, rows, owners, cap, number),
        name="expert",
        out_shape=[sds((total, width), BF), sds((total, width), BF), sds((owners, seq), F32)] + grads,
        in_specs=[SMEM, VMEM, VMEM] + [ANY] * (2 * owners + len(pieces)),
        out_specs=[ANY, ANY, VMEM] + [ANY] * len(grads),
        scratch_shapes=[
            pltpu.VMEM((owners, seq, width), BF),
            pltpu.VMEM((owners, seq, width), BF),
            pltpu.VMEM((3, width, ff), BF),
            pltpu.VMEM((total, width), BF),
            pltpu.VMEM((total, width), BF),
            pltpu.VMEM((total, 1), F32),
            pltpu.VMEM((total, ff), BF),
            pltpu.VMEM((total, ff), BF),
            pltpu.VMEM((total, ff), BF),
            pltpu.VMEM((total, 1), F32),
            pltpu.VMEM((total, width), BF),
            pltpu.VMEM((total, width), BF),
            pltpu.VMEM((3, width, ff), BF),
            pltpu.SemaphoreType.DMA((owners,)),
            pltpu.SemaphoreType.DMA((owners,)),
            pltpu.SemaphoreType.DMA((size,)),
            pltpu.SemaphoreType.DMA((2,)),
        ],
        compiler_params=params(),
        cost_estimate=cost(9e9, 20e6, 3e5),
    )(me, pos, p, *xs, *cs, *pieces)


def combine_kernel(owners, per, cap, pos, *rest):
    rows, rest = rest[:per], rest[per:]
    gates, outs = rest[: len(rest) - 2 * owners], rest[len(rest) - 2 * owners :]
    if not gates:
        gates, outs = (), rest
    r = pl.program_id(0)
    seq = pos.shape[2]
    slot = lax.broadcasted_iota(jnp.int32, (cap, seq), 0)
    hot = jnp.concatenate(
        [jnp.where(pos[l, pl.ds(r, 1), :] == slot, 1.0, 0.0).astype(BF) for l in range(per)], axis=0
    )
    stacked = jnp.concatenate([rows[l][...] for l in range(per)], axis=0)
    total = dot(hot, stacked, 0, 0).astype(BF)
    for o in range(owners):

        @pl.when(r == o)
        def _():
            outs[o][...] = total
            if gates:
                for l in range(per):
                    outs[owners + o][l : l + 1, :] = gates[l][o : o + 1, :]


def run_combine(pos, rows, gates, cap):
    per, owners, seq = pos.shape
    width = rows[0].shape[1]
    gate_rows = -(-per // 8) * 8
    shapes = [sds((seq, width), BF)] * owners
    if gates:
        shapes = shapes + [sds((gate_rows, seq), F32)] * owners

    def whole(shape):
        return pl.BlockSpec(shape, lambda r: (0,) * len(shape))

    return pl.pallas_call(
        functools.partial(combine_kernel, owners, per, cap),
        name="combine",
        grid=(owners,),
        out_shape=shapes,
        in_specs=[whole(pos.shape)]
        + [pl.BlockSpec((cap, width), lambda r: (r, 0))] * per
        + [whole((owners, seq))] * len(gates),
        out_specs=[whole(s.shape) for s in shapes],
        compiler_params=params(),
        cost_estimate=cost(2e9, 12e6),
    )(pos, *rows, *gates)


def second_kernel(size, rows, owners, per, me, z, own_p, ext, low_two, res, cot, ctx, *rest):
    backs, rest = rest[:owners], rest[owners:]
    gates, rest = rest[:owners], rest[owners:]
    count = 1 if size != 8 else size
    outs_count = 1 if size != 8 else 2
    refs, rest = rest[:count], rest[count:]
    res_grad, ctx_grad, ext_grad = rest[:3]
    rest = rest[3:]
    grads, rest = rest[:outs_count], rest[outs_count:]
    w, g, gate, sems, sems_g = rest
    copies = fetch(me[0], refs, lambda s: w.at[s], sems, rows, size)
    experts_pad = own_p.shape[0]
    gate[...] = jnp.zeros_like(gate)
    for r in range(owners):
        at = lax.rem(z[0] + r, owners) * per
        for l in range(per):
            gate[pl.ds(at + l, 1), :] = gates[r][l : l + 1, :]
    p = own_p[...]
    gate_grad = gate[...]
    weighted = jnp.sum(p * gate_grad, axis=0, keepdims=True)
    logit_grad = (p * (gate_grad - weighted)).astype(BF)
    router = ext[:experts_pad, :].astype(BF)
    ext_grad[:experts_pad, :] = dot(logit_grad, low_two[...])
    two = dot(logit_grad, router, 0, 0)
    for r in range(owners):
        two = two + backs[r][...].astype(F32)
    values = res[...]
    factor = lax.rsqrt(jnp.mean(values * values, axis=-1, keepdims=True) + norm_eps)
    normed = values * factor
    ext_grad[experts_pad:, :] = jnp.broadcast_to(
        jnp.sum(two * normed, axis=0, keepdims=True), (16, normed.shape[1])
    )
    scaled = two * ext[experts_pad + 8 : experts_pad + 9, :]
    inward = factor * (scaled - normed * jnp.mean(scaled * normed, axis=-1, keepdims=True))
    total = cot[...].astype(F32) + inward
    res_grad[...] = total
    low = total.astype(BF)
    step = QW // 4
    for j in range(4):
        at = slice(j * step, (j + 1) * step)
        g[at, :] = dot(ctx[at, :], low).astype(BF)
    copies_g = store_parts(me[0], lambda s: g.at[s], grads, sems_g, rows, size)
    for c in copies:
        c.wait()
    for j in range(4):
        at = slice(j * step, (j + 1) * step)
        ctx_grad[at, :] = dot(w[at, :], low, 1, 1).astype(BF)
    for c in copies_g:
        c.wait()


def run_second(me, z, own_p, ext, low_two, res, cot, ctx, backs, gates, pieces, size, per):
    seq, width = res.shape
    rows = QW // size
    grads = part_shapes(size, (rows, width))
    experts_pad = own_p.shape[0]
    return pl.pallas_call(
        functools.partial(second_kernel, size, rows, len(backs), per),
        name="second_back",
        out_shape=[sds((seq, width), F32), sds((QW, seq), BF), sds((experts_pad + 16, width), F32)] + grads,
        in_specs=[SMEM, SMEM] + [VMEM] * (6 + 2 * len(backs)) + [ANY] * len(pieces),
        out_specs=[VMEM] * 3 + [ANY] * len(grads),
        scratch_shapes=[
            pltpu.VMEM((QW, width), BF),
            pltpu.VMEM((QW, width), BF),
            pltpu.VMEM((experts_pad, seq), F32),
            pltpu.SemaphoreType.DMA((size,)),
            pltpu.SemaphoreType.DMA((size,)),
        ],
        compiler_params=params(),
        cost_estimate=cost(2.4e9, 20e6),
    )(me, z, own_p, ext, low_two, res, cot, ctx, *backs, *gates, *pieces)


def first_kernel(size, rows, me, ctx_grad, qkv, probs, low_one, tok, ext, ext_grad, res_grad, *rest):
    count = 1 if size != 8 else size
    outs_count = 1 if size != 8 else 2
    refs, rest = rest[:count], rest[count:]
    tok_grad, rest = rest[0], rest[1:]
    grads, rest = rest[:outs_count], rest[outs_count:]
    w, g, back, back_rows, sems, sems_g = rest
    copies = fetch(me[0], refs, lambda s: w.at[s], sems, rows, size)
    seq = tok.shape[0]
    scale = HEAD_DIM ** (-0.5)
    for h in range(KV_HEADS):

        def heads(ref):
            return jnp.concatenate(
                [
                    ref[(GROUPS * h + i) * HEAD_DIM : (GROUPS * h + i + 1) * HEAD_DIM, :]
                    for i in range(GROUPS)
                ],
                axis=1,
            )

        upstream = heads(ctx_grad)
        q = heads(qkv)
        k = qkv[QW + h * HEAD_DIM : QW + (h + 1) * HEAD_DIM, :]
        v = qkv[QW + KW + h * HEAD_DIM : QW + KW + (h + 1) * HEAD_DIM, :]
        low_p = probs[h]
        weights = low_p.astype(F32)
        prob_grad = dot(v, upstream, 0, 0)
        inner = jnp.sum(prob_grad * weights, axis=0, keepdims=True)
        score_grad = (weights * (prob_grad - inner)).astype(BF)
        value_grad = dot(upstream, low_p, 1, 1)
        key_grad = dot(q, score_grad, 1, 1) * scale
        query_grad = dot(k, score_grad) * scale
        back[QW + h * HEAD_DIM : QW + (h + 1) * HEAD_DIM, :] = key_grad.astype(BF)
        back[QW + KW + h * HEAD_DIM : QW + KW + (h + 1) * HEAD_DIM, :] = value_grad.astype(BF)
        for i in range(GROUPS):
            at = (GROUPS * h + i) * HEAD_DIM
            back[at : at + HEAD_DIM, :] = query_grad[:, i * seq : (i + 1) * seq].astype(BF)
    step = 512
    for j in range(QKV // step):
        at = slice(j * step, (j + 1) * step)
        back_rows[:, at] = back[at, :].astype(F32).T.astype(BF)
    for c in copies:
        c.wait()
    one = dot(back_rows[...], w[:, :QKV], 1, 1)
    x = tok[...].astype(F32)
    factor = lax.rsqrt(jnp.mean(x * x, axis=-1, keepdims=True) + norm_eps)
    normed = x * factor
    experts_pad = ext.shape[0] - 16
    gain = ext[experts_pad : experts_pad + 1, :]
    gain_grad = jnp.sum(one * normed, axis=0, keepdims=True)
    scaled = one * gain
    inward = factor * (scaled - normed * jnp.mean(scaled * normed, axis=-1, keepdims=True))
    tok_grad[...] = res_grad[...] + inward
    packed = jnp.concatenate(
        [
            ext_grad[:experts_pad, :],
            jnp.broadcast_to(gain_grad, (8, gain_grad.shape[1])),
            ext_grad[experts_pad + 8 :, :],
            jnp.zeros((EXT - experts_pad - 16, gain_grad.shape[1]), F32),
        ],
        axis=0,
    )
    g[:, QKV:] = packed.T.astype(BF)
    for j in range(QKV // step):
        at = slice(j * step, (j + 1) * step)
        g[:, at] = dot(low_one[...], back_rows[:, at], 0, 0).astype(BF)
    copies_g = store_parts(me[0], lambda s: g.at[s], grads, sems_g, rows, size)
    for c in copies_g:
        c.wait()


def run_first(me, ctx_grad, qkv, probs, low_one, tokens, ext, ext_grad, res_grad, pieces, size):
    seq, width = tokens.shape
    rows = width // size
    cols = QKV + EXT
    grads = part_shapes(size, (rows, cols))
    return pl.pallas_call(
        functools.partial(first_kernel, size, rows),
        name="first_back",
        out_shape=[sds((seq, width), F32)] + grads,
        in_specs=[SMEM] + [VMEM] * 8 + [ANY] * len(pieces),
        out_specs=[VMEM] + [ANY] * len(grads),
        scratch_shapes=[
            pltpu.VMEM((width, cols), BF),
            pltpu.VMEM((width, cols), BF),
            pltpu.VMEM((QKV, seq), BF),
            pltpu.VMEM((seq, QKV), BF),
            pltpu.SemaphoreType.DMA((size,)),
            pltpu.SemaphoreType.DMA((size,)),
        ],
        compiler_params=params(),
        cost_estimate=cost(6e9, 30e6),
    )(me, ctx_grad, qkv, probs, low_one, tokens, ext, ext_grad, res_grad, *pieces)


def body(
    tokens,
    segment_ids,
    expert_choices,
    attn_gain,
    query_weight,
    key_weight,
    value_weight,
    output_weight,
    ffn_gain,
    router_weight,
    expert_gate,
    expert_up,
    expert_down,
    cotangent,
):
    size = lax.axis_size("dp")
    owners = lax.axis_size("expert")
    me = lax.axis_index("dp").astype(jnp.int32).reshape(1)
    z = lax.axis_index("expert").astype(jnp.int32).reshape(1)
    seq, width = tokens.shape
    per = expert_gate.shape[0]
    experts = per * owners
    experts_pad = -(-experts // 8) * 8
    capacity = (seq * TOP * 9 + 8 * experts - 1) // (8 * experts)
    cap = -(-capacity // 16) * 16
    slim = query_weight.shape[0]

    ext = jnp.concatenate(
        [
            router_weight,
            jnp.zeros((slim, experts_pad - experts), BF),
            jnp.broadcast_to(attn_gain[:, None], (slim, 8)),
            jnp.broadcast_to(ffn_gain[:, None], (slim, 8)),
            jnp.zeros((slim, EXT - experts_pad - 16), BF),
        ],
        axis=1,
    )
    qkv_shard = jnp.concatenate([query_weight, key_weight, value_weight, ext], axis=1)
    qkv_pieces = gather_shards(qkv_shard, 0, size)
    out_pieces = gather_shards(output_weight, 1, size)
    expert_pieces = []
    for l in range(per):
        shard = jnp.stack([expert_gate[l], expert_up[l], expert_down[l].T])
        expert_pieces.append(gather_shards(shard, (l + 1) % 2, size))

    ids = jnp.arange(experts_pad, dtype=jnp.int32)
    hot = jnp.any(expert_choices[:, None, :] == ids[None, :, None], axis=2)
    hot = hot.astype(BF).T
    at = jnp.arange(seq, dtype=jnp.int32)
    earlier = (at[:, None] < at[None, :]).astype(BF)
    place = jnp.dot(hot, earlier, preferred_element_type=F32)
    place = jnp.where(hot > 0, place, -1.0)

    cots = [cotangent] + [send_along(cotangent, r) for r in range(1, owners)]
    places = [place] + [send_along(place, r) for r in range(1, owners)]

    low_one, qkv, ctx, probs, extra = run_attention(
        me, tokens, segment_ids, segment_ids.reshape(seq, 1), qkv_pieces, size, experts_pad + 16
    )
    res, low_two = run_residual(me, tokens, ctx, extra, out_pieces, size)
    xs = [low_two] + [send_along(low_two, r) for r in range(1, owners)]
    pos, p, own_p = run_router(z, extra, xs, places, per)

    out_rows, back_rows, gate_rows, totals = [], [], [], []
    for l in range(per):
        results = run_expert(me, pos, p, xs, cots, expert_pieces[l], size, l, cap)
        out_rows.append(results[0])
        back_rows.append(results[1])
        gate_rows.append(results[2])
        totals.append(results[3:])
    combined = run_combine(pos, back_rows, gate_rows, cap)
    backs, gates = combined[:owners], combined[owners:]
    backs = [backs[0]] + [send_along(backs[r], -r) for r in range(1, owners)]
    gates = [gates[0]] + [send_along(gates[r], -r) for r in range(1, owners)]
    outs = run_combine(pos, out_rows, [], cap)
    outs = [outs[0]] + [send_along(outs[r], -r) for r in range(1, owners)]
    mixed = res
    for r in range(owners):
        mixed = mixed + outs[r].astype(F32)
    mixed = mixed.astype(BF)

    results = run_second(
        me, z, own_p, extra, low_two, res, cotangent, ctx, backs, gates, out_pieces, size, per
    )
    res_grad, ctx_grad, ext_grad = results[:3]
    out_grads = results[3:]
    results = run_first(
        me, ctx_grad, qkv, probs, low_one, tokens, extra, ext_grad, res_grad, qkv_pieces, size
    )
    grad_tokens, qkv_grads = results[0], results[1:]

    expert_totals = [reduce_shards(totals[l], l % 2, size) for l in range(per)]
    out_total = reduce_shards(out_grads, 1, size)
    out_total = lax.psum(out_total.astype(BF), "expert").astype(F32)
    qkv_total = reduce_shards(qkv_grads, 0, size)
    qkv_total = lax.psum(qkv_total.astype(BF), "expert").astype(F32)

    stacked = jnp.stack(expert_totals)
    return (
        mixed,
        grad_tokens,
        qkv_total[:, QKV + experts_pad],
        qkv_total[:, :QW],
        qkv_total[:, QW : QW + KW],
        qkv_total[:, QW + KW : QKV],
        out_total,
        qkv_total[:, QKV + experts_pad + 8],
        qkv_total[:, QKV : QKV + experts],
        stacked[:, 0],
        stacked[:, 1],
        jnp.swapaxes(stacked[:, 2], 1, 2),
    )


def solution(mesh):
    return jax.shard_map(
        body,
        mesh=mesh,
        in_specs=(
            P(("dp", "expert"), None),
            P(("dp", "expert"), None),
            P(("dp", "expert"), None),
            P("dp"),
            P("dp", None),
            P("dp", None),
            P("dp", None),
            P("dp", None),
            P("dp"),
            P("dp", None),
            P("expert", "dp", None),
            P("expert", "dp", None),
            P("expert", None, "dp"),
            P(("dp", "expert"), None),
        ),
        out_specs=(
            P(("dp", "expert"), None),
            P(("dp", "expert"), None),
            P("dp"),
            P("dp", None),
            P("dp", None),
            P("dp", None),
            P("dp", None),
            P("dp"),
            P("dp", None),
            P("expert", "dp", None),
            P("expert", "dp", None),
            P("expert", None, "dp"),
        ),
        check_vma=False,
    )
```

time: 1630 us -> 821 us (0.50)
  waiting for transfers between devices: 921 us -> 483 us
  blocking collectives: 233 us -> 0 us
  matrix products: 168 us -> 0.15 us
  local copies, waits for them, and re-layouts: 196 us -> 29.4 us
  Pallas kernels: 0 us -> 139 us
  starting transfers between devices: 17.6 us -> 113 us
  other arithmetic: 59.1 us -> 32.7 us
    all_to_all x3 -> x0, waiting for transfers between devices: 446 us -> none  [the longest x1 153 us: body(): lax.all_to_all(send_rows, 'expert', split_axis=1, concat_axis=1, tiled=True)]
    ppermute x0 -> x88, waiting for transfers between devices: none -> 437 us  [the longest x70 229 us: swap(): return lax.ppermute(value, 'dp', [(i, i ^ bit) for i in range(size)])]
    reduce_scatter x7 -> x0, waiting for transfers between devices: 299 us -> none  [the longest x1 70.3 us: body(): lax.psum_scatter(grad_gate.astype(jnp.bfloat16), 'dp', scatter_dimension=...]
    dot_general x32 -> x1, matrix products: 168 us -> 0.15 us  [body(): place = jnp.dot(hot, earlier, preferred_element_type=F32)]
    all_to_all x1 -> x0, blocking collectives: 165 us -> none  [body(): lax.all_to_all(grad_send, 'expert', split_axis=1, concat_axis=1, tiled=True)]
    pallas_call x0 -> x12, Pallas kernels: none -> 139 us  [the longest x5 74.9 us: run_expert(): pl.pallas_call(functools.partial(expert_kernel, size, rows, owners, cap,...]
    ppermute x0 -> x88, starting transfers between devices: none -> 113 us  [the longest x18 71.3 us: send_along(): lax.ppermute(value, 'expert', [(i, (i + step) % count) for i in range(cou...]
    all_gather x7 -> x0, waiting for transfers between devices: 101 us -> none  [the longest x1 38.7 us: body(): lax.all_gather(query_weight, 'dp', axis=0, tiled=True)]
  transfers between devices with their start and end apart: 19 -> 89, of which waited for: 14 -> 23; matrix products, arithmetic and copies ran while one was open for 16% -> 5% of each run, Pallas kernels for 0% -> 11%
where the time goes in v1:
time: 821 us; the launch traced here: 812 us
  waiting for transfers between devices  483 us (59%)
  Pallas kernels  139 us (17%)
  starting transfers between devices  113 us (14%)
  other arithmetic  32.7 us (4%)
  local copies, waits for them, and re-layouts  29.4 us (4%)
  between operations  15.6 us (2%)
    ppermute x70, waiting for transfers between devices, swap(): return lax.ppermute(value, 'dp', [(i, i ^ bit) for i in range(size)])  229 us
    ppermute x18, waiting for transfers between devices, send_along(): lax.ppermute(value, 'expert', [(i, (i + step) % count) for i in range(cou...  207 us
    pallas_call x5, Pallas kernels, run_expert(): pl.pallas_call(functools.partial(expert_kernel, size, rows, owners, cap,...  74.9 us
    ppermute x18, starting transfers between devices, send_along(): lax.ppermute(value, 'expert', [(i, (i + step) % count) for i in range(cou...  71.3 us
    psum x1, waiting for transfers between devices, body(): qkv_total = lax.psum(qkv_total.astype(BF), 'expert').astype(F32)  46 us
    ppermute x70, starting transfers between devices, swap(): return lax.ppermute(value, 'dp', [(i, i ^ bit) for i in range(size)])  41.4 us
    pallas_call x1, Pallas kernels, run_first(): pl.pallas_call(functools.partial(first_kernel, size, rows), name='first_b...  16.6 us
  transfers between devices with their start and end apart: 89, of which 23 were waited for; matrix products, arithmetic and copies ran while one was open for 5% of the time, Pallas kernels for 11%

profile of v1, /device:TPU:0, one launch (start us, length us, event | category | flops | bytes accessed | tf_op | source)
XLA Modules:
  0.0 812.1 jit_solution(15775759390636741634)
XLA Ops:
  41.6 32.2 %collective-permute-done.45.rest_10_ = bf16[3,192,512]{2,1,0:T(8,128)(2,1)S(1)} collective-permute-done((bf16[3,192,512]{2,1,0:T(8,128)(2,1)S(1)}, bf16[3,192,512]{2,1,0:T(8,128)(2,1)S(1)}, u32[]{:S(2)}, u32[]{:S(2)}) %collective-permute-start.45) | collective-permute-done | bytes 589856 | tf_op jit(solution)/shard_map/ppermute | solution.py:48
  77.4 34.5 %collective-permute-done.40.rest_12_ = bf16[3,192,512]{2,1,0:T(8,128)(2,1)} collective-permute-done((bf16[3,192,512]{2,1,0:T(8,128)(2,1)}, bf16[3,192,512]{2,1,0:T(8,128)(2,1)}, u32[]{:S(2)}, u32[]{:S(2)}) %collective-permute-start.40) | collective-permute-done | bytes 589856 | tf_op jit(solution)/shard_map/ppermute | solution.py:48
  113.5 13.2 %collective-permute-done.12.rest_6_.rest_14_ = bf16[192,1536]{1,0:T(8,128)(2,1)S(1)} collective-permute-done((bf16[192,1536]{1,0:T(8,128)(2,1)S(1)}, bf16[192,1536]{1,0:T(8,128)(2,1)S(1)}, u32[]{:S(2)}, u32[]{:S(2)}) %collective-permute-start.12) | collective-permute-done | bytes 589856 | tf_op jit(solution)/shard_map/ppermute | solution.py:48
  137.7 12.0 %attention.1 = (bf16[256,1536]{1,0:T(8,128)(2,1)}, bf16[2560,256]{1,0:T(8,128)(2,1)}, bf16[1536,256]{1,0:T(8,128)(2,1)}, bf16[8,256,768]{2,1,0:T(8,128)(2,1)}, f32[40,1536]{1,0:T(8,128)}) custom-call(s32[1]{0:T(128)} %bitcast.me, bf16[256,1536]{1,0:T(8,128)(2,1)} %tok.5, s32[1,256]{1,0:T(1,128)} %seg_row.1, s32[256,1]{1,0:T(8,128)} %copy.34.seg_col, ...), custom_call_target="tpu_custom_call" | custom-call | flops 4000000000 | bytes 16000000 | tf_op jit(solution)/shard_map/attention/pallas_call | solution.py:174
  149.8 6.8 residual.1
  161.5 58.0 %collective-permute-done.21.rest_6_ = bf16[256,1536]{1,0:T(8,128)(2,1)S(1)} collective-permute-done((bf16[256,1536]{1,0:T(8,128)(2,1)}, bf16[256,1536]{1,0:T(8,128)(2,1)S(1)}, u32[]{:S(2)}, u32[]{:S(2)}) %collective-permute-start.21) | collective-permute-done | bytes 786464 | tf_op jit(solution)/shard_map/ppermute | solution.py:92
  221.4 15.0 %collective-permute-done.15.rest_2_ = bf16[256,1536]{1,0:T(8,128)(2,1)S(1)} collective-permute-done((bf16[256,1536]{1,0:T(8,128)(2,1)}, bf16[256,1536]{1,0:T(8,128)(2,1)S(1)}, u32[]{:S(2)}, u32[]{:S(2)}) %collective-permute-start.15) | collective-permute-done | bytes 786464 | tf_op jit(solution)/shard_map/ppermute | solution.py:92
  237.8 3.7 router.1
  241.5 11.7 %collective-permute-done.22.rest_7_ = bf16[256,1536]{1,0:T(8,128)(2,1)} collective-permute-done((bf16[256,1536]{1,0:T(8,128)(2,1)}, bf16[256,1536]{1,0:T(8,128)(2,1)}, u32[]{:S(2)}, u32[]{:S(2)}) %collective-permute-start.22) | collective-permute-done | bytes 786464 | tf_op jit(solution)/shard_map/ppermute | solution.py:92
  254.6 14.9 %expert.9 = (bf16[512,1536]{1,0:T(8,128)(2,1)}, bf16[512,1536]{1,0:T(8,128)(2,1)}, f32[4,256]{1,0:T(4,128)}, bf16[4,3,192,512]{3,2,1,0:T(8,128)(2,1)}, bf16[4,3,192,512]{3,2,1,0:T(8,128)(2,1)}) custom-call(s32[1]{0:T(128)} %bitcast.me, s32[5,4,256]{2,1,0:T(4,128)} %get-tuple-element.71.pos, f32[5,4,256]{2,1,0:T(4,128)} %get-tuple-element.72.p, ...), custom_call_target="tpu_custom_call" | custom-call | flops 8999999488 | bytes 20000000 | tf_op jit(solution)/shard_map/expert/pallas_call | solution.py:344
  272.9 15.1 %expert.8 = (bf16[512,1536]{1,0:T(8,128)(2,1)}, bf16[512,1536]{1,0:T(8,128)(2,1)}, f32[4,256]{1,0:T(4,128)}, bf16[4,3,192,512]{3,2,1,0:T(8,128)(2,1)}, bf16[4,3,192,512]{3,2,1,0:T(8,128)(2,1)}) custom-call(s32[1]{0:T(128)} %bitcast.me, s32[5,4,256]{2,1,0:T(4,128)} %get-tuple-element.71.pos, f32[5,4,256]{2,1,0:T(4,128)} %get-tuple-element.72.p, ...), custom_call_target="tpu_custom_call" | custom-call | flops 8999999488 | bytes 20000000 | tf_op jit(solution)/shard_map/expert/pallas_call | solution.py:344
  290.1 7.6 collective-permute-done.35.rest_14_
  300.0 15.3 %expert.7 = (bf16[512,1536]{1,0:T(8,128)(2,1)}, bf16[512,1536]{1,0:T(8,128)(2,1)}, f32[4,256]{1,0:T(4,128)}, bf16[4,3,192,512]{3,2,1,0:T(8,128)(2,1)}, bf16[4,3,192,512]{3,2,1,0:T(8,128)(2,1)}) custom-call(s32[1]{0:T(128)} %bitcast.me, s32[5,4,256]{2,1,0:T(4,128)} %get-tuple-element.71.pos, f32[5,4,256]{2,1,0:T(4,128)} %get-tuple-element.72.p, ...), custom_call_target="tpu_custom_call" | custom-call | flops 8999999488 | bytes 20000000 | tf_op jit(solution)/shard_map/expert/pallas_call | solution.py:344
  317.7 14.8 %expert.6 = (bf16[512,1536]{1,0:T(8,128)(2,1)}, bf16[512,1536]{1,0:T(8,128)(2,1)}, f32[4,256]{1,0:T(4,128)}, bf16[4,3,192,512]{3,2,1,0:T(8,128)(2,1)}, bf16[4,3,192,512]{3,2,1,0:T(8,128)(2,1)}) custom-call(s32[1]{0:T(128)} %bitcast.me, s32[5,4,256]{2,1,0:T(4,128)} %get-tuple-element.71.pos, f32[5,4,256]{2,1,0:T(4,128)} %get-tuple-element.72.p, ...), custom_call_target="tpu_custom_call" | custom-call | flops 8999999488 | bytes 20000000 | tf_op jit(solution)/shard_map/expert/pallas_call | solution.py:344
  334.6 14.8 %expert.5 = (bf16[512,1536]{1,0:T(8,128)(2,1)}, bf16[512,1536]{1,0:T(8,128)(2,1)}, f32[4,256]{1,0:T(4,128)}, bf16[4,3,192,512]{3,2,1,0:T(8,128)(2,1)}, bf16[4,3,192,512]{3,2,1,0:T(8,128)(2,1)}) custom-call(s32[1]{0:T(128)} %bitcast.me, s32[5,4,256]{2,1,0:T(4,128)} %get-tuple-element.71.pos, f32[5,4,256]{2,1,0:T(4,128)} %get-tuple-element.72.p, ...), custom_call_target="tpu_custom_call" | custom-call | flops 8999999488 | bytes 20000000 | tf_op jit(solution)/shard_map/expert/pallas_call | solution.py:344
  349.4 7.7 combine.3
  357.1 31.4 %collective-permute-start.61 = (bf16[256,1536]{1,0:T(8,128)(2,1)}, bf16[256,1536]{1,0:T(8,128)(2,1)S(1)}, u32[]{:S(2)}, u32[]{:S(2)}) collective-permute-start(bf16[256,1536]{1,0:T(8,128)(2,1)} %get-tuple-element.94), channel_id=1, source_target_pairs={{0,3},{1,0},{2,1},{3,2},{4,7},{5,4},{6,5},{7,6},{8,11},{9,8},{10,9... | collective-permute-start | bytes 2359304 | tf_op jit(solution)/shard_map/ppermute | solution.py:92
  393.5 46.6 %collective-permute-done.64.rest_5_ = f32[8,256]{1,0:T(8,128)S(1)} collective-permute-done((f32[8,256]{1,0:T(8,128)}, f32[8,256]{1,0:T(8,128)S(1)}, u32[]{:S(2)}, u32[]{:S(2)}) %collective-permute-start.64) | collective-permute-done | bytes 8224 | tf_op jit(solution)/shard_map/ppermute | solution.py:92
  440.1 17.1 %collective-permute-start.66 = (f32[8,256]{1,0:T(8,128)}, f32[8,256]{1,0:T(8,128)S(1)}, u32[]{:S(2)}, u32[]{:S(2)}) collective-permute-start(f32[8,256]{1,0:T(8,128)} %get-tuple-element.100), channel_id=1, source_target_pairs={{0,1},{1,2},{2,3},{3,0},{4,5},{5,6},{6,7},{7,4},{8,9},{9,10},{10,1... | collective-permute-start | bytes 24584 | tf_op jit(solution)/shard_map/ppermute | solution.py:92
  460.2 9.5 %second_back.1 = (f32[256,1536]{1,0:T(8,128)}, bf16[1536,256]{1,0:T(8,128)(2,1)}, f32[40,1536]{1,0:T(8,128)}, bf16[4,192,1536]{2,1,0:T(8,128)(2,1)}, bf16[4,192,1536]{2,1,0:T(8,128)(2,1)}) custom-call(s32[1]{0:T(128)} %bitcast.me, s32[1]{0:T(128)} %bitcast.2.z, f32[24,256]{1,0:T(8,128)} %get-tuple-element.82.own_p, f32[40,1536]{1,0:T(8,128)} %get-tuple-element.68.ext, ...), custom_call_target="tpu_custom_call" | custom-call | flops 2400000000 | bytes 20000000 | tf_op jit(solution)/shard_map/second_back/pallas_call | solution.py:478
  469.7 16.6 %first_back.1 = (f32[256,1536]{1,0:T(8,128)}, bf16[4,192,2688]{2,1,0:T(8,128)(2,1)}, bf16[4,192,2688]{2,1,0:T(8,128)(2,1)}) custom-call(s32[1]{0:T(128)} %bitcast.me, bf16[1536,256]{1,0:T(8,128)(2,1)} %get-tuple-element.101.ctx_grad, bf16[2560,256]{1,0:T(8,128)(2,1)} %get-tuple-element.102.qkv, bf16[8,256,768]{2,1,0:T(8,128)(2,1)} %get-tuple-element.103.probs, ...), custom_call_target="tpu_custom_call" | custom-call | flops 6000000000 | bytes 30000000 | tf_op jit(solution)/shard_map/first_back/pallas_call | solution.py:573
  486.5 7.7 combine.2
  498.4 16.4 %collective-permute-done.58 = bf16[256,1536]{1,0:T(8,128)(2,1)S(1)} collective-permute-done((bf16[256,1536]{1,0:T(8,128)(2,1)}, bf16[256,1536]{1,0:T(8,128)(2,1)S(1)}, u32[]{:S(2)}, u32[]{:S(2)}) %collective-permute-start.58) | collective-permute-done | bytes 786464 | tf_op jit(solution)/shard_map/ppermute | solution.py:92
  514.8 34.9 %collective-permute-done.59 = bf16[256,1536]{1,0:T(8,128)(2,1)S(1)} collective-permute-done((bf16[256,1536]{1,0:T(8,128)(2,1)}, bf16[256,1536]{1,0:T(8,128)(2,1)S(1)}, u32[]{:S(2)}, u32[]{:S(2)}) %collective-permute-start.59) | collective-permute-done | bytes 786464 | tf_op jit(solution)/shard_map/ppermute | solution.py:92
  549.9 21.1 %collective-permute-done.60 = bf16[256,1536]{1,0:T(8,128)(2,1)S(1)} collective-permute-done((bf16[256,1536]{1,0:T(8,128)(2,1)}, bf16[256,1536]{1,0:T(8,128)(2,1)S(1)}, u32[]{:S(2)}, u32[]{:S(2)}) %collective-permute-start.60) | collective-permute-done | bytes 786464 | tf_op jit(solution)/shard_map/ppermute | solution.py:92
  580.2 3.3 add_convert_fusion.1
  589.5 16.2 %collective-permute-done.86 = bf16[2,3,192,512]{3,2,1,0:T(8,128)(2,1)} collective-permute-done((bf16[2,3,192,512]{3,2,1,0:T(8,128)(2,1)S(1)}, bf16[2,3,192,512]{3,2,1,0:T(8,128)(2,1)}, u32[]{:S(2)}, u32[]{:S(2)}) %collective-permute-start.86) | collective-permute-done | bytes 1179680 | tf_op jit(solution)/shard_map/ppermute | solution.py:48
  611.5 63.6 %collective-permute-done.80 = bf16[2,3,192,512]{3,2,1,0:T(8,128)(2,1)S(1)} collective-permute-done((bf16[2,3,192,512]{3,2,1,0:T(8,128)(2,1)S(1)}, bf16[2,3,192,512]{3,2,1,0:T(8,128)(2,1)S(1)}, u32[]{:S(2)}, u32[]{:S(2)}) %collective-permute-start.80) | collective-permute-done | bytes 1179680 | tf_op jit(solution)/shard_map/ppermute | solution.py:48
  681.7 18.7 %collective-permute-done.74 = bf16[2,3,192,512]{3,2,1,0:T(8,128)(2,1)S(1)} collective-permute-done((bf16[2,3,192,512]{3,2,1,0:T(8,128)(2,1)S(1)}, bf16[2,3,192,512]{3,2,1,0:T(8,128)(2,1)S(1)}, u32[]{:S(2)}, u32[]{:S(2)}) %collective-permute-start.74) | collective-permute-done | bytes 1179680 | tf_op jit(solution)/shard_map/ppermute | solution.py:48
  701.8 23.3 %collective-permute-done.72 = bf16[192,1536]{1,0:T(8,128)(2,1)S(1)} collective-permute-done((bf16[192,1536]{1,0:T(8,128)(2,1)S(1)}, bf16[192,1536]{1,0:T(8,128)(2,1)S(1)}, u32[]{:S(2)}, u32[]{:S(2)}) %collective-permute-start.72) | collective-permute-done | bytes 589856 | tf_op jit(solution)/shard_map/ppermute | solution.py:48
  729.4 13.0 %collective-permute-done.75 = bf16[3,192,512]{2,1,0:T(8,128)(2,1)} collective-permute-done((bf16[3,192,512]{2,1,0:T(8,128)(2,1)}, bf16[3,192,512]{2,1,0:T(8,128)(2,1)}, u32[]{:S(2)}, u32[]{:S(2)}) %collective-permute-start.75) | collective-permute-done | bytes 589856 | tf_op jit(solution)/shard_map/ppermute | solution.py:48
  752.5 46.0 %all-reduce.3.cloned.1.call-done = (bf16[192,2688]{1,0:T(8,128)(2,1)}, bf16[192,1536]{1,0:T(8,128)(2,1)}) async-done(((bf16[192,2688]{1,0:T(8,128)(2,1)}, bf16[192,1536]{1,0:T(8,128)(2,1)}), (bf16[192,2688]{1,0:T(8,128)(2,1)}, bf16[192,1536]{1,0:T(8,128)(2,1)})) %all-reduce.3.cloned.1.call-update) | async-done | bytes 1622032 | tf_op jit(solution)/shard_map/psum | solution.py:688
  (369 shorter events, 133.7 us)
Async XLA Ops:
  7.2 791.3 %all-reduce.3.cloned.1.call-start = ((), (), s32[]{:S(2)}) async-start(), calls=%async_computation | async-start | bytes 3244032 | tf_op jit(solution)/shard_map/psum | solution.py:688
  32.6 41.2 %collective-permute-start.1 = (bf16[192,2688]{1,0:T(8,128)(2,1)}, bf16[192,2688]{1,0:T(8,128)(2,1)S(1)}, u32[]{:S(2)}, u32[]{:S(2)}) collective-permute-start(bf16[192,2688]{1,0:T(8,128)(2,1)} %concatenate.3.rest_0_), channel_id=1, source_target_pairs={{0,8},{4,12},{8,0},{12,4},{16,24},{20,28},{24,16},{28,20},{1,9},{5... | collective-permute-start | bytes 3096584 | tf_op jit(solution)/shard_map/ppermute | solution.py:48
  34.4 39.5 %collective-permute-start.45 = (bf16[3,192,512]{2,1,0:T(8,128)(2,1)S(1)}, bf16[3,192,512]{2,1,0:T(8,128)(2,1)S(1)}, u32[]{:S(2)}, u32[]{:S(2)}) collective-permute-start(bf16[3,192,512]{2,1,0:T(8,128)(2,1)S(1)} %pad_maximum_fusion.3.rest_8_), channel_id=1, source_target_pairs={{0,8},{4,12},{8,0},{12,4},{16,24},{20,28},{24,16},{28,20},{1,9},{5... | collective-permute-start | bytes 1769480 | tf_op jit(solution)/shard_map/ppermute | solution.py:48
  36.8 38.5 %collective-permute-start.47 = (bf16[3,192,512]{2,1,0:T(8,128)(2,1)S(1)}, bf16[3,192,512]{2,1,0:T(8,128)(2,1)S(1)}, u32[]{:S(2)}, u32[]{:S(2)}) collective-permute-start(bf16[3,192,512]{2,1,0:T(8,128)(2,1)S(1)} %pad_maximum_fusion.3.rest_8_), channel_id=1, source_target_pairs={{0,16},{4,20},{8,24},{12,28},{16,0},{20,4},{24,8},{28,12},{1,17},{... | collective-permute-start | bytes 1769480 | tf_op jit(solution)/shard_map/ppermute | solution.py:48
  41.1 71.3 %collective-permute-start.3 = (bf16[192,2688]{1,0:T(8,128)(2,1)}, bf16[192,2688]{1,0:T(8,128)(2,1)S(1)}, u32[]{:S(2)}, u32[]{:S(2)}) collective-permute-start(bf16[192,2688]{1,0:T(8,128)(2,1)} %concatenate.3.rest_0_), channel_id=1, source_target_pairs={{0,16},{4,20},{8,24},{12,28},{16,0},{20,4},{24,8},{28,12},{1,17},{... | collective-permute-start | bytes 3096584 | tf_op jit(solution)/shard_map/ppermute | solution.py:48
  73.8 39.1 %collective-permute-start = (bf16[192,2688]{1,0:T(8,128)(2,1)}, bf16[192,2688]{1,0:T(8,128)(2,1)S(1)}, u32[]{:S(2)}, u32[]{:S(2)}) collective-permute-start(bf16[192,2688]{1,0:T(8,128)(2,1)} %concatenate.3.rest_0_), channel_id=1, source_target_pairs={{0,4},{4,0},{8,12},{12,8},{16,20},{20,16},{24,28},{28,24},{1,5},{5... | collective-permute-start | bytes 3096584 | tf_op jit(solution)/shard_map/ppermute | solution.py:48
  73.8 39.2 %collective-permute-start.5 = (bf16[192,2688]{1,0:T(8,128)(2,1)S(1)}, bf16[192,2688]{1,0:T(8,128)(2,1)}, u32[]{:S(2)}, u32[]{:S(2)}) collective-permute-start(bf16[192,2688]{1,0:T(8,128)(2,1)S(1)} %collective-permute-done.1.rest_2_), channel_id=1, source_target_pairs={{0,16},{4,20},{8,24},{12,28},{16,0},{20,4},{24,8},{28,12},{1,17},{... | collective-permute-start | bytes 3096584 | tf_op jit(solution)/shard_map/ppermute | solution.py:48
  135.1 84.4 %collective-permute-start.21 = (bf16[256,1536]{1,0:T(8,128)(2,1)}, bf16[256,1536]{1,0:T(8,128)(2,1)S(1)}, u32[]{:S(2)}, u32[]{:S(2)}) collective-permute-start(bf16[256,1536]{1,0:T(8,128)(2,1)} %cot.1), channel_id=1, source_target_pairs={{0,2},{1,3},{2,0},{3,1},{4,6},{5,7},{6,4},{7,5},{8,10},{9,11},{10,... | collective-permute-start | bytes 2359304 | tf_op jit(solution)/shard_map/ppermute | solution.py:92
  156.6 64.3 %collective-permute-start.14 = (bf16[256,1536]{1,0:T(8,128)(2,1)}, bf16[256,1536]{1,0:T(8,128)(2,1)S(1)}, u32[]{:S(2)}, u32[]{:S(2)}) collective-permute-start(bf16[256,1536]{1,0:T(8,128)(2,1)} %get-tuple-element.70.rest_0_.low_two), channel_id=1, source_target_pairs={{0,1},{1,2},{2,3},{3,0},{4,5},{5,6},{6,7},{7,4},{8,9},{9,10},{10,1... | collective-permute-start | bytes 2359304 | tf_op jit(solution)/shard_map/ppermute | solution.py:92
  157.1 79.3 %collective-permute-start.15 = (bf16[256,1536]{1,0:T(8,128)(2,1)}, bf16[256,1536]{1,0:T(8,128)(2,1)S(1)}, u32[]{:S(2)}, u32[]{:S(2)}) collective-permute-start(bf16[256,1536]{1,0:T(8,128)(2,1)} %get-tuple-element.70.rest_0_.low_two), channel_id=1, source_target_pairs={{0,2},{1,3},{2,0},{3,1},{4,6},{5,7},{6,4},{7,5},{8,10},{9,11},{10,... | collective-permute-start | bytes 2359304 | tf_op jit(solution)/shard_map/ppermute | solution.py:92
  158.6 78.4 %collective-permute-start.16 = (bf16[256,1536]{1,0:T(8,128)(2,1)}, bf16[256,1536]{1,0:T(8,128)(2,1)S(1)}, u32[]{:S(2)}, u32[]{:S(2)}) collective-permute-start(bf16[256,1536]{1,0:T(8,128)(2,1)} %get-tuple-element.70.rest_0_.low_two), channel_id=1, source_target_pairs={{0,3},{1,0},{2,1},{3,2},{4,7},{5,4},{6,5},{7,6},{8,11},{9,8},{10,9... | collective-permute-start | bytes 2359304 | tf_op jit(solution)/shard_map/ppermute | solution.py:92
  160.5 60.4 %collective-permute-start.56 = (bf16[3,192,512]{2,1,0:T(8,128)(2,1)}, bf16[3,192,512]{2,1,0:T(8,128)(2,1)}, u32[]{:S(2)}, u32[]{:S(2)}) collective-permute-start(bf16[3,192,512]{2,1,0:T(8,128)(2,1)} %collective-permute-done.54.rest_12_), channel_id=1, source_target_pairs={{0,8},{4,12},{8,0},{12,4},{16,24},{20,28},{24,16},{28,20},{1,9},{5... | collective-permute-start | bytes 1769480 | tf_op jit(solution)/shard_map/ppermute | solution.py:48
  357.1 101.7 %collective-permute-start.61 = (bf16[256,1536]{1,0:T(8,128)(2,1)}, bf16[256,1536]{1,0:T(8,128)(2,1)S(1)}, u32[]{:S(2)}, u32[]{:S(2)}) collective-permute-start(bf16[256,1536]{1,0:T(8,128)(2,1)} %get-tuple-element.94), channel_id=1, source_target_pairs={{0,3},{1,0},{2,1},{3,2},{4,7},{5,4},{6,5},{7,6},{8,11},{9,8},{10,9... | collective-permute-start | bytes 2359304 | tf_op jit(solution)/shard_map/ppermute | solution.py:92
  388.5 70.2 %collective-permute-start.62 = (bf16[256,1536]{1,0:T(8,128)(2,1)}, bf16[256,1536]{1,0:T(8,128)(2,1)S(1)}, u32[]{:S(2)}, u32[]{:S(2)}) collective-permute-start(bf16[256,1536]{1,0:T(8,128)(2,1)} %get-tuple-element.95), channel_id=1, source_target_pairs={{0,2},{1,3},{2,0},{3,1},{4,6},{5,7},{6,4},{7,5},{8,10},{9,11},{10,... | collective-permute-start | bytes 2359304 | tf_op jit(solution)/shard_map/ppermute | solution.py:92
  388.5 70.2 %collective-permute-start.63 = (bf16[256,1536]{1,0:T(8,128)(2,1)}, bf16[256,1536]{1,0:T(8,128)(2,1)S(1)}, u32[]{:S(2)}, u32[]{:S(2)}) collective-permute-start(bf16[256,1536]{1,0:T(8,128)(2,1)} %get-tuple-element.96), channel_id=1, source_target_pairs={{0,1},{1,2},{2,3},{3,0},{4,5},{5,6},{6,7},{7,4},{8,9},{9,10},{10,1... | collective-permute-start | bytes 2359304 | tf_op jit(solution)/shard_map/ppermute | solution.py:92
  389.2 51.0 %collective-permute-start.64 = (f32[8,256]{1,0:T(8,128)}, f32[8,256]{1,0:T(8,128)S(1)}, u32[]{:S(2)}, u32[]{:S(2)}) collective-permute-start(f32[8,256]{1,0:T(8,128)} %get-tuple-element.98), channel_id=1, source_target_pairs={{0,3},{1,0},{2,1},{3,2},{4,7},{5,4},{6,5},{7,6},{8,11},{9,8},{10,9... | collective-permute-start | bytes 24584 | tf_op jit(solution)/shard_map/ppermute | solution.py:92
  392.3 64.8 %collective-permute-start.65 = (f32[8,256]{1,0:T(8,128)}, f32[8,256]{1,0:T(8,128)S(1)}, u32[]{:S(2)}, u32[]{:S(2)}) collective-permute-start(f32[8,256]{1,0:T(8,128)} %get-tuple-element.99), channel_id=1, source_target_pairs={{0,2},{1,3},{2,0},{3,1},{4,6},{5,7},{6,4},{7,5},{8,10},{9,11},{10,... | collective-permute-start | bytes 24584 | tf_op jit(solution)/shard_map/ppermute | solution.py:92
  486.4 92.4 %collective-permute-start.67 = (bf16[4,192,2688]{2,1,0:T(8,128)(2,1)}, bf16[4,192,2688]{2,1,0:T(8,128)(2,1)}, u32[]{:S(2)}, u32[]{:S(2)}) collective-permute-start(bf16[4,192,2688]{2,1,0:T(8,128)(2,1)} %get-tuple-element.109), channel_id=1, source_target_pairs={{0,4},{4,0},{8,12},{12,8},{16,20},{20,16},{24,28},{28,24},{1,5},{5... | collective-permute-start | bytes 12386312 | tf_op jit(solution)/shard_map/ppermute | solution.py:48
  496.1 77.6 %collective-permute-start.85 = (bf16[4,3,192,512]{3,2,1,0:T(8,128)(2,1)S(1)}, bf16[4,3,192,512]{3,2,1,0:T(8,128)(2,1)S(1)}, u32[]{:S(2)}, u32[]{:S(2)}) collective-permute-start(bf16[4,3,192,512]{3,2,1,0:T(8,128)(2,1)S(1)} %copy-done.51), channel_id=1, source_target_pairs={{0,4},{4,0},{8,12},{12,8},{16,20},{20,16},{24,28},{28,24},{1,5},{5... | collective-permute-start | bytes 7077896 | tf_op jit(solution)/shard_map/ppermute | solution.py:48
  496.3 77.9 %collective-permute-start.82 = (bf16[4,3,192,512]{3,2,1,0:T(8,128)(2,1)}, bf16[4,3,192,512]{3,2,1,0:T(8,128)(2,1)S(1)}, u32[]{:S(2)}, u32[]{:S(2)}) collective-permute-start(bf16[4,3,192,512]{3,2,1,0:T(8,128)(2,1)} %get-tuple-element.119), channel_id=1, source_target_pairs={{0,4},{4,0},{8,12},{12,8},{16,20},{20,16},{24,28},{28,24},{1,5},{5... | collective-permute-start | bytes 7077896 | tf_op jit(solution)/shard_map/ppermute | solution.py:48
  496.6 53.1 %collective-permute-start.59 = (bf16[256,1536]{1,0:T(8,128)(2,1)}, bf16[256,1536]{1,0:T(8,128)(2,1)S(1)}, u32[]{:S(2)}, u32[]{:S(2)}) collective-permute-start(bf16[256,1536]{1,0:T(8,128)(2,1)} %get-tuple-element.80), channel_id=1, source_target_pairs={{0,2},{1,3},{2,0},{3,1},{4,6},{5,7},{6,4},{7,5},{8,10},{9,11},{10,... | collective-permute-start | bytes 2359304 | tf_op jit(solution)/shard_map/ppermute | solution.py:92
  514.8 61.9 %collective-permute-start.79 = (bf16[4,3,192,512]{3,2,1,0:T(8,128)(2,1)}, bf16[4,3,192,512]{3,2,1,0:T(8,128)(2,1)S(1)}, u32[]{:S(2)}, u32[]{:S(2)}) collective-permute-start(bf16[4,3,192,512]{3,2,1,0:T(8,128)(2,1)} %get-tuple-element.117), channel_id=1, source_target_pairs={{0,4},{4,0},{8,12},{12,8},{16,20},{20,16},{24,28},{28,24},{1,5},{5... | collective-permute-start | bytes 7077896 | tf_op jit(solution)/shard_map/ppermute | solution.py:48
  583.5 94.5 %collective-permute-start.68 = (bf16[2,192,2688]{2,1,0:T(8,128)(2,1)S(1)}, bf16[2,192,2688]{2,1,0:T(8,128)(2,1)S(1)}, u32[]{:S(2)}, u32[]{:S(2)}) collective-permute-start(bf16[2,192,2688]{2,1,0:T(8,128)(2,1)S(1)} %get-tuple-element.163), channel_id=1, source_target_pairs={{0,8},{4,12},{8,0},{12,4},{16,24},{20,28},{24,16},{28,20},{1,9},{5... | collective-permute-start | bytes 6193160 | tf_op jit(solution)/shard_map/ppermute | solution.py:48
  585.1 90.0 %collective-permute-start.80 = (bf16[2,3,192,512]{3,2,1,0:T(8,128)(2,1)S(1)}, bf16[2,3,192,512]{3,2,1,0:T(8,128)(2,1)S(1)}, u32[]{:S(2)}, u32[]{:S(2)}) collective-permute-start(bf16[2,3,192,512]{3,2,1,0:T(8,128)(2,1)S(1)} %get-tuple-element.172), channel_id=1, source_target_pairs={{0,8},{4,12},{8,0},{12,4},{16,24},{20,28},{24,16},{28,20},{1,9},{5... | collective-permute-start | bytes 3538952 | tf_op jit(solution)/shard_map/ppermute | solution.py:48
  586.3 90.3 %collective-permute-start.71 = (bf16[2,192,1536]{2,1,0:T(8,128)(2,1)S(1)}, bf16[2,192,1536]{2,1,0:T(8,128)(2,1)S(1)}, u32[]{:S(2)}, u32[]{:S(2)}) collective-permute-start(bf16[2,192,1536]{2,1,0:T(8,128)(2,1)S(1)} %get-tuple-element.178), channel_id=1, source_target_pairs={{0,16},{4,20},{8,24},{12,28},{16,0},{20,4},{24,8},{28,12},{1,17},{... | collective-permute-start | bytes 3538952 | tf_op jit(solution)/shard_map/ppermute | solution.py:48
  605.7 73.4 %collective-permute-start.77 = (bf16[2,3,192,512]{3,2,1,0:T(8,128)(2,1)S(1)}, bf16[2,3,192,512]{3,2,1,0:T(8,128)(2,1)S(1)}, u32[]{:S(2)}, u32[]{:S(2)}) collective-permute-start(bf16[2,3,192,512]{3,2,1,0:T(8,128)(2,1)S(1)} %get-tuple-element.174), channel_id=1, source_target_pairs={{0,16},{4,20},{8,24},{12,28},{16,0},{20,4},{24,8},{28,12},{1,17},{... | collective-permute-start | bytes 3538952 | tf_op jit(solution)/shard_map/ppermute | solution.py:48
  608.2 92.2 %collective-permute-start.74 = (bf16[2,3,192,512]{3,2,1,0:T(8,128)(2,1)S(1)}, bf16[2,3,192,512]{3,2,1,0:T(8,128)(2,1)S(1)}, u32[]{:S(2)}, u32[]{:S(2)}) collective-permute-start(bf16[2,3,192,512]{3,2,1,0:T(8,128)(2,1)S(1)} %get-tuple-element.176), channel_id=1, source_target_pairs={{0,8},{4,12},{8,0},{12,4},{16,24},{20,28},{24,16},{28,20},{1,9},{5... | collective-permute-start | bytes 3538952 | tf_op jit(solution)/shard_map/ppermute | solution.py:48
  675.1 73.2 %collective-permute-start.87 = (bf16[3,192,512]{2,1,0:T(8,128)(2,1)}, bf16[3,192,512]{2,1,0:T(8,128)(2,1)}, u32[]{:S(2)}, u32[]{:S(2)}) collective-permute-start(bf16[3,192,512]{2,1,0:T(8,128)(2,1)} %fusion.8), channel_id=1, source_target_pairs={{0,16},{4,20},{8,24},{12,28},{16,0},{20,4},{24,8},{28,12},{1,17},{... | collective-permute-start | bytes 1769480 | tf_op jit(solution)/shard_map/ppermute | solution.py:48
  676.6 70.2 %collective-permute-start.84 = (bf16[3,192,512]{2,1,0:T(8,128)(2,1)}, bf16[3,192,512]{2,1,0:T(8,128)(2,1)}, u32[]{:S(2)}, u32[]{:S(2)}) collective-permute-start(bf16[3,192,512]{2,1,0:T(8,128)(2,1)} %fusion.7), channel_id=1, source_target_pairs={{0,8},{4,12},{8,0},{12,4},{16,24},{20,28},{24,16},{28,20},{1,9},{5... | collective-permute-start | bytes 1769480 | tf_op jit(solution)/shard_map/ppermute | solution.py:48
  678.0 47.2 %collective-permute-start.72 = (bf16[192,1536]{1,0:T(8,128)(2,1)S(1)}, bf16[192,1536]{1,0:T(8,128)(2,1)S(1)}, u32[]{:S(2)}, u32[]{:S(2)}) collective-permute-start(bf16[192,1536]{1,0:T(8,128)(2,1)S(1)} %fusion.3), channel_id=1, source_target_pairs={{0,8},{4,12},{8,0},{12,4},{16,24},{20,28},{24,16},{28,20},{1,9},{5... | collective-permute-start | bytes 1769480 | tf_op jit(solution)/shard_map/ppermute | solution.py:48
  679.1 48.3 %collective-permute-start.69 = (bf16[192,2688]{1,0:T(8,128)(2,1)S(1)}, bf16[192,2688]{1,0:T(8,128)(2,1)S(1)}, u32[]{:S(2)}, u32[]{:S(2)}) collective-permute-start(bf16[192,2688]{1,0:T(8,128)(2,1)S(1)} %fusion.2), channel_id=1, source_target_pairs={{0,16},{4,20},{8,24},{12,28},{16,0},{20,4},{24,8},{28,12},{1,17},{... | collective-permute-start | bytes 3096584 | tf_op jit(solution)/shard_map/ppermute | solution.py:48
  700.4 45.1 %collective-permute-start.81 = (bf16[3,192,512]{2,1,0:T(8,128)(2,1)}, bf16[3,192,512]{2,1,0:T(8,128)(2,1)}, u32[]{:S(2)}, u32[]{:S(2)}) collective-permute-start(bf16[3,192,512]{2,1,0:T(8,128)(2,1)} %fusion.6), channel_id=1, source_target_pairs={{0,16},{4,20},{8,24},{12,28},{16,0},{20,4},{24,8},{28,12},{1,17},{... | collective-permute-start | bytes 1769480 | tf_op jit(solution)/shard_map/ppermute | solution.py:48
  (139 other events, 3344.0 us)
Sparse Core Ops, SparseCore 0:
  729.5 68.9 all-reduce.2

commit v2 on v1

v2 whole, which is shorter than its diff:
```python
import functools

import jax
import jax.numpy as jnp
from jax import lax
from jax.experimental import pallas as pl
from jax.experimental.pallas import tpu as pltpu
from jax.sharding import PartitionSpec as P

HEADS = 24
KV_HEADS = 8
HEAD_DIM = 64
TOP = 8
GROUPS = HEADS // KV_HEADS
QW = HEADS * HEAD_DIM
KW = KV_HEADS * HEAD_DIM
QKV = QW + 2 * KW
EXT = 128
HALVES = 2
EXTRA = 16
COST_SCALE = 1.0

norm_eps = 1e-06
masked_score = -1e30
BF = jnp.bfloat16
F32 = jnp.float32
ANY = pl.BlockSpec(memory_space=pl.ANY)
VMEM = pl.BlockSpec(memory_space=pltpu.VMEM)
SMEM = pl.BlockSpec(memory_space=pltpu.SMEM)
VMEM_LIMIT = 56 * 1024 * 1024


def dot(a, b, ca=1, cb=0):
    return lax.dot_general(a, b, (((ca,), (cb,)), ((), ())), preferred_element_type=F32)


def params():
    return pltpu.CompilerParams(vmem_limit_bytes=VMEM_LIMIT)


def cost(us):
    return pl.CostEstimate(
        flops=int(us * 1e8), bytes_accessed=int(us * 3.6e6 * COST_SCALE), transcendentals=0
    )


def sds(shape, dtype):
    return jax.ShapeDtypeStruct(shape, dtype)


def swap(value, bit, size):
    return lax.ppermute(value, "dp", [(i, i ^ bit) for i in range(size)])


def after(value, *others):
    if not others:
        return value
    return lax.optimization_barrier((value,) + others)[0]


def gather_shards(shard, route, size, name):
    rows = shard.shape[-2]
    if size != 8:
        return [lax.all_gather(shard, "dp", axis=0, tiled=False)], [(i, 0, rows) for i in range(size)]
    half = rows // 2
    with jax.named_scope(name):
        across = swap(shard, 2, size)
        along = swap(shard, 4, size)
        arrays, plan = [shard, across, along], [(0, 0, rows), (2, 0, rows), (4, 0, rows)]
        if route == 0:
            arrays.append(swap(across, 4, size))
            plan.append((6, 0, rows))
        elif route == 1:
            arrays.append(swap(along, 2, size))
            plan.append((6, 0, rows))
        else:
            arrays.append(swap(across[..., :half, :], 4, size))
            arrays.append(swap(along[..., half:, :], 2, size))
            plan += [(6, 0, half), (6, half, rows - half)]
        for array, (mask, start, count) in list(zip(arrays, plan)):
            arrays.append(swap(array, 1, size))
            plan.append((mask + 1, start, count))
    return arrays, plan


def add(a, b):
    return (a.astype(F32) + b.astype(F32)).astype(BF)


def pair_sum(parts, route, *earlier):
    own, other = parts
    other = after(swap(other, 1, 8), *earlier)
    if route == 0:
        return add(own[1::2], other[1::2]), add(own[0::2], other[0::2])
    return add(own[2:], other[2:]), add(own[:2], other[:2])


def link_sum(sent, kept, route, *earlier):
    sent = after(swap(sent, 2 if route == 0 else 4, 8), *earlier)
    return add(kept[1], sent[1]), add(kept[0], sent[0])


def last_sum(sent, kept, route, *earlier):
    sent = after(swap(sent, 4 if route == 0 else 2, 8), *earlier)
    return add(kept, sent)


def owner_at(z, r, owners):
    return jnp.bitwise_xor(z, r) if owners == 4 else lax.rem(z - r + owners, owners)


def along(value, pairs):
    return lax.ppermute(value, "expert", pairs)


def cross(value, bit):
    return along(value, [(i, i ^ bit) for i in range(4)])


def gather_owners(value, z, owners, due):
    if owners != 4:
        turns = [[(i, (i + r) % owners) for i in range(owners)] for r in range(1, owners)]
        return [value] + [along(value, pairs) for pairs in turns]
    far, near = cross(value, 2), cross(value, 1)
    middle = along(after(value, far, near, *due), [(1, 2), (2, 1)])
    passed = along(far, [(2, 3), (1, 0)])
    inner = (z == 1) | (z == 2)
    return [value, near, far, jnp.where(inner, middle, passed)]


def return_owners(parts, owners):
    if owners != 4:
        turns = [[(i, (i - r) % owners) for i in range(owners)] for r in range(1, owners)]
        return [parts[0]] + [along(v, pairs) for v, pairs in zip(parts[1:], turns)]
    passed = along(parts[3], [(3, 2), (0, 1)])
    middle = along(parts[3], [(1, 2), (2, 1)])
    relay = (parts[2].astype(F32) + passed.astype(F32)).astype(BF)
    return [parts[0], cross(parts[1], 1), cross(relay, 2), middle]


def exchange(value):
    return lax.all_to_all(value, "expert", split_axis=0, concat_axis=0, tiled=True)


def spread(value):
    owners = lax.axis_size("expert")
    return exchange(jnp.concatenate([value] * owners, axis=0))


def owner_sum(low):
    owners = lax.axis_size("expert")
    parts = exchange(low).reshape(owners, -1, low.shape[1]).astype(F32)
    return jnp.sum(parts, axis=0).astype(BF)


def plain_sum(parts):
    total = lax.psum_scatter(parts[0], "dp", scatter_dimension=0, tiled=True)
    return lax.psum(total[0], "expert").astype(F32)


def part_shapes(size, shape):
    if size != 8:
        return [sds((size,) + shape, BF)]
    return [sds((4,) + shape, BF), sds((4,) + shape, BF)]


def fetch(me, refs, plan, target, sems, rows, size):
    copies = []
    for n, (i, start, count) in enumerate(plan):
        source = refs[0].at[i] if len(refs) == 1 else refs[n]
        at = (jnp.bitwise_xor(me, i) if size == 8 else i) * rows + start
        if size == 8:
            at = pl.multiple_of(at, rows // 2)
        copies.append(pltpu.make_async_copy(source, target(pl.ds(at, count)), sems.at[n]))
    for c in copies:
        c.start()
    return copies


def store_parts(me, source, outs, sems, rows, size):
    copies = []
    for i in range(size):
        if len(outs) == 1:
            target, at = outs[0].at[i], i * rows
        else:
            target = outs[i % 2].at[i // 2]
            at = pl.multiple_of(jnp.bitwise_xor(me, i) * rows, rows)
        copies.append(pltpu.make_async_copy(source(pl.ds(at, rows)), target, sems.at[i]))
    for c in copies:
        c.start()
    return copies


def pack_kernel(experts, q, k, v, router, gain_one, gain_two, out):
    rows = q.shape[0]
    pad = -(-experts // 8) * 8
    out[:, :QW] = q[...]
    out[:, QW : QW + KW] = k[...]
    out[:, QW + KW : QKV] = v[...]
    gains = [jnp.broadcast_to(g[...].astype(F32)[None, :], (8, rows)) for g in (gain_one, gain_two)]
    parts = [router[...].astype(F32)]
    if pad > experts:
        parts.append(jnp.zeros((pad - experts, rows), F32))
    parts += gains + [jnp.zeros((EXT - pad - 16, rows), F32)]
    out[:, QKV:] = jnp.concatenate(parts, axis=0).T.astype(BF)


def run_pack(q, k, v, router, gain_one, gain_two):
    rows, experts = router.shape
    return pl.pallas_call(
        functools.partial(pack_kernel, experts),
        name="pack",
        out_shape=sds((rows, QKV + EXT), BF),
        in_specs=[VMEM] * 6,
        out_specs=VMEM,
        compiler_params=params(),
        cost_estimate=cost(0.01),
    )(q, k, v, router.T, gain_one, gain_two)


def attention_kernel(size, rows, plan, me, tok, seg_row, seg_col, *rest):
    refs, rest = rest[:-7], rest[-7:]
    low_out, qkv_out, ctx_out, prob_out, ext_out, w, sems = rest
    copies = fetch(me[0], refs, plan, lambda s: w.at[s], sems, rows, size)
    seq = tok.shape[0]
    x = tok[...].astype(F32)
    factor = lax.rsqrt(jnp.mean(x * x, axis=-1, keepdims=True) + norm_eps)
    normed = x * factor
    same = seg_col[...] == seg_row[...]
    key_at = lax.broadcasted_iota(jnp.int32, (seq, seq), 0)
    query_at = lax.broadcasted_iota(jnp.int32, (seq, seq), 1)
    allowed = jnp.where(same & (key_at <= query_at), 0.0, masked_score)
    allowed = jnp.concatenate([allowed] * GROUPS, axis=1)
    for c in copies:
        c.wait()
    ext = w[:, QKV:].astype(F32).T[: ext_out.shape[0], :]
    ext_out[...] = ext
    experts_pad = ext_out.shape[0] - 16
    gain = ext[experts_pad : experts_pad + 1, :]
    low = (normed * gain).astype(BF)
    low_out[...] = low
    step = 512
    for j in range(QKV // step):
        at = slice(j * step, (j + 1) * step)
        part = dot(low, w[:, at])
        qkv_out[at, :] = part.T.astype(BF)
    for h in range(KV_HEADS):
        q = jnp.concatenate(
            [
                qkv_out[(GROUPS * h + g) * HEAD_DIM : (GROUPS * h + g + 1) * HEAD_DIM, :]
                for g in range(GROUPS)
            ],
            axis=1,
        )
        k = qkv_out[QW + h * HEAD_DIM : QW + (h + 1) * HEAD_DIM, :]
        v = qkv_out[QW + KW + h * HEAD_DIM : QW + KW + (h + 1) * HEAD_DIM, :]
        scores = dot(k, q, 0, 0) * HEAD_DIM ** (-0.5)
        scores = jnp.where(allowed < 0.0, masked_score, scores)
        top = jnp.max(scores, axis=0, keepdims=True)
        shifted = jnp.exp(scores - top)
        probs = (shifted * (1.0 / jnp.sum(shifted, axis=0, keepdims=True))).astype(BF)
        prob_out[h] = probs
        ctx = dot(v, probs).astype(BF)
        for g in range(GROUPS):
            at = (GROUPS * h + g) * HEAD_DIM
            ctx_out[at : at + HEAD_DIM, :] = ctx[:, g * seq : (g + 1) * seq]


def run_attention(me, tokens, seg_row, seg_col, pieces, size, ext_rows):
    seq, width = tokens.shape
    rows = width // size
    arrays, plan = pieces
    return pl.pallas_call(
        functools.partial(attention_kernel, size, rows, plan),
        name="attention",
        out_shape=[
            sds((seq, width), BF),
            sds((QKV, seq), BF),
            sds((QW, seq), BF),
            sds((KV_HEADS, seq, GROUPS * seq), BF),
            sds((ext_rows, width), F32),
        ],
        in_specs=[SMEM, VMEM, VMEM, VMEM] + [ANY] * len(arrays),
        out_specs=[VMEM] * 5,
        scratch_shapes=[
            pltpu.VMEM((width, QKV + EXT), BF),
            pltpu.SemaphoreType.DMA((len(plan),)),
        ],
        compiler_params=params(),
        cost_estimate=cost(0.01),
    )(me, tokens, seg_row, seg_col, *arrays)


def residual_kernel(size, rows, plan, me, tok, ctx, ext, place, *rest):
    refs, (res_out, low_out, w, sems) = rest[:-4], rest[-4:]
    copies = fetch(me[0], refs, plan, lambda s: w.at[s], sems, rows, size)
    experts_pad = ext.shape[0] - 16
    for c in copies:
        c.wait()
    res = tok[...].astype(F32) + dot(ctx[...], w[...], 0, 0)
    res_out[...] = res
    factor = lax.rsqrt(jnp.mean(res * res, axis=-1, keepdims=True) + norm_eps)
    seq = res.shape[0]
    low_out[:seq, :] = (res * factor * ext[experts_pad + 8 : experts_pad + 9, :]).astype(BF)
    low_out[seq:, :] = place[...]


def run_residual(me, tokens, ctx, ext, place, pieces, size):
    seq, width = tokens.shape
    rows = QW // size
    arrays, plan = pieces
    return pl.pallas_call(
        functools.partial(residual_kernel, size, rows, plan),
        name="residual",
        out_shape=[sds((seq, width), F32), sds((seq + EXTRA, width), BF)],
        in_specs=[SMEM, VMEM, VMEM, VMEM, VMEM] + [ANY] * len(arrays),
        out_specs=[VMEM] * 2,
        scratch_shapes=[pltpu.VMEM((QW, width), BF), pltpu.SemaphoreType.DMA((len(plan),))],
        compiler_params=params(),
        cost_estimate=cost(0.01),
    )(me, tokens, ctx, ext, place, *arrays)


def slot_of(block, seq, width):
    across = width // seq
    row, col = block // across * 8, block % across * seq
    return slice(row, row + 8), slice(col, col + seq)


def router_kernel(owners, per, z, ext, *rest):
    rows, rest = rest[:owners], rest[owners:]
    pos_out, p_out, own_out, all_p, all_pos = rest
    experts_pad = ext.shape[0] - 16
    seq, width = rows[0].shape[0] - EXTRA, rows[0].shape[1]
    router = ext[:experts_pad, :].astype(BF)
    at = z[0] * per
    for r in range(owners):
        logits = dot(router, rows[r][:seq, :], 1, 1)
        spots = rows[r][seq:, :].astype(F32)
        for b in range(experts_pad // 8):
            of, to = slot_of(b, seq, width)
            all_pos[b * 8 : (b + 1) * 8, :] = spots[of, to]
        where = all_pos[...]
        named = where >= 0.0
        logits = jnp.where(named, logits, masked_score)
        top = jnp.max(logits, axis=0, keepdims=True)
        shifted = jnp.where(named, jnp.exp(logits - top), 0.0)
        probs = shifted / jnp.sum(shifted, axis=0, keepdims=True)
        all_p[...] = probs
        if r == 0:
            own_out[...] = probs
        for l in range(per):
            p_out[l, r : r + 1, :] = all_p[pl.ds(at + l, 1), :]
            pos_out[l, r : r + 1, :] = all_pos[pl.ds(at + l, 1), :].astype(jnp.int32)


def run_router(z, ext, rows, per):
    owners = len(rows)
    seq = rows[0].shape[0] - EXTRA
    experts_pad = ext.shape[0] - 16
    return pl.pallas_call(
        functools.partial(router_kernel, owners, per),
        name="router",
        out_shape=[
            sds((per, owners, seq), jnp.int32),
            sds((per, owners, seq), F32),
            sds((experts_pad, seq), F32),
        ],
        in_specs=[SMEM, VMEM] + [VMEM] * owners,
        out_specs=[VMEM] * 3,
        scratch_shapes=[pltpu.VMEM((experts_pad, seq), F32)] * 2,
        compiler_params=params(),
        cost_estimate=cost(0.01),
    )(z, ext, *rows)


def pick_rows(owners, cap, number, z, pos, p, xs, cs, xv, cv, xr, cr, prow, sem_x, sem_c):
    seq = xv.shape[1]
    copies_x = [
        pltpu.make_async_copy(xs[r].at[pl.ds(0, seq)], xv.at[r], sem_x.at[r]) for r in range(owners)
    ]
    copies_c = []
    for r in range(owners):
        start = pl.multiple_of(owner_at(z[0], r, owners) * seq, seq)
        copies_c.append(pltpu.make_async_copy(cs.at[pl.ds(start, seq)], cv.at[r], sem_c.at[r]))
    for a, b in zip(copies_x, copies_c):
        a.start()
        b.start()

    def finish():
        slot = lax.broadcasted_iota(jnp.int32, (cap, seq), 0)
        for r in range(owners):
            copies_x[r].wait()
            copies_c[r].wait()
            hot = pos[number, r : r + 1, :] == slot
            low_hot = jnp.where(hot, 1.0, 0.0).astype(BF)
            at = pl.ds(r * cap, cap)
            xr[at, :] = dot(low_hot, xv[r]).astype(BF)
            cr[at, :] = dot(low_hot, cv[r]).astype(BF)
            prow[at, :] = jnp.sum(
                jnp.where(hot, p[number, r : r + 1, :], 0.0), axis=1, keepdims=True
            )

    return finish


def through_expert(owners, cap, number, pos, xr, cr, prow, w, hp, gg, ug, gate, gate_out):
    ff = w.shape[2]
    step = ff // HALVES
    gate[...] = jnp.zeros_like(gate)
    for j in range(HALVES):
        cols = slice(j * step, (j + 1) * step)
        gate_pre = dot(xr[...], w[0, :, cols])
        up_pre = dot(xr[...], w[1, :, cols])
        back = dot(cr[...], w[2, :, cols])
        probs = prow[...]
        s = jax.nn.sigmoid(gate_pre)
        silu = gate_pre * s
        hidden = silu * up_pre
        gate[...] += jnp.sum(hidden * back, axis=1, keepdims=True)
        hp[:, cols] = (hidden * probs).astype(BF)
        back = back * probs
        gg[:, cols] = (back * up_pre * (s + silu * (1.0 - s))).astype(BF)
        ug[:, cols] = (back * silu).astype(BF)
    seq = pos.shape[2]
    slot = lax.broadcasted_iota(jnp.int32, (cap, seq), 0)
    for r in range(owners):
        hot = pos[number, r : r + 1, :] == slot
        at = pl.ds(r * cap, cap)
        gate_out[r : r + 1, :] = jnp.sum(jnp.where(hot, gate[at, :], 0.0), axis=0, keepdims=True)


def load_weights(me, refs, plan, w, sems, slot_at, rows, size):
    shards = [ref.at[:, slot_at] if len(refs) == 1 else ref.at[slot_at] for ref in refs]
    return fetch(me, shards, plan, lambda s: w.at[:, s, :], sems, rows, size)


def weight_grads(xr, cr, hp, gg, ug, g, grads, sems, slot_at, rows, size):
    width = xr.shape[1]
    tile = width // HALVES
    for j in range(HALVES):
        cols = slice(j * tile, (j + 1) * tile)
        g[0, cols, :] = dot(xr[:, cols], gg[...], 0, 0).astype(BF)
        g[1, cols, :] = dot(xr[:, cols], ug[...], 0, 0).astype(BF)
        g[2, cols, :] = dot(cr[:, cols], hp[...], 0, 0).astype(BF)
    copies = [
        pltpu.make_async_copy(g.at[:, pl.ds(i * rows, rows), :], grads.at[i, slot_at], sems.at[i])
        for i in range(size)
    ]
    for c in copies:
        c.start()
    return copies


def rows_back(w, gg, ug, bv):
    tile = bv.shape[1] // HALVES
    for j in range(HALVES):
        cols = slice(j * tile, (j + 1) * tile)
        total = dot(gg[...], w[0, cols, :], 1, 1) + dot(ug[...], w[1, cols, :], 1, 1)
        bv[:, cols] = total.astype(BF)


def rows_out(w, hp, ov):
    tile = ov.shape[1] // HALVES
    for j in range(HALVES):
        cols = slice(j * tile, (j + 1) * tile)
        ov[:, cols] = dot(hp[...], w[cols, :], 1, 1).astype(BF)


def expert_kernel(
    size, rows, owners, cap, number, slot_at, weight_at, plan, count, me, z, pos, p, cs, *rest
):
    xs, refs, rest = rest[:owners], rest[owners : owners + count], rest[owners + count :]
    if slot_at > 0:
        rest = rest[1:]
    out_rows, back_rows, gate_out, grads = rest[:4]
    xv, cv, w, xr, cr, prow, hp, gg, ug, gate, ov, bv, g, sem_x, sem_c, sem_w, sem_o = rest[4:]
    finish = pick_rows(owners, cap, number, z, pos, p, xs, cs, xv, cv, xr, cr, prow, sem_x, sem_c)
    copies_w = load_weights(me[0], refs, plan, w, sem_w, weight_at, rows, size)
    finish()
    for c in copies_w:
        c.wait()
    through_expert(owners, cap, number, pos, xr, cr, prow, w, hp, gg, ug, gate, gate_out)
    copies = weight_grads(xr, cr, hp, gg, ug, g, grads, sem_w, slot_at, rows, size)
    rows_back(w, gg, ug, bv)
    copy_b = pltpu.make_async_copy(bv, back_rows, sem_o.at[0])
    copy_b.start()
    rows_out(w.at[2], hp, ov)
    copy_o = pltpu.make_async_copy(ov, out_rows, sem_o.at[1])
    copy_o.start()
    for c in copies + [copy_b, copy_o]:
        c.wait()


def grads_shape(size, count, rows, ff):
    return sds((size, count, 3, rows, ff), BF)


def run_expert(me, z, pos, p, xs, cs, pieces, weight_at, buffer, size, number, slot_at, count, cap):
    owners, seq = pos.shape[1:]
    width = xs[0].shape[1]
    refs, plan = pieces
    ff = refs[0].shape[-1]
    rows = width // size
    total = owners * cap
    given = [me, z, pos, p, cs, *xs, *refs] + ([] if buffer is None else [buffer])
    return pl.pallas_call(
        functools.partial(
            expert_kernel, size, rows, owners, cap, number, slot_at, weight_at, plan, len(refs)
        ),
        name="expert",
        out_shape=[
            sds((total, width), BF),
            sds((total, width), BF),
            sds((owners, seq), F32),
            grads_shape(size, count, rows, ff),
        ],
        in_specs=[SMEM, SMEM, VMEM, VMEM] + [ANY] * (len(given) - 4),
        out_specs=[ANY, ANY, VMEM, ANY],
        input_output_aliases={} if buffer is None else {len(given) - 1: 3},
        scratch_shapes=[
            pltpu.VMEM((owners, seq, width), BF),
            pltpu.VMEM((owners, seq, width), BF),
            pltpu.VMEM((3, width, ff), BF),
            pltpu.VMEM((total, width), BF),
            pltpu.VMEM((total, width), BF),
            pltpu.VMEM((total, 1), F32),
            pltpu.VMEM((total, ff), BF),
            pltpu.VMEM((total, ff), BF),
            pltpu.VMEM((total, ff), BF),
            pltpu.VMEM((total, 1), F32),
            pltpu.VMEM((total, width), BF),
            pltpu.VMEM((total, width), BF),
            pltpu.VMEM((3, width, ff), BF),
            pltpu.SemaphoreType.DMA((owners,)),
            pltpu.SemaphoreType.DMA((owners,)),
            pltpu.SemaphoreType.DMA((max(size, len(plan)),)),
            pltpu.SemaphoreType.DMA((2,)),
        ],
        compiler_params=params(),
        cost_estimate=cost(0.01),
    )(*given)


def combined_rows(per, cap, pos, r, rows):
    seq = pos.shape[2]
    slot = lax.broadcasted_iota(jnp.int32, (cap, seq), 0)
    hot = jnp.concatenate(
        [jnp.where(pos[l, pl.ds(r, 1), :] == slot, 1.0, 0.0).astype(BF) for l in range(per)], axis=0
    )
    stacked = jnp.concatenate([rows[l][...] for l in range(per)], axis=0)
    return dot(hot, stacked, 0, 0).astype(BF)


def combine_back_kernel(owners, per, cap, experts_pad, z, pos, *rest):
    rows, gates, rest = rest[:per], rest[per : 2 * per], rest[2 * per :]
    outs, block = rest[:owners], rest[owners]
    r = pl.program_id(0)
    seq, width = pos.shape[2], outs[0].shape[1]
    total = combined_rows(per, cap, pos, r, rows)
    block[...] = jnp.zeros_like(block)
    for l in range(per):
        block[pl.ds(z[0] * per + l, 1), :] = gates[l][pl.ds(r, 1), :]
    value = block[...]
    high = value.astype(BF)
    low = (value - high.astype(F32)).astype(BF)
    for o in range(owners):

        @pl.when(r == o)
        def _():
            outs[o][:seq, :] = total
            outs[o][seq:, :] = jnp.zeros((EXTRA, width), BF)
            both = jnp.concatenate([high, low], axis=0).astype(F32)
            for row in range(EXTRA // 8):
                across = width // seq
                blocks = [
                    both[(row * across + b) * 8 : (row * across + b + 1) * 8, :]
                    if row * across + b < 2 * experts_pad // 8
                    else jnp.zeros((8, seq), F32)
                    for b in range(across)
                ]
                outs[o][seq + row * 8 : seq + row * 8 + 8, :] = jnp.concatenate(
                    blocks, axis=1
                ).astype(BF)


def whole(shape):
    return pl.BlockSpec(shape, lambda r: (0,) * len(shape))


def run_combine_back(z, pos, rows, gates, cap, experts_pad):
    per, owners, seq = pos.shape
    width = rows[0].shape[1]
    shapes = [sds((seq + EXTRA, width), BF)] * owners
    return pl.pallas_call(
        functools.partial(combine_back_kernel, owners, per, cap, experts_pad),
        name="combine_back",
        grid=(owners,),
        out_shape=shapes,
        in_specs=[SMEM, whole(pos.shape)]
        + [pl.BlockSpec((cap, width), lambda r: (r, 0))] * per
        + [whole((owners, seq))] * per,
        out_specs=[whole(s.shape) for s in shapes],
        scratch_shapes=[pltpu.VMEM((experts_pad, seq), F32)],
        compiler_params=params(),
        cost_estimate=cost(0.01),
    )(z, pos, *rows, *gates)


def combine_out_kernel(per, cap, z, pos, *rest):
    rows, out = rest[:per], rest[per]
    out[...] = combined_rows(per, cap, pos, pl.program_id(0), rows)


def run_combine_out(z, pos, rows, cap):
    per, owners, seq = pos.shape
    width = rows[0].shape[1]
    grid_spec = pltpu.PrefetchScalarGridSpec(
        num_scalar_prefetch=1,
        grid=(owners,),
        in_specs=[pl.BlockSpec(pos.shape, lambda r, z: (0, 0, 0))]
        + [pl.BlockSpec((cap, width), lambda r, z: (r, 0))] * per,
        out_specs=pl.BlockSpec((seq, width), lambda r, z: (owner_at(z[0], r, owners), 0)),
    )
    return pl.pallas_call(
        functools.partial(combine_out_kernel, per, cap),
        name="combine_out",
        grid_spec=grid_spec,
        out_shape=sds((owners * seq, width), BF),
        compiler_params=params(),
        cost_estimate=cost(0.01),
    )(z, pos, *rows)


def second_kernel(
    size, rows, owners, per, plan, count, me, own_p, ext, low_two, res, cot, ctx, *rest
):
    backs, rest = rest[:owners], rest[owners:]
    outs_count = 1 if size != 8 else 2
    refs, rest = rest[:count], rest[count:]
    res_grad, ctx_grad, ext_grad = rest[:3]
    rest = rest[3:]
    grads, rest = rest[:outs_count], rest[outs_count:]
    w, g, gate, sems, sems_g = rest
    copies = fetch(me[0], refs, plan, lambda s: w.at[s], sems, rows, size)
    experts_pad = own_p.shape[0]
    seq, width = res.shape
    arrived = backs[0][seq:, :].astype(F32)
    for r in range(1, owners):
        arrived = arrived + backs[r][seq:, :].astype(F32)
    for b in range(experts_pad // 8):
        high_at = slot_of(b, seq, width)
        low_at = slot_of(b + experts_pad // 8, seq, width)
        gate[b * 8 : (b + 1) * 8, :] = arrived[high_at] + arrived[low_at]
    p = own_p[...]
    gate_grad = gate[...]
    weighted = jnp.sum(p * gate_grad, axis=0, keepdims=True)
    logit_grad = (p * (gate_grad - weighted)).astype(BF)
    router = ext[:experts_pad, :].astype(BF)
    ext_grad[:experts_pad, :] = dot(logit_grad, low_two[:seq, :])
    two = dot(logit_grad, router, 0, 0)
    for r in range(owners):
        two = two + backs[r][:seq, :].astype(F32)
    values = res[...]
    factor = lax.rsqrt(jnp.mean(values * values, axis=-1, keepdims=True) + norm_eps)
    normed = values * factor
    ext_grad[experts_pad:, :] = jnp.broadcast_to(
        jnp.sum(two * normed, axis=0, keepdims=True), (16, normed.shape[1])
    )
    scaled = two * ext[experts_pad + 8 : experts_pad + 9, :]
    inward = factor * (scaled - normed * jnp.mean(scaled * normed, axis=-1, keepdims=True))
    total = cot[...].astype(F32) + inward
    res_grad[...] = total
    low = total.astype(BF)
    step = QW // 4
    for j in range(4):
        at = slice(j * step, (j + 1) * step)
        g[at, :] = dot(ctx[at, :], low).astype(BF)
    copies_g = store_parts(me[0], lambda s: g.at[s], grads, sems_g, rows, size)
    for c in copies:
        c.wait()
    for j in range(4):
        at = slice(j * step, (j + 1) * step)
        ctx_grad[at, :] = dot(w[at, :], low, 1, 1).astype(BF)
    for c in copies_g:
        c.wait()


def run_second(me, own_p, ext, low_two, res, cot, ctx, backs, pieces, size, per):
    owners = len(backs)
    arrays, plan = pieces
    seq, width = res.shape
    rows = QW // size
    grads = part_shapes(size, (rows, width))
    experts_pad = own_p.shape[0]
    return pl.pallas_call(
        functools.partial(second_kernel, size, rows, owners, per, plan, len(arrays)),
        name="second_back",
        out_shape=[sds((seq, width), F32), sds((QW, seq), BF), sds((experts_pad + 16, width), F32)] + grads,
        in_specs=[SMEM] + [VMEM] * (6 + owners) + [ANY] * len(arrays),
        out_specs=[VMEM] * 3 + [ANY] * len(grads),
        scratch_shapes=[
            pltpu.VMEM((QW, width), BF),
            pltpu.VMEM((QW, width), BF),
            pltpu.VMEM((experts_pad, seq), F32),
            pltpu.SemaphoreType.DMA((len(plan),)),
            pltpu.SemaphoreType.DMA((size,)),
        ],
        compiler_params=params(),
        cost_estimate=cost(0.01),
    )(me, own_p, ext, low_two, res, cot, ctx, *backs, *arrays)


def heads_kernel(size, rows, me, ctx_grad, qkv, probs, low_one, *rest):
    outs_count = 1 if size != 8 else 2
    back_rows, rest = rest[0], rest[1:]
    grads, rest = rest[:outs_count], rest[outs_count:]
    g, back, sems_g = rest
    seq = low_one.shape[0]
    scale = HEAD_DIM ** (-0.5)
    for h in range(KV_HEADS):

        def heads(ref):
            return jnp.concatenate(
                [
                    ref[(GROUPS * h + i) * HEAD_DIM : (GROUPS * h + i + 1) * HEAD_DIM, :]
                    for i in range(GROUPS)
                ],
                axis=1,
            )

        upstream = heads(ctx_grad)
        q = heads(qkv)
        k = qkv[QW + h * HEAD_DIM : QW + (h + 1) * HEAD_DIM, :]
        v = qkv[QW + KW + h * HEAD_DIM : QW + KW + (h + 1) * HEAD_DIM, :]
        low_p = probs[h]
        weights = low_p.astype(F32)
        prob_grad = dot(v, upstream, 0, 0)
        inner = jnp.sum(prob_grad * weights, axis=0, keepdims=True)
        score_grad = (weights * (prob_grad - inner)).astype(BF)
        value_grad = dot(upstream, low_p, 1, 1)
        key_grad = dot(q, score_grad, 1, 1) * scale
        query_grad = dot(k, score_grad) * scale
        back[QW + h * HEAD_DIM : QW + (h + 1) * HEAD_DIM, :] = key_grad.astype(BF)
        back[QW + KW + h * HEAD_DIM : QW + KW + (h + 1) * HEAD_DIM, :] = value_grad.astype(BF)
        for i in range(GROUPS):
            at = (GROUPS * h + i) * HEAD_DIM
            back[at : at + HEAD_DIM, :] = query_grad[:, i * seq : (i + 1) * seq].astype(BF)
    step = 512
    for j in range(QKV // step):
        at = slice(j * step, (j + 1) * step)
        back_rows[:, at] = back[at, :].astype(F32).T.astype(BF)
    for j in range(QW // step):
        at = slice(j * step, (j + 1) * step)
        g[:, at] = dot(low_one[...], back_rows[:, at], 0, 0).astype(BF)
    copies_g = store_parts(me[0], lambda s: g.at[s], grads, sems_g, rows, size)
    for c in copies_g:
        c.wait()


def run_heads(me, ctx_grad, qkv, probs, low_one, size):
    seq, width = low_one.shape
    rows = width // size
    grads = part_shapes(size, (rows, QW))
    return pl.pallas_call(
        functools.partial(heads_kernel, size, rows),
        name="heads_back",
        out_shape=[sds((seq, QKV), BF)] + grads,
        in_specs=[SMEM] + [VMEM] * 4,
        out_specs=[VMEM] + [ANY] * len(grads),
        scratch_shapes=[
            pltpu.VMEM((width, QW), BF),
            pltpu.VMEM((QKV, seq), BF),
            pltpu.SemaphoreType.DMA((size,)),
        ],
        compiler_params=params(),
        cost_estimate=cost(0.01),
    )(me, ctx_grad, qkv, probs, low_one)


def first_kernel(
    size, rows, plan, count, me, back_rows, low_one, tok, ext, ext_grad, res_grad, *rest
):
    outs_count = 1 if size != 8 else 2
    refs, rest = rest[:count], rest[count:]
    tok_grad, rest = rest[0], rest[1:]
    grads, rest = rest[:outs_count], rest[outs_count:]
    w, g, sems, sems_g = rest
    copies = fetch(me[0], refs, plan, lambda s: w.at[s], sems, rows, size)
    step = 512
    for j in range(2 * KW // step):
        at = slice(j * step, (j + 1) * step)
        of = slice(QW + j * step, QW + (j + 1) * step)
        g[:, at] = dot(low_one[...], back_rows[:, of], 0, 0).astype(BF)
    for c in copies:
        c.wait()
    one = dot(back_rows[...], w[:, :QKV], 1, 1)
    x = tok[...].astype(F32)
    factor = lax.rsqrt(jnp.mean(x * x, axis=-1, keepdims=True) + norm_eps)
    normed = x * factor
    experts_pad = ext.shape[0] - 16
    gain = ext[experts_pad : experts_pad + 1, :]
    gain_grad = jnp.sum(one * normed, axis=0, keepdims=True)
    packed = jnp.concatenate(
        [
            ext_grad[:experts_pad, :],
            jnp.broadcast_to(gain_grad, (8, gain_grad.shape[1])),
            ext_grad[experts_pad + 8 :, :],
            jnp.zeros((EXT - experts_pad - 16, gain_grad.shape[1]), F32),
        ],
        axis=0,
    )
    g[:, 2 * KW :] = packed.T.astype(BF)
    copies_g = store_parts(me[0], lambda s: g.at[s], grads, sems_g, rows, size)
    scaled = one * gain
    inward = factor * (scaled - normed * jnp.mean(scaled * normed, axis=-1, keepdims=True))
    tok_grad[...] = res_grad[...] + inward
    for c in copies_g:
        c.wait()


def run_first(me, back_rows, low_one, tokens, ext, ext_grad, res_grad, pieces, size):
    arrays, plan = pieces
    seq, width = tokens.shape
    rows = width // size
    cols = 2 * KW + EXT
    grads = part_shapes(size, (rows, cols))
    return pl.pallas_call(
        functools.partial(first_kernel, size, rows, plan, len(arrays)),
        name="first_back",
        out_shape=[sds((seq, width), F32)] + grads,
        in_specs=[SMEM] + [VMEM] * 6 + [ANY] * len(arrays),
        out_specs=[VMEM] + [ANY] * len(grads),
        scratch_shapes=[
            pltpu.VMEM((width, QKV + EXT), BF),
            pltpu.VMEM((width, cols), BF),
            pltpu.SemaphoreType.DMA((len(plan),)),
            pltpu.SemaphoreType.DMA((size,)),
        ],
        compiler_params=params(),
        cost_estimate=cost(0.01),
    )(me, back_rows, low_one, tokens, ext, ext_grad, res_grad, *arrays)


def split_groups(per):
    cut = max(1, (2 * per) // 5)
    return [(0, cut), (cut, per)]


def weight_groups(per):
    return split_groups(per)


def body(
    tokens,
    segment_ids,
    expert_choices,
    attn_gain,
    query_weight,
    key_weight,
    value_weight,
    output_weight,
    ffn_gain,
    router_weight,
    expert_gate,
    expert_up,
    expert_down,
    cotangent,
):
    size = lax.axis_size("dp")
    owners = lax.axis_size("expert")
    me = lax.axis_index("dp").astype(jnp.int32).reshape(1)
    z = lax.axis_index("expert").astype(jnp.int32).reshape(1)
    seq, width = tokens.shape
    per = expert_gate.shape[0]
    experts = per * owners
    experts_pad = -(-experts // 8) * 8
    capacity = (seq * TOP * 9 + 8 * experts - 1) // (8 * experts)
    cap = -(-capacity // 16) * 16
    slim = query_weight.shape[0]

    packed = run_pack(query_weight, key_weight, value_weight, router_weight, attn_gain, ffn_gain)
    qkv_pieces = gather_shards(packed, 2, size, "qkv")
    early = output_weight
    if size == 8:
        early = after(early, *qkv_pieces[0][1:3])
    out_pieces = gather_shards(early, 1, size, "output")
    shards = jnp.stack([expert_gate, expert_up, jnp.swapaxes(expert_down, 1, 2)], axis=1)
    first, last = weight_groups(per)[0]
    part = shards[first:last]
    if size == 8:
        part = after(part, *out_pieces[0][1:3], *qkv_pieces[0][3:5])
    gathered = [gather_shards(part, 0, size, "experts0")]
    where_at = [
        (group, l - first)
        for group, (first, last) in enumerate(weight_groups(per))
        for l in range(first, last)
    ]

    ids = jnp.arange(experts_pad, dtype=jnp.int32)
    hot = jnp.any(expert_choices[:, None, :] == ids[None, :, None], axis=2)
    hot = hot.astype(BF).T
    at = jnp.arange(seq, dtype=jnp.int32)
    earlier = (at[:, None] < at[None, :]).astype(BF)
    place = jnp.dot(hot, earlier, preferred_element_type=F32)
    place = jnp.where(hot > 0, place, -1.0).astype(BF)
    across = width // seq
    place = jnp.pad(place, ((0, EXTRA * across - experts_pad), (0, 0)))
    place = place.reshape(EXTRA // 8, across, 8, seq).swapaxes(1, 2).reshape(EXTRA, width)
    cots = lax.all_gather(cotangent, "expert", axis=0, tiled=True)

    low_one, qkv, ctx, probs, extra = run_attention(
        me,
        tokens,
        segment_ids,
        segment_ids.reshape(seq, 1),
        qkv_pieces,
        size,
        experts_pad + 16,
    )
    res, low_two = run_residual(me, tokens, ctx, extra, place, out_pieces, size)
    xs = gather_owners(low_two, z[0], owners, gathered[0][0][1:3] if size == 8 else ())
    first, last = weight_groups(per)[1]
    part = shards[first:last]
    if size == 8:
        part = after(part, xs[2] if owners == 4 else low_two)
    gathered.append(gather_shards(part, 2, size, "experts1"))
    pos, p, own_p = run_router(z, extra, xs, per)

    out_rows, back_rows, gate_rows, expert_totals = [], [], [], []
    groups = split_groups(per)
    first, last = groups[0]
    buffer = None
    for l in range(first, last):
        group, at = where_at[l]
        if size == 8 and l == last - 1:
            p = after(p, *gathered[1][0][1:3])
        results = run_expert(
            me, z, pos, p, xs, cots, gathered[group], at, buffer, size, l, l - first, last - first, cap
        )
        out_rows.append(results[0])
        back_rows.append(results[1])
        gate_rows.append(results[2])
        buffer = results[3]
    total = lax.psum_scatter(buffer, "dp", scatter_dimension=0, tiled=False)
    expert_totals.append(total.astype(F32))
    first, last = groups[1]
    buffer = None
    for l in range(first, last):
        group, at = where_at[l]
        results = run_expert(
            me, z, pos, p, xs, cots, gathered[group], at, buffer, size, l, l - first, last - first, cap
        )
        out_rows.append(results[0])
        back_rows.append(results[1])
        gate_rows.append(results[2])
        buffer = results[3]
    total = lax.psum_scatter(buffer, "dp", scatter_dimension=0, tiled=False)
    expert_totals.append(total.astype(F32))
    backs = run_combine_back(z, pos, back_rows, gate_rows, cap, experts_pad)
    backs = return_owners(backs, owners)
    outs = run_combine_out(z, pos, out_rows, cap)
    ctx = after(ctx, outs)
    results = run_second(
        me, own_p, extra, low_two, res, cotangent, ctx, backs, out_pieces, size, per
    )
    res_grad, ctx_grad, ext_grad = results[:3]
    out_grads = results[3:]
    outs = exchange(after(outs, ctx_grad))
    mixed = res
    for r in range(owners):
        mixed = mixed + outs[r * seq : (r + 1) * seq].astype(F32)
    mixed = mixed.astype(BF)
    results = run_heads(me, ctx_grad, qkv, probs, low_one, size)
    back_heads, query_grads = results[0], results[1:]
    if size == 8:
        o_sent, o_kept = pair_sum(out_grads, 1)
        back_heads = after(back_heads, o_sent)
    results = run_first(
        me, back_heads, low_one, tokens, extra, ext_grad, res_grad, qkv_pieces, size
    )
    grad_tokens, rest_grads = results[0], results[1:]
    stacked = jnp.concatenate(expert_totals, axis=0)
    expert_outputs = (stacked[:, 0], stacked[:, 1], jnp.swapaxes(stacked[:, 2], 1, 2))
    if size == 8:
        q_sent, q_kept = pair_sum(query_grads, 0)
        r_sent, r_kept = pair_sum(rest_grads, 1, q_sent)
        o_sent, o_kept = link_sum(o_sent, o_kept, 1, r_sent, *expert_outputs)
        q_sent, q_kept = link_sum(q_sent, q_kept, 0, o_sent)
        r_sent, r_kept = link_sum(r_sent, r_kept, 1, q_sent)
        out_total = last_sum(o_sent, o_kept, 1, r_sent, mixed)
        query_total = last_sum(q_sent, q_kept, 0, out_total)
        rest_total = last_sum(r_sent, r_kept, 1, query_total)
        out_total = spread(owner_sum(out_total)).astype(F32)
        both = after(jnp.concatenate([query_total, rest_total], axis=1), out_total)
        both = spread(owner_sum(both)).astype(F32)
        query_total, rest_total = both[:, :QW], both[:, QW:]
    else:
        out_total, query_total, rest_total = map(plain_sum, (out_grads, query_grads, rest_grads))

    return (
        mixed,
        grad_tokens,
        rest_total[:, 2 * KW + experts_pad],
        query_total,
        rest_total[:, :KW],
        rest_total[:, KW : 2 * KW],
        out_total,
        rest_total[:, 2 * KW + experts_pad + 8],
        rest_total[:, 2 * KW : 2 * KW + experts],
        *expert_outputs,
    )


def solution(mesh):
    return jax.shard_map(
        body,
        mesh=mesh,
        in_specs=(
            P(("dp", "expert"), None),
            P(("dp", "expert"), None),
            P(("dp", "expert"), None),
            P("dp"),
            P("dp", None),
            P("dp", None),
            P("dp", None),
            P("dp", None),
            P("dp"),
            P("dp", None),
            P("expert", "dp", None),
            P("expert", "dp", None),
            P("expert", None, "dp"),
            P(("dp", "expert"), None),
        ),
        out_specs=(
            P(("dp", "expert"), None),
            P(("dp", "expert"), None),
            P("dp"),
            P("dp", None),
            P("dp", None),
            P("dp", None),
            P("dp", None),
            P("dp"),
            P("dp", None),
            P("expert", "dp", None),
            P("expert", "dp", None),
            P("expert", None, "dp"),
        ),
        check_vma=False,
    )
```

time: 821 us -> 584 us (0.71)
  waiting for transfers between devices: 483 us -> 245 us
  starting transfers between devices: 113 us -> 57.2 us
  blocking collectives: 0 us -> 54.7 us
  Pallas kernels: 139 us -> 161 us
  local copies, waits for them, and re-layouts: 29.4 us -> 18.1 us
    ppermute x70 -> x41, waiting for transfers between devices: 229 us -> 95 us  [swap(): return lax.ppermute(value, 'dp', [(i, i ^ bit) for i in range(size)])]
    ppermute x18 -> x8, waiting for transfers between devices: 207 us -> 96 us  [along(): return lax.ppermute(value, 'expert', pairs)]
    all_to_all x0 -> x2, blocking collectives: none -> 54.7 us  [exchange(): lax.all_to_all(value, 'expert', split_axis=0, concat_axis=0, tiled=True)]
    all_to_all x0 -> x3, waiting for transfers between devices: none -> 54.3 us  [exchange(): lax.all_to_all(value, 'expert', split_axis=0, concat_axis=0, tiled=True)]
    ppermute x18 -> x8, starting transfers between devices: 71.3 us -> 17 us  [along(): return lax.ppermute(value, 'expert', pairs)]
    psum x1 -> x0, waiting for transfers between devices: 46 us -> none  [body(): qkv_total = lax.psum(qkv_total.astype(BF), 'expert').astype(F32)]
    pallas_call x5, Pallas kernels: 74.9 us -> 88.5 us  [run_expert(): pl.pallas_call(functools.partial(expert_kernel, size, rows, owners, cap,...]
    ppermute x70 -> x41, starting transfers between devices: 41.4 us -> 29 us  [swap(): return lax.ppermute(value, 'dp', [(i, i ^ bit) for i in range(size)])]
  transfers between devices with their start and end apart: 89 -> 55, of which waited for: 23 -> 22; matrix products, arithmetic and copies ran while one was open for 5% -> 6% of each run, Pallas kernels for 11% -> 23%
where the time goes in v2:
time: 584 us; the launch traced here: 582 us
  waiting for transfers between devices  245 us (42%)
  Pallas kernels  161 us (28%)
  starting transfers between devices  57.2 us (10%)
  blocking collectives  54.7 us (9%)
  other arithmetic  30.7 us (5%)
  local copies, waits for them, and re-layouts  18.1 us (3%)
  between operations  14.6 us (2%)
    ppermute x8, waiting for transfers between devices, along(): return lax.ppermute(value, 'expert', pairs)  96 us
    ppermute x41, waiting for transfers between devices, swap(): return lax.ppermute(value, 'dp', [(i, i ^ bit) for i in range(size)])  95 us
    pallas_call x5, Pallas kernels, run_expert(): pl.pallas_call(functools.partial(expert_kernel, size, rows, owners, cap,...  88.5 us
    all_to_all x2, blocking collectives, exchange(): lax.all_to_all(value, 'expert', split_axis=0, concat_axis=0, tiled=True)  54.7 us
    all_to_all x3, waiting for transfers between devices, exchange(): lax.all_to_all(value, 'expert', split_axis=0, concat_axis=0, tiled=True)  54.3 us
    ppermute x41, starting transfers between devices, swap(): return lax.ppermute(value, 'dp', [(i, i ^ bit) for i in range(size)])  29 us
    ppermute x8, starting transfers between devices, along(): return lax.ppermute(value, 'expert', pairs)  17 us
    convert_element_type x9, other arithmetic, add(): return (a.astype(F32) + b.astype(F32)).astype(BF)  16.9 us
  transfers between devices with their start and end apart: 55, of which 22 were waited for; matrix products, arithmetic and copies ran while one was open for 6% of the time, Pallas kernels for 23%

profile of v2, /device:TPU:0, one launch (start us, length us, event | category | flops | bytes accessed | tf_op | source)
XLA Modules:
  0.0 582.1 jit_solution(4623643115007277397)
XLA Ops:
  14.0 21.5 %collective-permute-done.rest_1_ = bf16[192,2688]{1,0:T(8,128)(2,1)S(1)} collective-permute-done((bf16[192,2688]{1,0:T(8,128)(2,1)}, bf16[192,2688]{1,0:T(8,128)(2,1)S(1)}, u32[]{:S(2)}, u32[]{:S(2)}) %collective-permute-start) | collective-permute-done | bytes 1032224 | tf_op jit(solution)/shard_map/qkv/ppermute | solution.py:52
  41.5 9.9 %collective-permute-done.2.rest_3_ = bf16[96,2688]{1,0:T(8,128)(2,1)} collective-permute-done((bf16[96,2688]{1,0:T(8,128)(2,1)}, bf16[96,2688]{1,0:T(8,128)(2,1)}, u32[]{:S(2)}, u32[]{:S(2)}) %collective-permute-start.2) | collective-permute-done | bytes 516128 | tf_op jit(solution)/shard_map/qkv/ppermute | solution.py:52
  54.3 8.0 %collective-permute-done.10.rest_2_.rest_6_ = bf16[192,1536]{1,0:T(8,128)(2,1)} collective-permute-done((bf16[192,1536]{1,0:T(8,128)(2,1)}, bf16[192,1536]{1,0:T(8,128)(2,1)}, u32[]{:S(2)}, u32[]{:S(2)}) %collective-permute-start.10) | collective-permute-done | bytes 589856 | tf_op jit(solution)/shard_map/output/ppermute | solution.py:52
  69.3 11.7 %collective-permute-done.11.rest_3_.rest_7_ = bf16[192,1536]{1,0:T(8,128)(2,1)} collective-permute-done((bf16[192,1536]{1,0:T(8,128)(2,1)}, bf16[192,1536]{1,0:T(8,128)(2,1)}, u32[]{:S(2)}, u32[]{:S(2)}) %collective-permute-start.11) | collective-permute-done | bytes 589856 | tf_op jit(solution)/shard_map/output/ppermute | solution.py:52
  84.5 12.1 %attention.1 = (bf16[256,1536]{1,0:T(8,128)(2,1)}, bf16[2560,256]{1,0:T(8,128)(2,1)}, bf16[1536,256]{1,0:T(8,128)(2,1)}, bf16[8,256,768]{2,1,0:T(8,128)(2,1)}, f32[40,1536]{1,0:T(8,128)}) custom-call(s32[1]{0:T(128)} %bitcast.me, bf16[256,1536]{1,0:T(8,128)(2,1)} %tok.5, s32[1,256]{1,0:T(1,128)} %seg_row.1, s32[256,1]{1,0:T(8,128)} %copy.39.seg_col, ...), custom_call_target="tpu_custom_call" | custom-call | flops 1000000 | bytes 36000 | tf_op jit(solution)/shard_map/attention/pallas_call | solution.py:273
  97.4 6.8 %residual.1 = (f32[256,1536]{1,0:T(8,128)}, bf16[272,1536]{1,0:T(8,128)(2,1)}) custom-call(s32[1]{0:T(128)} %bitcast.me, bf16[256,1536]{1,0:T(8,128)(2,1)} %tok.5, bf16[1536,256]{1,0:T(8,128)(2,1)} %get-tuple-element.93.ctx, f32[40,1536]{1,0:T(8,128)} %get-tuple-element.74.ext, bf16[16,1536]{1,0:T(8,128)(2,1)} %bitcast.89, bf16[192,1536]{1,0:T(8,128)(2,1)} %rest_4_, ...), custom_call_target="tpu_custom_call" | custom-call | flops 1000000 | bytes 36000 | tf_op jit(solution)/shard_map/residual/pallas_call | solution.py:312
  109.8 33.3 %collective-permute-done.16.rest_1_ = bf16[272,1536]{1,0:T(8,128)(2,1)S(1)} collective-permute-done((bf16[272,1536]{1,0:T(8,128)(2,1)}, bf16[272,1536]{1,0:T(8,128)(2,1)S(1)}, u32[]{:S(2)}, u32[]{:S(2)}) %collective-permute-start.16) | collective-permute-done | bytes 835616 | tf_op jit(solution)/shard_map/ppermute | solution.py:113
  151.0 16.4 %collective-permute-done.21 = bf16[272,1536]{1,0:T(8,128)(2,1)S(1)} collective-permute-done((bf16[272,1536]{1,0:T(8,128)(2,1)S(1)}, bf16[272,1536]{1,0:T(8,128)(2,1)S(1)}, u32[]{:S(2)}, u32[]{:S(2)}) %collective-permute-start.21) | collective-permute-done | bytes 835616 | tf_op jit(solution)/shard_map/ppermute | solution.py:113
  170.5 3.7 router.1
  174.2 14.8 %expert.5 = (bf16[512,1536]{1,0:T(8,128)(2,1)}, bf16[512,1536]{1,0:T(8,128)(2,1)}, f32[4,256]{1,0:T(4,128)}, bf16[8,2,3,192,512]{4,3,2,1,0:T(8,128)(2,1)}) custom-call(s32[1]{0:T(128)} %bitcast.me, s32[1]{0:T(128)} %bitcast.7.z, s32[5,4,256]{2,1,0:T(4,128)} %get-tuple-element.80.pos, f32[5,4,256]{2,1,0:T(4,128)} %get-tuple-element.84.p, ...), custom_call_target="tpu_custom_call" | custom-call | flops 1000000 | bytes 36000 | tf_op jit(solution)/shard_map/expert/pallas_call | solution.py:507
  189.1 27.4 %expert.6 = (bf16[512,1536]{1,0:T(8,128)(2,1)}, bf16[512,1536]{1,0:T(8,128)(2,1)}, f32[4,256]{1,0:T(4,128)}, bf16[8,2,3,192,512]{4,3,2,1,0:T(8,128)(2,1)}) custom-call(s32[1]{0:T(128)} %bitcast.me, s32[1]{0:T(128)} %bitcast.7.z, s32[5,4,256]{2,1,0:T(4,128)} %get-tuple-element.80.pos, ...), custom_call_target="tpu_custom_call", output_to_operand_aliasing={{3}: (17, {})} | custom-call | flops 1000000 | bytes 36000 | tf_op jit(solution)/shard_map/expert/pallas_call | solution.py:507
  222.3 17.7 %collective-permute-done.29.rest_7_ = bf16[3,3,96,512]{3,2,1,0:T(8,128)(2,1)S(1)} collective-permute-done((bf16[3,3,96,512]{3,2,1,0:T(8,128)(2,1)S(1)}, bf16[3,3,96,512]{3,2,1,0:T(8,128)(2,1)S(1)}, u32[]{:S(2)}, u32[]{:S(2)}) %collective-permute-start.29) | collective-permute-done | bytes 884768 | tf_op jit(solution)/shard_map/experts1/ppermute | solution.py:52
  247.4 14.9 %expert.7 = (bf16[512,1536]{1,0:T(8,128)(2,1)}, bf16[512,1536]{1,0:T(8,128)(2,1)}, f32[4,256]{1,0:T(4,128)}, bf16[8,3,3,192,512]{4,3,2,1,0:T(8,128)(2,1)}) custom-call(s32[1]{0:T(128)} %bitcast.me, s32[1]{0:T(128)} %bitcast.7.z, s32[5,4,256]{2,1,0:T(4,128)} %get-tuple-element.80.pos, f32[5,4,256]{2,1,0:T(4,128)} %get-tuple-element.84.p, ...), custom_call_target="tpu_custom_call" | custom-call | flops 1000000 | bytes 36000 | tf_op jit(solution)/shard_map/expert/pallas_call | solution.py:507
  262.4 15.5 %expert.8 = (bf16[512,1536]{1,0:T(8,128)(2,1)}, bf16[512,1536]{1,0:T(8,128)(2,1)}, f32[4,256]{1,0:T(4,128)}, bf16[8,3,3,192,512]{4,3,2,1,0:T(8,128)(2,1)}) custom-call(s32[1]{0:T(128)} %bitcast.me, s32[1]{0:T(128)} %bitcast.7.z, s32[5,4,256]{2,1,0:T(4,128)} %get-tuple-element.80.pos, ...), custom_call_target="tpu_custom_call", output_to_operand_aliasing={{3}: (19, {})} | custom-call | flops 1000000 | bytes 36000 | tf_op jit(solution)/shard_map/expert/pallas_call | solution.py:507
  277.9 15.8 %expert.9 = (bf16[512,1536]{1,0:T(8,128)(2,1)}, bf16[512,1536]{1,0:T(8,128)(2,1)}, f32[4,256]{1,0:T(4,128)}, bf16[8,3,3,192,512]{4,3,2,1,0:T(8,128)(2,1)}) custom-call(s32[1]{0:T(128)} %bitcast.me, s32[1]{0:T(128)} %bitcast.7.z, s32[5,4,256]{2,1,0:T(4,128)} %get-tuple-element.80.pos, ...), custom_call_target="tpu_custom_call", output_to_operand_aliasing={{3}: (19, {})} | custom-call | flops 1000000 | bytes 36000 | tf_op jit(solution)/shard_map/expert/pallas_call | solution.py:507
  293.7 7.7 %combine_back.1 = (bf16[272,1536]{1,0:T(8,128)(2,1)}, bf16[272,1536]{1,0:T(8,128)(2,1)}, bf16[272,1536]{1,0:T(8,128)(2,1)}, bf16[272,1536]{1,0:T(8,128)(2,1)}) custom-call(s32[1]{0:T(128)} %bitcast.7.z, s32[5,4,256]{2,1,0:T(4,128)} %get-tuple-element.80.pos, bf16[512,1536]{1,0:T(8,128)(2,1)} %get-tuple-element.94.rest_0_, ...), custom_call_target="tpu_custom_call" | custom-call | flops 1000000 | bytes 36000 | tf_op jit(solution)/shard_map/combine_back/pallas_call | solution.py:595
  301.4 4.0 collective-permute-start.37
  308.4 16.2 %collective-permute-done.37 = bf16[272,1536]{1,0:T(8,128)(2,1)S(1)} collective-permute-done((bf16[272,1536]{1,0:T(8,128)(2,1)}, bf16[272,1536]{1,0:T(8,128)(2,1)S(1)}, u32[]{:S(2)}, u32[]{:S(2)}) %collective-permute-start.37) | collective-permute-done | bytes 835616 | tf_op jit(solution)/shard_map/ppermute | solution.py:113
  329.6 7.5 %combine_out.1 = bf16[1024,1536]{1,0:T(8,128)(2,1)} custom-call(s32[1]{0:T(128)} %bitcast.7.z, s32[5,4,256]{2,1,0:T(4,128)} %get-tuple-element.80.pos, bf16[512,1536]{1,0:T(8,128)(2,1)} %get-tuple-element.82.rest_0_, bf16[512,1536]{1,0:T(8,128)(2,1)} %get-tuple-element.86.rest_1_, bf16[512,1536]{1,0:T(8,128)(2,1)} %get-tuple-element.87.rest_2_, ...), custom_call_target="tpu_custom_call" | custom-call | flops 1000000 | bytes 36000 | tf_op jit(solution)/shard_map/combine_out/pallas_call | solution.py:625
  337.1 5.5 collective-permute-done.36.rest_1_
  342.5 22.3 %collective-permute-done.38.rest_2_ = bf16[272,1536]{1,0:T(8,128)(2,1)S(1)} collective-permute-done((bf16[272,1536]{1,0:T(8,128)(2,1)S(1)}, bf16[272,1536]{1,0:T(8,128)(2,1)S(1)}, u32[]{:S(2)}, u32[]{:S(2)}) %collective-permute-start.38) | collective-permute-done | bytes 835616 | tf_op jit(solution)/shard_map/ppermute | solution.py:113
  365.7 9.7 %second_back.1 = (f32[256,1536]{1,0:T(8,128)}, bf16[1536,256]{1,0:T(8,128)(2,1)}, f32[40,1536]{1,0:T(8,128)}, bf16[4,192,1536]{2,1,0:T(8,128)(2,1)}, bf16[4,192,1536]{2,1,0:T(8,128)(2,1)}) custom-call(s32[1]{0:T(128)} %bitcast.me, f32[24,256]{1,0:T(8,128)} %get-tuple-element.92.own_p, f32[40,1536]{1,0:T(8,128)} %get-tuple-element.74.ext, ...), custom_call_target="tpu_custom_call" | custom-call | flops 1000000 | bytes 36000 | tf_op jit(solution)/shard_map/second_back/pallas_call | solution.py:696
  375.5 4.1 all-to-all-start
  379.6 11.4 %heads_back.1 = (bf16[256,2560]{1,0:T(8,128)(2,1)}, bf16[4,192,1536]{2,1,0:T(8,128)(2,1)}, bf16[4,192,1536]{2,1,0:T(8,128)(2,1)}) custom-call(s32[1]{0:T(128)} %bitcast.me, bf16[1536,256]{1,0:T(8,128)(2,1)} %get-tuple-element.108.ctx_grad, bf16[2560,256]{1,0:T(8,128)(2,1)} %get-tuple-element.110.qkv, bf16[8,256,768]{2,1,0:T(8,128)(2,1)} %get-tuple-element.111.probs, ...), custom_call_target="tpu_custom_call" | custom-call | flops 1000000 | bytes 36000 | tf_op jit(solution)/shard_map/heads_back/pallas_call | solution.py:765
  395.1 11.7 %first_back.1 = (f32[256,1536]{1,0:T(8,128)}, bf16[4,192,1152]{2,1,0:T(8,128)(2,1)}, bf16[4,192,1152]{2,1,0:T(8,128)(2,1)}) custom-call(s32[1]{0:T(128)} %bitcast.me, bf16[256,2560]{1,0:T(8,128)(2,1)} %get-tuple-element.116.back_rows, bf16[256,1536]{1,0:T(8,128)(2,1)} %get-tuple-element.112.low_one, bf16[256,1536]{1,0:T(8,128)(2,1)} %tok.5, ...), custom_call_target="tpu_custom_call" | custom-call | flops 1000000 | bytes 36000 | tf_op jit(solution)/shard_map/first_back/pallas_call | solution.py:828
  414.2 36.6 %all-to-all-done = bf16[4,256,1536]{2,1,0:T(8,128)(2,1)S(1)} async-done(((bf16[4,256,1536]{2,1,0:T(8,128)(2,1)}), bf16[4,256,1536]{2,1,0:T(8,128)(2,1)S(1)}, u32[]{:S(2)}, u32[]{:S(2)}) %all-to-all-start) | async-done | bytes 3145760 | tf_op jit(solution)/shard_map/all_to_all | solution.py:142
  466.1 8.7 %collective-permute-done.46 = bf16[192,1536]{1,0:T(8,128)(2,1)S(1)} collective-permute-done((bf16[192,1536]{1,0:T(8,128)(2,1)S(1)}, bf16[192,1536]{1,0:T(8,128)(2,1)S(1)}, u32[]{:S(2)}, u32[]{:S(2)}) %collective-permute-start.46) | collective-permute-done | bytes 589856 | tf_op jit(solution)/shard_map/ppermute | solution.py:52
  483.6 8.1 %collective-permute-done.48 = bf16[192,1152]{1,0:T(8,128)(2,1)} collective-permute-done((bf16[192,1152]{1,0:T(8,128)(2,1)}, bf16[192,1152]{1,0:T(8,128)(2,1)}, u32[]{:S(2)}, u32[]{:S(2)}) %collective-permute-start.48) | collective-permute-done | bytes 442400 | tf_op jit(solution)/shard_map/ppermute | solution.py:52
  491.7 3.8 all-to-all-done.1
  501.3 14.0 %all-to-all-done.2 = bf16[4,48,1536]{2,1,0:T(8,128)(2,1)S(1)} async-done(((bf16[4,48,1536]{2,1,0:T(8,128)(2,1)}), bf16[4,48,1536]{2,1,0:T(8,128)(2,1)S(1)}, u32[]{:S(2)}, u32[]{:S(2)}) %all-to-all-start.2) | async-done | bytes 589856 | tf_op jit(solution)/shard_map/all_to_all | solution.py:142
  516.5 27.3 %all_to_all.45 = bf16[4,48,2688]{2,1,0:T(8,128)(2,1)S(1)} all-to-all(bf16[4,48,2688]{2,1,0:T(8,128)(2,1)S(1)} %bitcast.80), channel_id=1, replica_groups=mesh['dp'=8,'expert'=4] {'expert'}, dimensions={0} | all-to-all | bytes 2064384 | tf_op jit(solution)/shard_map/all_to_all | solution.py:142
  544.1 27.4 %all_to_all.46 = bf16[4,48,2688]{2,1,0:T(8,128)(2,1)S(1)} all-to-all(bf16[4,48,2688]{2,1,0:T(8,128)(2,1)S(1)} %bitcast.79), channel_id=1, replica_groups=mesh['dp'=8,'expert'=4] {'expert'}, dimensions={0} | all-to-all | bytes 2064384 | tf_op jit(solution)/shard_map/all_to_all | solution.py:142
  (201 shorter events, 112.2 us)
Async XLA Ops:
  7.2 167.0 %all-gather.2.cloned.1.call-start = ((), (), s32[]{:S(2)}) async-start(), calls=%async_computation.7 | async-start | bytes 3932160 | tf_op jit(solution)/shard_map/all_gather | solution.py:910
  9.5 26.0 %collective-permute-start = (bf16[192,2688]{1,0:T(8,128)(2,1)}, bf16[192,2688]{1,0:T(8,128)(2,1)S(1)}, u32[]{:S(2)}, u32[]{:S(2)}) collective-permute-start(bf16[192,2688]{1,0:T(8,128)(2,1)} %pack.1.rest_0_), channel_id=1, source_target_pairs={{0,8},{4,12},{8,0},{12,4},{16,24},{20,28},{24,16},{28,20},{1,9},{5... | collective-permute-start | bytes 3096584 | tf_op jit(solution)/shard_map/qkv/ppermute | solution.py:52
  12.5 25.7 %collective-permute-start.1 = (bf16[192,2688]{1,0:T(8,128)(2,1)}, bf16[192,2688]{1,0:T(8,128)(2,1)S(1)}, u32[]{:S(2)}, u32[]{:S(2)}) collective-permute-start(bf16[192,2688]{1,0:T(8,128)(2,1)} %pack.1.rest_0_), channel_id=1, source_target_pairs={{0,16},{4,20},{8,24},{12,28},{16,0},{20,4},{24,8},{28,12},{1,17},{... | collective-permute-start | bytes 3096584 | tf_op jit(solution)/shard_map/qkv/ppermute | solution.py:52
  14.0 27.5 %collective-permute-start.4 = (bf16[192,2688]{1,0:T(8,128)(2,1)}, bf16[192,2688]{1,0:T(8,128)(2,1)S(1)}, u32[]{:S(2)}, u32[]{:S(2)}) collective-permute-start(bf16[192,2688]{1,0:T(8,128)(2,1)} %pack.1.rest_0_), channel_id=1, source_target_pairs={{0,4},{4,0},{8,12},{12,8},{16,20},{20,16},{24,28},{28,24},{1,5},{5... | collective-permute-start | bytes 3096584 | tf_op jit(solution)/shard_map/qkv/ppermute | solution.py:52
  38.1 24.1 %collective-permute-start.10 = (bf16[192,1536]{1,0:T(8,128)(2,1)}, bf16[192,1536]{1,0:T(8,128)(2,1)}, u32[]{:S(2)}, u32[]{:S(2)}) collective-permute-start(bf16[192,1536]{1,0:T(8,128)(2,1)} %rest_4_), channel_id=1, source_target_pairs={{0,16},{4,20},{8,24},{12,28},{16,0},{20,4},{24,8},{28,12},{1,17},{... | collective-permute-start | bytes 1769480 | tf_op jit(solution)/shard_map/output/ppermute | solution.py:52
  41.0 412.6 %reduce-scatter.3.cloned.1.call-start = ((), (), s32[]{:S(2)}) async-start(), calls=%async_computation.8 | async-start | bytes 10616832 | tf_op jit(solution)/shard_map/reduce_scatter | solution.py:945
  41.0 23.5 %collective-permute-start.9 = (bf16[192,1536]{1,0:T(8,128)(2,1)}, bf16[192,1536]{1,0:T(8,128)(2,1)}, u32[]{:S(2)}, u32[]{:S(2)}) collective-permute-start(bf16[192,1536]{1,0:T(8,128)(2,1)} %rest_4_), channel_id=1, source_target_pairs={{0,8},{4,12},{8,0},{12,4},{16,24},{20,28},{24,16},{28,20},{1,9},{5... | collective-permute-start | bytes 1769480 | tf_op jit(solution)/shard_map/output/ppermute | solution.py:52
  41.5 23.1 %collective-permute-start.12 = (bf16[192,1536]{1,0:T(8,128)(2,1)}, bf16[192,1536]{1,0:T(8,128)(2,1)}, u32[]{:S(2)}, u32[]{:S(2)}) collective-permute-start(bf16[192,1536]{1,0:T(8,128)(2,1)} %rest_4_), channel_id=1, source_target_pairs={{0,4},{4,0},{8,12},{12,8},{16,20},{20,16},{24,28},{28,24},{1,5},{5... | collective-permute-start | bytes 1769480 | tf_op jit(solution)/shard_map/output/ppermute | solution.py:52
  54.3 26.7 %collective-permute-start.6 = (bf16[192,2688]{1,0:T(8,128)(2,1)S(1)}, bf16[192,2688]{1,0:T(8,128)(2,1)S(1)}, u32[]{:S(2)}, u32[]{:S(2)}) collective-permute-start(bf16[192,2688]{1,0:T(8,128)(2,1)S(1)} %collective-permute-done.1.rest_2_), channel_id=1, source_target_pairs={{0,4},{4,0},{8,12},{12,8},{16,20},{20,16},{24,28},{28,24},{1,5},{5... | collective-permute-start | bytes 3096584 | tf_op jit(solution)/shard_map/qkv/ppermute | solution.py:52
  68.7 39.7 %collective-permute-start.18 = (bf16[2,3,192,512]{3,2,1,0:T(8,128)(2,1)}, bf16[2,3,192,512]{3,2,1,0:T(8,128)(2,1)S(1)}, u32[]{:S(2)}, u32[]{:S(2)}) collective-permute-start(bf16[2,3,192,512]{3,2,1,0:T(8,128)(2,1)} %pad_maximum_fusion.2.rest_4_), channel_id=1, source_target_pairs={{0,8},{4,12},{8,0},{12,4},{16,24},{20,28},{24,16},{28,20},{1,9},{5... | collective-permute-start | bytes 3538952 | tf_op jit(solution)/shard_map/experts0/ppermute | solution.py:52
  69.3 27.3 %collective-permute-start.13 = (bf16[192,1536]{1,0:T(8,128)(2,1)}, bf16[192,1536]{1,0:T(8,128)(2,1)S(1)}, u32[]{:S(2)}, u32[]{:S(2)}) collective-permute-start(bf16[192,1536]{1,0:T(8,128)(2,1)} %collective-permute-done.9.rest_1_.rest_5_), channel_id=1, source_target_pairs={{0,4},{4,0},{8,12},{12,8},{16,20},{20,16},{24,28},{28,24},{1,5},{5... | collective-permute-start | bytes 1769480 | tf_op jit(solution)/shard_map/output/ppermute | solution.py:52
  81.0 28.7 %collective-permute-start.19 = (bf16[2,3,192,512]{3,2,1,0:T(8,128)(2,1)}, bf16[2,3,192,512]{3,2,1,0:T(8,128)(2,1)}, u32[]{:S(2)}, u32[]{:S(2)}) collective-permute-start(bf16[2,3,192,512]{3,2,1,0:T(8,128)(2,1)} %pad_maximum_fusion.2.rest_4_), channel_id=1, source_target_pairs={{0,16},{4,20},{8,24},{12,28},{16,0},{20,4},{24,8},{28,12},{1,17},{... | collective-permute-start | bytes 3538952 | tf_op jit(solution)/shard_map/experts0/ppermute | solution.py:52
  82.6 66.9 %collective-permute-start.23 = (bf16[2,3,192,512]{3,2,1,0:T(8,128)(2,1)}, bf16[2,3,192,512]{3,2,1,0:T(8,128)(2,1)}, u32[]{:S(2)}, u32[]{:S(2)}) collective-permute-start(bf16[2,3,192,512]{3,2,1,0:T(8,128)(2,1)} %pad_maximum_fusion.2.rest_4_), channel_id=1, source_target_pairs={{0,4},{4,0},{8,12},{12,8},{16,20},{20,16},{24,28},{28,24},{1,5},{5... | collective-permute-start | bytes 3538952 | tf_op jit(solution)/shard_map/experts0/ppermute | solution.py:52
  104.2 38.8 %collective-permute-start.16 = (bf16[272,1536]{1,0:T(8,128)(2,1)}, bf16[272,1536]{1,0:T(8,128)(2,1)S(1)}, u32[]{:S(2)}, u32[]{:S(2)}) collective-permute-start(bf16[272,1536]{1,0:T(8,128)(2,1)} %get-tuple-element.79.rest_0_.low_two), channel_id=1, source_target_pairs={{0,1},{1,0},{2,3},{3,2},{4,5},{5,4},{6,7},{7,6},{8,9},{9,8},{10,11... | collective-permute-start | bytes 2506760 | tf_op jit(solution)/shard_map/ppermute | solution.py:113
  105.9 39.6 %collective-permute-start.17 = (bf16[272,1536]{1,0:T(8,128)(2,1)}, bf16[272,1536]{1,0:T(8,128)(2,1)S(1)}, u32[]{:S(2)}, u32[]{:S(2)}) collective-permute-start(bf16[272,1536]{1,0:T(8,128)(2,1)} %get-tuple-element.79.rest_0_.low_two), channel_id=1, source_target_pairs={{0,2},{1,3},{2,0},{3,1},{4,6},{5,7},{6,4},{7,5},{8,10},{9,11},{10,... | collective-permute-start | bytes 2506760 | tf_op jit(solution)/shard_map/ppermute | solution.py:113
  108.5 42.0 %collective-permute-start.22 = (bf16[2,3,192,512]{3,2,1,0:T(8,128)(2,1)S(1)}, bf16[2,3,192,512]{3,2,1,0:T(8,128)(2,1)}, u32[]{:S(2)}, u32[]{:S(2)}) collective-permute-start(bf16[2,3,192,512]{3,2,1,0:T(8,128)(2,1)S(1)} %collective-permute-done.18.rest_5_), channel_id=1, source_target_pairs={{0,16},{4,20},{8,24},{12,28},{16,0},{20,4},{24,8},{28,12},{1,17},{... | collective-permute-start | bytes 3538952 | tf_op jit(solution)/shard_map/experts0/ppermute | solution.py:52
  148.0 41.0 %collective-permute-start.27 = (bf16[3,3,192,512]{3,2,1,0:T(8,128)(2,1)S(1)}, bf16[3,3,192,512]{3,2,1,0:T(8,128)(2,1)}, u32[]{:S(2)}, u32[]{:S(2)}) collective-permute-start(bf16[3,3,192,512]{3,2,1,0:T(8,128)(2,1)S(1)} %pad_maximum_fusion.rest_4_), channel_id=1, source_target_pairs={{0,8},{4,12},{8,0},{12,4},{16,24},{20,28},{24,16},{28,20},{1,9},{5... | collective-permute-start | bytes 5308424 | tf_op jit(solution)/shard_map/experts1/ppermute | solution.py:52
  149.5 39.5 %collective-permute-start.28 = (bf16[3,3,192,512]{3,2,1,0:T(8,128)(2,1)S(1)}, bf16[3,3,192,512]{3,2,1,0:T(8,128)(2,1)}, u32[]{:S(2)}, u32[]{:S(2)}) collective-permute-start(bf16[3,3,192,512]{3,2,1,0:T(8,128)(2,1)S(1)} %pad_maximum_fusion.rest_4_), channel_id=1, source_target_pairs={{0,16},{4,20},{8,24},{12,28},{16,0},{20,4},{24,8},{28,12},{1,17},{... | collective-permute-start | bytes 5308424 | tf_op jit(solution)/shard_map/experts1/ppermute | solution.py:52
  150.5 23.7 %collective-permute-start.24 = (bf16[2,3,192,512]{3,2,1,0:T(8,128)(2,1)S(1)}, bf16[2,3,192,512]{3,2,1,0:T(8,128)(2,1)}, u32[]{:S(2)}, u32[]{:S(2)}) collective-permute-start(bf16[2,3,192,512]{3,2,1,0:T(8,128)(2,1)S(1)} %collective-permute-done.18.rest_5_), channel_id=1, source_target_pairs={{0,4},{4,0},{8,12},{12,8},{16,20},{20,16},{24,28},{28,24},{1,5},{5... | collective-permute-start | bytes 3538952 | tf_op jit(solution)/shard_map/experts0/ppermute | solution.py:52
  150.5 23.7 %collective-permute-start.25 = (bf16[2,3,192,512]{3,2,1,0:T(8,128)(2,1)}, bf16[2,3,192,512]{3,2,1,0:T(8,128)(2,1)}, u32[]{:S(2)}, u32[]{:S(2)}) collective-permute-start(bf16[2,3,192,512]{3,2,1,0:T(8,128)(2,1)} %collective-permute-done.19.rest_6_), channel_id=1, source_target_pairs={{0,4},{4,0},{8,12},{12,8},{16,20},{20,16},{24,28},{28,24},{1,5},{5... | collective-permute-start | bytes 3538952 | tf_op jit(solution)/shard_map/experts0/ppermute | solution.py:52
  216.4 237.2 %reduce-scatter.5.cloned.1.call-start = ((), (), s32[]{:S(2)}) async-start(), calls=%async_computation.9 | async-start | bytes 15925248 | tf_op jit(solution)/shard_map/reduce_scatter | solution.py:958
  216.5 25.1 %collective-permute-start.31 = (bf16[3,3,192,512]{3,2,1,0:T(8,128)(2,1)S(1)}, bf16[3,3,192,512]{3,2,1,0:T(8,128)(2,1)S(1)}, u32[]{:S(2)}, u32[]{:S(2)}) collective-permute-start(bf16[3,3,192,512]{3,2,1,0:T(8,128)(2,1)S(1)} %pad_maximum_fusion.rest_4_), channel_id=1, source_target_pairs={{0,4},{4,0},{8,12},{12,8},{16,20},{20,16},{24,28},{28,24},{1,5},{5... | collective-permute-start | bytes 5308424 | tf_op jit(solution)/shard_map/experts1/ppermute | solution.py:52
  221.8 22.2 %collective-permute-start.32 = (bf16[3,3,192,512]{3,2,1,0:T(8,128)(2,1)}, bf16[3,3,192,512]{3,2,1,0:T(8,128)(2,1)S(1)}, u32[]{:S(2)}, u32[]{:S(2)}) collective-permute-start(bf16[3,3,192,512]{3,2,1,0:T(8,128)(2,1)} %collective-permute-done.27.rest_5_), channel_id=1, source_target_pairs={{0,4},{4,0},{8,12},{12,8},{16,20},{20,16},{24,28},{28,24},{1,5},{5... | collective-permute-start | bytes 5308424 | tf_op jit(solution)/shard_map/experts1/ppermute | solution.py:52
  221.8 23.2 %collective-permute-start.33 = (bf16[3,3,192,512]{3,2,1,0:T(8,128)(2,1)}, bf16[3,3,192,512]{3,2,1,0:T(8,128)(2,1)S(1)}, u32[]{:S(2)}, u32[]{:S(2)}) collective-permute-start(bf16[3,3,192,512]{3,2,1,0:T(8,128)(2,1)} %collective-permute-done.28.rest_6_), channel_id=1, source_target_pairs={{0,4},{4,0},{8,12},{12,8},{16,20},{20,16},{24,28},{28,24},{1,5},{5... | collective-permute-start | bytes 5308424 | tf_op jit(solution)/shard_map/experts1/ppermute | solution.py:52
  301.4 23.2 %collective-permute-start.37 = (bf16[272,1536]{1,0:T(8,128)(2,1)}, bf16[272,1536]{1,0:T(8,128)(2,1)S(1)}, u32[]{:S(2)}, u32[]{:S(2)}) collective-permute-start(bf16[272,1536]{1,0:T(8,128)(2,1)} %get-tuple-element.107), channel_id=1, source_target_pairs={{3,2},{0,1},{7,6},{4,5},{11,10},{8,9},{15,14},{12,13},{19,18},{16,... | collective-permute-start | bytes 2506760 | tf_op jit(solution)/shard_map/ppermute | solution.py:113
  305.4 37.1 %collective-permute-start.39 = (bf16[272,1536]{1,0:T(8,128)(2,1)}, bf16[272,1536]{1,0:T(8,128)(2,1)S(1)}, u32[]{:S(2)}, u32[]{:S(2)}) collective-permute-start(bf16[272,1536]{1,0:T(8,128)(2,1)} %get-tuple-element.107), channel_id=1, source_target_pairs={{1,2},{2,1},{5,6},{6,5},{9,10},{10,9},{13,14},{14,13},{17,18},{18,... | collective-permute-start | bytes 2506760 | tf_op jit(solution)/shard_map/ppermute | solution.py:113
  306.2 36.4 %collective-permute-start.36 = (bf16[272,1536]{1,0:T(8,128)(2,1)}, bf16[272,1536]{1,0:T(8,128)(2,1)S(1)}, u32[]{:S(2)}, u32[]{:S(2)}) collective-permute-start(bf16[272,1536]{1,0:T(8,128)(2,1)} %get-tuple-element.105), channel_id=1, source_target_pairs={{0,1},{1,0},{2,3},{3,2},{4,5},{5,4},{6,7},{7,6},{8,9},{9,8},{10,11... | collective-permute-start | bytes 2506760 | tf_op jit(solution)/shard_map/ppermute | solution.py:113
  326.0 38.8 %collective-permute-start.38 = (bf16[272,1536]{1,0:T(8,128)(2,1)S(1)}, bf16[272,1536]{1,0:T(8,128)(2,1)S(1)}, u32[]{:S(2)}, u32[]{:S(2)}) collective-permute-start(bf16[272,1536]{1,0:T(8,128)(2,1)S(1)} %add_convert_fusion.6), channel_id=1, source_target_pairs={{0,2},{1,3},{2,0},{3,1},{4,6},{5,7},{6,4},{7,5},{8,10},{9,11},{10,... | collective-permute-start | bytes 2506760 | tf_op jit(solution)/shard_map/ppermute | solution.py:113
  375.5 75.3 %all-to-all-start = ((bf16[4,256,1536]{2,1,0:T(8,128)(2,1)}), bf16[4,256,1536]{2,1,0:T(8,128)(2,1)S(1)}, u32[]{:S(2)}, u32[]{:S(2)}) async-start(bf16[4,256,1536]{2,1,0:T(8,128)(2,1)} %bitcast.12), calls=%async_computation | async-start | bytes 6291456 | tf_op jit(solution)/shard_map/all_to_all | solution.py:142
  407.0 51.5 %collective-permute-start.43 = (bf16[2,192,1536]{2,1,0:T(8,128)(2,1)}, bf16[2,192,1536]{2,1,0:T(8,128)(2,1)}, u32[]{:S(2)}, u32[]{:S(2)}) collective-permute-start(bf16[2,192,1536]{2,1,0:T(8,128)(2,1)} %get-tuple-element.188), channel_id=1, source_target_pairs={{0,16},{4,20},{8,24},{12,28},{16,0},{20,4},{24,8},{28,12},{1,17},{... | collective-permute-start | bytes 3538952 | tf_op jit(solution)/shard_map/ppermute | solution.py:52
  410.6 50.9 %collective-permute-start.42 = (bf16[2,192,1536]{2,1,0:T(8,128)(2,1)}, bf16[2,192,1536]{2,1,0:T(8,128)(2,1)}, u32[]{:S(2)}, u32[]{:S(2)}) collective-permute-start(bf16[2,192,1536]{2,1,0:T(8,128)(2,1)} %get-tuple-element.190), channel_id=1, source_target_pairs={{0,8},{4,12},{8,0},{12,4},{16,24},{20,28},{24,16},{28,20},{1,9},{5... | collective-permute-start | bytes 3538952 | tf_op jit(solution)/shard_map/ppermute | solution.py:52
  413.3 50.9 %collective-permute-start.47 = (bf16[2,192,1152]{2,1,0:T(8,128)(2,1)}, bf16[2,192,1152]{2,1,0:T(8,128)(2,1)}, u32[]{:S(2)}, u32[]{:S(2)}) collective-permute-start(bf16[2,192,1152]{2,1,0:T(8,128)(2,1)} %get-tuple-element.191), channel_id=1, source_target_pairs={{0,16},{4,20},{8,24},{12,28},{16,0},{20,4},{24,8},{28,12},{1,17},{... | collective-permute-start | bytes 2654216 | tf_op jit(solution)/shard_map/ppermute | solution.py:52
  (57 other events, 845.6 us)
Sparse Core Ops, SparseCore 0:
  41.1 63.8 all-gather.1
  216.6 79.1 reduce-scatter.2
  299.4 100.7 reduce-scatter.4

commit v3 on v2

v3 whole, which is shorter than its diff:
```python
import functools

import jax
import jax.numpy as jnp
from jax import lax
from jax.experimental import pallas as pl
from jax.experimental.pallas import tpu as pltpu
from jax.sharding import PartitionSpec as P

HEADS = 24
KV_HEADS = 8
HEAD_DIM = 64
TOP = 8
GROUPS = HEADS // KV_HEADS
QW = HEADS * HEAD_DIM
KW = KV_HEADS * HEAD_DIM
QKV = QW + 2 * KW
EXT = 128
HALVES = 2
EXTRA = 16
COST_SCALE = 1.0

norm_eps = 1e-06
masked_score = -1e30
BF = jnp.bfloat16
F32 = jnp.float32
ANY = pl.BlockSpec(memory_space=pl.ANY)
VMEM = pl.BlockSpec(memory_space=pltpu.VMEM)
SMEM = pl.BlockSpec(memory_space=pltpu.SMEM)
VMEM_LIMIT = 56 * 1024 * 1024


def dot(a, b, ca=1, cb=0):
    return lax.dot_general(a, b, (((ca,), (cb,)), ((), ())), preferred_element_type=F32)


def params():
    return pltpu.CompilerParams(vmem_limit_bytes=VMEM_LIMIT)


def cost(us):
    return pl.CostEstimate(
        flops=int(us * 1.1e9), bytes_accessed=int(us * 3.6e6 * COST_SCALE), transcendentals=0
    )


def sds(shape, dtype):
    return jax.ShapeDtypeStruct(shape, dtype)


def swap(value, bit, size):
    return lax.ppermute(value, "dp", [(i, i ^ bit) for i in range(size)])


def wait(order, *values):
    return lax.optimization_barrier((order,) + values)


def hold(order, value):
    return lax.optimization_barrier((order, value))[1]


def plain_shards(shard, size):
    rows = shard.shape[-2]
    arrays = [lax.all_gather(shard, "dp", axis=0, tiled=False)]
    return arrays, [(i, 0, rows) for i in range(size)]


def add(a, b):
    return (a.astype(F32) + b.astype(F32)).astype(BF)


def owner_at(z, r, owners):
    return jnp.bitwise_xor(z, r) if owners == 4 else lax.rem(z - r + owners, owners)


def along(value, pairs):
    return lax.ppermute(value, "expert", pairs)


def cross(value, bit):
    return along(value, [(i, i ^ bit) for i in range(4)])


def plain_owners(value, owners):
    turns = [[(i, (i + r) % owners) for i in range(owners)] for r in range(1, owners)]
    return [value] + [along(value, pairs) for pairs in turns]


def plain_return(parts, owners):
    turns = [[(i, (i - r) % owners) for i in range(owners)] for r in range(1, owners)]
    return [parts[0]] + [along(v, pairs) for v, pairs in zip(parts[1:], turns)]


def exchange(value):
    return lax.all_to_all(value, "expert", split_axis=0, concat_axis=0, tiled=True)


def part_shapes(size, shape):
    if size != 8:
        return [sds((size,) + shape, BF)]
    return [sds(shape, BF)] * 4 + [sds((4,) + shape, BF)]


def fetch(me, refs, plan, target, sems, rows, size):
    copies = []
    for n, (i, start, count) in enumerate(plan):
        source = refs[0].at[i] if len(refs) == 1 else refs[n]
        at = (jnp.bitwise_xor(me, i) if size == 8 else i) * rows + start
        if size == 8:
            at = pl.multiple_of(at, rows // 2)
        copies.append(pltpu.make_async_copy(source, target(pl.ds(at, count)), sems.at[n]))
    for c in copies:
        c.start()
    return copies


def pair_refs(own, other, size):
    if size != 8:
        return [own]
    return [(other if i % 2 else own).at[i // 2] for i in range(size)]


def store_parts(me, source, outs, sems, rows, size):
    copies = []
    for i in range(size):
        if len(outs) == 1:
            target, at = outs[0].at[i], i * rows
        else:
            target = outs[i]
            at = pl.multiple_of(jnp.bitwise_xor(me, i) * rows, rows)
        copies.append(pltpu.make_async_copy(source(pl.ds(at, rows)), target, sems.at[i]))
    for c in copies:
        c.start()
    return copies


def pack_kernel(experts, q, k, v, router, gain_one, gain_two, out):
    rows = q.shape[0]
    pad = -(-experts // 8) * 8
    out[:, :QW] = q[...]
    out[:, QW : QW + KW] = k[...]
    out[:, QW + KW : QKV] = v[...]
    gains = [jnp.broadcast_to(g[...].astype(F32)[None, :], (8, rows)) for g in (gain_one, gain_two)]
    parts = [router[...].astype(F32)]
    if pad > experts:
        parts.append(jnp.zeros((pad - experts, rows), F32))
    parts += gains + [jnp.zeros((EXT - pad - 16, rows), F32)]
    out[:, QKV:] = jnp.concatenate(parts, axis=0).T.astype(BF)


def run_pack(q, k, v, router, gain_one, gain_two):
    rows, experts = router.shape
    return pl.pallas_call(
        functools.partial(pack_kernel, experts),
        name="pack",
        out_shape=sds((rows, QKV + EXT), BF),
        in_specs=[VMEM] * 6,
        out_specs=VMEM,
        compiler_params=params(),
        cost_estimate=cost(0.01),
    )(q, k, v, router.T, gain_one, gain_two)


def attention_kernel(size, rows, plan, me, tok, seg_row, seg_col, *rest):
    refs, rest = rest[:-7], rest[-7:]
    low_out, qkv_out, ctx_out, prob_out, ext_out, w, sems = rest
    copies = fetch(me[0], refs, plan, lambda s: w.at[s], sems, rows, size)
    seq = tok.shape[0]
    x = tok[...].astype(F32)
    factor = lax.rsqrt(jnp.mean(x * x, axis=-1, keepdims=True) + norm_eps)
    normed = x * factor
    same = seg_col[...] == seg_row[...]
    key_at = lax.broadcasted_iota(jnp.int32, (seq, seq), 0)
    query_at = lax.broadcasted_iota(jnp.int32, (seq, seq), 1)
    allowed = jnp.where(same & (key_at <= query_at), 0.0, masked_score)
    allowed = jnp.concatenate([allowed] * GROUPS, axis=1)
    for c in copies:
        c.wait()
    ext = w[:, QKV:].astype(F32).T[: ext_out.shape[0], :]
    ext_out[...] = ext
    experts_pad = ext_out.shape[0] - 16
    gain = ext[experts_pad : experts_pad + 1, :]
    low = (normed * gain).astype(BF)
    step = 512
    for j in range(low.shape[1] // step):
        at = slice(j * step, (j + 1) * step)
        low_out[at, :] = low[:, at].astype(F32).T.astype(BF)
    for j in range(QKV // step):
        at = slice(j * step, (j + 1) * step)
        part = dot(low, w[:, at])
        qkv_out[at, :] = part.T.astype(BF)
    for h in range(KV_HEADS):
        q = jnp.concatenate(
            [
                qkv_out[(GROUPS * h + g) * HEAD_DIM : (GROUPS * h + g + 1) * HEAD_DIM, :]
                for g in range(GROUPS)
            ],
            axis=1,
        )
        k = qkv_out[QW + h * HEAD_DIM : QW + (h + 1) * HEAD_DIM, :]
        v = qkv_out[QW + KW + h * HEAD_DIM : QW + KW + (h + 1) * HEAD_DIM, :]
        scores = dot(k, q, 0, 0) * HEAD_DIM ** (-0.5)
        scores = jnp.where(allowed < 0.0, masked_score, scores)
        top = jnp.max(scores, axis=0, keepdims=True)
        shifted = jnp.exp(scores - top)
        probs = (shifted * (1.0 / jnp.sum(shifted, axis=0, keepdims=True))).astype(BF)
        prob_out[h] = probs
        ctx = dot(v, probs).astype(BF)
        for g in range(GROUPS):
            at = (GROUPS * h + g) * HEAD_DIM
            ctx_out[at : at + HEAD_DIM, :] = ctx[:, g * seq : (g + 1) * seq]


def run_attention(me, tokens, seg_row, seg_col, pieces, size, ext_rows):
    seq, width = tokens.shape
    rows = width // size
    arrays, plan = pieces
    return pl.pallas_call(
        functools.partial(attention_kernel, size, rows, plan),
        name="attention",
        out_shape=[
            sds((width, seq), BF),
            sds((QKV, seq), BF),
            sds((QW, seq), BF),
            sds((KV_HEADS, seq, GROUPS * seq), BF),
            sds((ext_rows, width), F32),
        ],
        in_specs=[SMEM, VMEM, VMEM, VMEM] + [ANY] * len(arrays),
        out_specs=[VMEM] * 5,
        scratch_shapes=[
            pltpu.VMEM((width, QKV + EXT), BF),
            pltpu.SemaphoreType.DMA((len(plan),)),
        ],
        compiler_params=params(),
        cost_estimate=cost(0.01),
    )(me, tokens, seg_row, seg_col, *arrays)


def residual_kernel(size, rows, plan, me, tok, ctx, ext, place, *rest):
    refs, (res_out, low_out, w, sems) = rest[:-4], rest[-4:]
    copies = fetch(me[0], refs, plan, lambda s: w.at[s], sems, rows, size)
    experts_pad = ext.shape[0] - 16
    for c in copies:
        c.wait()
    res = tok[...].astype(F32) + dot(ctx[...], w[...], 0, 0)
    res_out[...] = res
    factor = lax.rsqrt(jnp.mean(res * res, axis=-1, keepdims=True) + norm_eps)
    seq = res.shape[0]
    low_out[:seq, :] = (res * factor * ext[experts_pad + 8 : experts_pad + 9, :]).astype(BF)
    low_out[seq:, :] = place[...]


def run_residual(me, tokens, ctx, ext, place, pieces, size):
    seq, width = tokens.shape
    rows = QW // size
    arrays, plan = pieces
    return pl.pallas_call(
        functools.partial(residual_kernel, size, rows, plan),
        name="residual",
        out_shape=[sds((seq, width), F32), sds((seq + EXTRA, width), BF)],
        in_specs=[SMEM, VMEM, VMEM, VMEM, VMEM] + [ANY] * len(arrays),
        out_specs=[VMEM] * 2,
        scratch_shapes=[pltpu.VMEM((QW, width), BF), pltpu.SemaphoreType.DMA((len(plan),))],
        compiler_params=params(),
        cost_estimate=cost(0.01),
    )(me, tokens, ctx, ext, place, *arrays)


def slot_of(block, seq, width):
    across = width // seq
    row, col = block // across * 8, block % across * seq
    return slice(row, row + 8), slice(col, col + seq)


def router_kernel(owners, per, z, ext, *rest):
    rows, rest = rest[:owners], rest[owners:]
    pos_out, p_out, own_out, all_p, all_pos = rest
    experts_pad = ext.shape[0] - 16
    seq, width = rows[0].shape[0] - EXTRA, rows[0].shape[1]
    router = ext[:experts_pad, :].astype(BF)
    at = z[0] * per
    for r in range(owners):
        logits = dot(router, rows[r][:seq, :], 1, 1)
        spots = rows[r][seq:, :].astype(F32)
        for b in range(experts_pad // 8):
            of, to = slot_of(b, seq, width)
            all_pos[b * 8 : (b + 1) * 8, :] = spots[of, to]
        where = all_pos[...]
        named = where >= 0.0
        logits = jnp.where(named, logits, masked_score)
        top = jnp.max(logits, axis=0, keepdims=True)
        shifted = jnp.where(named, jnp.exp(logits - top), 0.0)
        probs = shifted / jnp.sum(shifted, axis=0, keepdims=True)
        all_p[...] = probs
        if r == 0:
            own_out[...] = probs
        for l in range(per):
            p_out[l, r : r + 1, :] = all_p[pl.ds(at + l, 1), :]
            pos_out[l, r : r + 1, :] = all_pos[pl.ds(at + l, 1), :].astype(jnp.int32)


def run_router(z, ext, rows, per):
    owners = len(rows)
    seq = rows[0].shape[0] - EXTRA
    experts_pad = ext.shape[0] - 16
    return pl.pallas_call(
        functools.partial(router_kernel, owners, per),
        name="router",
        out_shape=[
            sds((per, owners, seq), jnp.int32),
            sds((per, owners, seq), F32),
            sds((experts_pad, seq), F32),
        ],
        in_specs=[SMEM, VMEM] + [VMEM] * owners,
        out_specs=[VMEM] * 3,
        scratch_shapes=[pltpu.VMEM((experts_pad, seq), F32)] * 2,
        compiler_params=params(),
        cost_estimate=cost(0.01),
    )(z, ext, *rows)


def load_rows(owners, z, xs, cs, xv, cv, sem_x, sem_c):
    seq = xv.shape[1]
    copies = []
    for r in range(owners):
        start = pl.multiple_of(owner_at(z[0], r, owners) * seq, seq)
        copies.append(pltpu.make_async_copy(xs[r].at[pl.ds(0, seq)], xv.at[r], sem_x.at[r]))
        copies.append(pltpu.make_async_copy(cs.at[pl.ds(start, seq)], cv.at[r], sem_c.at[r]))
    for c in copies:
        c.start()

    def wait():
        for c in copies:
            c.wait()

    return wait


def pick_rows(owners, cap, number, pos, p, xv, cv, xr, cr, prow):
    seq = xv.shape[1]
    slot = lax.broadcasted_iota(jnp.int32, (cap, seq), 0)
    for r in range(owners):
        hot = pos[number, r : r + 1, :] == slot
        low_hot = jnp.where(hot, 1.0, 0.0).astype(BF)
        at = pl.ds(r * cap, cap)
        xr[at, :] = dot(low_hot, xv[r]).astype(BF)
        cr[at, :] = dot(low_hot, cv[r]).astype(BF)
        prow[at, :] = jnp.sum(jnp.where(hot, p[number, r : r + 1, :], 0.0), axis=1, keepdims=True)


def through_expert(owners, cap, number, pos, xr, cr, prow, w, hp, gg, ug, gate, gate_out):
    ff = w.shape[2]
    step = ff // HALVES
    gate[...] = jnp.zeros_like(gate)
    for j in range(HALVES):
        cols = slice(j * step, (j + 1) * step)
        gate_pre = dot(xr[...], w[0, :, cols])
        up_pre = dot(xr[...], w[1, :, cols])
        back = dot(cr[...], w[2, :, cols])
        probs = prow[...]
        s = jax.nn.sigmoid(gate_pre)
        silu = gate_pre * s
        hidden = silu * up_pre
        gate[...] += jnp.sum(hidden * back, axis=1, keepdims=True)
        hp[:, cols] = (hidden * probs).astype(BF)
        back = back * probs
        gg[:, cols] = (back * up_pre * (s + silu * (1.0 - s))).astype(BF)
        ug[:, cols] = (back * silu).astype(BF)
    seq = pos.shape[2]
    slot = lax.broadcasted_iota(jnp.int32, (cap, seq), 0)
    for r in range(owners):
        hot = pos[number, r : r + 1, :] == slot
        at = pl.ds(r * cap, cap)
        gate_out[r : r + 1, :] = jnp.sum(jnp.where(hot, gate[at, :], 0.0), axis=0, keepdims=True)


def load_weights(me, refs, plan, w, sems, slot_at, rows, size):
    shards = [ref.at[:, slot_at] if len(refs) == 1 else ref.at[slot_at] for ref in refs]
    return fetch(me, shards, plan, lambda s: w.at[:, s, :], sems, rows, size)


def weight_grads(xr, cr, hp, gg, ug, g, grads, sems, slot_at, rows, size):
    width = xr.shape[1]
    tile = width // HALVES
    for j in range(HALVES):
        cols = slice(j * tile, (j + 1) * tile)
        g[0, cols, :] = dot(xr[:, cols], gg[...], 0, 0).astype(BF)
        g[1, cols, :] = dot(xr[:, cols], ug[...], 0, 0).astype(BF)
        g[2, cols, :] = dot(cr[:, cols], hp[...], 0, 0).astype(BF)
    copies = [
        pltpu.make_async_copy(g.at[:, pl.ds(i * rows, rows), :], grads.at[i, slot_at], sems.at[i])
        for i in range(size)
    ]
    for c in copies:
        c.start()
    return copies


def rows_back(w, gg, ug, bv):
    tile = bv.shape[1] // HALVES
    for j in range(HALVES):
        cols = slice(j * tile, (j + 1) * tile)
        total = dot(gg[...], w[0, cols, :], 1, 1) + dot(ug[...], w[1, cols, :], 1, 1)
        bv[:, cols] = total.astype(BF)


def rows_out(w, hp, ov):
    tile = ov.shape[1] // HALVES
    for j in range(HALVES):
        cols = slice(j * tile, (j + 1) * tile)
        ov[:, cols] = dot(hp[...], w[cols, :], 1, 1).astype(BF)


def experts_kernel(size, rows, owners, cap, first, many, plan, count, me, z, pos, p, cs, *rest):
    xs, refs, rest = rest[:owners], rest[owners : owners + count], rest[owners + count :]
    if first > 0:
        rest = rest[1:]
    out_rows, back_rows, gate_out, grads = rest[:4]
    xv, cv, w, xr, cr, prow, hp, gg, ug, gate, ov, bv, g, sem_x, sem_c, sem_w, sem_g, sem_o = rest[4:]
    wait_rows = load_rows(owners, z, xs, cs, xv, cv, sem_x, sem_c)

    def load(i):
        return load_weights(me[0], refs, plan, w.at[i % 2], sem_w.at[i % 2], i, rows, size)

    coming = load(0)
    leaving = []
    for i in range(many):
        here = i % 2
        number = first + i
        if i == 0:
            wait_rows()
        pick_rows(owners, cap, number, pos, p, xv, cv, xr, cr, prow)
        for c in coming:
            c.wait()
        if i + 1 < many:
            coming = load(i + 1)
        if len(leaving) > 1:
            for c in leaving[i - 2]:
                c.wait()
        through_expert(
            owners, cap, number, pos, xr, cr, prow, w.at[here], hp, gg, ug, gate, gate_out.at[i]
        )
        copies = weight_grads(
            xr, cr, hp, gg, ug, g.at[here], grads, sem_g.at[here], number, rows, size
        )
        rows_back(w.at[here], gg, ug, bv.at[here])
        copies.append(pltpu.make_async_copy(bv.at[here], back_rows.at[i], sem_o.at[here, 0]))
        copies[-1].start()
        rows_out(w.at[here, 2], hp, ov.at[here])
        copies.append(pltpu.make_async_copy(ov.at[here], out_rows.at[i], sem_o.at[here, 1]))
        copies[-1].start()
        leaving.append(copies)
    for copies in leaving[-2:]:
        for c in copies:
            c.wait()


def run_experts(me, z, pos, p, xs, cs, pieces, buffer, size, first, many, cap):
    per, owners, seq = pos.shape
    width = xs[0].shape[1]
    refs, plan = pieces
    ff = refs[0].shape[-1]
    rows = width // size
    total = owners * cap
    given = [me, z, pos, p, cs, *xs, *refs] + ([] if buffer is None else [buffer])
    return pl.pallas_call(
        functools.partial(
            experts_kernel, size, rows, owners, cap, first, many, plan, len(refs)
        ),
        name="experts",
        out_shape=[
            sds((many, total, width), BF),
            sds((many, total, width), BF),
            sds((many, owners, seq), F32),
            sds((size, per, 3, rows, ff), BF),
        ],
        in_specs=[SMEM, SMEM, VMEM, VMEM] + [ANY] * (len(given) - 4),
        out_specs=[ANY, ANY, VMEM, ANY],
        input_output_aliases={} if buffer is None else {len(given) - 1: 3},
        scratch_shapes=[
            pltpu.VMEM((owners, seq, width), BF),
            pltpu.VMEM((owners, seq, width), BF),
            pltpu.VMEM((2, 3, width, ff), BF),
            pltpu.VMEM((total, width), BF),
            pltpu.VMEM((total, width), BF),
            pltpu.VMEM((total, 1), F32),
            pltpu.VMEM((total, ff), BF),
            pltpu.VMEM((total, ff), BF),
            pltpu.VMEM((total, ff), BF),
            pltpu.VMEM((total, 1), F32),
            pltpu.VMEM((2, total, width), BF),
            pltpu.VMEM((2, total, width), BF),
            pltpu.VMEM((2, 3, width, ff), BF),
            pltpu.SemaphoreType.DMA((owners,)),
            pltpu.SemaphoreType.DMA((owners,)),
            pltpu.SemaphoreType.DMA((2, len(plan))),
            pltpu.SemaphoreType.DMA((2, size)),
            pltpu.SemaphoreType.DMA((2, 2)),
        ],
        compiler_params=params(),
        cost_estimate=cost(0.01),
    )(*given)


def combined_rows(per, cap, pos, r, rows):
    seq = pos.shape[2]
    slot = lax.broadcasted_iota(jnp.int32, (cap, seq), 0)
    hot = jnp.concatenate(
        [jnp.where(pos[l, pl.ds(r, 1), :] == slot, 1.0, 0.0).astype(BF) for l in range(per)], axis=0
    )
    total, at = 0.0, 0
    for group in rows:
        count = group.shape[0] * cap
        total = total + dot(hot[at : at + count], group[...].reshape(count, -1), 0, 0)
        at += count
    return total.astype(BF)


def combine_back_kernel(start, owners, per, cap, experts_pad, groups, z, pos, *rest):
    rows, gates, rest = rest[:groups], rest[groups : 2 * groups], rest[2 * groups :]
    outs, block = rest[:owners], rest[owners]
    step = pl.program_id(0)
    r = step + start
    seq, width = pos.shape[2], outs[0].shape[1]
    total = combined_rows(per, cap, pos, r, rows)
    block[...] = jnp.zeros_like(block)
    gates = [group.at[l] for group in gates for l in range(group.shape[0])]
    for l in range(per):
        block[pl.ds(z[0] * per + l, 1), :] = gates[l][pl.ds(r, 1), :]
    value = block[...]
    high = value.astype(BF)
    low = (value - high.astype(F32)).astype(BF)
    for o in range(owners):

        @pl.when(step == o)
        def _():
            outs[o][:seq, :] = total
            outs[o][seq:, :] = jnp.zeros((EXTRA, width), BF)
            both = jnp.concatenate([high, low], axis=0).astype(F32)
            for row in range(EXTRA // 8):
                across = width // seq
                blocks = [
                    both[(row * across + b) * 8 : (row * across + b + 1) * 8, :]
                    if row * across + b < 2 * experts_pad // 8
                    else jnp.zeros((8, seq), F32)
                    for b in range(across)
                ]
                outs[o][seq + row * 8 : seq + row * 8 + 8, :] = jnp.concatenate(
                    blocks, axis=1
                ).astype(BF)


def whole(shape):
    return pl.BlockSpec(shape, lambda r: (0,) * len(shape))


def run_combine_back(z, pos, rows, gates, cap, experts_pad, start, owners):
    per, _, seq = pos.shape
    width = rows[0].shape[2]
    shapes = [sds((seq + EXTRA, width), BF)] * owners
    return pl.pallas_call(
        functools.partial(combine_back_kernel, start, owners, per, cap, experts_pad, len(rows)),
        name="combine_back",
        grid=(owners,),
        out_shape=shapes,
        in_specs=[SMEM, whole(pos.shape)]
        + [pl.BlockSpec((a.shape[0], cap, width), lambda r: (0, r + start, 0)) for a in rows]
        + [whole(a.shape) for a in gates],
        out_specs=[whole(s.shape) for s in shapes],
        scratch_shapes=[pltpu.VMEM((experts_pad, seq), F32)],
        compiler_params=params(),
        cost_estimate=cost(0.01),
    )(z, pos, *rows, *gates)


def combine_out_kernel(owners, per, cap, pos, *rest):
    rows, outs = rest[:-owners], rest[-owners:]
    r = pl.program_id(0)
    total = combined_rows(per, cap, pos, r, rows)
    for o in range(owners):

        @pl.when(r == o)
        def _():
            outs[o][...] = total


def run_combine_out(pos, rows, cap):
    per, owners, seq = pos.shape
    width = rows[0].shape[2]
    return pl.pallas_call(
        functools.partial(combine_out_kernel, owners, per, cap),
        name="combine_out",
        grid=(owners,),
        out_shape=[sds((seq, width), BF)] * owners,
        in_specs=[whole(pos.shape)]
        + [pl.BlockSpec((a.shape[0], cap, width), lambda r: (0, r, 0)) for a in rows],
        out_specs=[whole((seq, width))] * owners,
        compiler_params=params(),
        cost_estimate=cost(0.01),
    )(pos, *rows)


def join_kernel(owners, own, *rest):
    more, (parts, out) = rest[:-2], rest[-2:]
    rows, cols = own.shape
    total = own[...].astype(F32)
    for piece in more:
        total = total + piece[...].astype(F32)
    total = total.astype(BF)
    low = parts.shape[0] // owners
    summed = 0.0
    for r in range(owners):
        summed = summed + parts[r * low : (r + 1) * low, :].astype(F32)
    summed = summed.astype(BF)
    wide = summed.shape[1] // owners
    for r in range(owners):
        out[r * rows : (r + 1) * rows, :cols] = total
        for k in range(owners):
            at = r * rows + k * low
            out[at : at + low, cols:] = summed[:, k * wide : (k + 1) * wide]


def run_join(pieces, parts, owners):
    rows, cols = pieces[0].shape
    return pl.pallas_call(
        functools.partial(join_kernel, owners),
        name="join",
        out_shape=sds((owners * rows, cols + parts.shape[1] // owners), BF),
        in_specs=[VMEM] * (len(pieces) + 1),
        out_specs=VMEM,
        compiler_params=params(),
        cost_estimate=cost(0.01),
    )(*pieces, parts)


def finish_kernel(owners, total, query, key, value, out, router, gain_one, gain_two):
    rows = query.shape[0]
    wide, narrow = QW // owners, KW // owners
    one = wide + 2 * narrow
    low, out_wide = rows // owners, out.shape[1] // owners
    ext_sum = 0.0
    for j in range(owners):
        block = total[j * rows : (j + 1) * rows, :].astype(F32)
        query[:, j * wide : (j + 1) * wide] = block[:, :wide]
        key[:, j * narrow : (j + 1) * narrow] = block[:, wide : wide + narrow]
        value[:, j * narrow : (j + 1) * narrow] = block[:, wide + narrow : one]
        ext_sum = ext_sum + block[:, one : one + EXT]
        for k in range(owners):
            out[j * low : (j + 1) * low, k * out_wide : (k + 1) * out_wide] = block[
                k * low : (k + 1) * low, one + EXT :
            ]
    ext_sum = ext_sum.T
    experts = router.shape[0]
    pad = -(-experts // 8) * 8
    router[...] = ext_sum[:experts, :]
    gain_one[...] = ext_sum[pad, :]
    gain_two[...] = ext_sum[pad + 8, :]


def run_finish(total, owners, experts):
    rows = total.shape[0] // owners
    width = (total.shape[1] - EXT - (QW + 2 * KW) // owners) * owners
    return pl.pallas_call(
        functools.partial(finish_kernel, owners),
        name="finish",
        out_shape=[
            sds((rows, QW), F32),
            sds((rows, KW), F32),
            sds((rows, KW), F32),
            sds((rows, width), F32),
            sds((experts, rows), F32),
            sds((rows,), F32),
            sds((rows,), F32),
        ],
        in_specs=[VMEM],
        out_specs=[VMEM] * 7,
        compiler_params=params(),
        cost_estimate=cost(0.01),
    )(total)


def second_kernel(
    size, rows, owners, per, plan, count, me, own_p, ext, low_two, res, cot, ctx, *rest
):
    backs, rest = rest[:owners], rest[owners:]
    refs, rest = rest[:count], rest[count:]
    res_grad, ctx_grad, ext_grad, own, other, w, g, gate, sems, sems_g = rest
    copies = fetch(me[0], refs, plan, lambda s: w.at[s], sems, rows, size)
    experts_pad = own_p.shape[0]
    seq, width = res.shape
    arrived = backs[0][seq:, :].astype(F32)
    for r in range(1, owners):
        arrived = arrived + backs[r][seq:, :].astype(F32)
    for b in range(experts_pad // 8):
        high_at = slot_of(b, seq, width)
        low_at = slot_of(b + experts_pad // 8, seq, width)
        gate[b * 8 : (b + 1) * 8, :] = arrived[high_at] + arrived[low_at]
    p = own_p[...]
    gate_grad = gate[...]
    weighted = jnp.sum(p * gate_grad, axis=0, keepdims=True)
    logit_grad = (p * (gate_grad - weighted)).astype(BF)
    router = ext[:experts_pad, :].astype(BF)
    ext_grad[:experts_pad, :] = dot(logit_grad, low_two[:seq, :])
    two = dot(logit_grad, router, 0, 0)
    for r in range(owners):
        two = two + backs[r][:seq, :].astype(F32)
    values = res[...]
    factor = lax.rsqrt(jnp.mean(values * values, axis=-1, keepdims=True) + norm_eps)
    normed = values * factor
    ext_grad[experts_pad:, :] = jnp.broadcast_to(
        jnp.sum(two * normed, axis=0, keepdims=True), (16, normed.shape[1])
    )
    scaled = two * ext[experts_pad + 8 : experts_pad + 9, :]
    inward = factor * (scaled - normed * jnp.mean(scaled * normed, axis=-1, keepdims=True))
    total = cot[...].astype(F32) + inward
    res_grad[...] = total
    low = total.astype(BF)
    step = QW // 4
    for j in range(4):
        at = slice(j * step, (j + 1) * step)
        g[at, :] = dot(ctx[at, :], low).astype(BF)
    copies_g = store_parts(me[0], lambda s: g.at[s], pair_refs(own, other, size), sems_g, rows, size)
    for c in copies:
        c.wait()
    for j in range(4):
        at = slice(j * step, (j + 1) * step)
        ctx_grad[at, :] = dot(w[at, :], low, 1, 1).astype(BF)
    for c in copies_g:
        c.wait()


def run_second(me, own_p, ext, low_two, res, cot, ctx, backs, pieces, size, per):
    owners = len(backs)
    arrays, plan = pieces
    seq, width = res.shape
    rows = QW // size
    experts_pad = own_p.shape[0]
    return pl.pallas_call(
        functools.partial(second_kernel, size, rows, owners, per, plan, len(arrays)),
        name="second_back",
        out_shape=[
            sds((seq, width), F32),
            sds((QW, seq), BF),
            sds((experts_pad + 16, width), F32),
            sds((size if size != 8 else 4, rows, width), BF),
            sds((4, rows, width), BF),
        ],
        in_specs=[SMEM] + [VMEM] * (6 + owners) + [ANY] * len(arrays),
        out_specs=[VMEM] * 3 + [ANY] * 2,
        scratch_shapes=[
            pltpu.VMEM((QW, width), BF),
            pltpu.VMEM((QW, width), BF),
            pltpu.VMEM((experts_pad, seq), F32),
            pltpu.SemaphoreType.DMA((len(plan),)),
            pltpu.SemaphoreType.DMA((size,)),
        ],
        compiler_params=params(),
        cost_estimate=cost(0.01),
    )(me, own_p, ext, low_two, res, cot, ctx, *backs, *arrays)


def heads_kernel(ctx_grad, qkv, probs, back, blocks):
    seq = qkv.shape[1]
    scale = HEAD_DIM ** (-0.5)
    for h in range(KV_HEADS):

        def heads(ref):
            return jnp.concatenate(
                [
                    ref[(GROUPS * h + i) * HEAD_DIM : (GROUPS * h + i + 1) * HEAD_DIM, :]
                    for i in range(GROUPS)
                ],
                axis=1,
            )

        upstream = heads(ctx_grad)
        q = heads(qkv)
        k = qkv[QW + h * HEAD_DIM : QW + (h + 1) * HEAD_DIM, :]
        v = qkv[QW + KW + h * HEAD_DIM : QW + KW + (h + 1) * HEAD_DIM, :]
        low_p = probs[h]
        weights = low_p.astype(F32)
        prob_grad = dot(v, upstream, 0, 0)
        inner = jnp.sum(prob_grad * weights, axis=0, keepdims=True)
        score_grad = (weights * (prob_grad - inner)).astype(BF)
        value_grad = dot(upstream, low_p, 1, 1)
        key_grad = dot(q, score_grad, 1, 1) * scale
        query_grad = dot(k, score_grad) * scale
        back[QW + h * HEAD_DIM : QW + (h + 1) * HEAD_DIM, :] = key_grad.astype(BF)
        back[QW + KW + h * HEAD_DIM : QW + KW + (h + 1) * HEAD_DIM, :] = value_grad.astype(BF)
        for i in range(GROUPS):
            at = (GROUPS * h + i) * HEAD_DIM
            back[at : at + HEAD_DIM, :] = query_grad[:, i * seq : (i + 1) * seq].astype(BF)
    owners = blocks.shape[0] // seq
    wide, slim = QW // owners, KW // owners
    for j in range(owners):
        block = jnp.concatenate(
            [
                back[j * wide : (j + 1) * wide, :],
                back[QW + j * slim : QW + (j + 1) * slim, :],
                back[QW + KW + j * slim : QW + KW + (j + 1) * slim, :],
            ],
            axis=0,
        )
        blocks[j * seq : (j + 1) * seq, :] = block.astype(F32).T.astype(BF)


def run_heads(ctx_grad, qkv, probs, owners):
    seq = qkv.shape[1]
    return pl.pallas_call(
        heads_kernel,
        name="heads_back",
        out_shape=[sds((QKV, seq), BF), sds((owners * seq, QKV // owners), BF)],
        in_specs=[VMEM] * 3,
        out_specs=[VMEM] * 2,
        compiler_params=params(),
        cost_estimate=cost(0.01),
    )(ctx_grad, qkv, probs)


def first_kernel(size, rows, plan, me, back, tok, ext, ext_grad, res_grad, *rest):
    refs, (tok_grad, ext_cols, w, sems) = rest[:-4], rest[-4:]
    copies = fetch(me[0], refs, plan, lambda s: w.at[s], sems, rows, size)
    for c in copies:
        c.wait()
    one = dot(back[...], w[:, :QKV], 0, 1)
    x = tok[...].astype(F32)
    factor = lax.rsqrt(jnp.mean(x * x, axis=-1, keepdims=True) + norm_eps)
    normed = x * factor
    experts_pad = ext.shape[0] - 16
    gain = ext[experts_pad : experts_pad + 1, :]
    gain_grad = jnp.sum(one * normed, axis=0, keepdims=True)
    packed = jnp.concatenate(
        [
            ext_grad[:experts_pad, :],
            jnp.broadcast_to(gain_grad, (8, gain_grad.shape[1])),
            ext_grad[experts_pad + 8 :, :],
            jnp.zeros((EXT - experts_pad - 16, gain_grad.shape[1]), F32),
        ],
        axis=0,
    )
    ext_cols[...] = packed.T.astype(BF)
    scaled = one * gain
    inward = factor * (scaled - normed * jnp.mean(scaled * normed, axis=-1, keepdims=True))
    tok_grad[...] = res_grad[...] + inward


def run_first(me, back, tokens, ext, ext_grad, res_grad, pieces, size):
    arrays, plan = pieces
    seq, width = tokens.shape
    rows = width // size
    return pl.pallas_call(
        functools.partial(first_kernel, size, rows, plan),
        name="first_back",
        out_shape=[sds((seq, width), F32), sds((width, EXT), BF)],
        in_specs=[SMEM] + [VMEM] * 5 + [ANY] * len(arrays),
        out_specs=[VMEM] * 2,
        scratch_shapes=[
            pltpu.VMEM((width, QKV + EXT), BF),
            pltpu.SemaphoreType.DMA((len(plan),)),
        ],
        compiler_params=params(),
        cost_estimate=cost(60),
    )(me, back, tokens, ext, ext_grad, res_grad, *arrays)


def project_kernel(size, rows, me, low_all, back_all, ext_cols, *rest):
    grads, (g, sems_g) = rest[:-2], rest[-2:]
    owners, _, seq = low_all.shape
    cols = back_all.shape[1]
    g[:, cols:] = ext_cols[...]
    total = 0.0
    for r in range(owners):
        total = total + dot(low_all[r], back_all[r * seq : (r + 1) * seq, :])
    g[:, :cols] = total.astype(BF)
    if size == 8:
        grads = [grads[4].at[i // 2] if i % 2 else grads[i // 2] for i in range(size)]
    copies_g = store_parts(me[0], lambda s: g.at[s], grads, sems_g, rows, size)
    for c in copies_g:
        c.wait()


def run_project(me, low_all, back_all, ext_cols, size):
    width, cols = low_all.shape[1], back_all.shape[1] + EXT
    rows = width // size
    grads = part_shapes(size, (rows, cols))
    return pl.pallas_call(
        functools.partial(project_kernel, size, rows),
        name="project_back",
        out_shape=grads,
        in_specs=[SMEM] + [VMEM] * 3,
        out_specs=[ANY] * len(grads),
        scratch_shapes=[pltpu.VMEM((width, cols), BF), pltpu.SemaphoreType.DMA((size,))],
        compiler_params=params(),
        cost_estimate=cost(60),
    )(me, low_all, back_all, ext_cols)


def split_groups(per):
    cut = max(1, (2 * per) // 5)
    return [(0, cut), (cut, per)]


def body(
    tokens,
    segment_ids,
    expert_choices,
    attn_gain,
    query_weight,
    key_weight,
    value_weight,
    output_weight,
    ffn_gain,
    router_weight,
    expert_gate,
    expert_up,
    expert_down,
    cotangent,
):
    size = lax.axis_size("dp")
    owners = lax.axis_size("expert")
    paired = size == 8 and owners == 4
    me = lax.axis_index("dp").astype(jnp.int32).reshape(1)
    z = lax.axis_index("expert").astype(jnp.int32).reshape(1)
    seq, width = tokens.shape
    per = expert_gate.shape[0]
    experts = per * owners
    experts_pad = -(-experts // 8) * 8
    capacity = (seq * TOP * 9 + 8 * experts - 1) // (8 * experts)
    cap = -(-capacity // 16) * 16
    slim = query_weight.shape[0]
    segments = segment_ids.reshape(seq, 1)
    (a_first, a_last), (b_first, b_last) = split_groups(per)

    cots = lax.all_gather(cotangent, "expert", axis=0, tiled=True)
    packed = run_pack(query_weight, key_weight, value_weight, router_weight, attn_gain, ffn_gain)
    shards = jnp.stack([expert_gate, expert_up, jnp.swapaxes(expert_down, 1, 2)], axis=1)
    a_shard, b_shard = shards[a_first:a_last], shards[b_first:b_last]

    ids = jnp.arange(experts_pad, dtype=jnp.int32)
    hot = jnp.any(expert_choices[:, None, :] == ids[None, :, None], axis=2)
    hot = hot.astype(BF).T
    at = jnp.arange(seq, dtype=jnp.int32)
    earlier = (at[:, None] < at[None, :]).astype(BF)
    place = jnp.dot(hot, earlier, preferred_element_type=F32)
    place = jnp.where(hot > 0, place, -1.0).astype(BF)
    across = width // seq
    place = jnp.pad(place, ((0, EXTRA * across - experts_pad), (0, 0)))
    place = place.reshape(EXTRA // 8, across, 8, seq).swapaxes(1, 2).reshape(EXTRA, width)

    if paired:
        half = slim // 2
        full = [(0, 0, slim), (2, 0, slim), (4, 0, slim), (6, 0, slim)]
        full += [(m + 1, first, rows) for m, first, rows in full]
        split = [(0, 0, slim), (2, 0, slim), (4, 0, slim), (6, 0, half), (6, half, half)]
        split += [(m + 1, first, rows) for m, first, rows in split]
        order = segment_ids
        qx, qy, q1 = (swap(packed, bit, size) for bit in (2, 4, 1))
        order, qx, qy, q1 = wait(order, qx, qy, q1)
        qa, qb = swap(qx[:half], 4, size), swap(qy[half:], 2, size)
        q3 = swap(qx, 1, size)
        o_shard = hold(order, output_weight)
        ox, oy = swap(o_shard, 2, size), swap(o_shard, 4, size)
        order, qa, qb, q3 = wait(order, qa, qb, q3)
        q5, q6, q7 = swap(hold(order, qy), 1, size), swap(qa, 1, size), swap(qb, 1, size)
        order, q5, q6, q7, ox, oy = wait(order, q5, q6, q7, ox, oy)
        qkv_pieces = ([packed, qx, qy, qa, qb, q1, q3, q5, q6, q7], split)
        oc, o3, o5 = swap(oy, 2, size), swap(ox, 1, size), swap(oy, 1, size)
        ay, o1 = swap(hold(order, a_shard), 4, size), swap(hold(order, output_weight), 1, size)
        low_one, qkv, ctx, probs, extra = run_attention(
            me, hold(order, tokens), segment_ids, segments, qkv_pieces, size, experts_pad + 16
        )
        order, ctx, oc, o3, o5, o1 = wait(order, ctx, oc, o3, o5, o1)
        o7, ax = swap(oc, 1, size), swap(hold(order, a_shard), 2, size)
        order, o7, cots = wait(order, o7, cots)
        out_pieces = ([output_weight, ox, oy, oc, o1, o3, o5, o7], full)
        res, low_two = run_residual(
            me, hold(order, tokens), ctx, extra, place, out_pieces, size
        )
        order, low_two, ay = wait(order, low_two, ay)
        far, near = cross(low_two, 2), cross(low_two, 1)
        held = hold(order, b_shard)
        by, bx = swap(held, 4, size), swap(held, 2, size)
        order, ax = wait(order, ax)
        ac = swap(ax, 4, size)
        order, far, near = wait(order, far, near)
        middle = along(hold(order, low_two), [(1, 2), (2, 1)])
        passed = along(far, [(2, 3), (1, 0)])
        order, middle, passed, by, bx = wait(order, middle, passed, by, bx)
        inner = (z[0] == 1) | (z[0] == 2)
        xs = [low_two, near, far, jnp.where(inner, middle, passed)]
        low_all = lax.all_gather(hold(order, low_one), "expert", axis=0, tiled=True)
        ba, bb = swap(bx[..., :half, :], 4, size), swap(by[..., half:, :], 2, size)
        a1, a3, a5 = (swap(hold(order, v), 1, size) for v in (a_shard, ax, ay))
        pos, p, own_p = run_router(z, hold(order, extra), xs, per)
        order, p, ac, a1, a3, a5 = wait(order, p, ac, a1, a3, a5)
        a7, b3, b5 = swap(ac, 1, size), swap(hold(order, bx), 1, size), swap(hold(order, by), 1, size)
        order, a7 = wait(order, a7)
        b1 = swap(hold(order, b_shard), 1, size)
        a_pieces = ([a_shard, ax, ay, ac, a1, a3, a5, a7], full)
    else:
        qkv_pieces = plain_shards(packed, size)
        out_pieces = plain_shards(output_weight, size)
        a_pieces, b_pieces = plain_shards(a_shard, size), plain_shards(b_shard, size)
        low_one, qkv, ctx, probs, extra = run_attention(
            me, tokens, segment_ids, segments, qkv_pieces, size, experts_pad + 16
        )
        res, low_two = run_residual(me, tokens, ctx, extra, place, out_pieces, size)
        xs = plain_owners(low_two, owners)
        low_all = lax.all_gather(low_one, "expert", axis=0, tiled=True)
        pos, p, own_p = run_router(z, extra, xs, per)
        order = p
    low_all = low_all.reshape(owners, width, seq)

    a_rows = run_experts(
        me, z, pos, hold(order, p), xs, cots, a_pieces, None, size, a_first, a_last - a_first, cap
    )
    if paired:
        order, a_gate, ba, bb, b1, b3, b5 = wait(order, a_rows[2], ba, bb, b1, b3, b5)
        b6, b7 = swap(ba, 1, size), swap(bb, 1, size)
        order, b6, b7 = wait(order, b6, b7)
        b_pieces = ([b_shard, bx, by, ba, bb, b1, b3, b5, b6, b7], split)
    b_rows = run_experts(
        me, z, pos, hold(order, p), xs, cots, b_pieces, a_rows[3], size, b_first, b_last - b_first, cap
    )
    expert_total = lax.psum_scatter(b_rows[3], "dp", scatter_dimension=0, tiled=False)
    expert_total = expert_total.astype(F32)
    expert_outputs = (
        expert_total[:, 0],
        expert_total[:, 1],
        jnp.swapaxes(expert_total[:, 2], 1, 2),
    )
    back_rows = ([a_rows[1], b_rows[1]], [a_rows[2], b_rows[2]], cap, experts_pad)
    last_part = run_combine_back(z, pos, *back_rows, owners - 1, 1)[0]
    if paired:
        order, last_part = wait(order, last_part)
        passed, middle = along(last_part, [(3, 2), (0, 1)]), along(last_part, [(1, 2), (2, 1)])
    else:
        order = last_part
    backs = run_combine_back(z, hold(order, pos), *back_rows, 0, owners - 1)
    backs = [*backs, last_part]
    out_rows = [a_rows[0], b_rows[0]]
    if paired:
        outs = run_combine_out(hold(order, pos), out_rows, cap)
        order, passed, middle, *outs = wait(order, passed, middle, *outs)
        far, near = cross(add(backs[2], passed), 2), cross(hold(order, backs[1]), 1)
        order, far, near = wait(order, far, near)
        backs = [backs[0], near, far, middle]
        last_out = hold(order, outs[3])
        passed, middle = along(last_out, [(3, 2), (0, 1)]), along(last_out, [(1, 2), (2, 1)])
        near_out = cross(hold(order, outs[1]), 1)
    else:
        outs = run_combine_out(pos, out_rows, cap)
        backs = plain_return(backs, owners)
        outs = plain_return(outs, owners)
        order = backs[0]
    res_grad, ctx_grad, ext_grad, o_own, o_other = run_second(
        me, own_p, hold(order, extra), low_two, res, cotangent, ctx, backs, out_pieces, size, per
    )
    back, blocks = run_heads(ctx_grad, qkv, probs, owners)
    if paired:
        order, blocks, back, passed, middle, near_out = wait(
            order, blocks, back, passed, middle, near_out
        )
    back_all = exchange(blocks)
    if paired:
        o_other = swap(hold(order, o_other), 1, size)
        order, o_other = wait(order, o_other)
        mid = width // 2
        o_up, o_left = add(o_own[2:, :, :mid], o_other[2:, :, :mid]), add(
            o_own[1::2, :, mid:], o_other[1::2, :, mid:]
        )
        relay = add(outs[2], passed)
        order, o_up, o_left, relay = wait(order, o_up, o_left, relay)
        o_up, o_left = swap(o_up, 4, size), swap(o_left, 2, size)
    grad_tokens, ext_cols = run_first(
        me, hold(order, back), tokens, extra, ext_grad, res_grad, qkv_pieces, size
    )
    if paired:
        order, ext_cols, back_all, o_up, o_left = wait(order, ext_cols, back_all, o_up, o_left)
        lower = seq // 2
        relay = hold(order, relay)
        far_a = cross(relay[:lower], 2)

        def three(*values):
            return sum(v.astype(F32) for v in values)

        o_second = three(o_own[1, :, :mid], o_other[1, :, :mid], o_up[1]).astype(BF)
        o_third = three(o_own[2, :, mid:], o_other[2, :, mid:], o_left[1]).astype(BF)
        o_first = three(o_own[0, :, :mid], o_other[0, :, :mid], o_up[0])
        o_last = three(o_own[0, :, mid:], o_other[0, :, mid:], o_left[0])
        o_second, o_third = swap(o_second, 2, size), swap(o_third, 4, size)
    parts = run_project(me, low_all, back_all, ext_cols, size)
    if paired:
        order, far_a, o_second, o_third, *parts = wait(order, far_a, o_second, o_third, *parts)
        near = swap(parts[4], 1, size)
        far_b = cross(hold(order, relay)[lower:], 2)
        o_total = jnp.concatenate(
            [three(o_first, o_second).astype(BF), three(o_last, o_third).astype(BF)], axis=1
        )
        o_parts = exchange(o_total)
        order, near = wait(order, near)
        pair = [add(parts[m], near[m]) for m in (1, 2, 3)]
        order, *pair = wait(order, *pair)
        links = [swap(pair[m - 1], 2 * m, size) for m in (1, 2, 3)]
        order, o_parts, far_b, *links = wait(order, o_parts, far_b, *links)
        far_out = jnp.concatenate([far_a, far_b], axis=0)
        outs = [outs[0], near_out, far_out, middle]
        total = exchange(run_join([parts[0], near[0], *links], o_parts, owners))
    else:
        total = lax.psum_scatter(parts[0], "dp", scatter_dimension=0, tiled=False)
        total = exchange(jnp.concatenate([total] * owners, axis=0))
    mixed = res
    for part in outs:
        mixed = mixed + part.astype(F32)
    mixed = mixed.astype(BF)
    if paired:
        total, mixed, *expert_outputs = lax.optimization_barrier((total, mixed, *expert_outputs))
        results = run_finish(total, owners, experts)
        query_total, key_total, value_total, out_total, router_total, gain_one, gain_two = results
        router_total = router_total.T
    else:
        o_total = lax.psum_scatter(o_own, "dp", scatter_dimension=0, tiled=False)
        out_total = lax.psum(o_total, "expert").astype(F32)
        total = total.reshape(owners, slim, -1).astype(F32)
        wide, narrow = QW // owners, KW // owners

        def side_by_side(first, last):
            return jnp.concatenate([total[j, :, first:last] for j in range(owners)], axis=1)

        query_total = side_by_side(0, wide)
        key_total = side_by_side(wide, wide + narrow)
        value_total = side_by_side(wide + narrow, wide + 2 * narrow)
        ext_total = jnp.sum(total[:, :, wide + 2 * narrow :], axis=0)
        router_total = ext_total[:, :experts]
        gain_one, gain_two = ext_total[:, experts_pad], ext_total[:, experts_pad + 8]
    return (
        mixed,
        grad_tokens,
        gain_one,
        query_total,
        key_total,
        value_total,
        out_total,
        gain_two,
        router_total,
        *expert_outputs,
    )


def solution(mesh):
    return jax.shard_map(
        body,
        mesh=mesh,
        in_specs=(
            P(("dp", "expert"), None),
            P(("dp", "expert"), None),
            P(("dp", "expert"), None),
            P("dp"),
            P("dp", None),
            P("dp", None),
            P("dp", None),
            P("dp", None),
            P("dp"),
            P("dp", None),
            P("expert", "dp", None),
            P("expert", "dp", None),
            P("expert", None, "dp"),
            P(("dp", "expert"), None),
        ),
        out_specs=(
            P(("dp", "expert"), None),
            P(("dp", "expert"), None),
            P("dp"),
            P("dp", None),
            P("dp", None),
            P("dp", None),
            P("dp", None),
            P("dp"),
            P("dp", None),
            P("expert", "dp", None),
            P("expert", "dp", None),
            P("expert", None, "dp"),
        ),
        check_vma=False,
    )
```

time: 584 us -> 517 us (0.89)
  blocking collectives: 54.7 us -> 0 us
  Pallas kernels: 161 us -> 144 us
  other arithmetic: 30.7 us -> 20 us
  starting transfers between devices: 57.2 us -> 67.2 us
    all_to_all x2 -> x0, blocking collectives: 54.7 us -> none  [exchange(): lax.all_to_all(value, 'expert', split_axis=0, concat_axis=0, tiled=True)]
    ppermute x8 -> x13, waiting for transfers between devices: 96 us -> 123 us  [along(): return lax.ppermute(value, 'expert', pairs)]
    ppermute x41, waiting for transfers between devices: 95 us -> 75.2 us  [swap(): return lax.ppermute(value, 'dp', [(i, i ^ bit) for i in range(size)])]
    pallas_call x9 -> x10, Pallas kernels: 127 us -> 109 us  [the longest x2 58.5 us: run_experts(): pl.pallas_call(functools.partial(experts_kernel, size, rows, owners, cap,...]
    convert_element_type x9 -> x4, other arithmetic: 16.9 us -> 5.82 us  [add(): return (a.astype(F32) + b.astype(F32)).astype(BF)]
    ppermute x8 -> x13, starting transfers between devices: 17 us -> 26.6 us  [along(): return lax.ppermute(value, 'expert', pairs)]
    all_to_all x3, waiting for transfers between devices: 54.3 us -> 47.5 us  [exchange(): lax.all_to_all(value, 'expert', split_axis=0, concat_axis=0, tiled=True)]
  transfers between devices with their start and end apart: 55 -> 60, of which waited for: 22 -> 24; matrix products, arithmetic and copies ran while one was open for 6% -> 6% of each run, Pallas kernels for 23% -> 28%
where the time goes in v3:
time: 517 us; the launch traced here: 509 us
  waiting for transfers between devices  246 us (48%)
  Pallas kernels  144 us (28%)
  starting transfers between devices  67.2 us (13%)
  other arithmetic  20 us (4%)
  local copies, waits for them, and re-layouts  17.3 us (3%)
  between operations  14.7 us (3%)
    ppermute x13, waiting for transfers between devices, along(): return lax.ppermute(value, 'expert', pairs)  123 us
    ppermute x41, waiting for transfers between devices, swap(): return lax.ppermute(value, 'dp', [(i, i ^ bit) for i in range(size)])  75.2 us
    pallas_call x2, Pallas kernels, run_experts(): pl.pallas_call(functools.partial(experts_kernel, size, rows, owners, cap,...  58.5 us
    all_to_all x3, waiting for transfers between devices, exchange(): lax.all_to_all(value, 'expert', split_axis=0, concat_axis=0, tiled=True)  47.5 us
    ppermute x41, starting transfers between devices, swap(): return lax.ppermute(value, 'dp', [(i, i ^ bit) for i in range(size)])  28.6 us
    ppermute x13, starting transfers between devices, along(): return lax.ppermute(value, 'expert', pairs)  26.6 us
    pallas_call x1, Pallas kernels, run_attention(): pl.pallas_call(functools.partial(attention_kernel, size, rows, plan), nam...  12.4 us
    all_to_all x3, starting transfers between devices, exchange(): lax.all_to_all(value, 'expert', split_axis=0, concat_axis=0, tiled=True)  11.7 us
  transfers between devices with their start and end apart: 60, of which 24 were waited for; matrix products, arithmetic and copies ran while one was open for 6% of the time, Pallas kernels for 28%

profile of v3, /device:TPU:0, one launch (start us, length us, event | category | flops | bytes accessed | tf_op | source)
XLA Modules:
  0.0 509.4 jit_solution(6084929468888735240)
XLA Ops:
  14.9 21.5 %collective-permute-done.rest_1_ = bf16[192,2688]{1,0:T(8,128)(2,1)S(1)} collective-permute-done((bf16[192,2688]{1,0:T(8,128)(2,1)}, bf16[192,2688]{1,0:T(8,128)(2,1)S(1)}, u32[]{:S(2)}, u32[]{:S(2)}) %collective-permute-start) | collective-permute-done | bytes 1032224 | tf_op jit(solution)/shard_map/ppermute | solution.py:52
  40.2 12.0 %collective-permute-done.3.rest_3_ = bf16[96,2688]{1,0:T(8,128)(2,1)S(1)} collective-permute-done((bf16[96,2688]{1,0:T(8,128)(2,1)S(1)}, bf16[96,2688]{1,0:T(8,128)(2,1)S(1)}, u32[]{:S(2)}, u32[]{:S(2)}) %collective-permute-start.3) | collective-permute-done | bytes 516128 | tf_op jit(solution)/shard_map/ppermute | solution.py:52
  56.0 14.3 %collective-permute-done.10.rest_2_.rest_6_ = bf16[192,1536]{1,0:T(8,128)(2,1)S(1)} collective-permute-done((bf16[192,1536]{1,0:T(8,128)(2,1)S(1)}, bf16[192,1536]{1,0:T(8,128)(2,1)S(1)}, u32[]{:S(2)}, u32[]{:S(2)}) %collective-permute-start.10) | collective-permute-done | bytes 589856 | tf_op jit(solution)/shard_map/ppermute | solution.py:52
  76.1 12.4 %attention.1 = (bf16[1536,256]{1,0:T(8,128)(2,1)}, bf16[2560,256]{1,0:T(8,128)(2,1)}, bf16[1536,256]{1,0:T(8,128)(2,1)}, bf16[8,256,768]{2,1,0:T(8,128)(2,1)}, f32[40,1536]{1,0:T(8,128)}) custom-call(s32[1]{0:T(128)} %bitcast.1.me, bf16[256,1536]{1,0:T(8,128)(2,1)} %tok.3, s32[1,256]{1,0:T(1,128)} %seg_row.1, s32[256,1]{1,0:T(8,128)} %copy.30.seg_col, ...), custom_call_target="tpu_custom_call" | custom-call | flops 11000000 | bytes 36000 | tf_op jit(solution)/shard_map/attention/pallas_call | solution.py:219
  92.3 6.6 %residual.1 = (f32[256,1536]{1,0:T(8,128)}, bf16[272,1536]{1,0:T(8,128)(2,1)}) custom-call(s32[1]{0:T(128)} %bitcast.1.me, bf16[256,1536]{1,0:T(8,128)(2,1)} %tok.3, bf16[1536,256]{1,0:T(8,128)(2,1)} %get-tuple-element.214.ctx, f32[40,1536]{1,0:T(8,128)} %get-tuple-element.288.ext, bf16[16,1536]{1,0:T(8,128)(2,1)} %bitcast.69, bf16[192,1536]{1,0:T(8,128)(2,1)} %rest_4_.1, ...), custom_call_target="tpu_custom_call" | custom-call | flops 11000000 | bytes 36000 | tf_op jit(solution)/shard_map/residual/pallas_call | solution.py:258
  98.9 3.4 collective-permute-done.16.rest_6_
  109.6 8.4 %collective-permute-done.17.rest_5_ = bf16[2,3,192,512]{3,2,1,0:T(8,128)(2,1)} collective-permute-done((bf16[2,3,192,512]{3,2,1,0:T(8,128)(2,1)}, bf16[2,3,192,512]{3,2,1,0:T(8,128)(2,1)}, u32[]{:S(2)}, u32[]{:S(2)}) %collective-permute-start.17) | collective-permute-done | bytes 1179680 | tf_op jit(solution)/shard_map/ppermute | solution.py:52
  118.0 26.2 %collective-permute-done.18.rest_2_ = bf16[272,1536]{1,0:T(8,128)(2,1)S(1)} collective-permute-done((bf16[272,1536]{1,0:T(8,128)(2,1)}, bf16[272,1536]{1,0:T(8,128)(2,1)S(1)}, u32[]{:S(2)}, u32[]{:S(2)}) %collective-permute-start.18) | collective-permute-done | bytes 835616 | tf_op jit(solution)/shard_map/ppermute | solution.py:78
  147.0 19.9 %collective-permute-done.21 = bf16[272,1536]{1,0:T(8,128)(2,1)S(1)} collective-permute-done((bf16[272,1536]{1,0:T(8,128)(2,1)S(1)}, bf16[272,1536]{1,0:T(8,128)(2,1)S(1)}, u32[]{:S(2)}, u32[]{:S(2)}) %collective-permute-start.21) | collective-permute-done | bytes 835616 | tf_op jit(solution)/shard_map/ppermute | solution.py:78
  172.5 3.8 router.1
  183.7 24.6 %experts.2 = (bf16[2,512,1536]{2,1,0:T(8,128)(2,1)}, bf16[2,512,1536]{2,1,0:T(8,128)(2,1)}, f32[2,4,256]{2,1,0:T(4,128)}, bf16[8,5,3,192,512]{4,3,2,1,0:T(8,128)(2,1)}) custom-call(s32[1]{0:T(128)} %bitcast.1.me, s32[1]{0:T(128)} %bitcast.11.z, s32[5,4,256]{2,1,0:T(4,128)} %get-tuple-element.274.pos, f32[5,4,256]{2,1,0:T(4,128)} %get-tuple-element.263.p, ...), custom_call_target="tpu_custom_call" | custom-call | flops 11000000 | bytes 36000 | tf_op jit(solution)/shard_map/experts/pallas_call | solution.py:467
  213.1 33.9 %experts.3 = (bf16[3,512,1536]{2,1,0:T(8,128)(2,1)}, bf16[3,512,1536]{2,1,0:T(8,128)(2,1)}, f32[3,4,256]{2,1,0:T(4,128)}, bf16[8,5,3,192,512]{4,3,2,1,0:T(8,128)(2,1)}) custom-call(s32[1]{0:T(128)} %bitcast.1.me, s32[1]{0:T(128)} %bitcast.11.z, s32[5,4,256]{2,1,0:T(4,128)} %get-tuple-element.274.pos, ...), custom_call_target="tpu_custom_call", output_to_operand_aliasing={{3}: (19, {})} | custom-call | flops 11000000 | bytes 36000 | tf_op jit(solution)/shard_map/experts/pallas_call | solution.py:467
  253.9 7.0 %combine_back.3 = (bf16[272,1536]{1,0:T(8,128)(2,1)}, bf16[272,1536]{1,0:T(8,128)(2,1)}, bf16[272,1536]{1,0:T(8,128)(2,1)}) custom-call(s32[1]{0:T(128)} %bitcast.11.z, s32[5,4,256]{2,1,0:T(4,128)} %get-tuple-element.274.pos, bf16[2,512,1536]{2,1,0:T(8,128)(2,1)} %get-tuple-element.262.rest_0_, bf16[3,512,1536]{2,1,0:T(8,128)(2,1)} %get-tuple-element.270.rest_1_, ...), custom_call_target="tpu_custom_call" | custom-call | flops 11000000 | bytes 36000 | tf_op jit(solution)/shard_map/combine_back/pallas_call | solution.py:562
  260.9 9.2 %combine_out.1 = (bf16[256,1536]{1,0:T(8,128)(2,1)}, bf16[256,1536]{1,0:T(8,128)(2,1)}, bf16[256,1536]{1,0:T(8,128)(2,1)}, bf16[256,1536]{1,0:T(8,128)(2,1)}) custom-call(s32[5,4,256]{2,1,0:T(4,128)} %get-tuple-element.274.pos, bf16[2,512,1536]{2,1,0:T(8,128)(2,1)} %get-tuple-element.275.rest_0_, bf16[3,512,1536]{2,1,0:T(8,128)(2,1)} %get-tuple-element.276.rest_1_), custom_call_target="tpu_custom_call" | custom-call | flops 11000000 | bytes 36000 | tf_op jit(solution)/shard_map/combine_out/pallas_call | solution.py:591
  271.6 4.0 collective-permute-start.39
  277.1 34.3 %collective-permute-done.39.rest_1_ = bf16[272,1536]{1,0:T(8,128)(2,1)S(1)} collective-permute-done((bf16[272,1536]{1,0:T(8,128)(2,1)S(1)}, bf16[272,1536]{1,0:T(8,128)(2,1)S(1)}, u32[]{:S(2)}, u32[]{:S(2)}) %collective-permute-start.39) | collective-permute-done | bytes 835616 | tf_op jit(solution)/shard_map/ppermute | solution.py:78
  311.4 3.3 collective-permute-done.38.rest_2_
  314.7 4.8 collective-permute-start.40
  321.1 9.7 %second_back.1 = (f32[256,1536]{1,0:T(8,128)}, bf16[1536,256]{1,0:T(8,128)(2,1)}, f32[40,1536]{1,0:T(8,128)}, bf16[4,192,1536]{2,1,0:T(8,128)(2,1)}, bf16[4,192,1536]{2,1,0:T(8,128)(2,1)}) custom-call(s32[1]{0:T(128)} %bitcast.1.me, f32[24,256]{1,0:T(8,128)} %get-tuple-element.287.own_p, f32[40,1536]{1,0:T(8,128)} %get-tuple-element.288.ext, ...), custom_call_target="tpu_custom_call" | custom-call | flops 11000000 | bytes 36000 | tf_op jit(solution)/shard_map/second_back/pallas_call | solution.py:739
  330.8 8.2 %heads_back.1 = (bf16[2560,256]{1,0:T(8,128)(2,1)}, bf16[1024,640]{1,0:T(8,128)(2,1)}) custom-call(bf16[1536,256]{1,0:T(8,128)(2,1)} %get-tuple-element.294.ctx_grad, bf16[2560,256]{1,0:T(8,128)(2,1)} %get-tuple-element.295.qkv, bf16[8,256,768]{2,1,0:T(8,128)(2,1)} %get-tuple-element.296.probs), custom_call_target="tpu_custom_call" | custom-call | flops 11000000 | bytes 36000 | tf_op jit(solution)/shard_map/heads_back/pallas_call | solution.py:810
  339.0 7.8 %collective-permute-done.40 = bf16[256,1536]{1,0:T(8,128)(2,1)} collective-permute-done((bf16[256,1536]{1,0:T(8,128)(2,1)S(1)}, bf16[256,1536]{1,0:T(8,128)(2,1)}, u32[]{:S(2)}, u32[]{:S(2)}) %collective-permute-start.40) | collective-permute-done | bytes 786464 | tf_op jit(solution)/shard_map/ppermute | solution.py:78
  346.8 4.5 all-to-all-start
  359.0 10.2 %first_back.1 = (f32[256,1536]{1,0:T(8,128)}, bf16[1536,128]{1,0:T(8,128)(2,1)}) custom-call(s32[1]{0:T(128)} %bitcast.1.me, bf16[2560,256]{1,0:T(8,128)(2,1)} %get-tuple-element.313.back, bf16[256,1536]{1,0:T(8,128)(2,1)} %tok.3, f32[40,1536]{1,0:T(8,128)} %get-tuple-element.288.ext, f32[40,1536]{1,0:T(8,128)} %get-tuple-element.314.ext_grad, ...), custom_call_target="tpu_custom_call" | custom-call | flops 65999998976 | bytes 216000000 | tf_op jit(solution)/shard_map/first_back/pallas_call | solution.py:852
  369.2 14.8 %all-to-all-done = bf16[4,256,640]{2,1,0:T(8,128)(2,1)} async-done(((bf16[4,256,640]{2,1,0:T(8,128)(2,1)}), bf16[4,256,640]{2,1,0:T(8,128)(2,1)}, u32[]{:S(2)}, u32[]{:S(2)}) %all-to-all-start) | async-done | bytes 1310752 | tf_op jit(solution)/shard_map/all_to_all | solution.py:96
  391.5 6.4 %project_back.1 = (bf16[192,768]{1,0:T(8,128)(2,1)}, bf16[192,768]{1,0:T(8,128)(2,1)}, bf16[192,768]{1,0:T(8,128)(2,1)}, bf16[192,768]{1,0:T(8,128)(2,1)}, bf16[4,192,768]{2,1,0:T(8,128)(2,1)}) custom-call(s32[1]{0:T(128)} %bitcast.1.me, bf16[4,1536,256]{2,1,0:T(8,128)(2,1)} %bitcast.72, bf16[1024,640]{1,0:T(8,128)(2,1)} %bitcast.13.back_all, ...), custom_call_target="tpu_custom_call" | custom-call | flops 65999998976 | bytes 216000000 | tf_op jit(solution)/shard_map/project_back/pallas_call | solution.py:887
  397.9 4.5 collective-permute-done.47
  404.0 5.2 %collective-permute-done.46 = bf16[128,1536]{1,0:T(8,128)(2,1)} collective-permute-done((bf16[128,1536]{1,0:T(8,128)(2,1)S(1)}, bf16[128,1536]{1,0:T(8,128)(2,1)}, u32[]{:S(2)}, u32[]{:S(2)}) %collective-permute-start.46) | collective-permute-done | bytes 393248 | tf_op jit(solution)/shard_map/ppermute | solution.py:78
  411.8 3.5 all-to-all-start.1
  424.9 24.2 %collective-permute-done.50 = bf16[128,1536]{1,0:T(8,128)(2,1)} collective-permute-done((bf16[128,1536]{1,0:T(8,128)(2,1)S(1)}, bf16[128,1536]{1,0:T(8,128)(2,1)}, u32[]{:S(2)}, u32[]{:S(2)}) %collective-permute-start.50) | collective-permute-done | bytes 393248 | tf_op jit(solution)/shard_map/ppermute | solution.py:78
  453.1 3.7 all-to-all-start.2
  465.4 32.7 %all-to-all-done.2 = bf16[4,192,1152]{2,1,0:T(8,128)(2,1)S(1)} async-done(((bf16[4,192,1152]{2,1,0:T(8,128)(2,1)}), bf16[4,192,1152]{2,1,0:T(8,128)(2,1)S(1)}, u32[]{:S(2)}, u32[]{:S(2)}) %all-to-all-start.2) | async-done | bytes 1769504 | tf_op jit(solution)/shard_map/all_to_all | solution.py:96
  499.4 3.3 finish.1
  (234 shorter events, 106.4 us)
Async XLA Ops:
  7.2 84.3 %all-gather.3.cloned.1.call-start = ((), (), s32[]{:S(2)}) async-start(), calls=%async_computation.4 | async-start | bytes 3932160 | tf_op jit(solution)/shard_map/all_gather | solution.py:935
  7.9 383.6 %all-gather.5.cloned.1.call-start = ((), (), s32[]{:S(2)}) async-start(), calls=%async_computation.5 | async-start | bytes 3932160 | tf_op jit(solution)/shard_map/all_gather | solution.py:992
  10.5 26.0 %collective-permute-start = (bf16[192,2688]{1,0:T(8,128)(2,1)}, bf16[192,2688]{1,0:T(8,128)(2,1)S(1)}, u32[]{:S(2)}, u32[]{:S(2)}) collective-permute-start(bf16[192,2688]{1,0:T(8,128)(2,1)} %pack.1.rest_0_), channel_id=1, source_target_pairs={{0,8},{4,12},{8,0},{12,4},{16,24},{20,28},{24,16},{28,20},{1,9},{5... | collective-permute-start | bytes 3096584 | tf_op jit(solution)/shard_map/ppermute | solution.py:52
  13.4 24.5 %collective-permute-start.1 = (bf16[192,2688]{1,0:T(8,128)(2,1)}, bf16[192,2688]{1,0:T(8,128)(2,1)S(1)}, u32[]{:S(2)}, u32[]{:S(2)}) collective-permute-start(bf16[192,2688]{1,0:T(8,128)(2,1)} %pack.1.rest_0_), channel_id=1, source_target_pairs={{0,16},{4,20},{8,24},{12,28},{16,0},{20,4},{24,8},{28,12},{1,17},{... | collective-permute-start | bytes 3096584 | tf_op jit(solution)/shard_map/ppermute | solution.py:52
  14.9 23.0 %collective-permute-start.2 = (bf16[192,2688]{1,0:T(8,128)(2,1)}, bf16[192,2688]{1,0:T(8,128)(2,1)S(1)}, u32[]{:S(2)}, u32[]{:S(2)}) collective-permute-start(bf16[192,2688]{1,0:T(8,128)(2,1)} %pack.1.rest_0_), channel_id=1, source_target_pairs={{0,4},{4,0},{8,12},{12,8},{16,20},{20,16},{24,28},{28,24},{1,5},{5... | collective-permute-start | bytes 3096584 | tf_op jit(solution)/shard_map/ppermute | solution.py:52
  73.6 28.7 %collective-permute-start.16 = (bf16[2,3,192,512]{3,2,1,0:T(8,128)(2,1)}, bf16[2,3,192,512]{3,2,1,0:T(8,128)(2,1)}, u32[]{:S(2)}, u32[]{:S(2)}) collective-permute-start(bf16[2,3,192,512]{3,2,1,0:T(8,128)(2,1)} %pad_maximum_fusion.2.rest_4_), channel_id=1, source_target_pairs={{0,16},{4,20},{8,24},{12,28},{16,0},{20,4},{24,8},{28,12},{1,17},{... | collective-permute-start | bytes 3538952 | tf_op jit(solution)/shard_map/ppermute | solution.py:52
  88.9 29.2 %collective-permute-start.17 = (bf16[2,3,192,512]{3,2,1,0:T(8,128)(2,1)}, bf16[2,3,192,512]{3,2,1,0:T(8,128)(2,1)}, u32[]{:S(2)}, u32[]{:S(2)}) collective-permute-start(bf16[2,3,192,512]{3,2,1,0:T(8,128)(2,1)} %pad_maximum_fusion.2.rest_4_), channel_id=1, source_target_pairs={{0,8},{4,12},{8,0},{12,4},{16,24},{20,28},{24,16},{28,20},{1,9},{5... | collective-permute-start | bytes 3538952 | tf_op jit(solution)/shard_map/ppermute | solution.py:52
  102.3 64.5 %collective-permute-start.22 = (bf16[3,3,192,512]{3,2,1,0:T(8,128)(2,1)S(1)}, bf16[3,3,192,512]{3,2,1,0:T(8,128)(2,1)S(1)}, u32[]{:S(2)}, u32[]{:S(2)}) collective-permute-start(bf16[3,3,192,512]{3,2,1,0:T(8,128)(2,1)S(1)} %pad_maximum_fusion.rest_4_), channel_id=1, source_target_pairs={{0,16},{4,20},{8,24},{12,28},{16,0},{20,4},{24,8},{28,12},{1,17},{... | collective-permute-start | bytes 5308424 | tf_op jit(solution)/shard_map/ppermute | solution.py:52
  103.9 62.9 %collective-permute-start.23 = (bf16[3,3,192,512]{3,2,1,0:T(8,128)(2,1)S(1)}, bf16[3,3,192,512]{3,2,1,0:T(8,128)(2,1)S(1)}, u32[]{:S(2)}, u32[]{:S(2)}) collective-permute-start(bf16[3,3,192,512]{3,2,1,0:T(8,128)(2,1)S(1)} %pad_maximum_fusion.rest_4_), channel_id=1, source_target_pairs={{0,8},{4,12},{8,0},{12,4},{16,24},{20,28},{24,16},{28,20},{1,9},{5... | collective-permute-start | bytes 5308424 | tf_op jit(solution)/shard_map/ppermute | solution.py:52
  105.4 38.8 %collective-permute-start.18 = (bf16[272,1536]{1,0:T(8,128)(2,1)}, bf16[272,1536]{1,0:T(8,128)(2,1)S(1)}, u32[]{:S(2)}, u32[]{:S(2)}) collective-permute-start(bf16[272,1536]{1,0:T(8,128)(2,1)} %get-tuple-element.227.rest_0_.low_two), channel_id=1, source_target_pairs={{0,2},{1,3},{2,0},{3,1},{4,6},{5,7},{6,4},{7,5},{8,10},{9,11},{10,... | collective-permute-start | bytes 2506760 | tf_op jit(solution)/shard_map/ppermute | solution.py:78
  108.0 36.4 %collective-permute-start.19 = (bf16[272,1536]{1,0:T(8,128)(2,1)}, bf16[272,1536]{1,0:T(8,128)(2,1)S(1)}, u32[]{:S(2)}, u32[]{:S(2)}) collective-permute-start(bf16[272,1536]{1,0:T(8,128)(2,1)} %get-tuple-element.227.rest_0_.low_two), channel_id=1, source_target_pairs={{0,1},{1,0},{2,3},{3,2},{4,5},{5,4},{6,7},{7,6},{8,9},{9,8},{10,11... | collective-permute-start | bytes 2506760 | tf_op jit(solution)/shard_map/ppermute | solution.py:78
  146.4 29.9 %collective-permute-start.24 = (bf16[2,3,192,512]{3,2,1,0:T(8,128)(2,1)}, bf16[2,3,192,512]{3,2,1,0:T(8,128)(2,1)}, u32[]{:S(2)}, u32[]{:S(2)}) collective-permute-start(bf16[2,3,192,512]{3,2,1,0:T(8,128)(2,1)} %collective-permute-done.17.rest_5_), channel_id=1, source_target_pairs={{0,16},{4,20},{8,24},{12,28},{16,0},{20,4},{24,8},{28,12},{1,17},{... | collective-permute-start | bytes 3538952 | tf_op jit(solution)/shard_map/ppermute | solution.py:52
  170.1 290.0 %reduce-scatter.2.cloned.1.call-start = ((), (), s32[]{:S(2)}) async-start(), calls=%async_computation.6 | async-start | bytes 26542080 | tf_op jit(solution)/shard_map/reduce_scatter | solution.py:1026
  176.5 31.9 %collective-permute-start.32 = (bf16[3,3,192,512]{3,2,1,0:T(8,128)(2,1)S(1)}, bf16[3,3,192,512]{3,2,1,0:T(8,128)(2,1)S(1)}, u32[]{:S(2)}, u32[]{:S(2)}) collective-permute-start(bf16[3,3,192,512]{3,2,1,0:T(8,128)(2,1)S(1)} %copy-done.8), channel_id=1, source_target_pairs={{0,4},{4,0},{8,12},{12,8},{16,20},{20,16},{24,28},{28,24},{1,5},{5... | collective-permute-start | bytes 5308424 | tf_op jit(solution)/shard_map/ppermute | solution.py:52
  176.9 31.4 %collective-permute-start.33 = (bf16[3,3,192,512]{3,2,1,0:T(8,128)(2,1)S(1)}, bf16[3,3,192,512]{3,2,1,0:T(8,128)(2,1)}, u32[]{:S(2)}, u32[]{:S(2)}) collective-permute-start(bf16[3,3,192,512]{3,2,1,0:T(8,128)(2,1)S(1)} %copy-done.6), channel_id=1, source_target_pairs={{0,4},{4,0},{8,12},{12,8},{16,20},{20,16},{24,28},{28,24},{1,5},{5... | collective-permute-start | bytes 5308424 | tf_op jit(solution)/shard_map/ppermute | solution.py:52
  180.3 28.1 %collective-permute-start.31 = (bf16[3,3,192,512]{3,2,1,0:T(8,128)(2,1)S(1)}, bf16[3,3,192,512]{3,2,1,0:T(8,128)(2,1)}, u32[]{:S(2)}, u32[]{:S(2)}) collective-permute-start(bf16[3,3,192,512]{3,2,1,0:T(8,128)(2,1)S(1)} %pad_maximum_fusion.rest_4_), channel_id=1, source_target_pairs={{0,4},{4,0},{8,12},{12,8},{16,20},{20,16},{24,28},{28,24},{1,5},{5... | collective-permute-start | bytes 5308424 | tf_op jit(solution)/shard_map/ppermute | solution.py:52
  182.6 25.7 %collective-permute-start.29 = (bf16[3,3,96,512]{3,2,1,0:T(8,128)(2,1)}, bf16[3,3,96,512]{3,2,1,0:T(8,128)(2,1)}, u32[]{:S(2)}, u32[]{:S(2)}) collective-permute-start(bf16[3,3,96,512]{3,2,1,0:T(8,128)(2,1)} %slice.97), channel_id=1, source_target_pairs={{0,16},{4,20},{8,24},{12,28},{16,0},{20,4},{24,8},{28,12},{1,17},{... | collective-permute-start | bytes 2654216 | tf_op jit(solution)/shard_map/ppermute | solution.py:52
  183.1 25.2 %collective-permute-start.30 = (bf16[3,3,96,512]{3,2,1,0:T(8,128)(2,1)}, bf16[3,3,96,512]{3,2,1,0:T(8,128)(2,1)S(1)}, u32[]{:S(2)}, u32[]{:S(2)}) collective-permute-start(bf16[3,3,96,512]{3,2,1,0:T(8,128)(2,1)} %slice.98), channel_id=1, source_target_pairs={{0,8},{4,12},{8,0},{12,4},{16,24},{20,28},{24,16},{28,20},{1,9},{5... | collective-permute-start | bytes 2654216 | tf_op jit(solution)/shard_map/ppermute | solution.py:52
  271.6 39.8 %collective-permute-start.39 = (bf16[272,1536]{1,0:T(8,128)(2,1)S(1)}, bf16[272,1536]{1,0:T(8,128)(2,1)S(1)}, u32[]{:S(2)}, u32[]{:S(2)}) collective-permute-start(bf16[272,1536]{1,0:T(8,128)(2,1)S(1)} %copy-done.49), channel_id=1, source_target_pairs={{0,1},{1,0},{2,3},{3,2},{4,5},{5,4},{6,7},{7,6},{8,9},{9,8},{10,11... | collective-permute-start | bytes 2506760 | tf_op jit(solution)/shard_map/ppermute | solution.py:78
  275.8 38.9 %collective-permute-start.38 = (bf16[272,1536]{1,0:T(8,128)(2,1)S(1)}, bf16[272,1536]{1,0:T(8,128)(2,1)S(1)}, u32[]{:S(2)}, u32[]{:S(2)}) collective-permute-start(bf16[272,1536]{1,0:T(8,128)(2,1)S(1)} %add_convert_fusion), channel_id=1, source_target_pairs={{0,2},{1,3},{2,0},{3,1},{4,6},{5,7},{6,4},{7,5},{8,10},{9,11},{10,... | collective-permute-start | bytes 2506760 | tf_op jit(solution)/shard_map/ppermute | solution.py:78
  314.7 24.3 %collective-permute-start.42 = (bf16[256,1536]{1,0:T(8,128)(2,1)S(1)}, bf16[256,1536]{1,0:T(8,128)(2,1)}, u32[]{:S(2)}, u32[]{:S(2)}) collective-permute-start(bf16[256,1536]{1,0:T(8,128)(2,1)S(1)} %copy-done.51), channel_id=1, source_target_pairs={{0,1},{1,0},{2,3},{3,2},{4,5},{5,4},{6,7},{7,6},{8,9},{9,8},{10,11... | collective-permute-start | bytes 2359304 | tf_op jit(solution)/shard_map/ppermute | solution.py:78
  314.7 32.1 %collective-permute-start.40 = (bf16[256,1536]{1,0:T(8,128)(2,1)S(1)}, bf16[256,1536]{1,0:T(8,128)(2,1)}, u32[]{:S(2)}, u32[]{:S(2)}) collective-permute-start(bf16[256,1536]{1,0:T(8,128)(2,1)S(1)} %copy-done.50), channel_id=1, source_target_pairs={{3,2},{0,1},{7,6},{4,5},{11,10},{8,9},{15,14},{12,13},{19,18},{16,... | collective-permute-start | bytes 2359304 | tf_op jit(solution)/shard_map/ppermute | solution.py:78
  319.6 27.2 %collective-permute-start.41 = (bf16[256,1536]{1,0:T(8,128)(2,1)S(1)}, bf16[256,1536]{1,0:T(8,128)(2,1)}, u32[]{:S(2)}, u32[]{:S(2)}) collective-permute-start(bf16[256,1536]{1,0:T(8,128)(2,1)S(1)} %copy-done.50), channel_id=1, source_target_pairs={{1,2},{2,1},{5,6},{6,5},{9,10},{10,9},{13,14},{14,13},{17,18},{18,... | collective-permute-start | bytes 2359304 | tf_op jit(solution)/shard_map/ppermute | solution.py:78
  346.8 37.2 %all-to-all-start = ((bf16[4,256,640]{2,1,0:T(8,128)(2,1)}), bf16[4,256,640]{2,1,0:T(8,128)(2,1)}, u32[]{:S(2)}, u32[]{:S(2)}) async-start(bf16[4,256,640]{2,1,0:T(8,128)(2,1)} %bitcast.68), calls=%async_computation | async-start | bytes 2621440 | tf_op jit(solution)/shard_map/all_to_all | solution.py:96
  356.1 27.9 %collective-permute-start.44 = (bf16[2,192,768]{2,1,0:T(8,128)(2,1)}, bf16[2,192,768]{2,1,0:T(8,128)(2,1)}, u32[]{:S(2)}, u32[]{:S(2)}) collective-permute-start(bf16[2,192,768]{2,1,0:T(8,128)(2,1)} %get-tuple-element.318), channel_id=1, source_target_pairs={{0,16},{4,20},{8,24},{12,28},{16,0},{20,4},{24,8},{28,12},{1,17},{... | collective-permute-start | bytes 1769480 | tf_op jit(solution)/shard_map/ppermute | solution.py:52
  357.6 26.4 %collective-permute-start.45 = (bf16[2,192,768]{2,1,0:T(8,128)(2,1)}, bf16[2,192,768]{2,1,0:T(8,128)(2,1)}, u32[]{:S(2)}, u32[]{:S(2)}) collective-permute-start(bf16[2,192,768]{2,1,0:T(8,128)(2,1)} %get-tuple-element.319), channel_id=1, source_target_pairs={{0,8},{4,12},{8,0},{12,4},{16,24},{20,28},{24,16},{28,20},{1,9},{5... | collective-permute-start | bytes 1769480 | tf_op jit(solution)/shard_map/ppermute | solution.py:52
  411.8 37.2 %all-to-all-start.1 = ((bf16[4,48,1536]{2,1,0:T(8,128)(2,1)}), bf16[4,48,1536]{2,1,0:T(8,128)(2,1)S(1)}, u32[]{:S(2)}, u32[]{:S(2)}) async-start(bf16[4,48,1536]{2,1,0:T(8,128)(2,1)} %bitcast.20), calls=%async_computation.1 | async-start | bytes 1179648 | tf_op jit(solution)/shard_map/all_to_all | solution.py:96
  415.3 33.7 %collective-permute-start.50 = (bf16[128,1536]{1,0:T(8,128)(2,1)S(1)}, bf16[128,1536]{1,0:T(8,128)(2,1)}, u32[]{:S(2)}, u32[]{:S(2)}) collective-permute-start(bf16[128,1536]{1,0:T(8,128)(2,1)S(1)} %slice.117), channel_id=1, source_target_pairs={{0,2},{1,3},{2,0},{3,1},{4,6},{5,7},{6,4},{7,5},{8,10},{9,11},{10,... | collective-permute-start | bytes 1179656 | tf_op jit(solution)/shard_map/ppermute | solution.py:78
  419.6 29.4 %collective-permute-start.51 = (bf16[192,768]{1,0:T(8,128)(2,1)S(1)}, bf16[192,768]{1,0:T(8,128)(2,1)S(1)}, u32[]{:S(2)}, u32[]{:S(2)}) collective-permute-start(bf16[192,768]{1,0:T(8,128)(2,1)S(1)} %get-tuple-element.344), channel_id=1, source_target_pairs={{0,8},{4,12},{8,0},{12,4},{16,24},{20,28},{24,16},{28,20},{1,9},{5... | collective-permute-start | bytes 884744 | tf_op jit(solution)/shard_map/ppermute | solution.py:52
  420.0 29.0 %collective-permute-start.52 = (bf16[192,768]{1,0:T(8,128)(2,1)S(1)}, bf16[192,768]{1,0:T(8,128)(2,1)S(1)}, u32[]{:S(2)}, u32[]{:S(2)}) collective-permute-start(bf16[192,768]{1,0:T(8,128)(2,1)S(1)} %get-tuple-element.345), channel_id=1, source_target_pairs={{0,16},{4,20},{8,24},{12,28},{16,0},{20,4},{24,8},{28,12},{1,17},{... | collective-permute-start | bytes 884744 | tf_op jit(solution)/shard_map/ppermute | solution.py:52
  420.8 28.3 %collective-permute-start.53 = (bf16[192,768]{1,0:T(8,128)(2,1)S(1)}, bf16[192,768]{1,0:T(8,128)(2,1)S(1)}, u32[]{:S(2)}, u32[]{:S(2)}) collective-permute-start(bf16[192,768]{1,0:T(8,128)(2,1)S(1)} %get-tuple-element.346), channel_id=1, source_target_pairs={{0,24},{4,28},{8,16},{12,20},{16,8},{20,12},{24,0},{28,4},{1,25},{... | collective-permute-start | bytes 884744 | tf_op jit(solution)/shard_map/ppermute | solution.py:52
  453.1 45.0 %all-to-all-start.2 = ((bf16[4,192,1152]{2,1,0:T(8,128)(2,1)}), bf16[4,192,1152]{2,1,0:T(8,128)(2,1)S(1)}, u32[]{:S(2)}, u32[]{:S(2)}) async-start(bf16[4,192,1152]{2,1,0:T(8,128)(2,1)} %bitcast.60), calls=%async_computation.2 | async-start | bytes 3538944 | tf_op jit(solution)/shard_map/all_to_all | solution.py:96
  (80 other events, 1191.8 us)
Sparse Core Ops, SparseCore 0:
  9.6 66.1 all-gather.2
  170.2 63.1 all-gather.4
  247.1 165.6 reduce-scatter.1

commit v4 on v3

--- a/solution.py
+++ b/solution.py
@@ -274,8 +274,21 @@
 
 
 def router_kernel(owners, per, z, ext, *rest):
-    rows, rest = rest[:owners], rest[owners:]
-    pos_out, p_out, own_out, all_p, all_pos = rest
+    given, rest = rest[:-6], rest[-6:]
+    pos_out, p_out, own_out, last_out, all_p, all_pos = rest
+    if len(given) > owners:
+        inner = (z[0] == 1) | (z[0] == 2)
+
+        @pl.when(inner)
+        def _():
+            last_out[...] = given[owners - 1][...]
+
+        @pl.when(jnp.logical_not(inner))
+        def _():
+            last_out[...] = given[owners][...]
+    else:
+        last_out[...] = given[owners - 1][...]
+    rows = list(given[: owners - 1]) + [last_out]
     experts_pad = ext.shape[0] - 16
     seq, width = rows[0].shape[0] - EXTRA, rows[0].shape[1]
     router = ext[:experts_pad, :].astype(BF)
@@ -300,8 +313,7 @@
             pos_out[l, r : r + 1, :] = all_pos[pl.ds(at + l, 1), :].astype(jnp.int32)
 
 
-def run_router(z, ext, rows, per):
-    owners = len(rows)
+def run_router(z, ext, rows, per, owners):
     seq = rows[0].shape[0] - EXTRA
     experts_pad = ext.shape[0] - 16
     return pl.pallas_call(
@@ -311,9 +323,10 @@
             sds((per, owners, seq), jnp.int32),
             sds((per, owners, seq), F32),
             sds((experts_pad, seq), F32),
+            sds(rows[0].shape, BF),
         ],
-        in_specs=[SMEM, VMEM] + [VMEM] * owners,
-        out_specs=[VMEM] * 3,
+        in_specs=[SMEM, VMEM] + [VMEM] * len(rows),
+        out_specs=[VMEM] * 4,
         scratch_shapes=[pltpu.VMEM((experts_pad, seq), F32)] * 2,
         compiler_params=params(),
         cost_estimate=cost(0.01),
@@ -330,20 +343,22 @@
     for c in copies:
         c.start()
 
-    def wait():
-        for c in copies:
-            c.wait()
+    def wait(r):
+        copies[2 * r].wait()
+        copies[2 * r + 1].wait()
 
     return wait
 
 
-def pick_rows(owners, cap, number, pos, p, xv, cv, xr, cr, prow):
+def pick_rows(owners, cap, number, pos, p, xv, cv, xr, cr, prow, wait_rows):
     seq = xv.shape[1]
     slot = lax.broadcasted_iota(jnp.int32, (cap, seq), 0)
     for r in range(owners):
         hot = pos[number, r : r + 1, :] == slot
         low_hot = jnp.where(hot, 1.0, 0.0).astype(BF)
         at = pl.ds(r * cap, cap)
+        if wait_rows is not None:
+            wait_rows(r)
         xr[at, :] = dot(low_hot, xv[r]).astype(BF)
         cr[at, :] = dot(low_hot, cv[r]).astype(BF)
         prow[at, :] = jnp.sum(jnp.where(hot, p[number, r : r + 1, :], 0.0), axis=1, keepdims=True)
@@ -428,9 +443,9 @@
     for i in range(many):
         here = i % 2
         number = first + i
-        if i == 0:
-            wait_rows()
-        pick_rows(owners, cap, number, pos, p, xv, cv, xr, cr, prow)
+        pick_rows(
+            owners, cap, number, pos, p, xv, cv, xr, cr, prow, wait_rows if i == 0 else None
+        )
         for c in coming:
             c.wait()
         if i + 1 < many:
@@ -614,11 +629,9 @@
         summed = summed + parts[r * low : (r + 1) * low, :].astype(F32)
     summed = summed.astype(BF)
     wide = summed.shape[1] // owners
-    for r in range(owners):
-        out[r * rows : (r + 1) * rows, :cols] = total
-        for k in range(owners):
-            at = r * rows + k * low
-            out[at : at + low, cols:] = summed[:, k * wide : (k + 1) * wide]
+    out[:, :cols] = total
+    for k in range(owners):
+        out[k * low : (k + 1) * low, cols:] = summed[:, k * wide : (k + 1) * wide]
 
 
 def run_join(pieces, parts, owners):
@@ -626,7 +639,7 @@
     return pl.pallas_call(
         functools.partial(join_kernel, owners),
         name="join",
-        out_shape=sds((owners * rows, cols + parts.shape[1] // owners), BF),
+        out_shape=sds((rows, cols + parts.shape[1] // owners), BF),
         in_specs=[VMEM] * (len(pieces) + 1),
         out_specs=VMEM,
         compiler_params=params(),
@@ -634,20 +647,34 @@
     )(*pieces, parts)
 
 
-def finish_kernel(owners, total, query, key, value, out, router, gain_one, gain_two):
+def finish_kernel(owners, z, *rest):
+    given, (query, key, value, out, router, gain_one, gain_two, last) = rest[:-8], rest[-8:]
     rows = query.shape[0]
     wide, narrow = QW // owners, KW // owners
     one = wide + 2 * narrow
     low, out_wide = rows // owners, out.shape[1] // owners
+    inner = (z[0] == 1) | (z[0] == 2)
+
+    @pl.when(inner)
+    def _():
+        last[...] = given[3][...]
+
+    @pl.when(jnp.logical_not(inner))
+    def _():
+        last[...] = given[4][...]
+
     ext_sum = 0.0
-    for j in range(owners):
-        block = total[j * rows : (j + 1) * rows, :].astype(F32)
-        query[:, j * wide : (j + 1) * wide] = block[:, :wide]
-        key[:, j * narrow : (j + 1) * narrow] = block[:, wide : wide + narrow]
-        value[:, j * narrow : (j + 1) * narrow] = block[:, wide + narrow : one]
+    for r, ref in enumerate((given[0], given[1], given[2], last)):
+        j = jnp.bitwise_xor(z[0], r)
+        block = ref[...].astype(F32)
+        query[:, pl.ds(pl.multiple_of(j * wide, wide), wide)] = block[:, :wide]
+        slim = pl.ds(pl.multiple_of(j * narrow, narrow), narrow)
+        key[:, slim] = block[:, wide : wide + narrow]
+        value[:, slim] = block[:, wide + narrow : one]
         ext_sum = ext_sum + block[:, one : one + EXT]
+        to = pl.ds(pl.multiple_of(j * low, low), low)
         for k in range(owners):
-            out[j * low : (j + 1) * low, k * out_wide : (k + 1) * out_wide] = block[
+            out[to, k * out_wide : (k + 1) * out_wide] = block[
                 k * low : (k + 1) * low, one + EXT :
             ]
     ext_sum = ext_sum.T
@@ -658,9 +685,9 @@
     gain_two[...] = ext_sum[pad + 8, :]
 
 
-def run_finish(total, owners, experts):
-    rows = total.shape[0] // owners
-    width = (total.shape[1] - EXT - (QW + 2 * KW) // owners) * owners
+def run_finish(z, given, owners, experts):
+    rows, cols = given[0].shape
+    width = (cols - EXT - (QW + 2 * KW) // owners) * owners
     return pl.pallas_call(
         functools.partial(finish_kernel, owners),
         name="finish",
@@ -673,11 +700,12 @@
             sds((rows,), F32),
             sds((rows,), F32),
         ],
-        in_specs=[VMEM],
+        in_specs=[SMEM] + [VMEM] * len(given),
         out_specs=[VMEM] * 7,
+        scratch_shapes=[pltpu.VMEM((rows, cols), BF)],
         compiler_params=params(),
         cost_estimate=cost(0.01),
-    )(total)
+    )(z, *given)
 
 
 def second_kernel(
@@ -987,12 +1015,12 @@
         middle = along(hold(order, low_two), [(1, 2), (2, 1)])
         passed = along(far, [(2, 3), (1, 0)])
         order, middle, passed, by, bx = wait(order, middle, passed, by, bx)
-        inner = (z[0] == 1) | (z[0] == 2)
-        xs = [low_two, near, far, jnp.where(inner, middle, passed)]
+        xs = [low_two, near, far, middle, passed]
         low_all = lax.all_gather(hold(order, low_one), "expert", axis=0, tiled=True)
         ba, bb = swap(bx[..., :half, :], 4, size), swap(by[..., half:, :], 2, size)
         a1, a3, a5 = (swap(hold(order, v), 1, size) for v in (a_shard, ax, ay))
-        pos, p, own_p = run_router(z, hold(order, extra), xs, per)
+        pos, p, own_p, xs[3] = run_router(z, hold(order, extra), xs, per, owners)
+        xs = xs[:owners]
         order, p, ac, a1, a3, a5 = wait(order, p, ac, a1, a3, a5)
         a7, b3, b5 = swap(ac, 1, size), swap(hold(order, bx), 1, size), swap(hold(order, by), 1, size)
         order, a7 = wait(order, a7)
@@ -1008,7 +1036,7 @@
         res, low_two = run_residual(me, tokens, ctx, extra, place, out_pieces, size)
         xs = plain_owners(low_two, owners)
         low_all = lax.all_gather(low_one, "expert", axis=0, tiled=True)
-        pos, p, own_p = run_router(z, extra, xs, per)
+        pos, p, own_p, _ = run_router(z, extra, xs, per, owners)
         order = p
     low_all = low_all.reshape(owners, width, seq)
 
@@ -1048,7 +1076,6 @@
         backs = [backs[0], near, far, middle]
         last_out = hold(order, outs[3])
         passed, middle = along(last_out, [(3, 2), (0, 1)]), along(last_out, [(1, 2), (2, 1)])
-        near_out = cross(hold(order, outs[1]), 1)
     else:
         outs = run_combine_out(pos, out_rows, cap)
         backs = plain_return(backs, owners)
@@ -1059,9 +1086,7 @@
     )
     back, blocks = run_heads(ctx_grad, qkv, probs, owners)
     if paired:
-        order, blocks, back, passed, middle, near_out = wait(
-            order, blocks, back, passed, middle, near_out
-        )
+        order, blocks, back, passed, middle = wait(order, blocks, back, passed, middle)
     back_all = exchange(blocks)
     if paired:
         o_other = swap(hold(order, o_other), 1, size)
@@ -1077,10 +1102,7 @@
         me, hold(order, back), tokens, extra, ext_grad, res_grad, qkv_pieces, size
     )
     if paired:
-        order, ext_cols, back_all, o_up, o_left = wait(order, ext_cols, back_all, o_up, o_left)
-        lower = seq // 2
-        relay = hold(order, relay)
-        far_a = cross(relay[:lower], 2)
+        order, ext_cols, o_up, o_left = wait(order, ext_cols, o_up, o_left)
 
         def three(*values):
             return sum(v.astype(F32) for v in values)
@@ -1089,24 +1111,31 @@
         o_third = three(o_own[2, :, mid:], o_other[2, :, mid:], o_left[1]).astype(BF)
         o_first = three(o_own[0, :, :mid], o_other[0, :, :mid], o_up[0])
         o_last = three(o_own[0, :, mid:], o_other[0, :, mid:], o_left[0])
+        order, back_all, o_second, o_third, o_first, o_last = wait(
+            order, back_all, o_second, o_third, o_first, o_last
+        )
         o_second, o_third = swap(o_second, 2, size), swap(o_third, 4, size)
+        far_out, near_out = cross(hold(order, relay), 2), cross(hold(order, outs[1]), 1)
     parts = run_project(me, low_all, back_all, ext_cols, size)
     if paired:
-        order, far_a, o_second, o_third, *parts = wait(order, far_a, o_second, o_third, *parts)
         near = swap(parts[4], 1, size)
-        far_b = cross(hold(order, relay)[lower:], 2)
+        order, near = wait(order, near)
+        pair = [add(parts[m], near[m]) for m in (1, 2, 3)]
+        order, o_second, o_third, *pair = wait(order, o_second, o_third, *pair)
+        links = [swap(pair[m - 1], 2 * m, size) for m in (1, 2, 3)]
         o_total = jnp.concatenate(
             [three(o_first, o_second).astype(BF), three(o_last, o_third).astype(BF)], axis=1
         )
         o_parts = exchange(o_total)
-        order, near = wait(order, near)
-        pair = [add(parts[m], near[m]) for m in (1, 2, 3)]
-        order, *pair = wait(order, *pair)
-        links = [swap(pair[m - 1], 2 * m, size) for m in (1, 2, 3)]
-        order, o_parts, far_b, *links = wait(order, o_parts, far_b, *links)
-        far_out = jnp.concatenate([far_a, far_b], axis=0)
+        order, far_out, near_out = wait(order, far_out, near_out)
+        order, o_parts, *links = wait(order, o_parts, *links)
         outs = [outs[0], near_out, far_out, middle]
-        total = exchange(run_join([parts[0], near[0], *links], o_parts, owners))
+        total = run_join([parts[0], near[0], *links], o_parts, owners)
+        far, near = cross(total, 2), cross(total, 1)
+        order, far, near = wait(order, far, near)
+        middle_total = along(hold(order, total), [(1, 2), (2, 1)])
+        passed_total = along(far, [(2, 3), (1, 0)])
+        total = [total, near, far, middle_total, passed_total]
     else:
         total = lax.psum_scatter(parts[0], "dp", scatter_dimension=0, tiled=False)
         total = exchange(jnp.concatenate([total] * owners, axis=0))
@@ -1115,8 +1144,8 @@
         mixed = mixed + part.astype(F32)
     mixed = mixed.astype(BF)
     if paired:
-        total, mixed, *expert_outputs = lax.optimization_barrier((total, mixed, *expert_outputs))
-        results = run_finish(total, owners, experts)
+        last, mixed, *expert_outputs = wait(total[4], mixed, *expert_outputs)
+        results = run_finish(z, [*total[:4], last], owners, experts)
         query_total, key_total, value_total, out_total, router_total, gain_one, gain_two = results
         router_total = router_total.T
     else:

time: 517 us -> 491 us (0.950)
  waiting for transfers between devices: 246 us -> 229 us
  other arithmetic: 20 us -> 14.8 us
    all_to_all x3 -> x2, waiting for transfers between devices: 47.5 us -> 13.4 us  [exchange(): lax.all_to_all(value, 'expert', split_axis=0, concat_axis=0, tiled=True)]
    ppermute x41, waiting for transfers between devices: 75.2 us -> 88 us  [swap(): return lax.ppermute(value, 'dp', [(i, i ^ bit) for i in range(size)])]
    ppermute x13 -> x16, waiting for transfers between devices: 123 us -> 127 us  [along(): return lax.ppermute(value, 'expert', pairs)]
    all_to_all x3 -> x2, starting transfers between devices: 11.7 us -> 8.07 us  [exchange(): lax.all_to_all(value, 'expert', split_axis=0, concat_axis=0, tiled=True)]
    ppermute x13 -> x16, starting transfers between devices: 26.6 us -> 26.7 us  [along(): return lax.ppermute(value, 'expert', pairs)]
  transfers between devices with their start and end apart: 60 -> 62, of which waited for: 24 -> 28; matrix products, arithmetic and copies ran while one was open for 6% -> 5% of each run, Pallas kernels for 28% -> 29%
where the time goes in v4:
time: 491 us; the launch traced here: 483 us
  waiting for transfers between devices  229 us (47%)
  Pallas kernels  143 us (29%)
  starting transfers between devices  63.4 us (13%)
  local copies, waits for them, and re-layouts  18.1 us (4%)
  between operations  14.9 us (3%)
  other arithmetic  14.8 us (3%)
    ppermute x16, waiting for transfers between devices, along(): return lax.ppermute(value, 'expert', pairs)  127 us
    ppermute x41, waiting for transfers between devices, swap(): return lax.ppermute(value, 'dp', [(i, i ^ bit) for i in range(size)])  88 us
    pallas_call x2, Pallas kernels, run_experts(): pl.pallas_call(functools.partial(experts_kernel, size, rows, owners, cap,...  57.2 us
    ppermute x41, starting transfers between devices, swap(): return lax.ppermute(value, 'dp', [(i, i ^ bit) for i in range(size)])  28.5 us
    ppermute x16, starting transfers between devices, along(): return lax.ppermute(value, 'expert', pairs)  26.7 us
    all_to_all x2, waiting for transfers between devices, exchange(): lax.all_to_all(value, 'expert', split_axis=0, concat_axis=0, tiled=True)  13.4 us
    pallas_call x1, Pallas kernels, run_attention(): pl.pallas_call(functools.partial(attention_kernel, size, rows, plan), nam...  12.4 us
    pallas_call x2, Pallas kernels, run_combine_back(): pl.pallas_call(functools.partial(combine_back_kernel, start, owners, per,...  10.3 us
  transfers between devices with their start and end apart: 62, of which 28 were waited for; matrix products, arithmetic and copies ran while one was open for 5% of the time, Pallas kernels for 29%

profile of v4, /device:TPU:0, one launch (start us, length us, event | category | flops | bytes accessed | tf_op | source)
XLA Modules:
  0.0 482.8 jit_solution(10858925993827541633)
XLA Ops:
  15.0 21.5 %collective-permute-done.rest_1_ = bf16[192,2688]{1,0:T(8,128)(2,1)S(1)} collective-permute-done((bf16[192,2688]{1,0:T(8,128)(2,1)}, bf16[192,2688]{1,0:T(8,128)(2,1)S(1)}, u32[]{:S(2)}, u32[]{:S(2)}) %collective-permute-start) | collective-permute-done | bytes 1032224 | tf_op jit(solution)/shard_map/ppermute | solution.py:52
  40.3 12.0 %collective-permute-done.3.rest_3_ = bf16[96,2688]{1,0:T(8,128)(2,1)S(1)} collective-permute-done((bf16[96,2688]{1,0:T(8,128)(2,1)S(1)}, bf16[96,2688]{1,0:T(8,128)(2,1)S(1)}, u32[]{:S(2)}, u32[]{:S(2)}) %collective-permute-start.3) | collective-permute-done | bytes 516128 | tf_op jit(solution)/shard_map/ppermute | solution.py:52
  56.0 14.3 %collective-permute-done.10.rest_2_.rest_6_ = bf16[192,1536]{1,0:T(8,128)(2,1)S(1)} collective-permute-done((bf16[192,1536]{1,0:T(8,128)(2,1)S(1)}, bf16[192,1536]{1,0:T(8,128)(2,1)S(1)}, u32[]{:S(2)}, u32[]{:S(2)}) %collective-permute-start.10) | collective-permute-done | bytes 589856 | tf_op jit(solution)/shard_map/ppermute | solution.py:52
  76.1 12.4 %attention.1 = (bf16[1536,256]{1,0:T(8,128)(2,1)}, bf16[2560,256]{1,0:T(8,128)(2,1)}, bf16[1536,256]{1,0:T(8,128)(2,1)}, bf16[8,256,768]{2,1,0:T(8,128)(2,1)}, f32[40,1536]{1,0:T(8,128)}) custom-call(s32[1]{0:T(128)} %bitcast.me, bf16[256,1536]{1,0:T(8,128)(2,1)} %tok.3, s32[1,256]{1,0:T(1,128)} %seg_row.1, s32[256,1]{1,0:T(8,128)} %copy.30.seg_col, ...), custom_call_target="tpu_custom_call" | custom-call | flops 11000000 | bytes 36000 | tf_op jit(solution)/shard_map/attention/pallas_call | solution.py:219
  92.4 6.6 %residual.1 = (f32[256,1536]{1,0:T(8,128)}, bf16[272,1536]{1,0:T(8,128)(2,1)}) custom-call(s32[1]{0:T(128)} %bitcast.me, bf16[256,1536]{1,0:T(8,128)(2,1)} %tok.3, bf16[1536,256]{1,0:T(8,128)(2,1)} %get-tuple-element.214.ctx, f32[40,1536]{1,0:T(8,128)} %get-tuple-element.291.ext, bf16[16,1536]{1,0:T(8,128)(2,1)} %bitcast.61, bf16[192,1536]{1,0:T(8,128)(2,1)} %rest_4_.1, ...), custom_call_target="tpu_custom_call" | custom-call | flops 11000000 | bytes 36000 | tf_op jit(solution)/shard_map/residual/pallas_call | solution.py:258
  99.0 3.4 collective-permute-done.16.rest_6_
  109.6 8.4 %collective-permute-done.17.rest_5_ = bf16[2,3,192,512]{3,2,1,0:T(8,128)(2,1)} collective-permute-done((bf16[2,3,192,512]{3,2,1,0:T(8,128)(2,1)}, bf16[2,3,192,512]{3,2,1,0:T(8,128)(2,1)}, u32[]{:S(2)}, u32[]{:S(2)}) %collective-permute-start.17) | collective-permute-done | bytes 1179680 | tf_op jit(solution)/shard_map/ppermute | solution.py:52
  118.1 26.2 %collective-permute-done.18.rest_2_ = bf16[272,1536]{1,0:T(8,128)(2,1)S(1)} collective-permute-done((bf16[272,1536]{1,0:T(8,128)(2,1)}, bf16[272,1536]{1,0:T(8,128)(2,1)S(1)}, u32[]{:S(2)}, u32[]{:S(2)}) %collective-permute-start.18) | collective-permute-done | bytes 835616 | tf_op jit(solution)/shard_map/ppermute | solution.py:78
  147.0 19.9 %collective-permute-done.21.rest_4_ = bf16[272,1536]{1,0:T(8,128)(2,1)S(1)} collective-permute-done((bf16[272,1536]{1,0:T(8,128)(2,1)S(1)}, bf16[272,1536]{1,0:T(8,128)(2,1)S(1)}, u32[]{:S(2)}, u32[]{:S(2)}) %collective-permute-start.21) | collective-permute-done | bytes 835616 | tf_op jit(solution)/shard_map/ppermute | solution.py:78
  170.2 4.3 router.1
  181.7 24.0 %experts.2 = (bf16[2,512,1536]{2,1,0:T(8,128)(2,1)}, bf16[2,512,1536]{2,1,0:T(8,128)(2,1)}, f32[2,4,256]{2,1,0:T(4,128)}, bf16[8,5,3,192,512]{4,3,2,1,0:T(8,128)(2,1)}) custom-call(s32[1]{0:T(128)} %bitcast.me, s32[1]{0:T(128)} %bitcast.12.z, s32[5,4,256]{2,1,0:T(4,128)} %get-tuple-element.277.pos, f32[5,4,256]{2,1,0:T(4,128)} %get-tuple-element.266.p, ...), custom_call_target="tpu_custom_call" | custom-call | flops 11000000 | bytes 36000 | tf_op jit(solution)/shard_map/experts/pallas_call | solution.py:482
  210.4 33.2 %experts.3 = (bf16[3,512,1536]{2,1,0:T(8,128)(2,1)}, bf16[3,512,1536]{2,1,0:T(8,128)(2,1)}, f32[3,4,256]{2,1,0:T(4,128)}, bf16[8,5,3,192,512]{4,3,2,1,0:T(8,128)(2,1)}) custom-call(s32[1]{0:T(128)} %bitcast.me, s32[1]{0:T(128)} %bitcast.12.z, s32[5,4,256]{2,1,0:T(4,128)} %get-tuple-element.277.pos, ...), custom_call_target="tpu_custom_call", output_to_operand_aliasing={{3}: (19, {})} | custom-call | flops 11000000 | bytes 36000 | tf_op jit(solution)/shard_map/experts/pallas_call | solution.py:482
  246.9 4.1 collective-permute-start.36
  251.7 7.1 %combine_back.3 = (bf16[272,1536]{1,0:T(8,128)(2,1)}, bf16[272,1536]{1,0:T(8,128)(2,1)}, bf16[272,1536]{1,0:T(8,128)(2,1)}) custom-call(s32[1]{0:T(128)} %bitcast.12.z, s32[5,4,256]{2,1,0:T(4,128)} %get-tuple-element.277.pos, bf16[2,512,1536]{2,1,0:T(8,128)(2,1)} %get-tuple-element.265.rest_0_, bf16[3,512,1536]{2,1,0:T(8,128)(2,1)} %get-tuple-element.273.rest_1_, ...), custom_call_target="tpu_custom_call" | custom-call | flops 11000000 | bytes 36000 | tf_op jit(solution)/shard_map/combine_back/pallas_call | solution.py:577
  258.8 9.1 %combine_out.1 = (bf16[256,1536]{1,0:T(8,128)(2,1)}, bf16[256,1536]{1,0:T(8,128)(2,1)}, bf16[256,1536]{1,0:T(8,128)(2,1)}, bf16[256,1536]{1,0:T(8,128)(2,1)}) custom-call(s32[5,4,256]{2,1,0:T(4,128)} %get-tuple-element.277.pos, bf16[2,512,1536]{2,1,0:T(8,128)(2,1)} %get-tuple-element.278.rest_0_, bf16[3,512,1536]{2,1,0:T(8,128)(2,1)} %get-tuple-element.279.rest_1_), custom_call_target="tpu_custom_call" | custom-call | flops 11000000 | bytes 36000 | tf_op jit(solution)/shard_map/combine_out/pallas_call | solution.py:606
  269.4 4.9 %collective-permute-start.39 = (bf16[272,1536]{1,0:T(8,128)(2,1)S(1)}, bf16[272,1536]{1,0:T(8,128)(2,1)S(1)}, u32[]{:S(2)}, u32[]{:S(2)}) collective-permute-start(bf16[272,1536]{1,0:T(8,128)(2,1)S(1)} %copy-done.55), channel_id=1, source_target_pairs={{0,1},{1,0},{2,3},{3,2},{4,5},{5,4},{6,7},{7,6},{8,9},{9,8},{10,11... | collective-permute-start | bytes 2506760 | tf_op jit(solution)/shard_map/ppermute | solution.py:78
  275.8 34.3 %collective-permute-done.39.rest_1_ = bf16[272,1536]{1,0:T(8,128)(2,1)S(1)} collective-permute-done((bf16[272,1536]{1,0:T(8,128)(2,1)S(1)}, bf16[272,1536]{1,0:T(8,128)(2,1)S(1)}, u32[]{:S(2)}, u32[]{:S(2)}) %collective-permute-start.39) | collective-permute-done | bytes 835616 | tf_op jit(solution)/shard_map/ppermute | solution.py:78
  316.2 10.0 %second_back.1 = (f32[256,1536]{1,0:T(8,128)}, bf16[1536,256]{1,0:T(8,128)(2,1)}, f32[40,1536]{1,0:T(8,128)}, bf16[4,192,1536]{2,1,0:T(8,128)(2,1)}, bf16[4,192,1536]{2,1,0:T(8,128)(2,1)}) custom-call(s32[1]{0:T(128)} %bitcast.me, f32[24,256]{1,0:T(8,128)} %get-tuple-element.290.own_p, f32[40,1536]{1,0:T(8,128)} %get-tuple-element.291.ext, ...), custom_call_target="tpu_custom_call" | custom-call | flops 11000000 | bytes 36000 | tf_op jit(solution)/shard_map/second_back/pallas_call | solution.py:767
  326.2 8.1 %heads_back.1 = (bf16[2560,256]{1,0:T(8,128)(2,1)}, bf16[1024,640]{1,0:T(8,128)(2,1)}) custom-call(bf16[1536,256]{1,0:T(8,128)(2,1)} %get-tuple-element.297.ctx_grad, bf16[2560,256]{1,0:T(8,128)(2,1)} %get-tuple-element.298.qkv, bf16[8,256,768]{2,1,0:T(8,128)(2,1)} %get-tuple-element.299.probs), custom_call_target="tpu_custom_call" | custom-call | flops 11000000 | bytes 36000 | tf_op jit(solution)/shard_map/heads_back/pallas_call | solution.py:838
  335.5 4.6 all-to-all-start
  345.8 9.4 %first_back.1 = (f32[256,1536]{1,0:T(8,128)}, bf16[1536,128]{1,0:T(8,128)(2,1)}) custom-call(s32[1]{0:T(128)} %bitcast.me, bf16[2560,256]{1,0:T(8,128)(2,1)} %get-tuple-element.314.back, bf16[256,1536]{1,0:T(8,128)(2,1)} %tok.3, f32[40,1536]{1,0:T(8,128)} %get-tuple-element.291.ext, f32[40,1536]{1,0:T(8,128)} %get-tuple-element.315.ext_grad, ...), custom_call_target="tpu_custom_call" | custom-call | flops 65999998976 | bytes 216000000 | tf_op jit(solution)/shard_map/first_back/pallas_call | solution.py:880
  355.2 9.5 %collective-permute-done.43 = bf16[2,192,768]{2,1,0:T(8,128)(2,1)S(1)} collective-permute-done((bf16[2,192,768]{2,1,0:T(8,128)(2,1)S(1)}, bf16[2,192,768]{2,1,0:T(8,128)(2,1)S(1)}, u32[]{:S(2)}, u32[]{:S(2)}) %collective-permute-start.43) | collective-permute-done | bytes 589856 | tf_op jit(solution)/shard_map/ppermute | solution.py:52
  366.0 6.4 %all-to-all-done = bf16[4,256,640]{2,1,0:T(8,128)(2,1)} async-done(((bf16[4,256,640]{2,1,0:T(8,128)(2,1)}), bf16[4,256,640]{2,1,0:T(8,128)(2,1)}, u32[]{:S(2)}, u32[]{:S(2)}) %all-to-all-start) | async-done | bytes 1310752 | tf_op jit(solution)/shard_map/all_to_all | solution.py:96
  372.4 6.7 %project_back.1 = (bf16[192,768]{1,0:T(8,128)(2,1)}, bf16[192,768]{1,0:T(8,128)(2,1)}, bf16[192,768]{1,0:T(8,128)(2,1)}, bf16[192,768]{1,0:T(8,128)(2,1)}, bf16[4,192,768]{2,1,0:T(8,128)(2,1)}) custom-call(s32[1]{0:T(128)} %bitcast.me, bf16[4,1536,256]{2,1,0:T(8,128)(2,1)} %bitcast.64, bf16[1024,640]{1,0:T(8,128)(2,1)} %bitcast.14.back_all, ...), custom_call_target="tpu_custom_call" | custom-call | flops 65999998976 | bytes 216000000 | tf_op jit(solution)/shard_map/project_back/pallas_call | solution.py:915
  387.1 8.2 %collective-permute-done.46 = bf16[192,768]{1,0:T(8,128)(2,1)S(1)} collective-permute-done((bf16[192,768]{1,0:T(8,128)(2,1)S(1)}, bf16[192,768]{1,0:T(8,128)(2,1)S(1)}, u32[]{:S(2)}, u32[]{:S(2)}) %collective-permute-start.46) | collective-permute-done | bytes 294944 | tf_op jit(solution)/shard_map/ppermute | solution.py:52
  397.6 3.5 all-to-all-start.1
  404.6 14.9 %collective-permute-done.55 = bf16[256,1536]{1,0:T(8,128)(2,1)} collective-permute-done((bf16[256,1536]{1,0:T(8,128)(2,1)}, bf16[256,1536]{1,0:T(8,128)(2,1)}, u32[]{:S(2)}, u32[]{:S(2)}) %collective-permute-start.55) | collective-permute-done | bytes 786464 | tf_op jit(solution)/shard_map/ppermute | solution.py:78
  419.5 3.8 collective-permute-done.54
  425.1 6.9 %all-to-all-done.1 = bf16[4,48,1536]{2,1,0:T(8,128)(2,1)S(1)} async-done(((bf16[4,48,1536]{2,1,0:T(8,128)(2,1)}), bf16[4,48,1536]{2,1,0:T(8,128)(2,1)S(1)}, u32[]{:S(2)}, u32[]{:S(2)}) %all-to-all-start.1) | async-done | bytes 589856 | tf_op jit(solution)/shard_map/all_to_all | solution.py:96
  441.4 15.6 %collective-permute-done.51.rest_2_ = bf16[192,1152]{1,0:T(8,128)(2,1)S(1)} collective-permute-done((bf16[192,1152]{1,0:T(8,128)(2,1)}, bf16[192,1152]{1,0:T(8,128)(2,1)S(1)}, u32[]{:S(2)}, u32[]{:S(2)}) %collective-permute-start.51) | collective-permute-done | bytes 442400 | tf_op jit(solution)/shard_map/ppermute | solution.py:78
  463.9 7.0 %collective-permute-done.53.rest_4_ = bf16[192,1152]{1,0:T(8,128)(2,1)S(1)} collective-permute-done((bf16[192,1152]{1,0:T(8,128)(2,1)S(1)}, bf16[192,1152]{1,0:T(8,128)(2,1)S(1)}, u32[]{:S(2)}, u32[]{:S(2)}) %collective-permute-start.53) | collective-permute-done | bytes 442400 | tf_op jit(solution)/shard_map/ppermute | solution.py:78
  472.4 3.4 finish.1
  (245 shorter events, 104.2 us)
Async XLA Ops:
  7.2 84.3 %all-gather.3.cloned.1.call-start = ((), (), s32[]{:S(2)}) async-start(), calls=%async_computation.3 | async-start | bytes 3932160 | tf_op jit(solution)/shard_map/all_gather | solution.py:963
  7.9 364.5 %all-gather.5.cloned.1.call-start = ((), (), s32[]{:S(2)}) async-start(), calls=%async_computation.4 | async-start | bytes 3932160 | tf_op jit(solution)/shard_map/all_gather | solution.py:1019
  10.5 26.0 %collective-permute-start = (bf16[192,2688]{1,0:T(8,128)(2,1)}, bf16[192,2688]{1,0:T(8,128)(2,1)S(1)}, u32[]{:S(2)}, u32[]{:S(2)}) collective-permute-start(bf16[192,2688]{1,0:T(8,128)(2,1)} %pack.1.rest_0_), channel_id=1, source_target_pairs={{0,8},{4,12},{8,0},{12,4},{16,24},{20,28},{24,16},{28,20},{1,9},{5... | collective-permute-start | bytes 3096584 | tf_op jit(solution)/shard_map/ppermute | solution.py:52
  13.4 24.5 %collective-permute-start.1 = (bf16[192,2688]{1,0:T(8,128)(2,1)}, bf16[192,2688]{1,0:T(8,128)(2,1)S(1)}, u32[]{:S(2)}, u32[]{:S(2)}) collective-permute-start(bf16[192,2688]{1,0:T(8,128)(2,1)} %pack.1.rest_0_), channel_id=1, source_target_pairs={{0,16},{4,20},{8,24},{12,28},{16,0},{20,4},{24,8},{28,12},{1,17},{... | collective-permute-start | bytes 3096584 | tf_op jit(solution)/shard_map/ppermute | solution.py:52
  15.0 23.0 %collective-permute-start.2 = (bf16[192,2688]{1,0:T(8,128)(2,1)}, bf16[192,2688]{1,0:T(8,128)(2,1)S(1)}, u32[]{:S(2)}, u32[]{:S(2)}) collective-permute-start(bf16[192,2688]{1,0:T(8,128)(2,1)} %pack.1.rest_0_), channel_id=1, source_target_pairs={{0,4},{4,0},{8,12},{12,8},{16,20},{20,16},{24,28},{28,24},{1,5},{5... | collective-permute-start | bytes 3096584 | tf_op jit(solution)/shard_map/ppermute | solution.py:52
  73.6 28.7 %collective-permute-start.16 = (bf16[2,3,192,512]{3,2,1,0:T(8,128)(2,1)}, bf16[2,3,192,512]{3,2,1,0:T(8,128)(2,1)}, u32[]{:S(2)}, u32[]{:S(2)}) collective-permute-start(bf16[2,3,192,512]{3,2,1,0:T(8,128)(2,1)} %pad_maximum_fusion.2.rest_4_), channel_id=1, source_target_pairs={{0,16},{4,20},{8,24},{12,28},{16,0},{20,4},{24,8},{28,12},{1,17},{... | collective-permute-start | bytes 3538952 | tf_op jit(solution)/shard_map/ppermute | solution.py:52
  88.9 29.2 %collective-permute-start.17 = (bf16[2,3,192,512]{3,2,1,0:T(8,128)(2,1)}, bf16[2,3,192,512]{3,2,1,0:T(8,128)(2,1)}, u32[]{:S(2)}, u32[]{:S(2)}) collective-permute-start(bf16[2,3,192,512]{3,2,1,0:T(8,128)(2,1)} %pad_maximum_fusion.2.rest_4_), channel_id=1, source_target_pairs={{0,8},{4,12},{8,0},{12,4},{16,24},{20,28},{24,16},{28,20},{1,9},{5... | collective-permute-start | bytes 3538952 | tf_op jit(solution)/shard_map/ppermute | solution.py:52
  102.4 64.5 %collective-permute-start.22 = (bf16[3,3,192,512]{3,2,1,0:T(8,128)(2,1)S(1)}, bf16[3,3,192,512]{3,2,1,0:T(8,128)(2,1)S(1)}, u32[]{:S(2)}, u32[]{:S(2)}) collective-permute-start(bf16[3,3,192,512]{3,2,1,0:T(8,128)(2,1)S(1)} %pad_maximum_fusion.rest_4_), channel_id=1, source_target_pairs={{0,16},{4,20},{8,24},{12,28},{16,0},{20,4},{24,8},{28,12},{1,17},{... | collective-permute-start | bytes 5308424 | tf_op jit(solution)/shard_map/ppermute | solution.py:52
  104.0 62.9 %collective-permute-start.23 = (bf16[3,3,192,512]{3,2,1,0:T(8,128)(2,1)S(1)}, bf16[3,3,192,512]{3,2,1,0:T(8,128)(2,1)S(1)}, u32[]{:S(2)}, u32[]{:S(2)}) collective-permute-start(bf16[3,3,192,512]{3,2,1,0:T(8,128)(2,1)S(1)} %pad_maximum_fusion.rest_4_), channel_id=1, source_target_pairs={{0,8},{4,12},{8,0},{12,4},{16,24},{20,28},{24,16},{28,20},{1,9},{5... | collective-permute-start | bytes 5308424 | tf_op jit(solution)/shard_map/ppermute | solution.py:52
  105.5 38.8 %collective-permute-start.18 = (bf16[272,1536]{1,0:T(8,128)(2,1)}, bf16[272,1536]{1,0:T(8,128)(2,1)S(1)}, u32[]{:S(2)}, u32[]{:S(2)}) collective-permute-start(bf16[272,1536]{1,0:T(8,128)(2,1)} %get-tuple-element.227.rest_0_.low_two), channel_id=1, source_target_pairs={{0,2},{1,3},{2,0},{3,1},{4,6},{5,7},{6,4},{7,5},{8,10},{9,11},{10,... | collective-permute-start | bytes 2506760 | tf_op jit(solution)/shard_map/ppermute | solution.py:78
  108.1 36.4 %collective-permute-start.19 = (bf16[272,1536]{1,0:T(8,128)(2,1)}, bf16[272,1536]{1,0:T(8,128)(2,1)S(1)}, u32[]{:S(2)}, u32[]{:S(2)}) collective-permute-start(bf16[272,1536]{1,0:T(8,128)(2,1)} %get-tuple-element.227.rest_0_.low_two), channel_id=1, source_target_pairs={{0,1},{1,0},{2,3},{3,2},{4,5},{5,4},{6,7},{7,6},{8,9},{9,8},{10,11... | collective-permute-start | bytes 2506760 | tf_op jit(solution)/shard_map/ppermute | solution.py:78
  145.1 21.7 %collective-permute-start.21 = (bf16[272,1536]{1,0:T(8,128)(2,1)S(1)}, bf16[272,1536]{1,0:T(8,128)(2,1)S(1)}, u32[]{:S(2)}, u32[]{:S(2)}) collective-permute-start(bf16[272,1536]{1,0:T(8,128)(2,1)S(1)} %collective-permute-done.18.rest_2_), channel_id=1, source_target_pairs={{2,3},{1,0},{6,7},{5,4},{10,11},{9,8},{14,15},{13,12},{18,19},{17,... | collective-permute-start | bytes 2506760 | tf_op jit(solution)/shard_map/ppermute | solution.py:78
  146.4 28.1 %collective-permute-start.24 = (bf16[2,3,192,512]{3,2,1,0:T(8,128)(2,1)}, bf16[2,3,192,512]{3,2,1,0:T(8,128)(2,1)}, u32[]{:S(2)}, u32[]{:S(2)}) collective-permute-start(bf16[2,3,192,512]{3,2,1,0:T(8,128)(2,1)} %collective-permute-done.17.rest_5_), channel_id=1, source_target_pairs={{0,16},{4,20},{8,24},{12,28},{16,0},{20,4},{24,8},{28,12},{1,17},{... | collective-permute-start | bytes 3538952 | tf_op jit(solution)/shard_map/ppermute | solution.py:52
  170.1 288.4 %reduce-scatter.2.cloned.1.call-start = ((), (), s32[]{:S(2)}) async-start(), calls=%async_computation.5 | async-start | bytes 26542080 | tf_op jit(solution)/shard_map/reduce_scatter | solution.py:1054
  175.1 30.6 %collective-permute-start.32 = (bf16[3,3,192,512]{3,2,1,0:T(8,128)(2,1)S(1)}, bf16[3,3,192,512]{3,2,1,0:T(8,128)(2,1)S(1)}, u32[]{:S(2)}, u32[]{:S(2)}) collective-permute-start(bf16[3,3,192,512]{3,2,1,0:T(8,128)(2,1)S(1)} %copy-done.7), channel_id=1, source_target_pairs={{0,4},{4,0},{8,12},{12,8},{16,20},{20,16},{24,28},{28,24},{1,5},{5... | collective-permute-start | bytes 5308424 | tf_op jit(solution)/shard_map/ppermute | solution.py:52
  175.4 30.3 %collective-permute-start.33 = (bf16[3,3,192,512]{3,2,1,0:T(8,128)(2,1)S(1)}, bf16[3,3,192,512]{3,2,1,0:T(8,128)(2,1)}, u32[]{:S(2)}, u32[]{:S(2)}) collective-permute-start(bf16[3,3,192,512]{3,2,1,0:T(8,128)(2,1)S(1)} %copy-done.5), channel_id=1, source_target_pairs={{0,4},{4,0},{8,12},{12,8},{16,20},{20,16},{24,28},{28,24},{1,5},{5... | collective-permute-start | bytes 5308424 | tf_op jit(solution)/shard_map/ppermute | solution.py:52
  178.3 27.5 %collective-permute-start.31 = (bf16[3,3,192,512]{3,2,1,0:T(8,128)(2,1)S(1)}, bf16[3,3,192,512]{3,2,1,0:T(8,128)(2,1)}, u32[]{:S(2)}, u32[]{:S(2)}) collective-permute-start(bf16[3,3,192,512]{3,2,1,0:T(8,128)(2,1)S(1)} %pad_maximum_fusion.rest_4_), channel_id=1, source_target_pairs={{0,4},{4,0},{8,12},{12,8},{16,20},{20,16},{24,28},{28,24},{1,5},{5... | collective-permute-start | bytes 5308424 | tf_op jit(solution)/shard_map/ppermute | solution.py:52
  180.6 25.0 %collective-permute-start.29 = (bf16[3,3,96,512]{3,2,1,0:T(8,128)(2,1)}, bf16[3,3,96,512]{3,2,1,0:T(8,128)(2,1)}, u32[]{:S(2)}, u32[]{:S(2)}) collective-permute-start(bf16[3,3,96,512]{3,2,1,0:T(8,128)(2,1)} %slice.91), channel_id=1, source_target_pairs={{0,16},{4,20},{8,24},{12,28},{16,0},{20,4},{24,8},{28,12},{1,17},{... | collective-permute-start | bytes 2654216 | tf_op jit(solution)/shard_map/ppermute | solution.py:52
  181.1 24.5 %collective-permute-start.30 = (bf16[3,3,96,512]{3,2,1,0:T(8,128)(2,1)}, bf16[3,3,96,512]{3,2,1,0:T(8,128)(2,1)S(1)}, u32[]{:S(2)}, u32[]{:S(2)}) collective-permute-start(bf16[3,3,96,512]{3,2,1,0:T(8,128)(2,1)} %slice.92), channel_id=1, source_target_pairs={{0,8},{4,12},{8,0},{12,4},{16,24},{20,28},{24,16},{28,20},{1,9},{5... | collective-permute-start | bytes 2654216 | tf_op jit(solution)/shard_map/ppermute | solution.py:52
  246.9 22.5 %collective-permute-start.36 = (bf16[272,1536]{1,0:T(8,128)(2,1)}, bf16[272,1536]{1,0:T(8,128)(2,1)S(1)}, u32[]{:S(2)}, u32[]{:S(2)}) collective-permute-start(bf16[272,1536]{1,0:T(8,128)(2,1)} %combine_back.2), channel_id=1, source_target_pairs={{3,2},{0,1},{7,6},{4,5},{11,10},{8,9},{15,14},{12,13},{19,18},{16,... | collective-permute-start | bytes 2506760 | tf_op jit(solution)/shard_map/ppermute | solution.py:78
  269.4 40.6 %collective-permute-start.39 = (bf16[272,1536]{1,0:T(8,128)(2,1)S(1)}, bf16[272,1536]{1,0:T(8,128)(2,1)S(1)}, u32[]{:S(2)}, u32[]{:S(2)}) collective-permute-start(bf16[272,1536]{1,0:T(8,128)(2,1)S(1)} %copy-done.55), channel_id=1, source_target_pairs={{0,1},{1,0},{2,3},{3,2},{4,5},{5,4},{6,7},{7,6},{8,9},{9,8},{10,11... | collective-permute-start | bytes 2506760 | tf_op jit(solution)/shard_map/ppermute | solution.py:78
  274.5 38.8 %collective-permute-start.38 = (bf16[272,1536]{1,0:T(8,128)(2,1)S(1)}, bf16[272,1536]{1,0:T(8,128)(2,1)S(1)}, u32[]{:S(2)}, u32[]{:S(2)}) collective-permute-start(bf16[272,1536]{1,0:T(8,128)(2,1)S(1)} %add_convert_fusion), channel_id=1, source_target_pairs={{0,2},{1,3},{2,0},{3,1},{4,6},{5,7},{6,4},{7,5},{8,10},{9,11},{10,... | collective-permute-start | bytes 2506760 | tf_op jit(solution)/shard_map/ppermute | solution.py:78
  335.5 36.9 %all-to-all-start = ((bf16[4,256,640]{2,1,0:T(8,128)(2,1)}), bf16[4,256,640]{2,1,0:T(8,128)(2,1)}, u32[]{:S(2)}, u32[]{:S(2)}) async-start(bf16[4,256,640]{2,1,0:T(8,128)(2,1)} %bitcast.60), calls=%async_computation | async-start | bytes 2621440 | tf_op jit(solution)/shard_map/all_to_all | solution.py:96
  342.8 22.0 %collective-permute-start.43 = (bf16[2,192,768]{2,1,0:T(8,128)(2,1)S(1)}, bf16[2,192,768]{2,1,0:T(8,128)(2,1)S(1)}, u32[]{:S(2)}, u32[]{:S(2)}) collective-permute-start(bf16[2,192,768]{2,1,0:T(8,128)(2,1)S(1)} %get-tuple-element.318), channel_id=1, source_target_pairs={{0,16},{4,20},{8,24},{12,28},{16,0},{20,4},{24,8},{28,12},{1,17},{... | collective-permute-start | bytes 1769480 | tf_op jit(solution)/shard_map/ppermute | solution.py:52
  382.0 37.5 %collective-permute-start.55 = (bf16[256,1536]{1,0:T(8,128)(2,1)}, bf16[256,1536]{1,0:T(8,128)(2,1)}, u32[]{:S(2)}, u32[]{:S(2)}) collective-permute-start(bf16[256,1536]{1,0:T(8,128)(2,1)} %get-tuple-element.351), channel_id=1, source_target_pairs={{0,1},{1,0},{2,3},{3,2},{4,5},{5,4},{6,7},{7,6},{8,9},{9,8},{10,11... | collective-permute-start | bytes 2359304 | tf_op jit(solution)/shard_map/ppermute | solution.py:78
  382.0 41.3 %collective-permute-start.54 = (bf16[256,1536]{1,0:T(8,128)(2,1)}, bf16[256,1536]{1,0:T(8,128)(2,1)}, u32[]{:S(2)}, u32[]{:S(2)}) collective-permute-start(bf16[256,1536]{1,0:T(8,128)(2,1)} %add_convert_fusion.2), channel_id=1, source_target_pairs={{0,2},{1,3},{2,0},{3,1},{4,6},{5,7},{6,4},{7,5},{8,10},{9,11},{10,... | collective-permute-start | bytes 2359304 | tf_op jit(solution)/shard_map/ppermute | solution.py:78
  397.6 34.4 %all-to-all-start.1 = ((bf16[4,48,1536]{2,1,0:T(8,128)(2,1)}), bf16[4,48,1536]{2,1,0:T(8,128)(2,1)S(1)}, u32[]{:S(2)}, u32[]{:S(2)}) async-start(bf16[4,48,1536]{2,1,0:T(8,128)(2,1)} %bitcast.23), calls=%async_computation.1 | async-start | bytes 1179648 | tf_op jit(solution)/shard_map/all_to_all | solution.py:96
  401.1 24.0 %collective-permute-start.48 = (bf16[192,768]{1,0:T(8,128)(2,1)}, bf16[192,768]{1,0:T(8,128)(2,1)S(1)}, u32[]{:S(2)}, u32[]{:S(2)}) collective-permute-start(bf16[192,768]{1,0:T(8,128)(2,1)} %get-tuple-element.339), channel_id=1, source_target_pairs={{0,8},{4,12},{8,0},{12,4},{16,24},{20,28},{24,16},{28,20},{1,9},{5... | collective-permute-start | bytes 884744 | tf_op jit(solution)/shard_map/ppermute | solution.py:52
  401.8 23.3 %collective-permute-start.49 = (bf16[192,768]{1,0:T(8,128)(2,1)}, bf16[192,768]{1,0:T(8,128)(2,1)S(1)}, u32[]{:S(2)}, u32[]{:S(2)}) collective-permute-start(bf16[192,768]{1,0:T(8,128)(2,1)} %get-tuple-element.340), channel_id=1, source_target_pairs={{0,16},{4,20},{8,24},{12,28},{16,0},{20,4},{24,8},{28,12},{1,17},{... | collective-permute-start | bytes 884744 | tf_op jit(solution)/shard_map/ppermute | solution.py:52
  403.2 21.9 %collective-permute-start.50 = (bf16[192,768]{1,0:T(8,128)(2,1)}, bf16[192,768]{1,0:T(8,128)(2,1)}, u32[]{:S(2)}, u32[]{:S(2)}) collective-permute-start(bf16[192,768]{1,0:T(8,128)(2,1)} %get-tuple-element.341), channel_id=1, source_target_pairs={{0,24},{4,28},{8,16},{12,20},{16,8},{20,12},{24,0},{28,4},{1,25},{... | collective-permute-start | bytes 884744 | tf_op jit(solution)/shard_map/ppermute | solution.py:52
  435.4 21.8 %collective-permute-start.52 = (bf16[192,1152]{1,0:T(8,128)(2,1)}, bf16[192,1152]{1,0:T(8,128)(2,1)}, u32[]{:S(2)}, u32[]{:S(2)}) collective-permute-start(bf16[192,1152]{1,0:T(8,128)(2,1)} %join.1.rest_0_), channel_id=1, source_target_pairs={{0,1},{1,0},{2,3},{3,2},{4,5},{5,4},{6,7},{7,6},{8,9},{9,8},{10,11... | collective-permute-start | bytes 1327112 | tf_op jit(solution)/shard_map/ppermute | solution.py:78
  440.7 30.2 %collective-permute-start.56 = (bf16[192,1152]{1,0:T(8,128)(2,1)S(1)}, bf16[192,1152]{1,0:T(8,128)(2,1)S(1)}, u32[]{:S(2)}, u32[]{:S(2)}) collective-permute-start(bf16[192,1152]{1,0:T(8,128)(2,1)S(1)} %copy-done.22), channel_id=1, source_target_pairs={{1,2},{2,1},{5,6},{6,5},{9,10},{10,9},{13,14},{14,13},{17,18},{18,... | collective-permute-start | bytes 1327112 | tf_op jit(solution)/shard_map/ppermute | solution.py:78
  (87 other events, 1261.2 us)
Sparse Core Ops, SparseCore 0:
  9.6 66.1 all-gather.2
  170.2 63.1 all-gather.4
  243.8 164.2 reduce-scatter.1

commit v5 on v4

--- a/solution.py
+++ b/solution.py
@@ -1014,10 +1014,12 @@
         order, far, near = wait(order, far, near)
         middle = along(hold(order, low_two), [(1, 2), (2, 1)])
         passed = along(far, [(2, 3), (1, 0)])
-        order, middle, passed, by, bx = wait(order, middle, passed, by, bx)
+        order, by, bx = wait(order, by, bx)
+        order, b_left, b_up = wait(order, bx[..., :half, :], by[..., half:, :])
+        order, middle, passed = wait(order, middle, passed)
         xs = [low_two, near, far, middle, passed]
         low_all = lax.all_gather(hold(order, low_one), "expert", axis=0, tiled=True)
-        ba, bb = swap(bx[..., :half, :], 4, size), swap(by[..., half:, :], 2, size)
+        ba, bb = swap(b_left, 4, size), swap(b_up, 2, size)
         a1, a3, a5 = (swap(hold(order, v), 1, size) for v in (a_shard, ax, ay))
         pos, p, own_p, xs[3] = run_router(z, hold(order, extra), xs, per, owners)
         xs = xs[:owners]

time: 491 us -> 489 us (level)
    ppermute x16, waiting for transfers between devices: 127 us -> 116 us  [along(): return lax.ppermute(value, 'expert', pairs)]
    ppermute x41, waiting for transfers between devices: 88 us -> 97.6 us  [swap(): return lax.ppermute(value, 'dp', [(i, i ^ bit) for i in range(size)])]
    unnamed x114 -> x110, local copies, waits for them, and re-layouts: 9.94 us -> 7.66 us
  transfers between devices with their start and end apart: 62 -> 62, of which waited for: 28 -> 30; matrix products, arithmetic and copies ran while one was open for 5% -> 5% of each run, Pallas kernels for 29% -> 29%
where the time goes in v5:
time: 489 us; the launch traced here: 481 us
  waiting for transfers between devices  228 us (47%)
  Pallas kernels  143 us (29%)
  starting transfers between devices  64.7 us (13%)
  local copies, waits for them, and re-layouts  15.7 us (3%)
  between operations  14.9 us (3%)
  other arithmetic  14.7 us (3%)
    ppermute x16, waiting for transfers between devices, along(): return lax.ppermute(value, 'expert', pairs)  116 us
    ppermute x41, waiting for transfers between devices, swap(): return lax.ppermute(value, 'dp', [(i, i ^ bit) for i in range(size)])  97.6 us
    pallas_call x2, Pallas kernels, run_experts(): pl.pallas_call(functools.partial(experts_kernel, size, rows, owners, cap,...  57.1 us
    ppermute x41, starting transfers between devices, swap(): return lax.ppermute(value, 'dp', [(i, i ^ bit) for i in range(size)])  28.3 us
    ppermute x16, starting transfers between devices, along(): return lax.ppermute(value, 'expert', pairs)  28.2 us
    all_to_all x2, waiting for transfers between devices, exchange(): lax.all_to_all(value, 'expert', split_axis=0, concat_axis=0, tiled=True)  13.4 us
    pallas_call x1, Pallas kernels, run_attention(): pl.pallas_call(functools.partial(attention_kernel, size, rows, plan), nam...  12.4 us
    pallas_call x2, Pallas kernels, run_combine_back(): pl.pallas_call(functools.partial(combine_back_kernel, start, owners, per,...  10.4 us
  transfers between devices with their start and end apart: 62, of which 30 were waited for; matrix products, arithmetic and copies ran while one was open for 5% of the time, Pallas kernels for 29%

profile of v5, /device:TPU:0, one launch (start us, length us, event | category | flops | bytes accessed | tf_op | source)
XLA Modules:
  0.0 480.7 jit_solution(3553759782235551220)
XLA Ops:
  14.9 21.5 %collective-permute-done.rest_1_ = bf16[192,2688]{1,0:T(8,128)(2,1)S(1)} collective-permute-done((bf16[192,2688]{1,0:T(8,128)(2,1)}, bf16[192,2688]{1,0:T(8,128)(2,1)S(1)}, u32[]{:S(2)}, u32[]{:S(2)}) %collective-permute-start) | collective-permute-done | bytes 1032224 | tf_op jit(solution)/shard_map/ppermute | solution.py:52
  40.3 12.0 %collective-permute-done.3.rest_3_ = bf16[96,2688]{1,0:T(8,128)(2,1)S(1)} collective-permute-done((bf16[96,2688]{1,0:T(8,128)(2,1)S(1)}, bf16[96,2688]{1,0:T(8,128)(2,1)S(1)}, u32[]{:S(2)}, u32[]{:S(2)}) %collective-permute-start.3) | collective-permute-done | bytes 516128 | tf_op jit(solution)/shard_map/ppermute | solution.py:52
  56.0 14.3 %collective-permute-done.10.rest_2_.rest_6_ = bf16[192,1536]{1,0:T(8,128)(2,1)S(1)} collective-permute-done((bf16[192,1536]{1,0:T(8,128)(2,1)S(1)}, bf16[192,1536]{1,0:T(8,128)(2,1)S(1)}, u32[]{:S(2)}, u32[]{:S(2)}) %collective-permute-start.10) | collective-permute-done | bytes 589856 | tf_op jit(solution)/shard_map/ppermute | solution.py:52
  76.1 12.4 %attention.1 = (bf16[1536,256]{1,0:T(8,128)(2,1)}, bf16[2560,256]{1,0:T(8,128)(2,1)}, bf16[1536,256]{1,0:T(8,128)(2,1)}, bf16[8,256,768]{2,1,0:T(8,128)(2,1)}, f32[40,1536]{1,0:T(8,128)}) custom-call(s32[1]{0:T(128)} %bitcast.me, bf16[256,1536]{1,0:T(8,128)(2,1)} %tok.3, s32[1,256]{1,0:T(1,128)} %seg_row.1, s32[256,1]{1,0:T(8,128)} %copy.30.seg_col, ...), custom_call_target="tpu_custom_call" | custom-call | flops 11000000 | bytes 36000 | tf_op jit(solution)/shard_map/attention/pallas_call | solution.py:219
  92.3 6.6 %residual.1 = (f32[256,1536]{1,0:T(8,128)}, bf16[272,1536]{1,0:T(8,128)(2,1)}) custom-call(s32[1]{0:T(128)} %bitcast.me, bf16[256,1536]{1,0:T(8,128)(2,1)} %tok.3, bf16[1536,256]{1,0:T(8,128)(2,1)} %get-tuple-element.218.ctx, f32[40,1536]{1,0:T(8,128)} %get-tuple-element.299.ext, bf16[16,1536]{1,0:T(8,128)(2,1)} %bitcast.61, bf16[192,1536]{1,0:T(8,128)(2,1)} %rest_4_.1, ...), custom_call_target="tpu_custom_call" | custom-call | flops 11000000 | bytes 36000 | tf_op jit(solution)/shard_map/residual/pallas_call | solution.py:258
  99.0 3.4 collective-permute-done.16.rest_6_
  109.6 8.4 %collective-permute-done.17.rest_5_ = bf16[2,3,192,512]{3,2,1,0:T(8,128)(2,1)} collective-permute-done((bf16[2,3,192,512]{3,2,1,0:T(8,128)(2,1)}, bf16[2,3,192,512]{3,2,1,0:T(8,128)(2,1)}, u32[]{:S(2)}, u32[]{:S(2)}) %collective-permute-start.17) | collective-permute-done | bytes 1179680 | tf_op jit(solution)/shard_map/ppermute | solution.py:52
  118.1 26.2 %collective-permute-done.18.rest_2_ = bf16[272,1536]{1,0:T(8,128)(2,1)S(1)} collective-permute-done((bf16[272,1536]{1,0:T(8,128)(2,1)}, bf16[272,1536]{1,0:T(8,128)(2,1)S(1)}, u32[]{:S(2)}, u32[]{:S(2)}) %collective-permute-start.18) | collective-permute-done | bytes 835616 | tf_op jit(solution)/shard_map/ppermute | solution.py:78
  147.0 8.2 %collective-permute-done.21.rest_5_ = bf16[3,3,192,512]{3,2,1,0:T(8,128)(2,1)S(1)} collective-permute-done((bf16[3,3,192,512]{3,2,1,0:T(8,128)(2,1)S(1)}, bf16[3,3,192,512]{3,2,1,0:T(8,128)(2,1)S(1)}, u32[]{:S(2)}, u32[]{:S(2)}) %collective-permute-start.21) | collective-permute-done | bytes 1769504 | tf_op jit(solution)/shard_map/ppermute | solution.py:52
  157.4 9.4 %collective-permute-done.23.rest_4_ = bf16[272,1536]{1,0:T(8,128)(2,1)S(1)} collective-permute-done((bf16[272,1536]{1,0:T(8,128)(2,1)S(1)}, bf16[272,1536]{1,0:T(8,128)(2,1)S(1)}, u32[]{:S(2)}, u32[]{:S(2)}) %collective-permute-start.23) | collective-permute-done | bytes 835616 | tf_op jit(solution)/shard_map/ppermute | solution.py:78
  167.9 4.3 router.1
  178.0 24.0 %experts.2 = (bf16[2,512,1536]{2,1,0:T(8,128)(2,1)}, bf16[2,512,1536]{2,1,0:T(8,128)(2,1)}, f32[2,4,256]{2,1,0:T(4,128)}, bf16[8,5,3,192,512]{4,3,2,1,0:T(8,128)(2,1)}) custom-call(s32[1]{0:T(128)} %bitcast.me, s32[1]{0:T(128)} %bitcast.12.z, s32[5,4,256]{2,1,0:T(4,128)} %get-tuple-element.285.pos, f32[5,4,256]{2,1,0:T(4,128)} %get-tuple-element.274.p, ...), custom_call_target="tpu_custom_call" | custom-call | flops 11000000 | bytes 36000 | tf_op jit(solution)/shard_map/experts/pallas_call | solution.py:482
  206.9 33.2 %experts.3 = (bf16[3,512,1536]{2,1,0:T(8,128)(2,1)}, bf16[3,512,1536]{2,1,0:T(8,128)(2,1)}, f32[3,4,256]{2,1,0:T(4,128)}, bf16[8,5,3,192,512]{4,3,2,1,0:T(8,128)(2,1)}) custom-call(s32[1]{0:T(128)} %bitcast.me, s32[1]{0:T(128)} %bitcast.12.z, s32[5,4,256]{2,1,0:T(4,128)} %get-tuple-element.285.pos, ...), custom_call_target="tpu_custom_call", output_to_operand_aliasing={{3}: (19, {})} | custom-call | flops 11000000 | bytes 36000 | tf_op jit(solution)/shard_map/experts/pallas_call | solution.py:482
  243.3 5.6 %collective-permute-start.36 = (bf16[272,1536]{1,0:T(8,128)(2,1)}, bf16[272,1536]{1,0:T(8,128)(2,1)S(1)}, u32[]{:S(2)}, u32[]{:S(2)}) collective-permute-start(bf16[272,1536]{1,0:T(8,128)(2,1)} %combine_back.2), channel_id=1, source_target_pairs={{3,2},{0,1},{7,6},{4,5},{11,10},{8,9},{15,14},{12,13},{19,18},{16,... | collective-permute-start | bytes 2506760 | tf_op jit(solution)/shard_map/ppermute | solution.py:78
  249.7 7.1 %combine_back.3 = (bf16[272,1536]{1,0:T(8,128)(2,1)}, bf16[272,1536]{1,0:T(8,128)(2,1)}, bf16[272,1536]{1,0:T(8,128)(2,1)}) custom-call(s32[1]{0:T(128)} %bitcast.12.z, s32[5,4,256]{2,1,0:T(4,128)} %get-tuple-element.285.pos, bf16[2,512,1536]{2,1,0:T(8,128)(2,1)} %get-tuple-element.273.rest_0_, bf16[3,512,1536]{2,1,0:T(8,128)(2,1)} %get-tuple-element.281.rest_1_, ...), custom_call_target="tpu_custom_call" | custom-call | flops 11000000 | bytes 36000 | tf_op jit(solution)/shard_map/combine_back/pallas_call | solution.py:577
  256.8 9.1 %combine_out.1 = (bf16[256,1536]{1,0:T(8,128)(2,1)}, bf16[256,1536]{1,0:T(8,128)(2,1)}, bf16[256,1536]{1,0:T(8,128)(2,1)}, bf16[256,1536]{1,0:T(8,128)(2,1)}) custom-call(s32[5,4,256]{2,1,0:T(4,128)} %get-tuple-element.285.pos, bf16[2,512,1536]{2,1,0:T(8,128)(2,1)} %get-tuple-element.286.rest_0_, bf16[3,512,1536]{2,1,0:T(8,128)(2,1)} %get-tuple-element.287.rest_1_), custom_call_target="tpu_custom_call" | custom-call | flops 11000000 | bytes 36000 | tf_op jit(solution)/shard_map/combine_out/pallas_call | solution.py:606
  267.4 4.9 %collective-permute-start.39 = (bf16[272,1536]{1,0:T(8,128)(2,1)S(1)}, bf16[272,1536]{1,0:T(8,128)(2,1)S(1)}, u32[]{:S(2)}, u32[]{:S(2)}) collective-permute-start(bf16[272,1536]{1,0:T(8,128)(2,1)S(1)} %copy-done.53), channel_id=1, source_target_pairs={{0,1},{1,0},{2,3},{3,2},{4,5},{5,4},{6,7},{7,6},{8,9},{9,8},{10,11... | collective-permute-start | bytes 2506760 | tf_op jit(solution)/shard_map/ppermute | solution.py:78
  273.7 34.3 %collective-permute-done.39.rest_1_ = bf16[272,1536]{1,0:T(8,128)(2,1)S(1)} collective-permute-done((bf16[272,1536]{1,0:T(8,128)(2,1)S(1)}, bf16[272,1536]{1,0:T(8,128)(2,1)S(1)}, u32[]{:S(2)}, u32[]{:S(2)}) %collective-permute-start.39) | collective-permute-done | bytes 835616 | tf_op jit(solution)/shard_map/ppermute | solution.py:78
  314.2 10.0 %second_back.1 = (f32[256,1536]{1,0:T(8,128)}, bf16[1536,256]{1,0:T(8,128)(2,1)}, f32[40,1536]{1,0:T(8,128)}, bf16[4,192,1536]{2,1,0:T(8,128)(2,1)}, bf16[4,192,1536]{2,1,0:T(8,128)(2,1)}) custom-call(s32[1]{0:T(128)} %bitcast.me, f32[24,256]{1,0:T(8,128)} %get-tuple-element.298.own_p, f32[40,1536]{1,0:T(8,128)} %get-tuple-element.299.ext, ...), custom_call_target="tpu_custom_call" | custom-call | flops 11000000 | bytes 36000 | tf_op jit(solution)/shard_map/second_back/pallas_call | solution.py:767
  324.2 8.1 %heads_back.1 = (bf16[2560,256]{1,0:T(8,128)(2,1)}, bf16[1024,640]{1,0:T(8,128)(2,1)}) custom-call(bf16[1536,256]{1,0:T(8,128)(2,1)} %get-tuple-element.305.ctx_grad, bf16[2560,256]{1,0:T(8,128)(2,1)} %get-tuple-element.306.qkv, bf16[8,256,768]{2,1,0:T(8,128)(2,1)} %get-tuple-element.307.probs), custom_call_target="tpu_custom_call" | custom-call | flops 11000000 | bytes 36000 | tf_op jit(solution)/shard_map/heads_back/pallas_call | solution.py:838
  333.4 4.6 all-to-all-start
  343.7 9.4 %first_back.1 = (f32[256,1536]{1,0:T(8,128)}, bf16[1536,128]{1,0:T(8,128)(2,1)}) custom-call(s32[1]{0:T(128)} %bitcast.me, bf16[2560,256]{1,0:T(8,128)(2,1)} %get-tuple-element.322.back, bf16[256,1536]{1,0:T(8,128)(2,1)} %tok.3, f32[40,1536]{1,0:T(8,128)} %get-tuple-element.299.ext, f32[40,1536]{1,0:T(8,128)} %get-tuple-element.323.ext_grad, ...), custom_call_target="tpu_custom_call" | custom-call | flops 65999998976 | bytes 216000000 | tf_op jit(solution)/shard_map/first_back/pallas_call | solution.py:880
  353.1 9.6 %collective-permute-done.43 = bf16[2,192,768]{2,1,0:T(8,128)(2,1)S(1)} collective-permute-done((bf16[2,192,768]{2,1,0:T(8,128)(2,1)S(1)}, bf16[2,192,768]{2,1,0:T(8,128)(2,1)S(1)}, u32[]{:S(2)}, u32[]{:S(2)}) %collective-permute-start.43) | collective-permute-done | bytes 589856 | tf_op jit(solution)/shard_map/ppermute | solution.py:52
  363.9 6.4 %all-to-all-done = bf16[4,256,640]{2,1,0:T(8,128)(2,1)} async-done(((bf16[4,256,640]{2,1,0:T(8,128)(2,1)}), bf16[4,256,640]{2,1,0:T(8,128)(2,1)}, u32[]{:S(2)}, u32[]{:S(2)}) %all-to-all-start) | async-done | bytes 1310752 | tf_op jit(solution)/shard_map/all_to_all | solution.py:96
  370.4 6.7 %project_back.1 = (bf16[192,768]{1,0:T(8,128)(2,1)}, bf16[192,768]{1,0:T(8,128)(2,1)}, bf16[192,768]{1,0:T(8,128)(2,1)}, bf16[192,768]{1,0:T(8,128)(2,1)}, bf16[4,192,768]{2,1,0:T(8,128)(2,1)}) custom-call(s32[1]{0:T(128)} %bitcast.me, bf16[4,1536,256]{2,1,0:T(8,128)(2,1)} %bitcast.64, bf16[1024,640]{1,0:T(8,128)(2,1)} %bitcast.14.back_all, ...), custom_call_target="tpu_custom_call" | custom-call | flops 65999998976 | bytes 216000000 | tf_op jit(solution)/shard_map/project_back/pallas_call | solution.py:915
  385.0 8.2 %collective-permute-done.46 = bf16[192,768]{1,0:T(8,128)(2,1)S(1)} collective-permute-done((bf16[192,768]{1,0:T(8,128)(2,1)S(1)}, bf16[192,768]{1,0:T(8,128)(2,1)S(1)}, u32[]{:S(2)}, u32[]{:S(2)}) %collective-permute-start.46) | collective-permute-done | bytes 294944 | tf_op jit(solution)/shard_map/ppermute | solution.py:52
  395.5 3.5 all-to-all-start.1
  402.6 14.8 %collective-permute-done.55 = bf16[256,1536]{1,0:T(8,128)(2,1)} collective-permute-done((bf16[256,1536]{1,0:T(8,128)(2,1)}, bf16[256,1536]{1,0:T(8,128)(2,1)}, u32[]{:S(2)}, u32[]{:S(2)}) %collective-permute-start.55) | collective-permute-done | bytes 786464 | tf_op jit(solution)/shard_map/ppermute | solution.py:78
  417.4 3.8 collective-permute-done.54
  423.0 6.9 %all-to-all-done.1 = bf16[4,48,1536]{2,1,0:T(8,128)(2,1)S(1)} async-done(((bf16[4,48,1536]{2,1,0:T(8,128)(2,1)}), bf16[4,48,1536]{2,1,0:T(8,128)(2,1)S(1)}, u32[]{:S(2)}, u32[]{:S(2)}) %all-to-all-start.1) | async-done | bytes 589856 | tf_op jit(solution)/shard_map/all_to_all | solution.py:96
  439.3 15.6 %collective-permute-done.51.rest_2_ = bf16[192,1152]{1,0:T(8,128)(2,1)S(1)} collective-permute-done((bf16[192,1152]{1,0:T(8,128)(2,1)}, bf16[192,1152]{1,0:T(8,128)(2,1)S(1)}, u32[]{:S(2)}, u32[]{:S(2)}) %collective-permute-start.51) | collective-permute-done | bytes 442400 | tf_op jit(solution)/shard_map/ppermute | solution.py:78
  461.8 7.0 %collective-permute-done.53.rest_4_ = bf16[192,1152]{1,0:T(8,128)(2,1)S(1)} collective-permute-done((bf16[192,1152]{1,0:T(8,128)(2,1)S(1)}, bf16[192,1152]{1,0:T(8,128)(2,1)S(1)}, u32[]{:S(2)}, u32[]{:S(2)}) %collective-permute-start.53) | collective-permute-done | bytes 442400 | tf_op jit(solution)/shard_map/ppermute | solution.py:78
  (241 shorter events, 106.1 us)
Async XLA Ops:
  7.2 84.3 %all-gather.3.cloned.1.call-start = ((), (), s32[]{:S(2)}) async-start(), calls=%async_computation.3 | async-start | bytes 3932160 | tf_op jit(solution)/shard_map/all_gather | solution.py:963
  7.9 362.4 %all-gather.5.cloned.1.call-start = ((), (), s32[]{:S(2)}) async-start(), calls=%async_computation.4 | async-start | bytes 3932160 | tf_op jit(solution)/shard_map/all_gather | solution.py:1021
  10.5 26.0 %collective-permute-start = (bf16[192,2688]{1,0:T(8,128)(2,1)}, bf16[192,2688]{1,0:T(8,128)(2,1)S(1)}, u32[]{:S(2)}, u32[]{:S(2)}) collective-permute-start(bf16[192,2688]{1,0:T(8,128)(2,1)} %pack.1.rest_0_), channel_id=1, source_target_pairs={{0,8},{4,12},{8,0},{12,4},{16,24},{20,28},{24,16},{28,20},{1,9},{5... | collective-permute-start | bytes 3096584 | tf_op jit(solution)/shard_map/ppermute | solution.py:52
  13.4 24.5 %collective-permute-start.1 = (bf16[192,2688]{1,0:T(8,128)(2,1)}, bf16[192,2688]{1,0:T(8,128)(2,1)S(1)}, u32[]{:S(2)}, u32[]{:S(2)}) collective-permute-start(bf16[192,2688]{1,0:T(8,128)(2,1)} %pack.1.rest_0_), channel_id=1, source_target_pairs={{0,16},{4,20},{8,24},{12,28},{16,0},{20,4},{24,8},{28,12},{1,17},{... | collective-permute-start | bytes 3096584 | tf_op jit(solution)/shard_map/ppermute | solution.py:52
  14.9 23.0 %collective-permute-start.2 = (bf16[192,2688]{1,0:T(8,128)(2,1)}, bf16[192,2688]{1,0:T(8,128)(2,1)S(1)}, u32[]{:S(2)}, u32[]{:S(2)}) collective-permute-start(bf16[192,2688]{1,0:T(8,128)(2,1)} %pack.1.rest_0_), channel_id=1, source_target_pairs={{0,4},{4,0},{8,12},{12,8},{16,20},{20,16},{24,28},{28,24},{1,5},{5... | collective-permute-start | bytes 3096584 | tf_op jit(solution)/shard_map/ppermute | solution.py:52
  73.6 28.7 %collective-permute-start.16 = (bf16[2,3,192,512]{3,2,1,0:T(8,128)(2,1)}, bf16[2,3,192,512]{3,2,1,0:T(8,128)(2,1)}, u32[]{:S(2)}, u32[]{:S(2)}) collective-permute-start(bf16[2,3,192,512]{3,2,1,0:T(8,128)(2,1)} %pad_maximum_fusion.2.rest_4_), channel_id=1, source_target_pairs={{0,16},{4,20},{8,24},{12,28},{16,0},{20,4},{24,8},{28,12},{1,17},{... | collective-permute-start | bytes 3538952 | tf_op jit(solution)/shard_map/ppermute | solution.py:52
  88.9 29.2 %collective-permute-start.17 = (bf16[2,3,192,512]{3,2,1,0:T(8,128)(2,1)}, bf16[2,3,192,512]{3,2,1,0:T(8,128)(2,1)}, u32[]{:S(2)}, u32[]{:S(2)}) collective-permute-start(bf16[2,3,192,512]{3,2,1,0:T(8,128)(2,1)} %pad_maximum_fusion.2.rest_4_), channel_id=1, source_target_pairs={{0,8},{4,12},{8,0},{12,4},{16,24},{20,28},{24,16},{28,20},{1,9},{5... | collective-permute-start | bytes 3538952 | tf_op jit(solution)/shard_map/ppermute | solution.py:52
  102.4 44.6 %collective-permute-start.20 = (bf16[3,3,192,512]{3,2,1,0:T(8,128)(2,1)S(1)}, bf16[3,3,192,512]{3,2,1,0:T(8,128)(2,1)S(1)}, u32[]{:S(2)}, u32[]{:S(2)}) collective-permute-start(bf16[3,3,192,512]{3,2,1,0:T(8,128)(2,1)S(1)} %pad_maximum_fusion.rest_4_), channel_id=1, source_target_pairs={{0,16},{4,20},{8,24},{12,28},{16,0},{20,4},{24,8},{28,12},{1,17},{... | collective-permute-start | bytes 5308424 | tf_op jit(solution)/shard_map/ppermute | solution.py:52
  104.0 51.3 %collective-permute-start.21 = (bf16[3,3,192,512]{3,2,1,0:T(8,128)(2,1)S(1)}, bf16[3,3,192,512]{3,2,1,0:T(8,128)(2,1)S(1)}, u32[]{:S(2)}, u32[]{:S(2)}) collective-permute-start(bf16[3,3,192,512]{3,2,1,0:T(8,128)(2,1)S(1)} %pad_maximum_fusion.rest_4_), channel_id=1, source_target_pairs={{0,8},{4,12},{8,0},{12,4},{16,24},{20,28},{24,16},{28,20},{1,9},{5... | collective-permute-start | bytes 5308424 | tf_op jit(solution)/shard_map/ppermute | solution.py:52
  105.5 38.8 %collective-permute-start.18 = (bf16[272,1536]{1,0:T(8,128)(2,1)}, bf16[272,1536]{1,0:T(8,128)(2,1)S(1)}, u32[]{:S(2)}, u32[]{:S(2)}) collective-permute-start(bf16[272,1536]{1,0:T(8,128)(2,1)} %get-tuple-element.236.rest_0_.low_two), channel_id=1, source_target_pairs={{0,2},{1,3},{2,0},{3,1},{4,6},{5,7},{6,4},{7,5},{8,10},{9,11},{10,... | collective-permute-start | bytes 2506760 | tf_op jit(solution)/shard_map/ppermute | solution.py:78
  108.0 36.4 %collective-permute-start.19 = (bf16[272,1536]{1,0:T(8,128)(2,1)}, bf16[272,1536]{1,0:T(8,128)(2,1)S(1)}, u32[]{:S(2)}, u32[]{:S(2)}) collective-permute-start(bf16[272,1536]{1,0:T(8,128)(2,1)} %get-tuple-element.236.rest_0_.low_two), channel_id=1, source_target_pairs={{0,1},{1,0},{2,3},{3,2},{4,5},{5,4},{6,7},{7,6},{8,9},{9,8},{10,11... | collective-permute-start | bytes 2506760 | tf_op jit(solution)/shard_map/ppermute | solution.py:78
  145.1 21.7 %collective-permute-start.23 = (bf16[272,1536]{1,0:T(8,128)(2,1)S(1)}, bf16[272,1536]{1,0:T(8,128)(2,1)S(1)}, u32[]{:S(2)}, u32[]{:S(2)}) collective-permute-start(bf16[272,1536]{1,0:T(8,128)(2,1)S(1)} %collective-permute-done.18.rest_2_), channel_id=1, source_target_pairs={{2,3},{1,0},{6,7},{5,4},{10,11},{9,8},{14,15},{13,12},{18,19},{17,... | collective-permute-start | bytes 2506760 | tf_op jit(solution)/shard_map/ppermute | solution.py:78
  146.4 26.9 %collective-permute-start.24 = (bf16[2,3,192,512]{3,2,1,0:T(8,128)(2,1)}, bf16[2,3,192,512]{3,2,1,0:T(8,128)(2,1)}, u32[]{:S(2)}, u32[]{:S(2)}) collective-permute-start(bf16[2,3,192,512]{3,2,1,0:T(8,128)(2,1)} %collective-permute-done.17.rest_5_), channel_id=1, source_target_pairs={{0,16},{4,20},{8,24},{12,28},{16,0},{20,4},{24,8},{28,12},{1,17},{... | collective-permute-start | bytes 3538952 | tf_op jit(solution)/shard_map/ppermute | solution.py:52
  167.8 288.6 %reduce-scatter.2.cloned.1.call-start = ((), (), s32[]{:S(2)}) async-start(), calls=%async_computation.5 | async-start | bytes 26542080 | tf_op jit(solution)/shard_map/reduce_scatter | solution.py:1056
  173.6 28.4 %collective-permute-start.32 = (bf16[3,3,192,512]{3,2,1,0:T(8,128)(2,1)S(1)}, bf16[3,3,192,512]{3,2,1,0:T(8,128)(2,1)S(1)}, u32[]{:S(2)}, u32[]{:S(2)}) collective-permute-start(bf16[3,3,192,512]{3,2,1,0:T(8,128)(2,1)S(1)} %copy-done.6), channel_id=1, source_target_pairs={{0,4},{4,0},{8,12},{12,8},{16,20},{20,16},{24,28},{28,24},{1,5},{5... | collective-permute-start | bytes 5308424 | tf_op jit(solution)/shard_map/ppermute | solution.py:52
  174.0 28.0 %collective-permute-start.33 = (bf16[3,3,192,512]{3,2,1,0:T(8,128)(2,1)S(1)}, bf16[3,3,192,512]{3,2,1,0:T(8,128)(2,1)}, u32[]{:S(2)}, u32[]{:S(2)}) collective-permute-start(bf16[3,3,192,512]{3,2,1,0:T(8,128)(2,1)S(1)} %collective-permute-done.20.rest_6_), channel_id=1, source_target_pairs={{0,4},{4,0},{8,12},{12,8},{16,20},{20,16},{24,28},{28,24},{1,5},{5... | collective-permute-start | bytes 5308424 | tf_op jit(solution)/shard_map/ppermute | solution.py:52
  176.9 25.1 %collective-permute-start.31 = (bf16[3,3,192,512]{3,2,1,0:T(8,128)(2,1)S(1)}, bf16[3,3,192,512]{3,2,1,0:T(8,128)(2,1)}, u32[]{:S(2)}, u32[]{:S(2)}) collective-permute-start(bf16[3,3,192,512]{3,2,1,0:T(8,128)(2,1)S(1)} %pad_maximum_fusion.rest_4_), channel_id=1, source_target_pairs={{0,4},{4,0},{8,12},{12,8},{16,20},{20,16},{24,28},{28,24},{1,5},{5... | collective-permute-start | bytes 5308424 | tf_op jit(solution)/shard_map/ppermute | solution.py:52
  177.1 24.9 %collective-permute-start.29 = (bf16[3,3,96,512]{3,2,1,0:T(8,128)(2,1)}, bf16[3,3,96,512]{3,2,1,0:T(8,128)(2,1)}, u32[]{:S(2)}, u32[]{:S(2)}) collective-permute-start(bf16[3,3,96,512]{3,2,1,0:T(8,128)(2,1)} %slice.91), channel_id=1, source_target_pairs={{0,16},{4,20},{8,24},{12,28},{16,0},{20,4},{24,8},{28,12},{1,17},{... | collective-permute-start | bytes 2654216 | tf_op jit(solution)/shard_map/ppermute | solution.py:52
  177.6 24.4 %collective-permute-start.30 = (bf16[3,3,96,512]{3,2,1,0:T(8,128)(2,1)}, bf16[3,3,96,512]{3,2,1,0:T(8,128)(2,1)}, u32[]{:S(2)}, u32[]{:S(2)}) collective-permute-start(bf16[3,3,96,512]{3,2,1,0:T(8,128)(2,1)} %slice.92), channel_id=1, source_target_pairs={{0,8},{4,12},{8,0},{12,4},{16,24},{20,28},{24,16},{28,20},{1,9},{5... | collective-permute-start | bytes 2654216 | tf_op jit(solution)/shard_map/ppermute | solution.py:52
  243.3 24.0 %collective-permute-start.36 = (bf16[272,1536]{1,0:T(8,128)(2,1)}, bf16[272,1536]{1,0:T(8,128)(2,1)S(1)}, u32[]{:S(2)}, u32[]{:S(2)}) collective-permute-start(bf16[272,1536]{1,0:T(8,128)(2,1)} %combine_back.2), channel_id=1, source_target_pairs={{3,2},{0,1},{7,6},{4,5},{11,10},{8,9},{15,14},{12,13},{19,18},{16,... | collective-permute-start | bytes 2506760 | tf_op jit(solution)/shard_map/ppermute | solution.py:78
  267.4 40.6 %collective-permute-start.39 = (bf16[272,1536]{1,0:T(8,128)(2,1)S(1)}, bf16[272,1536]{1,0:T(8,128)(2,1)S(1)}, u32[]{:S(2)}, u32[]{:S(2)}) collective-permute-start(bf16[272,1536]{1,0:T(8,128)(2,1)S(1)} %copy-done.53), channel_id=1, source_target_pairs={{0,1},{1,0},{2,3},{3,2},{4,5},{5,4},{6,7},{7,6},{8,9},{9,8},{10,11... | collective-permute-start | bytes 2506760 | tf_op jit(solution)/shard_map/ppermute | solution.py:78
  272.5 38.8 %collective-permute-start.38 = (bf16[272,1536]{1,0:T(8,128)(2,1)S(1)}, bf16[272,1536]{1,0:T(8,128)(2,1)S(1)}, u32[]{:S(2)}, u32[]{:S(2)}) collective-permute-start(bf16[272,1536]{1,0:T(8,128)(2,1)S(1)} %add_convert_fusion), channel_id=1, source_target_pairs={{0,2},{1,3},{2,0},{3,1},{4,6},{5,7},{6,4},{7,5},{8,10},{9,11},{10,... | collective-permute-start | bytes 2506760 | tf_op jit(solution)/shard_map/ppermute | solution.py:78
  333.4 36.9 %all-to-all-start = ((bf16[4,256,640]{2,1,0:T(8,128)(2,1)}), bf16[4,256,640]{2,1,0:T(8,128)(2,1)}, u32[]{:S(2)}, u32[]{:S(2)}) async-start(bf16[4,256,640]{2,1,0:T(8,128)(2,1)} %bitcast.60), calls=%async_computation | async-start | bytes 2621440 | tf_op jit(solution)/shard_map/all_to_all | solution.py:96
  340.7 22.0 %collective-permute-start.43 = (bf16[2,192,768]{2,1,0:T(8,128)(2,1)S(1)}, bf16[2,192,768]{2,1,0:T(8,128)(2,1)S(1)}, u32[]{:S(2)}, u32[]{:S(2)}) collective-permute-start(bf16[2,192,768]{2,1,0:T(8,128)(2,1)S(1)} %get-tuple-element.326), channel_id=1, source_target_pairs={{0,16},{4,20},{8,24},{12,28},{16,0},{20,4},{24,8},{28,12},{1,17},{... | collective-permute-start | bytes 1769480 | tf_op jit(solution)/shard_map/ppermute | solution.py:52
  379.9 37.5 %collective-permute-start.55 = (bf16[256,1536]{1,0:T(8,128)(2,1)}, bf16[256,1536]{1,0:T(8,128)(2,1)}, u32[]{:S(2)}, u32[]{:S(2)}) collective-permute-start(bf16[256,1536]{1,0:T(8,128)(2,1)} %get-tuple-element.359), channel_id=1, source_target_pairs={{0,1},{1,0},{2,3},{3,2},{4,5},{5,4},{6,7},{7,6},{8,9},{9,8},{10,11... | collective-permute-start | bytes 2359304 | tf_op jit(solution)/shard_map/ppermute | solution.py:78
  379.9 41.3 %collective-permute-start.54 = (bf16[256,1536]{1,0:T(8,128)(2,1)}, bf16[256,1536]{1,0:T(8,128)(2,1)}, u32[]{:S(2)}, u32[]{:S(2)}) collective-permute-start(bf16[256,1536]{1,0:T(8,128)(2,1)} %add_convert_fusion.2), channel_id=1, source_target_pairs={{0,2},{1,3},{2,0},{3,1},{4,6},{5,7},{6,4},{7,5},{8,10},{9,11},{10,... | collective-permute-start | bytes 2359304 | tf_op jit(solution)/shard_map/ppermute | solution.py:78
  395.5 34.4 %all-to-all-start.1 = ((bf16[4,48,1536]{2,1,0:T(8,128)(2,1)}), bf16[4,48,1536]{2,1,0:T(8,128)(2,1)S(1)}, u32[]{:S(2)}, u32[]{:S(2)}) async-start(bf16[4,48,1536]{2,1,0:T(8,128)(2,1)} %bitcast.23), calls=%async_computation.1 | async-start | bytes 1179648 | tf_op jit(solution)/shard_map/all_to_all | solution.py:96
  399.0 23.9 %collective-permute-start.48 = (bf16[192,768]{1,0:T(8,128)(2,1)}, bf16[192,768]{1,0:T(8,128)(2,1)S(1)}, u32[]{:S(2)}, u32[]{:S(2)}) collective-permute-start(bf16[192,768]{1,0:T(8,128)(2,1)} %get-tuple-element.347), channel_id=1, source_target_pairs={{0,8},{4,12},{8,0},{12,4},{16,24},{20,28},{24,16},{28,20},{1,9},{5... | collective-permute-start | bytes 884744 | tf_op jit(solution)/shard_map/ppermute | solution.py:52
  399.7 23.2 %collective-permute-start.49 = (bf16[192,768]{1,0:T(8,128)(2,1)}, bf16[192,768]{1,0:T(8,128)(2,1)S(1)}, u32[]{:S(2)}, u32[]{:S(2)}) collective-permute-start(bf16[192,768]{1,0:T(8,128)(2,1)} %get-tuple-element.348), channel_id=1, source_target_pairs={{0,16},{4,20},{8,24},{12,28},{16,0},{20,4},{24,8},{28,12},{1,17},{... | collective-permute-start | bytes 884744 | tf_op jit(solution)/shard_map/ppermute | solution.py:52
  401.2 21.8 %collective-permute-start.50 = (bf16[192,768]{1,0:T(8,128)(2,1)}, bf16[192,768]{1,0:T(8,128)(2,1)}, u32[]{:S(2)}, u32[]{:S(2)}) collective-permute-start(bf16[192,768]{1,0:T(8,128)(2,1)} %get-tuple-element.349), channel_id=1, source_target_pairs={{0,24},{4,28},{8,16},{12,20},{16,8},{20,12},{24,0},{28,4},{1,25},{... | collective-permute-start | bytes 884744 | tf_op jit(solution)/shard_map/ppermute | solution.py:52
  433.3 21.8 %collective-permute-start.52 = (bf16[192,1152]{1,0:T(8,128)(2,1)}, bf16[192,1152]{1,0:T(8,128)(2,1)}, u32[]{:S(2)}, u32[]{:S(2)}) collective-permute-start(bf16[192,1152]{1,0:T(8,128)(2,1)} %join.1.rest_0_), channel_id=1, source_target_pairs={{0,1},{1,0},{2,3},{3,2},{4,5},{5,4},{6,7},{7,6},{8,9},{9,8},{10,11... | collective-permute-start | bytes 1327112 | tf_op jit(solution)/shard_map/ppermute | solution.py:78
  438.6 30.2 %collective-permute-start.56 = (bf16[192,1152]{1,0:T(8,128)(2,1)S(1)}, bf16[192,1152]{1,0:T(8,128)(2,1)S(1)}, u32[]{:S(2)}, u32[]{:S(2)}) collective-permute-start(bf16[192,1152]{1,0:T(8,128)(2,1)S(1)} %copy-done.21), channel_id=1, source_target_pairs={{1,2},{2,1},{5,6},{6,5},{9,10},{10,9},{13,14},{14,13},{17,18},{18,... | collective-permute-start | bytes 1327112 | tf_op jit(solution)/shard_map/ppermute | solution.py:78
  (85 other events, 1258.0 us)
Sparse Core Ops, SparseCore 0:
  9.6 66.1 all-gather.2
  168.0 63.2 all-gather.4
  240.2 165.8 reduce-scatter.1

commit v6 on v5

--- a/solution.py
+++ b/solution.py
@@ -989,7 +989,9 @@
         q3 = swap(qx, 1, size)
         o_shard = hold(order, output_weight)
         ox, oy = swap(o_shard, 2, size), swap(o_shard, 4, size)
-        order, qa, qb, q3 = wait(order, qa, qb, q3)
+        order, qa, qb, q3, a_shard, b_shard, segments, place = wait(
+            order, qa, qb, q3, a_shard, b_shard, segments, place
+        )
         q5, q6, q7 = swap(hold(order, qy), 1, size), swap(qa, 1, size), swap(qb, 1, size)
         order, q5, q6, q7, ox, oy = wait(order, q5, q6, q7, ox, oy)
         qkv_pieces = ([packed, qx, qy, qa, qb, q1, q3, q5, q6, q7], split)

time: 489 us -> 485 us (level)
  transfers between devices with their start and end apart: 62 -> 62, of which waited for: 30 -> 31; matrix products, arithmetic and copies ran while one was open for 5% -> 5% of each run, Pallas kernels for 29% -> 29%
where the time goes in v6:
time: 485 us; the launch traced here: 477 us
  waiting for transfers between devices  228 us (47%)
  Pallas kernels  142 us (29%)
  starting transfers between devices  63 us (13%)
  local copies, waits for them, and re-layouts  14.9 us (3%)
  between operations  14.8 us (3%)
  other arithmetic  14.6 us (3%)
    ppermute x16, waiting for transfers between devices, along(): return lax.ppermute(value, 'expert', pairs)  115 us
    ppermute x41, waiting for transfers between devices, swap(): return lax.ppermute(value, 'dp', [(i, i ^ bit) for i in range(size)])  98.3 us
    pallas_call x2, Pallas kernels, run_experts(): pl.pallas_call(functools.partial(experts_kernel, size, rows, owners, cap,...  57.1 us
    ppermute x16, starting transfers between devices, along(): return lax.ppermute(value, 'expert', pairs)  28.1 us
    ppermute x41, starting transfers between devices, swap(): return lax.ppermute(value, 'dp', [(i, i ^ bit) for i in range(size)])  26.7 us
    all_to_all x2, waiting for transfers between devices, exchange(): lax.all_to_all(value, 'expert', split_axis=0, concat_axis=0, tiled=True)  13.7 us
    pallas_call x1, Pallas kernels, run_attention(): pl.pallas_call(functools.partial(attention_kernel, size, rows, plan), nam...  12.2 us
    pallas_call x2, Pallas kernels, run_combine_back(): pl.pallas_call(functools.partial(combine_back_kernel, start, owners, per,...  10.2 us
  transfers between devices with their start and end apart: 62, of which 31 were waited for; matrix products, arithmetic and copies ran while one was open for 5% of the time, Pallas kernels for 29%

profile of v6, /device:TPU:0, one launch (start us, length us, event | category | flops | bytes accessed | tf_op | source)
XLA Modules:
  0.0 477.0 jit_solution(5243502432877864408)
XLA Ops:
  14.9 21.5 %collective-permute-done.rest_1_ = bf16[192,2688]{1,0:T(8,128)(2,1)S(1)} collective-permute-done((bf16[192,2688]{1,0:T(8,128)(2,1)}, bf16[192,2688]{1,0:T(8,128)(2,1)S(1)}, u32[]{:S(2)}, u32[]{:S(2)}) %collective-permute-start) | collective-permute-done | bytes 1032224 | tf_op jit(solution)/shard_map/ppermute | solution.py:52
  42.3 9.8 %collective-permute-done.3.rest_3_ = bf16[96,2688]{1,0:T(8,128)(2,1)S(1)} collective-permute-done((bf16[96,2688]{1,0:T(8,128)(2,1)S(1)}, bf16[96,2688]{1,0:T(8,128)(2,1)S(1)}, u32[]{:S(2)}, u32[]{:S(2)}) %collective-permute-start.3) | collective-permute-done | bytes 516128 | tf_op jit(solution)/shard_map/ppermute | solution.py:52
  55.1 14.3 %collective-permute-done.10.rest_2_.rest_6_ = bf16[192,1536]{1,0:T(8,128)(2,1)S(1)} collective-permute-done((bf16[192,1536]{1,0:T(8,128)(2,1)S(1)}, bf16[192,1536]{1,0:T(8,128)(2,1)S(1)}, u32[]{:S(2)}, u32[]{:S(2)}) %collective-permute-start.10) | collective-permute-done | bytes 589856 | tf_op jit(solution)/shard_map/ppermute | solution.py:52
  73.3 12.2 %attention.1 = (bf16[1536,256]{1,0:T(8,128)(2,1)}, bf16[2560,256]{1,0:T(8,128)(2,1)}, bf16[1536,256]{1,0:T(8,128)(2,1)}, bf16[8,256,768]{2,1,0:T(8,128)(2,1)}, f32[40,1536]{1,0:T(8,128)}) custom-call(s32[1]{0:T(128)} %bitcast.me, bf16[256,1536]{1,0:T(8,128)(2,1)} %tok.3, s32[1,256]{1,0:T(1,128)} %seg_row.1, s32[256,1]{1,0:T(8,128)} %copy.30.seg_col, ...), custom_call_target="tpu_custom_call" | custom-call | flops 11000000 | bytes 36000 | tf_op jit(solution)/shard_map/attention/pallas_call | solution.py:219
  88.7 6.6 %residual.1 = (f32[256,1536]{1,0:T(8,128)}, bf16[272,1536]{1,0:T(8,128)(2,1)}) custom-call(s32[1]{0:T(128)} %bitcast.me, bf16[256,1536]{1,0:T(8,128)(2,1)} %tok.3, bf16[1536,256]{1,0:T(8,128)(2,1)} %get-tuple-element.223.ctx, f32[40,1536]{1,0:T(8,128)} %get-tuple-element.307.ext, bf16[16,1536]{1,0:T(8,128)(2,1)} %bitcast.61, bf16[192,1536]{1,0:T(8,128)(2,1)} %rest_4_.1, ...), custom_call_target="tpu_custom_call" | custom-call | flops 11000000 | bytes 36000 | tf_op jit(solution)/shard_map/residual/pallas_call | solution.py:258
  95.3 4.3 collective-permute-done.16.rest_6_
  106.3 8.7 %collective-permute-done.17.rest_5_ = bf16[2,3,192,512]{3,2,1,0:T(8,128)(2,1)} collective-permute-done((bf16[2,3,192,512]{3,2,1,0:T(8,128)(2,1)}, bf16[2,3,192,512]{3,2,1,0:T(8,128)(2,1)}, u32[]{:S(2)}, u32[]{:S(2)}) %collective-permute-start.17) | collective-permute-done | bytes 1179680 | tf_op jit(solution)/shard_map/ppermute | solution.py:52
  115.0 25.6 %collective-permute-done.18.rest_2_ = bf16[272,1536]{1,0:T(8,128)(2,1)S(1)} collective-permute-done((bf16[272,1536]{1,0:T(8,128)(2,1)}, bf16[272,1536]{1,0:T(8,128)(2,1)S(1)}, u32[]{:S(2)}, u32[]{:S(2)}) %collective-permute-start.18) | collective-permute-done | bytes 835616 | tf_op jit(solution)/shard_map/ppermute | solution.py:78
  143.4 8.8 %collective-permute-done.21.rest_5_ = bf16[3,3,192,512]{3,2,1,0:T(8,128)(2,1)S(1)} collective-permute-done((bf16[3,3,192,512]{3,2,1,0:T(8,128)(2,1)S(1)}, bf16[3,3,192,512]{3,2,1,0:T(8,128)(2,1)S(1)}, u32[]{:S(2)}, u32[]{:S(2)}) %collective-permute-start.21) | collective-permute-done | bytes 1769504 | tf_op jit(solution)/shard_map/ppermute | solution.py:52
  154.3 8.9 %collective-permute-done.23.rest_4_ = bf16[272,1536]{1,0:T(8,128)(2,1)S(1)} collective-permute-done((bf16[272,1536]{1,0:T(8,128)(2,1)S(1)}, bf16[272,1536]{1,0:T(8,128)(2,1)S(1)}, u32[]{:S(2)}, u32[]{:S(2)}) %collective-permute-start.23) | collective-permute-done | bytes 835616 | tf_op jit(solution)/shard_map/ppermute | solution.py:78
  164.3 4.3 router.1
  175.4 24.0 %experts.2 = (bf16[2,512,1536]{2,1,0:T(8,128)(2,1)}, bf16[2,512,1536]{2,1,0:T(8,128)(2,1)}, f32[2,4,256]{2,1,0:T(4,128)}, bf16[8,5,3,192,512]{4,3,2,1,0:T(8,128)(2,1)}) custom-call(s32[1]{0:T(128)} %bitcast.me, s32[1]{0:T(128)} %bitcast.12.z, s32[5,4,256]{2,1,0:T(4,128)} %get-tuple-element.293.pos, f32[5,4,256]{2,1,0:T(4,128)} %get-tuple-element.282.p, ...), custom_call_target="tpu_custom_call" | custom-call | flops 11000000 | bytes 36000 | tf_op jit(solution)/shard_map/experts/pallas_call | solution.py:482
  204.3 33.2 %experts.3 = (bf16[3,512,1536]{2,1,0:T(8,128)(2,1)}, bf16[3,512,1536]{2,1,0:T(8,128)(2,1)}, f32[3,4,256]{2,1,0:T(4,128)}, bf16[8,5,3,192,512]{4,3,2,1,0:T(8,128)(2,1)}) custom-call(s32[1]{0:T(128)} %bitcast.me, s32[1]{0:T(128)} %bitcast.12.z, s32[5,4,256]{2,1,0:T(4,128)} %get-tuple-element.293.pos, ...), custom_call_target="tpu_custom_call", output_to_operand_aliasing={{3}: (19, {})} | custom-call | flops 11000000 | bytes 36000 | tf_op jit(solution)/shard_map/experts/pallas_call | solution.py:482
  240.7 5.5 %collective-permute-start.36 = (bf16[272,1536]{1,0:T(8,128)(2,1)}, bf16[272,1536]{1,0:T(8,128)(2,1)S(1)}, u32[]{:S(2)}, u32[]{:S(2)}) collective-permute-start(bf16[272,1536]{1,0:T(8,128)(2,1)} %combine_back.2), channel_id=1, source_target_pairs={{3,2},{0,1},{7,6},{4,5},{11,10},{8,9},{15,14},{12,13},{19,18},{16,... | collective-permute-start | bytes 2506760 | tf_op jit(solution)/shard_map/ppermute | solution.py:78
  246.9 7.0 %combine_back.3 = (bf16[272,1536]{1,0:T(8,128)(2,1)}, bf16[272,1536]{1,0:T(8,128)(2,1)}, bf16[272,1536]{1,0:T(8,128)(2,1)}) custom-call(s32[1]{0:T(128)} %bitcast.12.z, s32[5,4,256]{2,1,0:T(4,128)} %get-tuple-element.293.pos, bf16[2,512,1536]{2,1,0:T(8,128)(2,1)} %get-tuple-element.281.rest_0_, bf16[3,512,1536]{2,1,0:T(8,128)(2,1)} %get-tuple-element.289.rest_1_, ...), custom_call_target="tpu_custom_call" | custom-call | flops 11000000 | bytes 36000 | tf_op jit(solution)/shard_map/combine_back/pallas_call | solution.py:577
  253.9 9.1 %combine_out.1 = (bf16[256,1536]{1,0:T(8,128)(2,1)}, bf16[256,1536]{1,0:T(8,128)(2,1)}, bf16[256,1536]{1,0:T(8,128)(2,1)}, bf16[256,1536]{1,0:T(8,128)(2,1)}) custom-call(s32[5,4,256]{2,1,0:T(4,128)} %get-tuple-element.293.pos, bf16[2,512,1536]{2,1,0:T(8,128)(2,1)} %get-tuple-element.294.rest_0_, bf16[3,512,1536]{2,1,0:T(8,128)(2,1)} %get-tuple-element.295.rest_1_), custom_call_target="tpu_custom_call" | custom-call | flops 11000000 | bytes 36000 | tf_op jit(solution)/shard_map/combine_out/pallas_call | solution.py:606
  264.6 4.9 %collective-permute-start.39 = (bf16[272,1536]{1,0:T(8,128)(2,1)S(1)}, bf16[272,1536]{1,0:T(8,128)(2,1)S(1)}, u32[]{:S(2)}, u32[]{:S(2)}) collective-permute-start(bf16[272,1536]{1,0:T(8,128)(2,1)S(1)} %copy-done.48), channel_id=1, source_target_pairs={{0,1},{1,0},{2,3},{3,2},{4,5},{5,4},{6,7},{7,6},{8,9},{9,8},{10,11... | collective-permute-start | bytes 2506760 | tf_op jit(solution)/shard_map/ppermute | solution.py:78
  271.0 34.3 %collective-permute-done.39.rest_1_ = bf16[272,1536]{1,0:T(8,128)(2,1)S(1)} collective-permute-done((bf16[272,1536]{1,0:T(8,128)(2,1)S(1)}, bf16[272,1536]{1,0:T(8,128)(2,1)S(1)}, u32[]{:S(2)}, u32[]{:S(2)}) %collective-permute-start.39) | collective-permute-done | bytes 835616 | tf_op jit(solution)/shard_map/ppermute | solution.py:78
  311.4 10.0 %second_back.1 = (f32[256,1536]{1,0:T(8,128)}, bf16[1536,256]{1,0:T(8,128)(2,1)}, f32[40,1536]{1,0:T(8,128)}, bf16[4,192,1536]{2,1,0:T(8,128)(2,1)}, bf16[4,192,1536]{2,1,0:T(8,128)(2,1)}) custom-call(s32[1]{0:T(128)} %bitcast.me, f32[24,256]{1,0:T(8,128)} %get-tuple-element.306.own_p, f32[40,1536]{1,0:T(8,128)} %get-tuple-element.307.ext, ...), custom_call_target="tpu_custom_call" | custom-call | flops 11000000 | bytes 36000 | tf_op jit(solution)/shard_map/second_back/pallas_call | solution.py:767
  321.4 8.0 %heads_back.1 = (bf16[2560,256]{1,0:T(8,128)(2,1)}, bf16[1024,640]{1,0:T(8,128)(2,1)}) custom-call(bf16[1536,256]{1,0:T(8,128)(2,1)} %get-tuple-element.313.ctx_grad, bf16[2560,256]{1,0:T(8,128)(2,1)} %get-tuple-element.314.qkv, bf16[8,256,768]{2,1,0:T(8,128)(2,1)} %get-tuple-element.315.probs), custom_call_target="tpu_custom_call" | custom-call | flops 11000000 | bytes 36000 | tf_op jit(solution)/shard_map/heads_back/pallas_call | solution.py:838
  330.6 4.6 all-to-all-start
  340.0 9.4 %first_back.1 = (f32[256,1536]{1,0:T(8,128)}, bf16[1536,128]{1,0:T(8,128)(2,1)}) custom-call(s32[1]{0:T(128)} %bitcast.me, bf16[2560,256]{1,0:T(8,128)(2,1)} %get-tuple-element.330.back, bf16[256,1536]{1,0:T(8,128)(2,1)} %tok.3, f32[40,1536]{1,0:T(8,128)} %get-tuple-element.307.ext, f32[40,1536]{1,0:T(8,128)} %get-tuple-element.331.ext_grad, ...), custom_call_target="tpu_custom_call" | custom-call | flops 65999998976 | bytes 216000000 | tf_op jit(solution)/shard_map/first_back/pallas_call | solution.py:880
  349.5 9.5 %collective-permute-done.43 = bf16[2,192,768]{2,1,0:T(8,128)(2,1)S(1)} collective-permute-done((bf16[2,192,768]{2,1,0:T(8,128)(2,1)S(1)}, bf16[2,192,768]{2,1,0:T(8,128)(2,1)S(1)}, u32[]{:S(2)}, u32[]{:S(2)}) %collective-permute-start.43) | collective-permute-done | bytes 589856 | tf_op jit(solution)/shard_map/ppermute | solution.py:52
  360.2 7.2 %all-to-all-done = bf16[4,256,640]{2,1,0:T(8,128)(2,1)} async-done(((bf16[4,256,640]{2,1,0:T(8,128)(2,1)}), bf16[4,256,640]{2,1,0:T(8,128)(2,1)}, u32[]{:S(2)}, u32[]{:S(2)}) %all-to-all-start) | async-done | bytes 1310752 | tf_op jit(solution)/shard_map/all_to_all | solution.py:96
  367.5 6.5 %project_back.1 = (bf16[192,768]{1,0:T(8,128)(2,1)}, bf16[192,768]{1,0:T(8,128)(2,1)}, bf16[192,768]{1,0:T(8,128)(2,1)}, bf16[192,768]{1,0:T(8,128)(2,1)}, bf16[4,192,768]{2,1,0:T(8,128)(2,1)}) custom-call(s32[1]{0:T(128)} %bitcast.me, bf16[4,1536,256]{2,1,0:T(8,128)(2,1)} %bitcast.64, bf16[1024,640]{1,0:T(8,128)(2,1)} %bitcast.14.back_all, ...), custom_call_target="tpu_custom_call" | custom-call | flops 65999998976 | bytes 216000000 | tf_op jit(solution)/shard_map/project_back/pallas_call | solution.py:915
  381.0 9.2 %collective-permute-done.46 = bf16[192,768]{1,0:T(8,128)(2,1)S(1)} collective-permute-done((bf16[192,768]{1,0:T(8,128)(2,1)S(1)}, bf16[192,768]{1,0:T(8,128)(2,1)S(1)}, u32[]{:S(2)}, u32[]{:S(2)}) %collective-permute-start.46) | collective-permute-done | bytes 294944 | tf_op jit(solution)/shard_map/ppermute | solution.py:52
  391.9 3.5 all-to-all-start.1
  398.9 14.9 %collective-permute-done.55 = bf16[256,1536]{1,0:T(8,128)(2,1)} collective-permute-done((bf16[256,1536]{1,0:T(8,128)(2,1)}, bf16[256,1536]{1,0:T(8,128)(2,1)}, u32[]{:S(2)}, u32[]{:S(2)}) %collective-permute-start.55) | collective-permute-done | bytes 786464 | tf_op jit(solution)/shard_map/ppermute | solution.py:78
  413.8 3.8 collective-permute-done.54
  419.8 6.5 %all-to-all-done.1 = bf16[4,48,1536]{2,1,0:T(8,128)(2,1)S(1)} async-done(((bf16[4,48,1536]{2,1,0:T(8,128)(2,1)}), bf16[4,48,1536]{2,1,0:T(8,128)(2,1)S(1)}, u32[]{:S(2)}, u32[]{:S(2)}) %all-to-all-start.1) | async-done | bytes 589856 | tf_op jit(solution)/shard_map/all_to_all | solution.py:96
  435.9 15.3 %collective-permute-done.51.rest_2_ = bf16[192,1152]{1,0:T(8,128)(2,1)S(1)} collective-permute-done((bf16[192,1152]{1,0:T(8,128)(2,1)}, bf16[192,1152]{1,0:T(8,128)(2,1)S(1)}, u32[]{:S(2)}, u32[]{:S(2)}) %collective-permute-start.51) | collective-permute-done | bytes 442400 | tf_op jit(solution)/shard_map/ppermute | solution.py:78
  458.0 7.1 %collective-permute-done.53.rest_4_ = bf16[192,1152]{1,0:T(8,128)(2,1)S(1)} collective-permute-done((bf16[192,1152]{1,0:T(8,128)(2,1)S(1)}, bf16[192,1152]{1,0:T(8,128)(2,1)S(1)}, u32[]{:S(2)}, u32[]{:S(2)}) %collective-permute-start.53) | collective-permute-done | bytes 442400 | tf_op jit(solution)/shard_map/ppermute | solution.py:78
  (231 shorter events, 103.7 us)
Async XLA Ops:
  7.2 80.7 %all-gather.3.cloned.1.call-start = ((), (), s32[]{:S(2)}) async-start(), calls=%async_computation.3 | async-start | bytes 3932160 | tf_op jit(solution)/shard_map/all_gather | solution.py:963
  7.9 359.5 %all-gather.5.cloned.1.call-start = ((), (), s32[]{:S(2)}) async-start(), calls=%async_computation.4 | async-start | bytes 3932160 | tf_op jit(solution)/shard_map/all_gather | solution.py:1023
  10.4 26.0 %collective-permute-start = (bf16[192,2688]{1,0:T(8,128)(2,1)}, bf16[192,2688]{1,0:T(8,128)(2,1)S(1)}, u32[]{:S(2)}, u32[]{:S(2)}) collective-permute-start(bf16[192,2688]{1,0:T(8,128)(2,1)} %pack.1.rest_0_), channel_id=1, source_target_pairs={{0,8},{4,12},{8,0},{12,4},{16,24},{20,28},{24,16},{28,20},{1,9},{5... | collective-permute-start | bytes 3096584 | tf_op jit(solution)/shard_map/ppermute | solution.py:52
  13.3 24.5 %collective-permute-start.1 = (bf16[192,2688]{1,0:T(8,128)(2,1)}, bf16[192,2688]{1,0:T(8,128)(2,1)S(1)}, u32[]{:S(2)}, u32[]{:S(2)}) collective-permute-start(bf16[192,2688]{1,0:T(8,128)(2,1)} %pack.1.rest_0_), channel_id=1, source_target_pairs={{0,16},{4,20},{8,24},{12,28},{16,0},{20,4},{24,8},{28,12},{1,17},{... | collective-permute-start | bytes 3096584 | tf_op jit(solution)/shard_map/ppermute | solution.py:52
  14.8 23.0 %collective-permute-start.2 = (bf16[192,2688]{1,0:T(8,128)(2,1)}, bf16[192,2688]{1,0:T(8,128)(2,1)}, u32[]{:S(2)}, u32[]{:S(2)}) collective-permute-start(bf16[192,2688]{1,0:T(8,128)(2,1)} %pack.1.rest_0_), channel_id=1, source_target_pairs={{0,4},{4,0},{8,12},{12,8},{16,20},{20,16},{24,28},{28,24},{1,5},{5... | collective-permute-start | bytes 3096584 | tf_op jit(solution)/shard_map/ppermute | solution.py:52
  71.0 28.7 %collective-permute-start.16 = (bf16[2,3,192,512]{3,2,1,0:T(8,128)(2,1)}, bf16[2,3,192,512]{3,2,1,0:T(8,128)(2,1)}, u32[]{:S(2)}, u32[]{:S(2)}) collective-permute-start(bf16[2,3,192,512]{3,2,1,0:T(8,128)(2,1)} %pad_maximum_fusion.2.rest_4_), channel_id=1, source_target_pairs={{0,16},{4,20},{8,24},{12,28},{16,0},{20,4},{24,8},{28,12},{1,17},{... | collective-permute-start | bytes 3538952 | tf_op jit(solution)/shard_map/ppermute | solution.py:52
  85.9 29.1 %collective-permute-start.17 = (bf16[2,3,192,512]{3,2,1,0:T(8,128)(2,1)}, bf16[2,3,192,512]{3,2,1,0:T(8,128)(2,1)}, u32[]{:S(2)}, u32[]{:S(2)}) collective-permute-start(bf16[2,3,192,512]{3,2,1,0:T(8,128)(2,1)} %pad_maximum_fusion.2.rest_4_), channel_id=1, source_target_pairs={{0,8},{4,12},{8,0},{12,4},{16,24},{20,28},{24,16},{28,20},{1,9},{5... | collective-permute-start | bytes 3538952 | tf_op jit(solution)/shard_map/ppermute | solution.py:52
  99.7 43.7 %collective-permute-start.20 = (bf16[3,3,192,512]{3,2,1,0:T(8,128)(2,1)S(1)}, bf16[3,3,192,512]{3,2,1,0:T(8,128)(2,1)S(1)}, u32[]{:S(2)}, u32[]{:S(2)}) collective-permute-start(bf16[3,3,192,512]{3,2,1,0:T(8,128)(2,1)S(1)} %pad_maximum_fusion.rest_4_), channel_id=1, source_target_pairs={{0,16},{4,20},{8,24},{12,28},{16,0},{20,4},{24,8},{28,12},{1,17},{... | collective-permute-start | bytes 5308424 | tf_op jit(solution)/shard_map/ppermute | solution.py:52
  101.2 51.0 %collective-permute-start.21 = (bf16[3,3,192,512]{3,2,1,0:T(8,128)(2,1)S(1)}, bf16[3,3,192,512]{3,2,1,0:T(8,128)(2,1)S(1)}, u32[]{:S(2)}, u32[]{:S(2)}) collective-permute-start(bf16[3,3,192,512]{3,2,1,0:T(8,128)(2,1)S(1)} %pad_maximum_fusion.rest_4_), channel_id=1, source_target_pairs={{0,8},{4,12},{8,0},{12,4},{16,24},{20,28},{24,16},{28,20},{1,9},{5... | collective-permute-start | bytes 5308424 | tf_op jit(solution)/shard_map/ppermute | solution.py:52
  102.2 38.4 %collective-permute-start.18 = (bf16[272,1536]{1,0:T(8,128)(2,1)}, bf16[272,1536]{1,0:T(8,128)(2,1)S(1)}, u32[]{:S(2)}, u32[]{:S(2)}) collective-permute-start(bf16[272,1536]{1,0:T(8,128)(2,1)} %get-tuple-element.244.rest_0_.low_two), channel_id=1, source_target_pairs={{0,2},{1,3},{2,0},{3,1},{4,6},{5,7},{6,4},{7,5},{8,10},{9,11},{10,... | collective-permute-start | bytes 2506760 | tf_op jit(solution)/shard_map/ppermute | solution.py:78
  104.8 36.0 %collective-permute-start.19 = (bf16[272,1536]{1,0:T(8,128)(2,1)}, bf16[272,1536]{1,0:T(8,128)(2,1)S(1)}, u32[]{:S(2)}, u32[]{:S(2)}) collective-permute-start(bf16[272,1536]{1,0:T(8,128)(2,1)} %get-tuple-element.244.rest_0_.low_two), channel_id=1, source_target_pairs={{0,1},{1,0},{2,3},{3,2},{4,5},{5,4},{6,7},{7,6},{8,9},{9,8},{10,11... | collective-permute-start | bytes 2506760 | tf_op jit(solution)/shard_map/ppermute | solution.py:78
  141.5 21.7 %collective-permute-start.23 = (bf16[272,1536]{1,0:T(8,128)(2,1)S(1)}, bf16[272,1536]{1,0:T(8,128)(2,1)S(1)}, u32[]{:S(2)}, u32[]{:S(2)}) collective-permute-start(bf16[272,1536]{1,0:T(8,128)(2,1)S(1)} %collective-permute-done.18.rest_2_), channel_id=1, source_target_pairs={{2,3},{1,0},{6,7},{5,4},{10,11},{9,8},{14,15},{13,12},{18,19},{17,... | collective-permute-start | bytes 2506760 | tf_op jit(solution)/shard_map/ppermute | solution.py:78
  142.8 26.9 %collective-permute-start.24 = (bf16[2,3,192,512]{3,2,1,0:T(8,128)(2,1)}, bf16[2,3,192,512]{3,2,1,0:T(8,128)(2,1)}, u32[]{:S(2)}, u32[]{:S(2)}) collective-permute-start(bf16[2,3,192,512]{3,2,1,0:T(8,128)(2,1)} %collective-permute-done.17.rest_5_), channel_id=1, source_target_pairs={{0,16},{4,20},{8,24},{12,28},{16,0},{20,4},{24,8},{28,12},{1,17},{... | collective-permute-start | bytes 3538952 | tf_op jit(solution)/shard_map/ppermute | solution.py:52
  164.2 288.5 %reduce-scatter.2.cloned.1.call-start = ((), (), s32[]{:S(2)}) async-start(), calls=%async_computation.5 | async-start | bytes 26542080 | tf_op jit(solution)/shard_map/reduce_scatter | solution.py:1058
  169.9 29.4 %collective-permute-start.32 = (bf16[3,3,192,512]{3,2,1,0:T(8,128)(2,1)S(1)}, bf16[3,3,192,512]{3,2,1,0:T(8,128)(2,1)S(1)}, u32[]{:S(2)}, u32[]{:S(2)}) collective-permute-start(bf16[3,3,192,512]{3,2,1,0:T(8,128)(2,1)S(1)} %copy-done.6), channel_id=1, source_target_pairs={{0,4},{4,0},{8,12},{12,8},{16,20},{20,16},{24,28},{28,24},{1,5},{5... | collective-permute-start | bytes 5308424 | tf_op jit(solution)/shard_map/ppermute | solution.py:52
  170.3 29.1 %collective-permute-start.33 = (bf16[3,3,192,512]{3,2,1,0:T(8,128)(2,1)S(1)}, bf16[3,3,192,512]{3,2,1,0:T(8,128)(2,1)}, u32[]{:S(2)}, u32[]{:S(2)}) collective-permute-start(bf16[3,3,192,512]{3,2,1,0:T(8,128)(2,1)S(1)} %collective-permute-done.20.rest_6_), channel_id=1, source_target_pairs={{0,4},{4,0},{8,12},{12,8},{16,20},{20,16},{24,28},{28,24},{1,5},{5... | collective-permute-start | bytes 5308424 | tf_op jit(solution)/shard_map/ppermute | solution.py:52
  173.3 26.1 %collective-permute-start.31 = (bf16[3,3,192,512]{3,2,1,0:T(8,128)(2,1)S(1)}, bf16[3,3,192,512]{3,2,1,0:T(8,128)(2,1)}, u32[]{:S(2)}, u32[]{:S(2)}) collective-permute-start(bf16[3,3,192,512]{3,2,1,0:T(8,128)(2,1)S(1)} %pad_maximum_fusion.rest_4_), channel_id=1, source_target_pairs={{0,4},{4,0},{8,12},{12,8},{16,20},{20,16},{24,28},{28,24},{1,5},{5... | collective-permute-start | bytes 5308424 | tf_op jit(solution)/shard_map/ppermute | solution.py:52
  173.4 25.9 %collective-permute-start.29 = (bf16[3,3,96,512]{3,2,1,0:T(8,128)(2,1)}, bf16[3,3,96,512]{3,2,1,0:T(8,128)(2,1)}, u32[]{:S(2)}, u32[]{:S(2)}) collective-permute-start(bf16[3,3,96,512]{3,2,1,0:T(8,128)(2,1)} %slice.91), channel_id=1, source_target_pairs={{0,16},{4,20},{8,24},{12,28},{16,0},{20,4},{24,8},{28,12},{1,17},{... | collective-permute-start | bytes 2654216 | tf_op jit(solution)/shard_map/ppermute | solution.py:52
  174.0 25.4 %collective-permute-start.30 = (bf16[3,3,96,512]{3,2,1,0:T(8,128)(2,1)}, bf16[3,3,96,512]{3,2,1,0:T(8,128)(2,1)}, u32[]{:S(2)}, u32[]{:S(2)}) collective-permute-start(bf16[3,3,96,512]{3,2,1,0:T(8,128)(2,1)} %slice.92), channel_id=1, source_target_pairs={{0,8},{4,12},{8,0},{12,4},{16,24},{20,28},{24,16},{28,20},{1,9},{5... | collective-permute-start | bytes 2654216 | tf_op jit(solution)/shard_map/ppermute | solution.py:52
  240.7 23.9 %collective-permute-start.36 = (bf16[272,1536]{1,0:T(8,128)(2,1)}, bf16[272,1536]{1,0:T(8,128)(2,1)S(1)}, u32[]{:S(2)}, u32[]{:S(2)}) collective-permute-start(bf16[272,1536]{1,0:T(8,128)(2,1)} %combine_back.2), channel_id=1, source_target_pairs={{3,2},{0,1},{7,6},{4,5},{11,10},{8,9},{15,14},{12,13},{19,18},{16,... | collective-permute-start | bytes 2506760 | tf_op jit(solution)/shard_map/ppermute | solution.py:78
  264.6 40.6 %collective-permute-start.39 = (bf16[272,1536]{1,0:T(8,128)(2,1)S(1)}, bf16[272,1536]{1,0:T(8,128)(2,1)S(1)}, u32[]{:S(2)}, u32[]{:S(2)}) collective-permute-start(bf16[272,1536]{1,0:T(8,128)(2,1)S(1)} %copy-done.48), channel_id=1, source_target_pairs={{0,1},{1,0},{2,3},{3,2},{4,5},{5,4},{6,7},{7,6},{8,9},{9,8},{10,11... | collective-permute-start | bytes 2506760 | tf_op jit(solution)/shard_map/ppermute | solution.py:78
  269.7 38.8 %collective-permute-start.38 = (bf16[272,1536]{1,0:T(8,128)(2,1)S(1)}, bf16[272,1536]{1,0:T(8,128)(2,1)S(1)}, u32[]{:S(2)}, u32[]{:S(2)}) collective-permute-start(bf16[272,1536]{1,0:T(8,128)(2,1)S(1)} %add_convert_fusion), channel_id=1, source_target_pairs={{0,2},{1,3},{2,0},{3,1},{4,6},{5,7},{6,4},{7,5},{8,10},{9,11},{10,... | collective-permute-start | bytes 2506760 | tf_op jit(solution)/shard_map/ppermute | solution.py:78
  330.6 36.9 %all-to-all-start = ((bf16[4,256,640]{2,1,0:T(8,128)(2,1)}), bf16[4,256,640]{2,1,0:T(8,128)(2,1)}, u32[]{:S(2)}, u32[]{:S(2)}) async-start(bf16[4,256,640]{2,1,0:T(8,128)(2,1)} %bitcast.60), calls=%async_computation | async-start | bytes 2621440 | tf_op jit(solution)/shard_map/all_to_all | solution.py:96
  376.2 37.5 %collective-permute-start.55 = (bf16[256,1536]{1,0:T(8,128)(2,1)}, bf16[256,1536]{1,0:T(8,128)(2,1)}, u32[]{:S(2)}, u32[]{:S(2)}) collective-permute-start(bf16[256,1536]{1,0:T(8,128)(2,1)} %get-tuple-element.367), channel_id=1, source_target_pairs={{0,1},{1,0},{2,3},{3,2},{4,5},{5,4},{6,7},{7,6},{8,9},{9,8},{10,11... | collective-permute-start | bytes 2359304 | tf_op jit(solution)/shard_map/ppermute | solution.py:78
  376.2 41.3 %collective-permute-start.54 = (bf16[256,1536]{1,0:T(8,128)(2,1)}, bf16[256,1536]{1,0:T(8,128)(2,1)}, u32[]{:S(2)}, u32[]{:S(2)}) collective-permute-start(bf16[256,1536]{1,0:T(8,128)(2,1)} %add_convert_fusion.2), channel_id=1, source_target_pairs={{0,2},{1,3},{2,0},{3,1},{4,6},{5,7},{6,4},{7,5},{8,10},{9,11},{10,... | collective-permute-start | bytes 2359304 | tf_op jit(solution)/shard_map/ppermute | solution.py:78
  391.9 34.4 %all-to-all-start.1 = ((bf16[4,48,1536]{2,1,0:T(8,128)(2,1)}), bf16[4,48,1536]{2,1,0:T(8,128)(2,1)S(1)}, u32[]{:S(2)}, u32[]{:S(2)}) async-start(bf16[4,48,1536]{2,1,0:T(8,128)(2,1)} %bitcast.23), calls=%async_computation.1 | async-start | bytes 1179648 | tf_op jit(solution)/shard_map/all_to_all | solution.py:96
  395.4 23.0 %collective-permute-start.48 = (bf16[192,768]{1,0:T(8,128)(2,1)}, bf16[192,768]{1,0:T(8,128)(2,1)S(1)}, u32[]{:S(2)}, u32[]{:S(2)}) collective-permute-start(bf16[192,768]{1,0:T(8,128)(2,1)} %get-tuple-element.355), channel_id=1, source_target_pairs={{0,8},{4,12},{8,0},{12,4},{16,24},{20,28},{24,16},{28,20},{1,9},{5... | collective-permute-start | bytes 884744 | tf_op jit(solution)/shard_map/ppermute | solution.py:52
  396.6 21.7 %collective-permute-start.49 = (bf16[192,768]{1,0:T(8,128)(2,1)}, bf16[192,768]{1,0:T(8,128)(2,1)S(1)}, u32[]{:S(2)}, u32[]{:S(2)}) collective-permute-start(bf16[192,768]{1,0:T(8,128)(2,1)} %get-tuple-element.356), channel_id=1, source_target_pairs={{0,16},{4,20},{8,24},{12,28},{16,0},{20,4},{24,8},{28,12},{1,17},{... | collective-permute-start | bytes 884744 | tf_op jit(solution)/shard_map/ppermute | solution.py:52
  398.1 21.6 %collective-permute-start.50 = (bf16[192,768]{1,0:T(8,128)(2,1)}, bf16[192,768]{1,0:T(8,128)(2,1)}, u32[]{:S(2)}, u32[]{:S(2)}) collective-permute-start(bf16[192,768]{1,0:T(8,128)(2,1)} %get-tuple-element.357), channel_id=1, source_target_pairs={{0,24},{4,28},{8,16},{12,20},{16,8},{20,12},{24,0},{28,4},{1,25},{... | collective-permute-start | bytes 884744 | tf_op jit(solution)/shard_map/ppermute | solution.py:52
  429.6 21.6 %collective-permute-start.51 = (bf16[192,1152]{1,0:T(8,128)(2,1)}, bf16[192,1152]{1,0:T(8,128)(2,1)S(1)}, u32[]{:S(2)}, u32[]{:S(2)}) collective-permute-start(bf16[192,1152]{1,0:T(8,128)(2,1)} %join.1.rest_0_), channel_id=1, source_target_pairs={{0,2},{1,3},{2,0},{3,1},{4,6},{5,7},{6,4},{7,5},{8,10},{9,11},{10,... | collective-permute-start | bytes 1327112 | tf_op jit(solution)/shard_map/ppermute | solution.py:78
  429.6 21.7 %collective-permute-start.52 = (bf16[192,1152]{1,0:T(8,128)(2,1)}, bf16[192,1152]{1,0:T(8,128)(2,1)S(1)}, u32[]{:S(2)}, u32[]{:S(2)}) collective-permute-start(bf16[192,1152]{1,0:T(8,128)(2,1)} %join.1.rest_0_), channel_id=1, source_target_pairs={{0,1},{1,0},{2,3},{3,2},{4,5},{5,4},{6,7},{7,6},{8,9},{9,8},{10,11... | collective-permute-start | bytes 1327112 | tf_op jit(solution)/shard_map/ppermute | solution.py:78
  435.2 29.9 %collective-permute-start.56 = (bf16[192,1152]{1,0:T(8,128)(2,1)S(1)}, bf16[192,1152]{1,0:T(8,128)(2,1)S(1)}, u32[]{:S(2)}, u32[]{:S(2)}) collective-permute-start(bf16[192,1152]{1,0:T(8,128)(2,1)S(1)} %copy-done.18), channel_id=1, source_target_pairs={{1,2},{2,1},{5,6},{6,5},{9,10},{10,9},{13,14},{14,13},{17,18},{18,... | collective-permute-start | bytes 1327112 | tf_op jit(solution)/shard_map/ppermute | solution.py:78
  (80 other events, 1092.5 us)
Sparse Core Ops, SparseCore 0:
  9.6 66.1 all-gather.2
  164.3 64.1 all-gather.4
  237.6 164.7 reduce-scatter.1
